TPU v7x, 32 devices: a whole 2x2x4 slice. The times are simulated.
32 devices in a mesh: face: 4 (over y, x), tile: 8 (over z, core).
Axes of the slice: x: 2, y: 2, z: 4, core: 2. Of those that a mesh axis runs over, the one named last changes fastest.
Arguments:
- latitude_rows: bfloat16 [128, 4096, 128], P(None, ('face', 'tile')), may hold values from -6 to 6
- tile_order: int32 [128], replicated, may hold values from 0 to 127, each once
- neighbours: int32 [128, 8], P(('face', 'tile')), may hold values from 0 to 127, as said below
- rotations: int32 [128, 8], P(('face', 'tile')), may hold values from 0 to 3
- w_first: bfloat16 [3, 3, 128, 128], replicated, may hold values from -0.1875 to 0.1875
- b_first: float32 [128], replicated, may hold values from -3 to 3
- w_second: bfloat16 [3, 3, 128, 128], replicated, may hold values from -0.1875 to 0.1875
- b_second: float32 [128], replicated, may hold values from -3 to 3
Outputs:
- level_output: bfloat16 [128, 64, 64, 128], P(('face', 'tile'))
Inputs may be any that keep to these rules, and one draw needn't show every extreme that they name: `neighbours`: tiles are held in order, 4 a device, devices ordered face-major. Entry k of a row names a tile held by the device whose face index and tile index differ, counted cyclically, from those of the device that holds the row's tile by (-1,0), (+1,0), (0,-1), (0,+1), (-1,-1), (-1,+1), (+1,-1), (+1,+1) for k = 0 to 7.
All inputs are finite; a program needn't handle non-finite values.
Results may differ from a plain program's by a relative error of at most 0.0033.
Values may be sent and summed in bfloat16 or wider, within the bound.
No kernel may reach another device: no remote copies, remote signals or barrier semaphores. Data moves between devices by JAX's collectives and lax.ppermute only.
A program may use at most 64 MiB of HBM per device.

v0:
```python
import jax
import jax.numpy as jnp
import numpy as np
from jax import lax
from jax.sharding import PartitionSpec as P

SIDE = 64


STRIP_TABLE = np.array(
    [
        [1, 2, 0, 3],
        [0, 3, 1, 2],
        [3, 1, 2, 0],
        [2, 0, 3, 1],
        [1, 2, 0, 3],
        [1, 2, 0, 3],
        [0, 3, 1, 2],
        [0, 3, 1, 2],
    ],
    np.int32,
)
FLIP_TABLE = np.array(
    [
        [0, 0, 1, 1],
        [0, 0, 1, 1],
        [0, 1, 1, 0],
        [0, 1, 1, 0],
        [0, 0, 1, 1],
        [0, 0, 1, 1],
        [0, 0, 1, 1],
        [0, 0, 1, 1],
    ],
    np.int32,
)
DIRECTIONS = [(-1, 0), (1, 0), (0, -1), (0, 1), (-1, -1), (-1, 1), (1, -1), (1, 1)]


def padded_2(array, sides, width):
    for axis, dim in sides:
        count, length = (lax.axis_size(axis), array.shape[dim])
        up = [(i, (i + 1) % count) for i in range(count)]
        down = [(j, i) for i, j in up]
        last = lax.slice_in_dim(array, length - width, length, axis=dim)
        first = lax.slice_in_dim(array, 0, width, axis=dim)
        before = lax.ppermute(last, axis, up)
        after = lax.ppermute(first, axis, down)
        array = jnp.concatenate([before, array, after], axis=dim)
    return array


def convolve(padded, weight, bias):
    summed = lax.conv_general_dilated(
        padded,
        weight,
        (1, 1),
        "VALID",
        dimension_numbers=("NHWC", "HWIO", "NHWC"),
        preferred_element_type=jnp.float32,
    )
    return summed + bias


def table_pick(table_row, turns):
    matches = turns[:, None] == jnp.arange(4, dtype=jnp.int32)[None]
    return jnp.sum(jnp.where(matches, jnp.asarray(table_row)[None], 0), axis=1)


def requested_lines(borders, tables):
    tile_count = borders.shape[0]
    tile_side = borders.shape[2]
    chan_count = borders.shape[3]
    flat_borders = borders.reshape(tile_count * 4, tile_side, chan_count)
    edge_grid = [
        [jnp.zeros((tile_count, tile_side, chan_count), borders.dtype) for column in range(3)]
        for row in range(3)
    ]
    corner_grid = [
        [jnp.zeros((tile_count, chan_count), borders.dtype) for column in range(3)]
        for row in range(3)
    ]
    for direction in range(8):
        face_off, tile_off = DIRECTIONS[direction]
        row_at = 1 - face_off
        col_at = 1 - tile_off
        wanted = tables[row_at, col_at]
        slots = wanted[0, :, direction]
        turns = wanted[1, :, direction]
        strip = table_pick(STRIP_TABLE[direction], turns)
        flips = table_pick(FLIP_TABLE[direction], turns)
        lines = jnp.take(flat_borders, slots * 4 + strip, axis=0)
        lines = jnp.where((flips == 1)[:, None, None], lines[:, ::-1], lines)
        if direction < 4:
            edge_grid[row_at][col_at] = lines
        elif direction == 4 or direction == 6:
            corner_grid[row_at][col_at] = lines[:, tile_side - 1]
        else:
            corner_grid[row_at][col_at] = lines[:, 0]
    edge_stack = jnp.stack([jnp.stack(row, 0) for row in edge_grid], 0)
    corner_stack = jnp.stack([jnp.stack(row, 0) for row in corner_grid], 0)
    got_edges = padded_2(edge_stack, (("face", 0), ("tile", 1)), 1)
    got_corners = padded_2(corner_stack, (("face", 0), ("tile", 1)), 1)
    received = []
    for direction in range(8):
        face_off, tile_off = DIRECTIONS[direction]
        if direction < 4:
            received.append(got_edges[2 + 2 * face_off, 2 + 2 * tile_off])
        else:
            received.append(got_corners[2 + 2 * face_off, 2 + 2 * tile_off])
    return received


def pad_tiles(centre_tiles, tables):
    tile_side = centre_tiles.shape[1]
    local_borders = jnp.stack(
        [
            centre_tiles[:, 0],
            centre_tiles[:, tile_side - 1],
            centre_tiles[:, :, 0],
            centre_tiles[:, :, tile_side - 1],
        ],
        1,
    )
    received = requested_lines(local_borders, tables)
    upper = jnp.concatenate([received[4][:, None], received[0], received[5][:, None]], 1)
    lower = jnp.concatenate([received[6][:, None], received[1], received[7][:, None]], 1)
    middle = jnp.concatenate([received[2][:, :, None], centre_tiles, received[3][:, :, None]], 2)
    return jnp.concatenate([upper[:, None], middle, lower[:, None]], 1)


def shards(latitude_rows, tile_order, neighbours, rotations, w_first, b_first, w_second, b_second):
    ordered = jnp.take(latitude_rows, tile_order, axis=0)
    tile_count = neighbours.shape[0]
    chan_count = ordered.shape[2]
    tables = None
    packed = jnp.stack([neighbours % tile_count, rotations], 0)[None, None]
    tables = padded_2(packed, (("face", 0), ("tile", 1)), 1)
    gathered = lax.all_to_all(ordered, ("face", "tile"), split_axis=0, concat_axis=1, tiled=True)
    nested = gathered.reshape(tile_count, SIDE, SIDE, chan_count)
    first_pad = pad_tiles(nested, tables)
    hidden = jax.nn.gelu(convolve(first_pad, w_first, b_first), approximate=False).astype(
        jnp.bfloat16
    )
    second_pad = pad_tiles(hidden, tables)
    second = convolve(second_pad, w_second, b_second)
    return (nested.astype(jnp.float32) + second).astype(jnp.bfloat16)


def solution(mesh):
    return jax.shard_map(
        shards,
        mesh=mesh,
        in_specs=(
            P(None, ("face", "tile"), None),
            P(),
            P(("face", "tile"), None),
            P(("face", "tile"), None),
            P(),
            P(),
            P(),
            P(),
        ),
        out_specs=P(("face", "tile"), None, None, None),
        check_vma=False,
    )
```

profile of v0, /device:TPU:0, one launch (start us, length us, event | category | flops | bytes accessed | tf_op | source)
XLA Modules:
  0.0 281.3 jit_solution(5760223138535567613)
XLA Ops:
  1.4 5.3 %gather_fusion = bf16[128,128,128]{2,1,0:T(8,128)(2,1)} fusion(bf16[128,128,128]{2,1,0:T(8,128)(2,1)} %param.42, s32[1024]{0:T(1024)S(1)} %pad_clamp_fusion.8), kind=kCustom, calls=%fused_computation.16 | custom fusion | bytes 8389120 | tf_op jit(solution)/shard_map/jit(_take)/gather | solution.py:132
  6.7 4.7 %broadcast_select_fusion = bf16[128,128,128]{2,1,0:T(8,128)(2,1)} fusion(bf16[128,128,128]{2,1,0:T(8,128)(2,1)} %gather_fusion, pred[128]{0:T(512)(128)(4,1)S(1)} %compare_and_fusion.8), kind=kLoop, calls=%fused_computation.55 | loop fusion | flops 2097152 | bytes 8388736 | tf_op jit(solution)/shard_map/jit(_take)/select_n | solution.py:132
  11.4 7.4 %all-to-all-start = ((bf16[128,128,128]{2,1,0:T(8,128)(2,1)}), bf16[128,128,128]{2,1,0:T(8,128)(2,1)}, u32[]{:S(2)}, u32[]{:S(2)}) async-start(bf16[128,128,128]{2,1,0:T(8,128)(2,1)} %broadcast_select_fusion), calls=%async_computation | async-start | bytes 8388608 | tf_op jit(solution)/shard_map/all_to_all | solution.py:138
  18.9 2.6 collective-permute-start.1
  21.6 22.9 %collective-permute-done.1 = s32[1,1,2,4,8]{4,3,2,1,0:T(4,128)S(1)} collective-permute-done((s32[1,1,2,4,8]{4,3,2,1,0:T(4,128)S(1)}, s32[1,1,2,4,8]{4,3,2,1,0:T(4,128)S(1)}, u32[]{:S(2)}, u32[]{:S(2)}) %collective-permute-start.1) | collective-permute-done | bytes 288 | tf_op jit(solution)/shard_map/ppermute | solution.py:47
  45.7 6.4 %collective-permute-start.3 = (s32[3,1,2,4,8]{4,3,2,1,0:T(4,128)S(1)}, s32[3,1,2,4,8]{4,3,2,1,0:T(4,128)S(1)}, u32[]{:S(2)}, u32[]{:S(2)}) collective-permute-start(s32[3,1,2,4,8]{4,3,2,1,0:T(4,128)S(1)} %pad_add_fusion), channel_id=1, source_target_pairs={{1,0},{2,1},{3,2},{4,3},{5,4},{6,5},{7,6},{0,7},{9,8},{10,9},{11,1... | collective-permute-start | bytes 2312 | tf_op jit(solution)/shard_map/ppermute | solution.py:47
  52.4 35.2 %collective-permute-done.3 = s32[3,1,2,4,8]{4,3,2,1,0:T(4,128)S(1)} collective-permute-done((s32[3,1,2,4,8]{4,3,2,1,0:T(4,128)S(1)}, s32[3,1,2,4,8]{4,3,2,1,0:T(4,128)S(1)}, u32[]{:S(2)}, u32[]{:S(2)}) %collective-permute-start.3) | collective-permute-done | bytes 800 | tf_op jit(solution)/shard_map/ppermute | solution.py:47
  88.3 3.1 %collective-permute-done.2 = s32[3,1,2,4,8]{4,3,2,1,0:T(4,128)S(1)} collective-permute-done((s32[3,1,2,4,8]{4,3,2,1,0:T(4,128)S(1)}, s32[3,1,2,4,8]{4,3,2,1,0:T(4,128)S(1)}, u32[]{:S(2)}, u32[]{:S(2)}) %collective-permute-start.2) | collective-permute-done | bytes 800 | tf_op jit(solution)/shard_map/ppermute | solution.py:46
  93.0 21.1 %all-to-all-done = bf16[128,128,128]{2,1,0:T(8,128)(2,1)} async-done(((bf16[128,128,128]{2,1,0:T(8,128)(2,1)}), bf16[128,128,128]{2,1,0:T(8,128)(2,1)}, u32[]{:S(2)}, u32[]{:S(2)}) %all-to-all-start) | async-done | bytes 4194336 | tf_op jit(solution)/shard_map/all_to_all | solution.py:138
  114.1 2.5 copy.541
  124.9 2.0 collective-permute-start.7
  128.1 2.0 collective-permute-start.5
  130.3 6.5 %collective-permute-done.5 = bf16[1,3,4,128]{3,2,1,0:T(4,128)(2,1)S(1)} collective-permute-done((bf16[1,3,4,128]{3,2,1,0:T(4,128)(2,1)S(1)}, bf16[1,3,4,128]{3,2,1,0:T(4,128)(2,1)S(1)}, u32[]{:S(2)}, u32[]{:S(2)}) %collective-permute-start.5) | collective-permute-done | bytes 3104 | tf_op jit(solution)/shard_map/ppermute | solution.py:47
  137.0 3.6 %collective-permute-start.8 = (bf16[5,1,4,128]{3,2,1,0:T(4,128)(2,1)S(1)}, bf16[5,1,4,128]{3,2,1,0:T(4,128)(2,1)S(1)}, u32[]{:S(2)}, u32[]{:S(2)}) collective-permute-start(bf16[5,1,4,128]{3,2,1,0:T(4,128)(2,1)S(1)} %get-tuple-element.73), channel_id=1, source_target_pairs={{1,0},{2,1},{3,2},{4,3},{5,4},{6,5},{7,6},{0,7},{9,8},{10,9},{11,1... | collective-permute-start | bytes 15368 | tf_op jit(solution)/shard_map/ppermute | solution.py:47
  142.3 4.1 %collective-permute-start.11 = (bf16[5,1,4,64,128]{4,3,2,1,0:T(8,128)(2,1)S(1)}, bf16[5,1,4,64,128]{4,3,2,1,0:T(8,128)(2,1)S(1)}, u32[]{:S(2)}, u32[]{:S(2)}) collective-permute-start(bf16[5,1,4,64,128]{4,3,2,1,0:T(8,128)(2,1)S(1)} %get-tuple-element.65), channel_id=1, source_target_pairs={{1,0},{2,1},{3,2},{4,3},{5,4},{6,5},{7,6},{0,7},{9,8},{10,9},{11,1... | collective-permute-start | bytes 983048 | tf_op jit(solution)/shard_map/ppermute | solution.py:47
  146.5 6.6 %collective-permute-done.10 = bf16[5,1,4,64,128]{4,3,2,1,0:T(8,128)(2,1)S(1)} collective-permute-done((bf16[5,1,4,64,128]{4,3,2,1,0:T(8,128)(2,1)S(1)}, bf16[5,1,4,64,128]{4,3,2,1,0:T(8,128)(2,1)S(1)}, u32[]{:S(2)}, u32[]{:S(2)}) %collective-permute-start.10) | collective-permute-done | bytes 327712 | tf_op jit(solution)/shard_map/ppermute | solution.py:46
  153.3 5.1 %maximum_bitcast_fusion = bf16[66,4,66,128]{3,2,0,1:T(8,128)(2,1)S(1)} fusion(bf16[4,1,66,128]{3,2,1,0:T(8,128)(2,1)S(1)} %maximum_bitcast_fusion.3, bf16[4,64,1,128]{3,2,1,0:T(2,128)(2,1)S(1)} %copy.547, bf16[4,64,64,128]{3,2,1,0:T(8,128)(2,1)} %bitcast.196, bf16[4,64,1,128]{3,2,1,0:T(2,128)(2,1)S(1)} %copy.546, ...), kind=kLoop, calls=%fused_computation.52 | loop fusion | flops 22302720 | bytes 8921088 | tf_op jit(solution)/shard_map/concatenate | solution.py:128
  162.4 2.7 fusion.15
  165.1 32.1 %fusion.4 = bf16[64,32,9,128]{3,1,2,0:T(8,128)(2,1)S(1)} fusion(f32[128]{0:T(128)S(1)} %copy-done.13, pred[32,9]{0,1:T(8,128)(4,1)S(1)} %copy-done.15, bf16[3,3,128,128]{3,2,1,0:T(8,128)(2,1)S(1)} %copy-done, bf16[66,4,8,11,128]{4,1,3,2,0:T(4,128)(2,1)S(1)} %fusion.15), kind=kOutput, calls=%fused_computation.23 | convolution fusion | flops 5593890816 | bytes 10961696 | tf_op jit(solution)/shard_map/conv_general_dilated | solution.py:53
  199.1 2.9 %copy_bitcast_fusion.1 = bf16[4,64,64,128]{3,1,0,2:T(8,128)(2,1)} fusion(bf16[64,4,72,128]{3,0,2,1:T(8,128)(2,1)S(1)} %bitcast.203), kind=kLoop, calls=%fused_computation.54 | loop fusion | bytes 8388608 | tf_op jit(solution)/shard_map/convert_element_type | solution.py:141
  208.6 2.1 collective-permute-start.13
  211.5 3.8 %collective-permute-done.12 = bf16[1,3,4,128]{3,2,1,0:T(4,128)(2,1)S(1)} collective-permute-done((bf16[1,3,4,128]{3,2,1,0:T(4,128)(2,1)S(1)}, bf16[1,3,4,128]{3,2,1,0:T(4,128)(2,1)S(1)}, u32[]{:S(2)}, u32[]{:S(2)}) %collective-permute-start.12) | collective-permute-done | bytes 3104 | tf_op jit(solution)/shard_map/ppermute | solution.py:46
  215.7 2.9 %collective-permute-start.17 = (bf16[1,3,4,64,128]{4,3,2,1,0:T(8,128)(2,1)S(1)}, bf16[1,3,4,64,128]{4,3,2,1,0:T(8,128)(2,1)S(1)}, u32[]{:S(2)}, u32[]{:S(2)}) collective-permute-start(bf16[1,3,4,64,128]{4,3,2,1,0:T(8,128)(2,1)S(1)} %get-tuple-element.67), channel_id=1, source_target_pairs={{8,0},{16,8},{24,16},{0,24},{9,1},{17,9},{25,17},{1,25},{10,2},{18... | collective-permute-start | bytes 589832 | tf_op jit(solution)/shard_map/ppermute | solution.py:47
  218.6 3.0 %collective-permute-start.16 = (bf16[5,1,4,128]{3,2,1,0:T(4,128)(2,1)S(1)}, bf16[5,1,4,128]{3,2,1,0:T(4,128)(2,1)S(1)}, u32[]{:S(2)}, u32[]{:S(2)}) collective-permute-start(bf16[5,1,4,128]{3,2,1,0:T(4,128)(2,1)S(1)} %get-tuple-element.71), channel_id=1, source_target_pairs={{1,0},{2,1},{3,2},{4,3},{5,4},{6,5},{7,6},{0,7},{9,8},{10,9},{11,1... | collective-permute-start | bytes 15368 | tf_op jit(solution)/shard_map/ppermute | solution.py:47
  223.8 4.2 %collective-permute-start.19 = (bf16[5,1,4,64,128]{4,3,2,1,0:T(8,128)(2,1)S(1)}, bf16[5,1,4,64,128]{4,3,2,1,0:T(8,128)(2,1)S(1)}, u32[]{:S(2)}, u32[]{:S(2)}) collective-permute-start(bf16[5,1,4,64,128]{4,3,2,1,0:T(8,128)(2,1)S(1)} %get-tuple-element.63), channel_id=1, source_target_pairs={{1,0},{2,1},{3,2},{4,3},{5,4},{6,5},{7,6},{0,7},{9,8},{10,9},{11,1... | collective-permute-start | bytes 983048 | tf_op jit(solution)/shard_map/ppermute | solution.py:47
  228.2 6.9 %collective-permute-done.18 = bf16[5,1,4,64,128]{4,3,2,1,0:T(8,128)(2,1)S(1)} collective-permute-done((bf16[5,1,4,64,128]{4,3,2,1,0:T(8,128)(2,1)S(1)}, bf16[5,1,4,64,128]{4,3,2,1,0:T(8,128)(2,1)S(1)}, u32[]{:S(2)}, u32[]{:S(2)}) %collective-permute-start.18) | collective-permute-done | bytes 327712 | tf_op jit(solution)/shard_map/ppermute | solution.py:46
  235.2 6.6 %maximum_bitcast_fusion.1 = bf16[66,4,66,128]{3,0,1,2:T(8,128)(2,1)S(1)} fusion(bf16[4,1,66,128]{3,1,0,2:T(2,128)(2,1)S(1)} %copy.565, bf16[4,64,1,128]{3,1,0,2:T(8,128)(2,1)S(1)} %slice_bitcast_fusion.1, bf16[4,64,64,128]{3,1,0,2:T(8,128)(2,1)} %copy_bitcast_fusion.1, bf16[4,64,1,128]{3,1,0,2:T(8,128)(2,1)S(1)} %slice_bitcast_fusion.2, ...), kind=kLoop, calls=%fused_computation.53 | loop fusion | flops 22302720 | bytes 8921088 | tf_op jit(solution)/shard_map/concatenate | solution.py:128
  245.5 3.0 %fusion.16 = bf16[66,4,8,11,128]{4,1,3,2,0:T(4,128)(2,1)S(1)} fusion(bf16[66,4,7,2,128]{4,1,3,2,0:T(4,128)(2,1)S(1)} %slice.386, bf16[66,4,8,9,128]{4,1,3,2,0:T(4,128)(2,1)S(1)} %bitcast.200), kind=kLoop, calls=%fused_computation.45 | loop fusion | flops 17842176 | bytes 11759616 | tf_op jit(solution)/shard_map/conv_general_dilated | solution.py:53
  248.5 11.4 %select_add_fusion = f32[64,32,9,128]{3,1,2,0:T(8,128)S(1)} fusion(f32[128]{0:T(128)S(1)} %copy-done.14, pred[32,9]{0,1:T(8,128)(4,1)S(1)} %copy-done.15, bf16[3,3,128,128]{3,2,1,0:T(8,128)(2,1)S(1)} %copy-done.12, bf16[66,4,8,11,128]{4,1,3,2,0:T(4,128)(2,1)S(1)} %fusion.16), kind=kOutput, calls=%fused_computation.24 | convolution fusion | flops 5440536576 | bytes 15680288 | tf_op jit(solution)/shard_map/conv_general_dilated | solution.py:53
  260.0 5.7 %copy.568 = f32[64,32,9,128]{3,0,2,1:T(8,128)S(1)} copy(f32[64,32,9,128]{3,1,2,0:T(8,128)S(1)} %select_add_fusion) | data formatting | bytes 18874368 | tf_op jit(solution)/shard_map/add | solution.py:61
  265.7 4.2 %slice.387 = f32[64,4,64,128]{3,0,2,1:T(8,128)} slice(f32[64,4,72,128]{3,0,2,1:T(8,128)S(1)} %bitcast.198), slice={[0:64], [0:4], [0:64], [0:128]} | slice | bytes 16777216 | tf_op jit(solution)/shard_map/add | solution.py:61
  269.9 10.9 %fusion.14 = bf16[4,64,64,128]{3,2,1,0:T(8,128)(2,1)} fusion(f32[64,4,64,128]{3,0,2,1:T(8,128)} %slice.387, bf16[4,64,64,128]{3,2,1,0:T(8,128)(2,1)S(1)} %bitcast.197), kind=kLoop, calls=%fused_computation.43 | loop fusion | flops 6291456 | bytes 16777216 | tf_op jit(solution)/shard_map/convert_element_type | solution.py:146
  (240 shorter events, 36.1 us)
Async XLA Ops:
  0.0 165.1 %copy-start = (bf16[3,3,128,128]{3,2,1,0:T(8,128)(2,1)S(1)}, bf16[3,3,128,128]{3,2,1,0:T(8,128)(2,1)}, u32[]{:S(2)}) copy-start(bf16[3,3,128,128]{3,2,1,0:T(8,128)(2,1)} %param.46) | copy-start | bytes 884740
  6.7 12.2 %copy-start.4 = (s32[4,8]{1,0:T(4,128)S(1)}, s32[4,8]{1,0:T(4,128)}, u32[]{:S(2)}) copy-start(s32[4,8]{1,0:T(4,128)} %param.44) | copy-start | bytes 388
  6.7 12.2 %copy-start.5 = (s32[4,8]{1,0:T(4,128)S(1)}, s32[4,8]{1,0:T(4,128)}, u32[]{:S(2)}) copy-start(s32[4,8]{1,0:T(4,128)} %param.45) | copy-start | bytes 388
  6.7 85.4 %copy-start.9 = (s32[4]{0:T(128)S(1)}, s32[4]{0:T(128)}, u32[]{:S(2)}) copy-start(s32[4]{0:T(128)} %constant.122.clone) | copy-start | bytes 52
  6.7 85.4 %copy-start.10 = (s32[4]{0:T(128)S(1)}, s32[4]{0:T(128)}, u32[]{:S(2)}) copy-start(s32[4]{0:T(128)} %constant.121.clone) | copy-start | bytes 52
  6.7 85.4 %copy-start.11 = (s32[4]{0:T(128)S(1)}, s32[4]{0:T(128)}, u32[]{:S(2)}) copy-start(s32[4]{0:T(128)} %constant.120.clone) | copy-start | bytes 52
  6.7 85.9 %copy-start.6 = (s32[4]{0:T(128)S(1)}, s32[4]{0:T(128)}, u32[]{:S(2)}) copy-start(s32[4]{0:T(128)} %constant.125.clone) | copy-start | bytes 52
  6.7 85.9 %copy-start.7 = (s32[4]{0:T(128)S(1)}, s32[4]{0:T(128)}, u32[]{:S(2)}) copy-start(s32[4]{0:T(128)} %constant.124.clone) | copy-start | bytes 52
  6.7 85.9 %copy-start.8 = (s32[4]{0:T(128)S(1)}, s32[4]{0:T(128)}, u32[]{:S(2)}) copy-start(s32[4]{0:T(128)} %constant.123.clone) | copy-start | bytes 52
  11.4 102.6 %all-to-all-start = ((bf16[128,128,128]{2,1,0:T(8,128)(2,1)}), bf16[128,128,128]{2,1,0:T(8,128)(2,1)}, u32[]{:S(2)}, u32[]{:S(2)}) async-start(bf16[128,128,128]{2,1,0:T(8,128)(2,1)} %broadcast_select_fusion), calls=%async_computation | async-start | bytes 8388608 | tf_op jit(solution)/shard_map/all_to_all | solution.py:138
  18.9 25.6 %collective-permute-start.1 = (s32[1,1,2,4,8]{4,3,2,1,0:T(4,128)S(1)}, s32[1,1,2,4,8]{4,3,2,1,0:T(4,128)S(1)}, u32[]{:S(2)}, u32[]{:S(2)}) collective-permute-start(s32[1,1,2,4,8]{4,3,2,1,0:T(4,128)S(1)} %add_bitcast_fusion), channel_id=1, source_target_pairs={{8,0},{16,8},{24,16},{0,24},{9,1},{17,9},{25,17},{1,25},{10,2},{18... | collective-permute-start | bytes 776 | tf_op jit(solution)/shard_map/ppermute | solution.py:47
  21.6 24.1 %collective-permute-start = (s32[1,1,2,4,8]{4,3,2,1,0:T(4,128)S(1)}, s32[1,1,2,4,8]{4,3,2,1,0:T(4,128)S(1)}, u32[]{:S(2)}, u32[]{:S(2)}) collective-permute-start(s32[1,1,2,4,8]{4,3,2,1,0:T(4,128)S(1)} %add_bitcast_fusion), channel_id=1, source_target_pairs={{0,8},{8,16},{16,24},{24,0},{1,9},{9,17},{17,25},{25,1},{2,10},{10... | collective-permute-start | bytes 776 | tf_op jit(solution)/shard_map/ppermute | solution.py:46
  45.7 42.0 %collective-permute-start.3 = (s32[3,1,2,4,8]{4,3,2,1,0:T(4,128)S(1)}, s32[3,1,2,4,8]{4,3,2,1,0:T(4,128)S(1)}, u32[]{:S(2)}, u32[]{:S(2)}) collective-permute-start(s32[3,1,2,4,8]{4,3,2,1,0:T(4,128)S(1)} %pad_add_fusion), channel_id=1, source_target_pairs={{1,0},{2,1},{3,2},{4,3},{5,4},{6,5},{7,6},{0,7},{9,8},{10,9},{11,1... | collective-permute-start | bytes 2312 | tf_op jit(solution)/shard_map/ppermute | solution.py:47
  52.0 39.4 %collective-permute-start.2 = (s32[3,1,2,4,8]{4,3,2,1,0:T(4,128)S(1)}, s32[3,1,2,4,8]{4,3,2,1,0:T(4,128)S(1)}, u32[]{:S(2)}, u32[]{:S(2)}) collective-permute-start(s32[3,1,2,4,8]{4,3,2,1,0:T(4,128)S(1)} %pad_add_fusion), channel_id=1, source_target_pairs={{0,1},{1,2},{2,3},{3,4},{4,5},{5,6},{6,7},{7,0},{8,9},{9,10},{10,1... | collective-permute-start | bytes 2312 | tf_op jit(solution)/shard_map/ppermute | solution.py:46
  124.6 5.5 %collective-permute-start.4 = (bf16[1,3,4,128]{3,2,1,0:T(4,128)(2,1)S(1)}, bf16[1,3,4,128]{3,2,1,0:T(4,128)(2,1)S(1)}, u32[]{:S(2)}, u32[]{:S(2)}) collective-permute-start(bf16[1,3,4,128]{3,2,1,0:T(4,128)(2,1)S(1)} %get-tuple-element.91), channel_id=1, source_target_pairs={{0,8},{8,16},{16,24},{24,0},{1,9},{9,17},{17,25},{25,1},{2,10},{10... | collective-permute-start | bytes 9224 | tf_op jit(solution)/shard_map/ppermute | solution.py:46
  124.9 17.1 %collective-permute-start.7 = (bf16[1,3,4,64,128]{4,3,2,1,0:T(8,128)(2,1)S(1)}, bf16[1,3,4,64,128]{4,3,2,1,0:T(8,128)(2,1)S(1)}, u32[]{:S(2)}, u32[]{:S(2)}) collective-permute-start(bf16[1,3,4,64,128]{4,3,2,1,0:T(8,128)(2,1)S(1)} %get-tuple-element.68), channel_id=1, source_target_pairs={{0,8},{8,16},{16,24},{24,0},{1,9},{9,17},{17,25},{25,1},{2,10},{10... | collective-permute-start | bytes 589832 | tf_op jit(solution)/shard_map/ppermute | solution.py:46
  126.9 15.2 %collective-permute-start.9 = (bf16[1,3,4,64,128]{4,3,2,1,0:T(8,128)(2,1)S(1)}, bf16[1,3,4,64,128]{4,3,2,1,0:T(8,128)(2,1)S(1)}, u32[]{:S(2)}, u32[]{:S(2)}) collective-permute-start(bf16[1,3,4,64,128]{4,3,2,1,0:T(8,128)(2,1)S(1)} %get-tuple-element.69), channel_id=1, source_target_pairs={{8,0},{16,8},{24,16},{0,24},{9,1},{17,9},{25,17},{1,25},{10,2},{18... | collective-permute-start | bytes 589832 | tf_op jit(solution)/shard_map/ppermute | solution.py:47
  128.1 8.7 %collective-permute-start.5 = (bf16[1,3,4,128]{3,2,1,0:T(4,128)(2,1)S(1)}, bf16[1,3,4,128]{3,2,1,0:T(4,128)(2,1)S(1)}, u32[]{:S(2)}, u32[]{:S(2)}) collective-permute-start(bf16[1,3,4,128]{3,2,1,0:T(4,128)(2,1)S(1)} %get-tuple-element.90), channel_id=1, source_target_pairs={{8,0},{16,8},{24,16},{0,24},{9,1},{17,9},{25,17},{1,25},{10,2},{18... | collective-permute-start | bytes 9224 | tf_op jit(solution)/shard_map/ppermute | solution.py:47
  136.8 4.9 %collective-permute-start.6 = (bf16[5,1,4,128]{3,2,1,0:T(4,128)(2,1)S(1)}, bf16[5,1,4,128]{3,2,1,0:T(4,128)(2,1)S(1)}, u32[]{:S(2)}, u32[]{:S(2)}) collective-permute-start(bf16[5,1,4,128]{3,2,1,0:T(4,128)(2,1)S(1)} %get-tuple-element.72), channel_id=1, source_target_pairs={{0,1},{1,2},{2,3},{3,4},{4,5},{5,6},{6,7},{7,0},{8,9},{9,10},{10,1... | collective-permute-start | bytes 15368 | tf_op jit(solution)/shard_map/ppermute | solution.py:46
  137.0 4.9 %collective-permute-start.8 = (bf16[5,1,4,128]{3,2,1,0:T(4,128)(2,1)S(1)}, bf16[5,1,4,128]{3,2,1,0:T(4,128)(2,1)S(1)}, u32[]{:S(2)}, u32[]{:S(2)}) collective-permute-start(bf16[5,1,4,128]{3,2,1,0:T(4,128)(2,1)S(1)} %get-tuple-element.73), channel_id=1, source_target_pairs={{1,0},{2,1},{3,2},{4,3},{5,4},{6,5},{7,6},{0,7},{9,8},{10,9},{11,1... | collective-permute-start | bytes 15368 | tf_op jit(solution)/shard_map/ppermute | solution.py:47
  142.2 10.9 %collective-permute-start.10 = (bf16[5,1,4,64,128]{4,3,2,1,0:T(8,128)(2,1)S(1)}, bf16[5,1,4,64,128]{4,3,2,1,0:T(8,128)(2,1)S(1)}, u32[]{:S(2)}, u32[]{:S(2)}) collective-permute-start(bf16[5,1,4,64,128]{4,3,2,1,0:T(8,128)(2,1)S(1)} %get-tuple-element.64), channel_id=1, source_target_pairs={{0,1},{1,2},{2,3},{3,4},{4,5},{5,6},{6,7},{7,0},{8,9},{9,10},{10,1... | collective-permute-start | bytes 983048 | tf_op jit(solution)/shard_map/ppermute | solution.py:46
  142.3 10.9 %collective-permute-start.11 = (bf16[5,1,4,64,128]{4,3,2,1,0:T(8,128)(2,1)S(1)}, bf16[5,1,4,64,128]{4,3,2,1,0:T(8,128)(2,1)S(1)}, u32[]{:S(2)}, u32[]{:S(2)}) collective-permute-start(bf16[5,1,4,64,128]{4,3,2,1,0:T(8,128)(2,1)S(1)} %get-tuple-element.65), channel_id=1, source_target_pairs={{1,0},{2,1},{3,2},{4,3},{5,4},{6,5},{7,6},{0,7},{9,8},{10,9},{11,1... | collective-permute-start | bytes 983048 | tf_op jit(solution)/shard_map/ppermute | solution.py:47
  208.6 6.9 %collective-permute-start.13 = (bf16[1,3,4,128]{3,2,1,0:T(4,128)(2,1)S(1)}, bf16[1,3,4,128]{3,2,1,0:T(4,128)(2,1)S(1)}, u32[]{:S(2)}, u32[]{:S(2)}) collective-permute-start(bf16[1,3,4,128]{3,2,1,0:T(4,128)(2,1)S(1)} %get-tuple-element.88), channel_id=1, source_target_pairs={{8,0},{16,8},{24,16},{0,24},{9,1},{17,9},{25,17},{1,25},{10,2},{18... | collective-permute-start | bytes 9224 | tf_op jit(solution)/shard_map/ppermute | solution.py:47
  210.7 4.6 %collective-permute-start.12 = (bf16[1,3,4,128]{3,2,1,0:T(4,128)(2,1)S(1)}, bf16[1,3,4,128]{3,2,1,0:T(4,128)(2,1)S(1)}, u32[]{:S(2)}, u32[]{:S(2)}) collective-permute-start(bf16[1,3,4,128]{3,2,1,0:T(4,128)(2,1)S(1)} %get-tuple-element.89), channel_id=1, source_target_pairs={{0,8},{8,16},{16,24},{24,0},{1,9},{9,17},{17,25},{25,1},{2,10},{10... | collective-permute-start | bytes 9224 | tf_op jit(solution)/shard_map/ppermute | solution.py:46
  215.5 6.1 %collective-permute-start.14 = (bf16[5,1,4,128]{3,2,1,0:T(4,128)(2,1)S(1)}, bf16[5,1,4,128]{3,2,1,0:T(4,128)(2,1)S(1)}, u32[]{:S(2)}, u32[]{:S(2)}) collective-permute-start(bf16[5,1,4,128]{3,2,1,0:T(4,128)(2,1)S(1)} %get-tuple-element.70), channel_id=1, source_target_pairs={{0,1},{1,2},{2,3},{3,4},{4,5},{5,6},{6,7},{7,0},{8,9},{9,10},{10,1... | collective-permute-start | bytes 15368 | tf_op jit(solution)/shard_map/ppermute | solution.py:46
  215.6 7.3 %collective-permute-start.15 = (bf16[1,3,4,64,128]{4,3,2,1,0:T(8,128)(2,1)S(1)}, bf16[1,3,4,64,128]{4,3,2,1,0:T(8,128)(2,1)S(1)}, u32[]{:S(2)}, u32[]{:S(2)}) collective-permute-start(bf16[1,3,4,64,128]{4,3,2,1,0:T(8,128)(2,1)S(1)} %get-tuple-element.66), channel_id=1, source_target_pairs={{0,8},{8,16},{16,24},{24,0},{1,9},{9,17},{17,25},{25,1},{2,10},{10... | collective-permute-start | bytes 589832 | tf_op jit(solution)/shard_map/ppermute | solution.py:46
  215.7 8.0 %collective-permute-start.17 = (bf16[1,3,4,64,128]{4,3,2,1,0:T(8,128)(2,1)S(1)}, bf16[1,3,4,64,128]{4,3,2,1,0:T(8,128)(2,1)S(1)}, u32[]{:S(2)}, u32[]{:S(2)}) collective-permute-start(bf16[1,3,4,64,128]{4,3,2,1,0:T(8,128)(2,1)S(1)} %get-tuple-element.67), channel_id=1, source_target_pairs={{8,0},{16,8},{24,16},{0,24},{9,1},{17,9},{25,17},{1,25},{10,2},{18... | collective-permute-start | bytes 589832 | tf_op jit(solution)/shard_map/ppermute | solution.py:47
  218.6 4.3 %collective-permute-start.16 = (bf16[5,1,4,128]{3,2,1,0:T(4,128)(2,1)S(1)}, bf16[5,1,4,128]{3,2,1,0:T(4,128)(2,1)S(1)}, u32[]{:S(2)}, u32[]{:S(2)}) collective-permute-start(bf16[5,1,4,128]{3,2,1,0:T(4,128)(2,1)S(1)} %get-tuple-element.71), channel_id=1, source_target_pairs={{1,0},{2,1},{3,2},{4,3},{5,4},{6,5},{7,6},{0,7},{9,8},{10,9},{11,1... | collective-permute-start | bytes 15368 | tf_op jit(solution)/shard_map/ppermute | solution.py:47
  223.8 11.4 %collective-permute-start.18 = (bf16[5,1,4,64,128]{4,3,2,1,0:T(8,128)(2,1)S(1)}, bf16[5,1,4,64,128]{4,3,2,1,0:T(8,128)(2,1)S(1)}, u32[]{:S(2)}, u32[]{:S(2)}) collective-permute-start(bf16[5,1,4,64,128]{4,3,2,1,0:T(8,128)(2,1)S(1)} %get-tuple-element.62), channel_id=1, source_target_pairs={{0,1},{1,2},{2,3},{3,4},{4,5},{5,6},{6,7},{7,0},{8,9},{9,10},{10,1... | collective-permute-start | bytes 983048 | tf_op jit(solution)/shard_map/ppermute | solution.py:46
  223.8 11.3 %collective-permute-start.19 = (bf16[5,1,4,64,128]{4,3,2,1,0:T(8,128)(2,1)S(1)}, bf16[5,1,4,64,128]{4,3,2,1,0:T(8,128)(2,1)S(1)}, u32[]{:S(2)}, u32[]{:S(2)}) collective-permute-start(bf16[5,1,4,64,128]{4,3,2,1,0:T(8,128)(2,1)S(1)} %get-tuple-element.63), channel_id=1, source_target_pairs={{1,0},{2,1},{3,2},{4,3},{5,4},{6,5},{7,6},{0,7},{9,8},{10,9},{11,1... | collective-permute-start | bytes 983048 | tf_op jit(solution)/shard_map/ppermute | solution.py:47
  243.5 5.1 %copy-start.12 = (bf16[3,3,128,128]{3,2,1,0:T(8,128)(2,1)S(1)}, bf16[3,3,128,128]{3,2,1,0:T(8,128)(2,1)}, u32[]{:S(2)}) copy-start(bf16[3,3,128,128]{3,2,1,0:T(8,128)(2,1)} %param.48) | copy-start | bytes 884740
  265.7 15.1 %copy-start.1 = (bf16[3,3,128,128]{3,2,1,0:T(8,128)(2,1)S(1)}, bf16[3,3,128,128]{3,2,1,0:T(8,128)(2,1)}, u32[]{:S(2)}) copy-start(bf16[3,3,128,128]{3,2,1,0:T(8,128)(2,1)} %param.46) | copy-start | bytes 884740
  (5 other events, 21.0 us)
where the time goes:
time: 286 us; the launch traced here: 281 us
  waiting for transfers between devices  110 us (38%)
  local copies, waits for them, and re-layouts  43.9 us (15%)
  matrix products  43.5 us (15%)
  starting transfers between devices  41.7 us (15%)
  other arithmetic  40.4 us (14%)
    ppermute x10, waiting for transfers between devices, padded_2(): after = lax.ppermute(first, axis, down)  66.6 us
    conv_general_dilated x2, matrix products, convolve(): lax.conv_general_dilated(padded, weight, (1, 1), 'VALID', dimension_numbe...  43.5 us
    ppermute x10, starting transfers between devices, padded_2(): after = lax.ppermute(first, axis, down)  32 us
    ppermute x10, waiting for transfers between devices, padded_2(): before = lax.ppermute(last, axis, up)  22.7 us
    all_to_all x1, waiting for transfers between devices, shards(): lax.all_to_all(ordered, ('face', 'tile'), split_axis=0, concat_axis=1, ti...  21.1 us
    concatenate x2, other arithmetic, pad_tiles(): return jnp.concatenate([upper[:, None], middle, lower[:, None]], 1)  11.7 us
    convert_element_type x1, other arithmetic, shards(): return (nested.astype(jnp.float32) + second).astype(jnp.bfloat16)  10.9 us
    add x2, local copies, waits for them, and re-layouts, convolve(): return summed + bias  9.9 us
  transfers between devices with their start and end apart: 21, of which 13 were waited for; matrix products, arithmetic and copies ran while one was open for 2% of the time, Pallas kernels for 0%

commit v1 on v0

v1 whole, which is shorter than its diff:
```python
import functools

import jax
import jax.numpy as jnp
import numpy as np
from jax import lax
from jax.experimental import pallas as pl
from jax.experimental.pallas import tpu as pltpu
from jax.sharding import PartitionSpec as P

STRIP_TABLE = np.array(
    [
        [1, 2, 0, 3],
        [0, 3, 1, 2],
        [3, 1, 2, 0],
        [2, 0, 3, 1],
        [1, 2, 0, 3],
        [1, 2, 0, 3],
        [0, 3, 1, 2],
        [0, 3, 1, 2],
    ],
    np.int32,
)
FLIP_TABLE = np.array(
    [
        [0, 0, 1, 1],
        [0, 0, 1, 1],
        [0, 1, 1, 0],
        [0, 1, 1, 0],
        [0, 0, 1, 1],
        [0, 0, 1, 1],
        [0, 0, 1, 1],
        [0, 0, 1, 1],
    ],
    np.int32,
)
DIRECTIONS = [(-1, 0), (1, 0), (0, -1), (0, 1), (-1, -1), (-1, 1), (1, -1), (1, 1)]
AXES = ("face", "tile")
VMEM = pltpu.VMEM
F32 = jnp.float32
BF16 = jnp.bfloat16
LIMIT = 48 * 1024 * 1024


def shift_down(line, first):
    moved = pltpu.roll(line, 1, 0)
    rows = lax.broadcasted_iota(jnp.int32, moved.shape, 0)
    return jnp.where(rows == 0, first, moved)


def shift_up(line, last):
    size = line.shape[0]
    moved = pltpu.roll(line, size - 1, 0)
    rows = lax.broadcasted_iota(jnp.int32, moved.shape, 0)
    return jnp.where(rows == size - 1, last, moved)


def gelu(value):
    return (0.5 * value) * (1.0 + lax.erf(value * np.float32(np.sqrt(0.5))))


def pick_lines(codes_ref, req_ref, lines, edge_refs, corner_refs):
    tiles = edge_refs[0].shape[0]
    side = edge_refs[0].shape[1]
    rows = lax.broadcasted_iota(jnp.int32, corner_refs[0].shape, 0)
    for direction in range(8):
        corner = jnp.zeros(corner_refs[0].shape, F32)
        for tile in range(tiles):
            code = codes_ref[req_ref[direction], tile * 8 + direction]
            line = lines[code]
            if direction < 4:
                edge_refs[direction][tile] = line
            else:
                at = side - 1 if direction in (4, 6) else 0
                pixel = line.astype(F32)[at : at + 1]
                corner = jnp.where(rows == tile, pixel, corner)
        if direction >= 4:
            corner_refs[direction - 4][...] = corner.astype(BF16)


def flip_line(line):
    size = line.shape[0]
    row = lax.broadcasted_iota(jnp.int32, (size, size), 0)
    col = lax.broadcasted_iota(jnp.int32, (size, size), 1)
    turn = jnp.where(row + col == size - 1, 1.0, 0.0).astype(BF16)
    return jnp.dot(turn, line, preferred_element_type=F32).astype(BF16)


def border_kernel(side, codes_ref, req_ref, x_ref, ring_ref, *rest):
    edge_refs, corner_refs, lines = rest[:4], rest[4:8], rest[8]
    tile = pl.program_id(0)
    tiles = edge_refs[0].shape[0]
    image = x_ref[...].reshape(side, side, x_ref.shape[-1])
    ring = [image[0], image[1], image[side - 2], image[side - 1]]
    low = image[:, :16].astype(F32)
    high = image[:, side - 16 :].astype(F32)
    ring += [v.astype(BF16) for v in (low[:, 0], low[:, 1], high[:, 14], high[:, 15])]
    for at, line in enumerate(ring):
        ring_ref[0, at] = line
    for strip, at in enumerate((0, 3, 4, 7)):
        lines[tile * 4 + strip] = ring[at]
        lines[tiles * 4 + tile * 4 + strip] = flip_line(ring[at])

    @pl.when(tile == tiles - 1)
    def _():
        pick_lines(codes_ref, req_ref, lines, edge_refs, corner_refs)


def ring_kernel(codes_ref, req_ref, ring_ref, w_ref, b_ref, *rest):
    pad_refs, pad_corner_refs = rest[:4], rest[4:8]
    edge_refs, corner_refs, lines = rest[8:12], rest[12:16], rest[16]
    tiles = ring_ref.shape[0]
    side = ring_ref.shape[2]
    corners = [ref[...].astype(F32) for ref in pad_corner_refs]
    plans = [
        (0, 0, 1, 0, 1, 2, 3, 0, 1),
        (1, 2, 3, 3, 2, 2, 3, side - 1, side - 2),
        (2, 0, 2, 4, 5, 0, 1, 0, 1),
        (3, 1, 3, 7, 6, 0, 1, side - 1, side - 2),
    ]
    for edge, (pad, c_first, c_last, line_0, line_1, end_a, end_b, at_0, at_1) in enumerate(plans):
        stacked = []
        for tile in range(tiles):
            begin = pad_refs[end_a][tile].astype(F32)
            finish = pad_refs[end_b][tile].astype(F32)
            parts = []
            for line, first, last in (
                (
                    pad_refs[pad][tile],
                    corners[c_first][tile : tile + 1],
                    corners[c_last][tile : tile + 1],
                ),
                (ring_ref[tile, line_0], begin[at_0 : at_0 + 1], finish[at_0 : at_0 + 1]),
                (ring_ref[tile, line_1], begin[at_1 : at_1 + 1], finish[at_1 : at_1 + 1]),
            ):
                wide = line.astype(F32)
                parts += [
                    shift_down(wide, first).astype(BF16),
                    line,
                    shift_up(wide, last).astype(BF16),
                ]
            stacked.append(jnp.concatenate(parts, axis=1))
        summed = jnp.dot(
            jnp.concatenate(stacked, axis=0), w_ref[edge], preferred_element_type=F32
        )
        hidden = gelu(summed + b_ref[...]).astype(BF16)
        for tile in range(tiles):
            line = hidden[tile * side : (tile + 1) * side]
            lines[tile * 4 + edge] = line
            lines[tiles * 4 + tile * 4 + edge] = flip_line(line)
    pick_lines(codes_ref, req_ref, lines, edge_refs, corner_refs)


def convolve_tile(padded, left, right, c_left, c_right, w_ref, w_side_ref, bias, y, ends, finish):
    side = padded.shape[2]
    chan = padded.shape[3]
    for at, (column, (first, last)) in enumerate(((left, c_left), (right, c_right))):
        wide = column.astype(F32)
        taps = jnp.concatenate(
            [
                shift_down(wide, first).astype(BF16),
                column,
                shift_up(wide, last).astype(BF16),
            ],
            axis=1,
        )
        ends[at] = jnp.dot(taps, w_side_ref[at], preferred_element_type=F32)
    pairs = side // 2
    blocks = y.shape[0]
    step = pairs // blocks
    rows = lax.broadcasted_iota(jnp.int32, (side, chan), 0)
    for block in range(blocks):
        lhs = jnp.concatenate(
            [
                padded[pl.ds(step * block + j // 2, step), j % 2].reshape(step * side, chan)
                for j in range(4)
            ],
            axis=1,
        )
        y[block] = jnp.dot(lhs, w_ref[...], preferred_element_type=F32)
    for block in range(blocks):
        for i in range(step):
            for half in range(2):
                row = (block * step + i) * 2 + half
                a, b, c = (
                    y[block, pl.ds(i * side, side), pl.ds((half * 3 + dx) * chan, chan)]
                    for dx in range(3)
                )
                a = jnp.where(rows == 0, ends[0, row : row + 1], pltpu.roll(a, 1, 0))
                c = jnp.where(
                    rows == side - 1, ends[1, row : row + 1], pltpu.roll(c, side - 1, 0)
                )
                finish(row, (a + c) + (b + bias))


def level_kernel(side, x_ref, *rest):
    pads = (rest[0:4], rest[8:12])
    corners = (rest[4:8], rest[12:16])
    w_refs, w_side_refs, b_refs = rest[16:18], rest[18:20], rest[20:22]
    out_ref, padded, hidden, y, ends = rest[22:]
    chan = x_ref.shape[-1]
    half = side // 2
    image = x_ref[...].reshape(side, side, chan)
    fields = (padded, hidden)
    for field, pad in zip(fields, pads):
        field[0, 0] = pad[0][0]
        field[half, 1] = pad[1][0]
    padded[0, 1] = image[0]
    padded[1:half] = image[1 : side - 1].reshape(half - 1, 2, side, chan)
    padded[half, 0] = image[side - 1]

    def keep_hidden(row, value):
        hidden[(row + 1) // 2, (row + 1) % 2] = gelu(value).astype(BF16)

    def keep_out(row, value):
        centre = padded[(row + 1) // 2, (row + 1) % 2].astype(F32)
        out_ref[0, row] = (centre + value).astype(BF16)

    for at, finish in enumerate((keep_hidden, keep_out)):
        upper_left, upper_right, lower_left, lower_right = (
            ref[0, 0:1].astype(F32) for ref in corners[at]
        )
        convolve_tile(
            fields[at],
            pads[at][2][0],
            pads[at][3][0],
            (upper_left, lower_left),
            (upper_right, lower_right),
            w_refs[at],
            w_side_refs[at],
            b_refs[at][...],
            y,
            ends,
            finish,
        )


def paired_weights(weight):
    chan_in, chan_out = weight.shape[2:]
    by_tap = weight.transpose(0, 2, 1, 3).reshape(3, chan_in, 3 * chan_out)
    zero = jnp.zeros((1, chan_in, 3 * chan_out), weight.dtype)
    first = jnp.concatenate([by_tap, zero], 0)
    second = jnp.concatenate([zero, by_tap], 0)
    return jnp.stack([first, second], 2).reshape(4 * chan_in, 6 * chan_out)


def side_weights(weight):
    chan_in, chan_out = weight.shape[2:]
    return jnp.stack([weight[:, 0], weight[:, 2]], 0).reshape(2, 3 * chan_in, chan_out)


def edge_weights(weight):
    chan_in, chan_out = weight.shape[2:]
    turned = weight.transpose(1, 0, 2, 3)
    stacked = jnp.stack([weight, weight[::-1], turned, turned[::-1]], 0)
    return stacked.reshape(4, 9 * chan_in, chan_out)


def exchange(arrays, faces, columns):
    got = []
    for array, (face_off, tile_off) in zip(arrays, DIRECTIONS):
        pairs = []
        for face in range(faces):
            for tile in range(columns):
                to = ((face - face_off) % faces) * columns + (tile - tile_off) % columns
                pairs.append((face * columns + tile, to))
        got.append(lax.ppermute(array, AXES, pairs))
    return got


def shards(latitude_rows, tile_order, neighbours, rotations, w_first, b_first, w_second, b_second):
    faces, columns = lax.axis_size("face"), lax.axis_size("tile")
    devices = faces * columns
    tiles = neighbours.shape[0]
    piece, chan = latitude_rows.shape[1:]
    side = int(round((piece * devices) ** 0.5))
    vmem_spec = pl.BlockSpec(memory_space=VMEM)
    smem_spec = pl.BlockSpec(memory_space=pltpu.SMEM)
    params = pltpu.CompilerParams(vmem_limit_bytes=LIMIT)

    turn = rotations[..., None] == jnp.arange(4, dtype=jnp.int32)
    strip = jnp.sum(jnp.where(turn, jnp.asarray(STRIP_TABLE)[None], 0), -1)
    flip = jnp.sum(jnp.where(turn, jnp.asarray(FLIP_TABLE)[None], 0), -1)
    code = (flip * tiles + neighbours % tiles) * 4 + strip
    codes = lax.all_gather(code.reshape(1, tiles * 8), AXES, axis=0, tiled=True)
    face, column = lax.axis_index("face"), lax.axis_index("tile")
    asking = jnp.stack(
        [((face - f) % faces) * columns + (column - t) % columns for f, t in DIRECTIONS]
    ).astype(jnp.int32)

    ordered = latitude_rows.at[tile_order].get(mode="promise_in_bounds")
    gathered = lax.all_to_all(ordered, AXES, split_axis=0, concat_axis=0, tiled=True)
    pieces = gathered.reshape(devices, tiles, piece, chan)
    tile_spec = pl.BlockSpec((devices, 1, piece, chan), lambda t: (0, t, 0, 0))

    edge_shape = jax.ShapeDtypeStruct((tiles, side, chan), BF16)
    corner_shape = jax.ShapeDtypeStruct((16, chan), BF16)
    lines_scratch = VMEM((8 * tiles, side, chan), BF16)
    edge_out = pl.BlockSpec((tiles, side, chan), lambda t: (0, 0, 0))
    corner_out = pl.BlockSpec((16, chan), lambda t: (0, 0))
    ring, *sends = pl.pallas_call(
        functools.partial(border_kernel, side),
        grid=(tiles,),
        in_specs=[smem_spec, smem_spec, tile_spec],
        out_specs=[pl.BlockSpec((1, 8, side, chan), lambda t: (t, 0, 0, 0))]
        + [edge_out] * 4
        + [corner_out] * 4,
        out_shape=[jax.ShapeDtypeStruct((tiles, 8, side, chan), BF16)]
        + [edge_shape] * 4
        + [corner_shape] * 4,
        scratch_shapes=[lines_scratch],
        compiler_params=params,
        name="borders",
    )(codes, asking, pieces)
    pads_first = exchange(sends, faces, columns)

    sends = pl.pallas_call(
        ring_kernel,
        in_specs=[smem_spec, smem_spec] + [vmem_spec] * 11,
        out_specs=[vmem_spec] * 8,
        out_shape=[edge_shape] * 4 + [corner_shape] * 4,
        scratch_shapes=[lines_scratch],
        compiler_params=params,
        name="hidden_ring",
    )(codes, asking, ring, edge_weights(w_first), b_first.reshape(1, chan), *pads_first)
    pads_second = exchange(sends, faces, columns)

    edge_in = pl.BlockSpec((1, side, chan), lambda t: (t, 0, 0))
    corner_in = pl.BlockSpec((1, 8, chan), lambda t: (t, 0, 0))

    def whole(array):
        return pl.BlockSpec(array.shape, lambda t: (0,) * array.ndim)

    def spread(pads):
        corners = [jnp.broadcast_to(c[:tiles, None], (tiles, 8, chan)) for c in pads[4:]]
        return list(pads[:4]) + corners

    constants = [
        paired_weights(w_first),
        paired_weights(w_second),
        side_weights(w_first),
        side_weights(w_second),
        b_first.reshape(1, chan),
        b_second.reshape(1, chan),
    ]
    blocks = 4
    field = VMEM((side // 2 + 1, 2, side, chan), BF16)
    return pl.pallas_call(
        functools.partial(level_kernel, side),
        grid=(tiles,),
        in_specs=[tile_spec]
        + ([edge_in] * 4 + [corner_in] * 4) * 2
        + [whole(c) for c in constants],
        out_specs=pl.BlockSpec((1, side, side, chan), lambda t: (t, 0, 0, 0)),
        out_shape=jax.ShapeDtypeStruct((tiles, side, side, chan), BF16),
        scratch_shapes=[
            field,
            field,
            VMEM((blocks, side // 2 // blocks * side, 6 * chan), F32),
            VMEM((2, side, chan), F32),
        ],
        compiler_params=params,
        name="level",
    )(pieces, *spread(pads_first), *spread(pads_second), *constants)


def solution(mesh):
    return jax.shard_map(
        shards,
        mesh=mesh,
        in_specs=(
            P(None, ("face", "tile"), None),
            P(),
            P(("face", "tile"), None),
            P(("face", "tile"), None),
            P(),
            P(),
            P(),
            P(),
        ),
        out_specs=P(("face", "tile"), None, None, None),
        check_vma=False,
    )
```

time: 286 us -> 196 us (0.69); the launches traced: 281 us -> 195 us
  blocking collectives: 0 us -> 122 us
  waiting for transfers between devices: 110 us -> 2.98 us
  matrix products: 43.5 us -> 0 us
  other arithmetic: 40.4 us -> 1.04 us
  local copies, waits for them, and re-layouts: 43.9 us -> 14.6 us
  Pallas kernels: 0 us -> 22.6 us
  starting transfers between devices: 41.7 us -> 31.7 us
    all_gather x0 -> x1, blocking collectives: none -> 122 us  [shards(): codes = lax.all_gather(code.reshape(1, tiles * 8), AXES, axis=0, tiled=True)]
    ppermute x20 -> x16, waiting for transfers between devices: 89.3 us -> 2.98 us  [exchange(): got.append(lax.ppermute(array, AXES, pairs))]
    conv_general_dilated x2 -> x0, matrix products: 43.5 us -> none  [convolve(): lax.conv_general_dilated(padded, weight, (1, 1), 'VALID', dimension_numbe...]
    pallas_call x0 -> x3, Pallas kernels: none -> 22.6 us  [the longest x1 16.9 us: shards(): pl.pallas_call(functools.partial(level_kernel, side), grid=(tiles,), in_s...]
    all_to_all x1, waiting for transfers between devices: 21.1 us -> 0.01 us  [shards(): lax.all_to_all(ordered, AXES, split_axis=0, concat_axis=0, tiled=True)]
    concatenate x3 -> x0, other arithmetic: 11.7 us -> none  [the longest x2 11.7 us: pad_tiles(): return jnp.concatenate([upper[:, None], middle, lower[:, None]], 1)]
    convert_element_type x1 -> x0, other arithmetic: 10.9 us -> none  [shards(): return (nested.astype(jnp.float32) + second).astype(jnp.bfloat16)]
    ppermute x20 -> x16, starting transfers between devices: 34.3 us -> 24.3 us  [exchange(): got.append(lax.ppermute(array, AXES, pairs))]
  transfers between devices with their start and end apart: 21 -> 17, of which waited for: 13 -> 1; matrix products, arithmetic and copies ran while one was open for 2% -> 5% of each run, Pallas kernels for 0% -> 0%
where the time goes in v1:
time: 196 us; the launch traced here: 195 us
  blocking collectives  122 us (62%)
  starting transfers between devices  31.7 us (16%)
  Pallas kernels  22.6 us (12%)
  local copies, waits for them, and re-layouts  14.6 us (7%)
  waiting for transfers between devices  2.98 us (2%)
    all_gather x1, blocking collectives, shards(): codes = lax.all_gather(code.reshape(1, tiles * 8), AXES, axis=0, tiled=True)  122 us
    ppermute x16, starting transfers between devices, exchange(): got.append(lax.ppermute(array, AXES, pairs))  24.3 us
    pallas_call x1, Pallas kernels, shards(): pl.pallas_call(functools.partial(level_kernel, side), grid=(tiles,), in_s...  16.9 us
    all_to_all x1, starting transfers between devices, shards(): lax.all_to_all(ordered, AXES, split_axis=0, concat_axis=0, tiled=True)  7.43 us
    gather x1, local copies, waits for them, and re-layouts, shards(): ordered = latitude_rows.at[tile_order].get(mode='promise_in_bounds')  5.28 us
    another operation x4, local copies, waits for them, and re-layouts, paired_weights(): return jnp.stack([first, second], 2).reshape(4 * chan_in, 6 * chan_out)  4.56 us
  transfers between devices with their start and end apart: 17, of which 1 were waited for; matrix products, arithmetic and copies ran while one was open for 5% of the time, Pallas kernels for 0%

profile of v1, /device:TPU:0, one launch (start us, length us, event | category | flops | bytes accessed | tf_op | source)
XLA Modules:
  0.0 195.3 jit_solution(4472441447254649464)
XLA Ops:
  0.0 0.7 compare_select_fusion
  0.7 5.3 %gather_fusion = bf16[128,128,128]{2,1,0:T(8,128)(2,1)} fusion(bf16[128,128,128]{2,1,0:T(8,128)(2,1)} %param.10, s32[1024]{0:T(1024)S(1)} %pad_clamp_fusion), kind=kCustom, calls=%fused_computation | custom fusion | bytes 8389120 | tf_op jit(solution)/shard_map/gather | solution.py:291
  6.0 7.4 %all-to-all-start = ((bf16[128,128,128]{2,1,0:T(8,128)(2,1)}), bf16[128,128,128]{2,1,0:T(8,128)(2,1)}, u32[]{:S(2)}, u32[]{:S(2)}) async-start(bf16[128,128,128]{2,1,0:T(8,128)(2,1)} %gather_fusion), calls=%async_computation | async-start | bytes 8388608 | tf_op jit(solution)/shard_map/all_to_all | solution.py:292
  13.6 0.2 copy.39
  13.9 0.1 reshape.72
  14.0 0.2 copy.43
  14.3 0.1 stack.82.req_ref
  14.3 121.9 %all-gather = s32[32,1,32]{2,1,0:T(1,128)S(1)} all-gather(s32[1,1,32]{2,1,0:T(1,128)S(1)} %reshape.72), channel_id=1, replica_groups=mesh['face'=4,'tile'=8] {'face','tile'}, dimensions={0}, use_global_device_ids=true | all-gather | bytes 4224 | tf_op jit(solution)/shard_map/all_gather | solution.py:285
  136.2 0.9 pad_bitcast_fusion.3
  137.0 0.7 fusion.5
  137.8 0.7 fusion.4
  138.4 0.1 pad_maximum_fusion.w_ref
  138.6 3.5 %borders.1 = (bf16[4,8,64,128]{3,2,1,0:T(8,128)(2,1)S(1)}, bf16[4,64,128]{2,1,0:T(8,128)(2,1)S(1)}, bf16[4,64,128]{2,1,0:T(8,128)(2,1)S(1)}, bf16[4,64,128]{2,1,...) custom-call(s32[32,32]{1,0:T(8,128)S(1)} %bitcast.43, ...), custom_call_target="tpu_custom_call" | custom-call | tf_op jit(solution)/shard_map/borders/pallas_call | solution.py:301
  142.1 0.1 collective-permute-start.4
  142.2 5.3 %collective-permute-start.5 = (bf16[16,128]{1,0:T(8,128)(2,1)S(1)}, bf16[16,128]{1,0:T(8,128)(2,1)S(1)}, u32[]{:S(2)}, u32[]{:S(2)}) collective-permute-start(bf16[16,128]{1,0:T(8,128)(2,1)S(1)} %get-tuple-element.27), channel_id=1, source_target_pairs={{0,15},{1,8},{2,9},{3,10},{4,11},{5,12},{6,13},{7,14},{8,23},{9,16... | collective-permute-start | bytes 12296 | tf_op jit(solution)/shard_map/ppermute | solution.py:267
  147.5 0.1 pad_bitcast_fusion.1
  147.7 2.9 %collective-permute-start.1 = (bf16[4,64,128]{2,1,0:T(8,128)(2,1)S(1)}, bf16[4,64,128]{2,1,0:T(8,128)(2,1)S(1)}, u32[]{:S(2)}, u32[]{:S(2)}) collective-permute-start(bf16[4,64,128]{2,1,0:T(8,128)(2,1)S(1)} %get-tuple-element.23), channel_id=1, source_target_pairs={{0,24},{1,25},{2,26},{3,27},{4,28},{5,29},{6,30},{7,31},{8,0},{9,1... | collective-permute-start | bytes 196616 | tf_op jit(solution)/shard_map/ppermute | solution.py:267
  150.6 3.5 %collective-permute-start.3 = (bf16[4,64,128]{2,1,0:T(8,128)(2,1)S(1)}, bf16[4,64,128]{2,1,0:T(8,128)(2,1)S(1)}, u32[]{:S(2)}, u32[]{:S(2)}) collective-permute-start(bf16[4,64,128]{2,1,0:T(8,128)(2,1)S(1)} %get-tuple-element.25), channel_id=1, source_target_pairs={{0,7},{1,0},{2,1},{3,2},{4,3},{5,4},{6,5},{7,6},{8,15},{9,8},{10,9... | collective-permute-start | bytes 196616 | tf_op jit(solution)/shard_map/ppermute | solution.py:267
  154.2 0.1 pad_maximum_fusion.1
  154.3 2.9 %collective-permute-done.7.rest_7_ = bf16[16,128]{1,0:T(8,128)(2,1)S(1)} collective-permute-done((bf16[16,128]{1,0:T(8,128)(2,1)S(1)}, bf16[16,128]{1,0:T(8,128)(2,1)S(1)}, u32[]{:S(2)}, u32[]{:S(2)}) %collective-permute-start.7) | collective-permute-done | bytes 4128 | tf_op jit(solution)/shard_map/ppermute | solution.py:267
  157.2 2.2 %hidden_ring.1 = (bf16[4,64,128]{2,1,0:T(8,128)(2,1)S(1)}, bf16[4,64,128]{2,1,0:T(8,128)(2,1)S(1)}, bf16[4,64,128]{2,1,0:T(8,128)(2,1)S(1)}, bf16[4,64,128]{2,1,...) custom-call(s32[32,32]{1,0:T(8,128)S(1)} %bitcast.44, ...), custom_call_target="tpu_custom_call" | custom-call | tf_op jit(solution)/shard_map/hidden_ring/pallas_call | solution.py:317
  159.4 0.1 collective-permute-start.12
  159.5 4.4 %collective-permute-start.13 = (bf16[16,128]{1,0:T(8,128)(2,1)S(1)}, bf16[16,128]{1,0:T(8,128)(2,1)S(1)}, u32[]{:S(2)}, u32[]{:S(2)}) collective-permute-start(bf16[16,128]{1,0:T(8,128)(2,1)S(1)} %get-tuple-element.36), channel_id=1, source_target_pairs={{0,15},{1,8},{2,9},{3,10},{4,11},{5,12},{6,13},{7,14},{8,23},{9,16... | collective-permute-start | bytes 12296 | tf_op jit(solution)/shard_map/ppermute | solution.py:267
  163.9 0.1 pad_maximum_fusion.2
  164.1 4.9 %collective-permute-start.11 = (bf16[4,64,128]{2,1,0:T(8,128)(2,1)S(1)}, bf16[4,64,128]{2,1,0:T(8,128)(2,1)S(1)}, u32[]{:S(2)}, u32[]{:S(2)}) collective-permute-start(bf16[4,64,128]{2,1,0:T(8,128)(2,1)S(1)} %get-tuple-element.34), channel_id=1, source_target_pairs={{0,7},{1,0},{2,1},{3,2},{4,3},{5,4},{6,5},{7,6},{8,15},{9,8},{10,9... | collective-permute-start | bytes 196616 | tf_op jit(solution)/shard_map/ppermute | solution.py:267
  169.0 0.2 collective-permute-start.8
  169.1 2.8 %collective-permute-start.9 = (bf16[4,64,128]{2,1,0:T(8,128)(2,1)S(1)}, bf16[4,64,128]{2,1,0:T(8,128)(2,1)S(1)}, u32[]{:S(2)}, u32[]{:S(2)}) collective-permute-start(bf16[4,64,128]{2,1,0:T(8,128)(2,1)S(1)} %get-tuple-element.32), channel_id=1, source_target_pairs={{0,24},{1,25},{2,26},{3,27},{4,28},{5,29},{6,30},{7,31},{8,0},{9,1... | collective-permute-start | bytes 196616 | tf_op jit(solution)/shard_map/ppermute | solution.py:267
  172.0 1.8 copy.42
  173.8 1.3 copy.49
  175.0 1.8 copy.46
  176.8 1.3 copy.50
  178.3 16.9 %level.1 = bf16[4,64,64,128]{3,2,1,0:T(8,128)(2,1)} custom-call(bf16[32,4,128,128]{3,2,1,0:T(8,128)(2,1)} %bitcast.x_ref, bf16[4,64,128]{2,1,0:T(8,128)(2,1)S(1)} %collective-permute-done.rest_0_, bf16[4,64,128]{2,1,0:T(8,128)(2,1)S(1)} %collective-permute-done.1.rest_1_, bf16[4,64,128]{2,1,0:T(8,128)(2,1)S(1)} %collective-permute-done.2.rest_2_, ...), custom_call_target="tpu_custom_call" | custom-call | tf_op jit(solution)/shard_map/level/pallas_call | solution.py:348
  (73 shorter events, 0.5 us)
Async XLA Ops:
  6.0 7.6 %copy-start.2 = (bf16[3,3,128,128]{3,2,1,0:T(8,128)(2,1)S(1)}, bf16[3,3,128,128]{3,2,1,0:T(8,128)(2,1)}, u32[]{:S(2)}) copy-start(bf16[3,3,128,128]{3,2,1,0:T(8,128)(2,1)} %param.14) | copy-start | bytes 884740
  6.0 7.9 %copy-start.9 = (s32[4,8]{1,0:T(4,128)S(1)}, s32[4,8]{1,0:T(4,128)}, u32[]{:S(2)}) copy-start(s32[4,8]{1,0:T(4,128)} %param.13) | copy-start | bytes 388
  6.0 7.9 %copy-start.10 = (s32[8,4]{0,1:T(4,128)S(1)}, s32[8,4]{0,1:T(4,128)}, u32[]{:S(2)}) copy-start(s32[8,4]{0,1:T(4,128)} %constant.94.clone) | copy-start | bytes 388
  6.0 7.9 %copy-start.11 = (s32[8,4]{0,1:T(4,128)S(1)}, s32[8,4]{0,1:T(4,128)}, u32[]{:S(2)}) copy-start(s32[8,4]{0,1:T(4,128)} %constant.95.clone) | copy-start | bytes 388
  6.0 7.9 %copy-start.12 = (s32[4,8]{1,0:T(4,128)S(1)}, s32[4,8]{1,0:T(4,128)}, u32[]{:S(2)}) copy-start(s32[4,8]{1,0:T(4,128)} %param.12) | copy-start | bytes 388
  6.0 8.0 %copy-start.4 = (bf16[3,3,128,128]{3,2,1,0:T(8,128)(2,1)S(1)}, bf16[3,3,128,128]{3,2,1,0:T(8,128)(2,1)}, u32[]{:S(2)}) copy-start(bf16[3,3,128,128]{3,2,1,0:T(8,128)(2,1)} %param.16) | copy-start | bytes 884740
  6.0 132.6 %all-to-all-start = ((bf16[128,128,128]{2,1,0:T(8,128)(2,1)}), bf16[128,128,128]{2,1,0:T(8,128)(2,1)}, u32[]{:S(2)}, u32[]{:S(2)}) async-start(bf16[128,128,128]{2,1,0:T(8,128)(2,1)} %gather_fusion), calls=%async_computation | async-start | bytes 8388608 | tf_op jit(solution)/shard_map/all_to_all | solution.py:292
  138.4 18.8 %copy-start = (f32[128]{0:T(128)S(1)}, f32[128]{0:T(128)}, u32[]{:S(2)}) copy-start(f32[128]{0:T(128)} %param.15) | copy-start | bytes 1540
  138.6 15.6 %copy-start.3 = (bf16[4,128,1,384]{1,3,0,2:T(8,128)(2,1)S(1)}, bf16[4,128,1,384]{1,3,0,2:T(8,128)(2,1)}, u32[]{:S(2)}) copy-start(bf16[4,128,1,384]{1,3,0,2:T(8,128)(2,1)} %get-tuple-element.48) | copy-start | bytes 1179652
  142.1 29.8 %copy-start.5 = (bf16[3,1,128,128]{3,2,1,0:T(8,128)(2,1)S(1)}, bf16[3,1,128,128]{3,2,1,0:T(8,128)(2,1)}, u32[]{:S(2)}) copy-start(bf16[3,1,128,128]{3,2,1,0:T(8,128)(2,1)} %get-tuple-element.43) | copy-start | bytes 294916
  142.1 29.8 %copy-start.6 = (bf16[3,1,128,128]{3,2,1,0:T(8,128)(2,1)S(1)}, bf16[3,1,128,128]{3,2,1,0:T(8,128)(2,1)}, u32[]{:S(2)}) copy-start(bf16[3,1,128,128]{3,2,1,0:T(8,128)(2,1)} %get-tuple-element.44) | copy-start | bytes 294916
  142.1 29.8 %copy-start.7 = (bf16[3,1,128,128]{3,2,1,0:T(8,128)(2,1)S(1)}, bf16[3,1,128,128]{3,2,1,0:T(8,128)(2,1)}, u32[]{:S(2)}) copy-start(bf16[3,1,128,128]{3,2,1,0:T(8,128)(2,1)} %get-tuple-element.41) | copy-start | bytes 294916
  142.1 29.8 %copy-start.8 = (bf16[3,1,128,128]{3,2,1,0:T(8,128)(2,1)S(1)}, bf16[3,1,128,128]{3,2,1,0:T(8,128)(2,1)}, u32[]{:S(2)}) copy-start(bf16[3,1,128,128]{3,2,1,0:T(8,128)(2,1)} %get-tuple-element.42) | copy-start | bytes 294916
  142.1 8.5 %collective-permute-start.4 = (bf16[16,128]{1,0:T(8,128)(2,1)S(1)}, bf16[16,128]{1,0:T(8,128)(2,1)S(1)}, u32[]{:S(2)}, u32[]{:S(2)}) collective-permute-start(bf16[16,128]{1,0:T(8,128)(2,1)S(1)} %get-tuple-element.26), channel_id=1, source_target_pairs={{0,9},{1,10},{2,11},{3,12},{4,13},{5,14},{6,15},{7,8},{8,17},{9,18... | collective-permute-start | bytes 12296 | tf_op jit(solution)/shard_map/ppermute | solution.py:267
  142.2 8.4 %collective-permute-start.5 = (bf16[16,128]{1,0:T(8,128)(2,1)S(1)}, bf16[16,128]{1,0:T(8,128)(2,1)S(1)}, u32[]{:S(2)}, u32[]{:S(2)}) collective-permute-start(bf16[16,128]{1,0:T(8,128)(2,1)S(1)} %get-tuple-element.27), channel_id=1, source_target_pairs={{0,15},{1,8},{2,9},{3,10},{4,11},{5,12},{6,13},{7,14},{8,23},{9,16... | collective-permute-start | bytes 12296 | tf_op jit(solution)/shard_map/ppermute | solution.py:267
  147.5 6.6 %collective-permute-start.6 = (bf16[16,128]{1,0:T(8,128)(2,1)S(1)}, bf16[16,128]{1,0:T(8,128)(2,1)S(1)}, u32[]{:S(2)}, u32[]{:S(2)}) collective-permute-start(bf16[16,128]{1,0:T(8,128)(2,1)S(1)} %get-tuple-element.28), channel_id=1, source_target_pairs={{0,25},{1,26},{2,27},{3,28},{4,29},{5,30},{6,31},{7,24},{8,1},{9,2... | collective-permute-start | bytes 12296 | tf_op jit(solution)/shard_map/ppermute | solution.py:267
  147.6 9.6 %collective-permute-start = (bf16[4,64,128]{2,1,0:T(8,128)(2,1)S(1)}, bf16[4,64,128]{2,1,0:T(8,128)(2,1)S(1)}, u32[]{:S(2)}, u32[]{:S(2)}) collective-permute-start(bf16[4,64,128]{2,1,0:T(8,128)(2,1)S(1)} %get-tuple-element.22), channel_id=1, source_target_pairs={{0,8},{1,9},{2,10},{3,11},{4,12},{5,13},{6,14},{7,15},{8,16},{9,17... | collective-permute-start | bytes 196616 | tf_op jit(solution)/shard_map/ppermute | solution.py:267
  147.7 9.5 %collective-permute-start.1 = (bf16[4,64,128]{2,1,0:T(8,128)(2,1)S(1)}, bf16[4,64,128]{2,1,0:T(8,128)(2,1)S(1)}, u32[]{:S(2)}, u32[]{:S(2)}) collective-permute-start(bf16[4,64,128]{2,1,0:T(8,128)(2,1)S(1)} %get-tuple-element.23), channel_id=1, source_target_pairs={{0,24},{1,25},{2,26},{3,27},{4,28},{5,29},{6,30},{7,31},{8,0},{9,1... | collective-permute-start | bytes 196616 | tf_op jit(solution)/shard_map/ppermute | solution.py:267
  150.6 6.6 %collective-permute-start.2 = (bf16[4,64,128]{2,1,0:T(8,128)(2,1)S(1)}, bf16[4,64,128]{2,1,0:T(8,128)(2,1)S(1)}, u32[]{:S(2)}, u32[]{:S(2)}) collective-permute-start(bf16[4,64,128]{2,1,0:T(8,128)(2,1)S(1)} %get-tuple-element.24), channel_id=1, source_target_pairs={{0,1},{1,2},{2,3},{3,4},{4,5},{5,6},{6,7},{7,0},{8,9},{9,10},{10,1... | collective-permute-start | bytes 196616 | tf_op jit(solution)/shard_map/ppermute | solution.py:267
  150.6 6.6 %collective-permute-start.3 = (bf16[4,64,128]{2,1,0:T(8,128)(2,1)S(1)}, bf16[4,64,128]{2,1,0:T(8,128)(2,1)S(1)}, u32[]{:S(2)}, u32[]{:S(2)}) collective-permute-start(bf16[4,64,128]{2,1,0:T(8,128)(2,1)S(1)} %get-tuple-element.25), channel_id=1, source_target_pairs={{0,7},{1,0},{2,1},{3,2},{4,3},{5,4},{6,5},{7,6},{8,15},{9,8},{10,9... | collective-permute-start | bytes 196616 | tf_op jit(solution)/shard_map/ppermute | solution.py:267
  154.2 3.0 %collective-permute-start.7 = (bf16[16,128]{1,0:T(8,128)(2,1)S(1)}, bf16[16,128]{1,0:T(8,128)(2,1)S(1)}, u32[]{:S(2)}, u32[]{:S(2)}) collective-permute-start(bf16[16,128]{1,0:T(8,128)(2,1)S(1)} %get-tuple-element.29), channel_id=1, source_target_pairs={{0,31},{1,24},{2,25},{3,26},{4,27},{5,28},{6,29},{7,30},{8,7},{9,0... | collective-permute-start | bytes 12296 | tf_op jit(solution)/shard_map/ppermute | solution.py:267
  159.4 9.5 %collective-permute-start.12 = (bf16[16,128]{1,0:T(8,128)(2,1)S(1)}, bf16[16,128]{1,0:T(8,128)(2,1)S(1)}, u32[]{:S(2)}, u32[]{:S(2)}) collective-permute-start(bf16[16,128]{1,0:T(8,128)(2,1)S(1)} %get-tuple-element.35), channel_id=1, source_target_pairs={{0,9},{1,10},{2,11},{3,12},{4,13},{5,14},{6,15},{7,8},{8,17},{9,18... | collective-permute-start | bytes 12296 | tf_op jit(solution)/shard_map/ppermute | solution.py:267
  159.5 9.6 %collective-permute-start.13 = (bf16[16,128]{1,0:T(8,128)(2,1)S(1)}, bf16[16,128]{1,0:T(8,128)(2,1)S(1)}, u32[]{:S(2)}, u32[]{:S(2)}) collective-permute-start(bf16[16,128]{1,0:T(8,128)(2,1)S(1)} %get-tuple-element.36), channel_id=1, source_target_pairs={{0,15},{1,8},{2,9},{3,10},{4,11},{5,12},{6,13},{7,14},{8,23},{9,16... | collective-permute-start | bytes 12296 | tf_op jit(solution)/shard_map/ppermute | solution.py:267
  163.9 8.0 %collective-permute-start.14 = (bf16[16,128]{1,0:T(8,128)(2,1)S(1)}, bf16[16,128]{1,0:T(8,128)(2,1)S(1)}, u32[]{:S(2)}, u32[]{:S(2)}) collective-permute-start(bf16[16,128]{1,0:T(8,128)(2,1)S(1)} %get-tuple-element.37), channel_id=1, source_target_pairs={{0,25},{1,26},{2,27},{3,28},{4,29},{5,30},{6,31},{7,24},{8,1},{9,2... | collective-permute-start | bytes 12296 | tf_op jit(solution)/shard_map/ppermute | solution.py:267
  163.9 14.4 %copy-start.1 = (f32[128]{0:T(128)S(1)}, f32[128]{0:T(128)}, u32[]{:S(2)}) copy-start(f32[128]{0:T(128)} %param.17) | copy-start | bytes 1540
  164.0 14.2 %collective-permute-start.10 = (bf16[4,64,128]{2,1,0:T(8,128)(2,1)S(1)}, bf16[4,64,128]{2,1,0:T(8,128)(2,1)S(1)}, u32[]{:S(2)}, u32[]{:S(2)}) collective-permute-start(bf16[4,64,128]{2,1,0:T(8,128)(2,1)S(1)} %get-tuple-element.33), channel_id=1, source_target_pairs={{0,1},{1,2},{2,3},{3,4},{4,5},{5,6},{6,7},{7,0},{8,9},{9,10},{10,1... | collective-permute-start | bytes 196616 | tf_op jit(solution)/shard_map/ppermute | solution.py:267
  164.1 14.1 %collective-permute-start.11 = (bf16[4,64,128]{2,1,0:T(8,128)(2,1)S(1)}, bf16[4,64,128]{2,1,0:T(8,128)(2,1)S(1)}, u32[]{:S(2)}, u32[]{:S(2)}) collective-permute-start(bf16[4,64,128]{2,1,0:T(8,128)(2,1)S(1)} %get-tuple-element.34), channel_id=1, source_target_pairs={{0,7},{1,0},{2,1},{3,2},{4,3},{5,4},{6,5},{7,6},{8,15},{9,8},{10,9... | collective-permute-start | bytes 196616 | tf_op jit(solution)/shard_map/ppermute | solution.py:267
  169.0 9.3 %collective-permute-start.8 = (bf16[4,64,128]{2,1,0:T(8,128)(2,1)S(1)}, bf16[4,64,128]{2,1,0:T(8,128)(2,1)S(1)}, u32[]{:S(2)}, u32[]{:S(2)}) collective-permute-start(bf16[4,64,128]{2,1,0:T(8,128)(2,1)S(1)} %get-tuple-element.31), channel_id=1, source_target_pairs={{0,8},{1,9},{2,10},{3,11},{4,12},{5,13},{6,14},{7,15},{8,16},{9,17... | collective-permute-start | bytes 196616 | tf_op jit(solution)/shard_map/ppermute | solution.py:267
  169.1 9.1 %collective-permute-start.9 = (bf16[4,64,128]{2,1,0:T(8,128)(2,1)S(1)}, bf16[4,64,128]{2,1,0:T(8,128)(2,1)S(1)}, u32[]{:S(2)}, u32[]{:S(2)}) collective-permute-start(bf16[4,64,128]{2,1,0:T(8,128)(2,1)S(1)} %get-tuple-element.32), channel_id=1, source_target_pairs={{0,24},{1,25},{2,26},{3,27},{4,28},{5,29},{6,30},{7,31},{8,0},{9,1... | collective-permute-start | bytes 196616 | tf_op jit(solution)/shard_map/ppermute | solution.py:267
  171.9 6.3 %collective-permute-start.15 = (bf16[16,128]{1,0:T(8,128)(2,1)S(1)}, bf16[16,128]{1,0:T(8,128)(2,1)S(1)}, u32[]{:S(2)}, u32[]{:S(2)}) collective-permute-start(bf16[16,128]{1,0:T(8,128)(2,1)S(1)} %get-tuple-element.38), channel_id=1, source_target_pairs={{0,31},{1,24},{2,25},{3,26},{4,27},{5,28},{6,29},{7,30},{8,7},{9,0... | collective-permute-start | bytes 12296 | tf_op jit(solution)/shard_map/ppermute | solution.py:267

commit v2 on v1

--- a/solution.py
+++ b/solution.py
@@ -40,6 +40,7 @@
 F32 = jnp.float32
 BF16 = jnp.bfloat16
 LIMIT = 48 * 1024 * 1024
+CORNERS = 16
 
 
 def shift_down(line, first):
@@ -59,23 +60,23 @@
     return (0.5 * value) * (1.0 + lax.erf(value * np.float32(np.sqrt(0.5))))
 
 
-def pick_lines(codes_ref, req_ref, lines, edge_refs, corner_refs):
-    tiles = edge_refs[0].shape[0]
-    side = edge_refs[0].shape[1]
-    rows = lax.broadcasted_iota(jnp.int32, corner_refs[0].shape, 0)
+def pick_lines(codes_ref, lines, message_refs, tiles):
+    side = lines.shape[1]
+    shape = (CORNERS, lines.shape[2])
+    rows = lax.broadcasted_iota(jnp.int32, shape, 0)
     for direction in range(8):
-        corner = jnp.zeros(corner_refs[0].shape, F32)
+        corner = jnp.zeros(shape, F32)
         for tile in range(tiles):
-            code = codes_ref[req_ref[direction], tile * 8 + direction]
-            line = lines[code]
+            line = lines[codes_ref[direction, tile * 8 + direction]]
             if direction < 4:
-                edge_refs[direction][tile] = line
+                message_refs[direction][pl.ds(tile * side, side), :] = line
             else:
                 at = side - 1 if direction in (4, 6) else 0
                 pixel = line.astype(F32)[at : at + 1]
                 corner = jnp.where(rows == tile, pixel, corner)
         if direction >= 4:
-            corner_refs[direction - 4][...] = corner.astype(BF16)
+            group = tiles * side + (direction % 2) * CORNERS
+            message_refs[direction // 2 - 2][pl.ds(group, CORNERS), :] = corner.astype(BF16)
 
 
 def flip_line(line):
@@ -86,10 +87,18 @@
     return jnp.dot(turn, line, preferred_element_type=F32).astype(BF16)
 
 
-def border_kernel(side, codes_ref, req_ref, x_ref, ring_ref, *rest):
-    edge_refs, corner_refs, lines = rest[:4], rest[4:8], rest[8]
+def gather_kernel(order_ref, x_ref, o_ref, sem):
+    def start(at, carry):
+        pltpu.make_async_copy(x_ref.at[order_ref[at]], o_ref.at[at], sem).start()
+        return carry
+
+    lax.fori_loop(0, order_ref.shape[0], start, 0)
+    pltpu.make_async_copy(x_ref, o_ref, sem).wait()
+
+
+def border_kernel(side, tiles, codes_ref, x_ref, ring_ref, *rest):
+    message_refs, lines = rest[:4], rest[4]
     tile = pl.program_id(0)
-    tiles = edge_refs[0].shape[0]
     image = x_ref[...].reshape(side, side, x_ref.shape[-1])
     ring = [image[0], image[1], image[side - 2], image[side - 1]]
     low = image[:, :16].astype(F32)
@@ -103,15 +112,18 @@
 
     @pl.when(tile == tiles - 1)
     def _():
-        pick_lines(codes_ref, req_ref, lines, edge_refs, corner_refs)
-
-
-def ring_kernel(codes_ref, req_ref, ring_ref, w_ref, b_ref, *rest):
-    pad_refs, pad_corner_refs = rest[:4], rest[4:8]
-    edge_refs, corner_refs, lines = rest[8:12], rest[12:16], rest[16]
+        pick_lines(codes_ref, lines, message_refs, tiles)
+
+
+def ring_kernel(codes_ref, ring_ref, w_ref, b_ref, *rest):
+    got_refs, message_refs, lines = rest[:4], rest[4:8], rest[8]
     tiles = ring_ref.shape[0]
     side = ring_ref.shape[2]
-    corners = [ref[...].astype(F32) for ref in pad_corner_refs]
+    pads = [[ref[pl.ds(t * side, side), :] for t in range(tiles)] for ref in got_refs]
+    corners = [
+        got_refs[2 + k % 2][pl.ds(tiles * side + k // 2 * CORNERS, CORNERS), :].astype(F32)
+        for k in range(4)
+    ]
     plans = [
         (0, 0, 1, 0, 1, 2, 3, 0, 1),
         (1, 2, 3, 3, 2, 2, 3, side - 1, side - 2),
@@ -121,12 +133,12 @@
     for edge, (pad, c_first, c_last, line_0, line_1, end_a, end_b, at_0, at_1) in enumerate(plans):
         stacked = []
         for tile in range(tiles):
-            begin = pad_refs[end_a][tile].astype(F32)
-            finish = pad_refs[end_b][tile].astype(F32)
+            begin = pads[end_a][tile].astype(F32)
+            finish = pads[end_b][tile].astype(F32)
             parts = []
             for line, first, last in (
                 (
-                    pad_refs[pad][tile],
+                    pads[pad][tile],
                     corners[c_first][tile : tile + 1],
                     corners[c_last][tile : tile + 1],
                 ),
@@ -148,7 +160,7 @@
             line = hidden[tile * side : (tile + 1) * side]
             lines[tile * 4 + edge] = line
             lines[tiles * 4 + tile * 4 + edge] = flip_line(line)
-    pick_lines(codes_ref, req_ref, lines, edge_refs, corner_refs)
+    pick_lines(codes_ref, lines, message_refs, tiles)
 
 
 def convolve_tile(padded, left, right, c_left, c_right, w_ref, w_side_ref, bias, y, ends, finish):
@@ -203,8 +215,8 @@
     image = x_ref[...].reshape(side, side, chan)
     fields = (padded, hidden)
     for field, pad in zip(fields, pads):
-        field[0, 0] = pad[0][0]
-        field[half, 1] = pad[1][0]
+        field[0, 0] = pad[0][...]
+        field[half, 1] = pad[1][...]
     padded[0, 1] = image[0]
     padded[1:half] = image[1 : side - 1].reshape(half - 1, 2, side, chan)
     padded[half, 0] = image[side - 1]
@@ -217,13 +229,15 @@
         out_ref[0, row] = (centre + value).astype(BF16)
 
     for at, finish in enumerate((keep_hidden, keep_out)):
+        own = lax.broadcasted_iota(jnp.int32, (CORNERS, chan), 0) == pl.program_id(0)
         upper_left, upper_right, lower_left, lower_right = (
-            ref[0, 0:1].astype(F32) for ref in corners[at]
+            jnp.sum(jnp.where(own, ref[...].astype(F32), 0.0), axis=0, keepdims=True)
+            for ref in corners[at]
         )
         convolve_tile(
             fields[at],
-            pads[at][2][0],
-            pads[at][3][0],
+            pads[at][2][...],
+            pads[at][3][...],
             (upper_left, lower_left),
             (upper_right, lower_right),
             w_refs[at],
@@ -256,85 +270,55 @@
     return stacked.reshape(4, 9 * chan_in, chan_out)
 
 
-def exchange(arrays, faces, columns):
-    got = []
-    for array, (face_off, tile_off) in zip(arrays, DIRECTIONS):
-        pairs = []
-        for face in range(faces):
-            for tile in range(columns):
-                to = ((face - face_off) % faces) * columns + (tile - tile_off) % columns
-                pairs.append((face * columns + tile, to))
-        got.append(lax.ppermute(array, AXES, pairs))
-    return got
+def along(array, axis, step):
+    size = lax.axis_size(axis)
+    return lax.ppermute(array, axis, [(i, (i + step) % size) for i in range(size)])
+
+
+def exchange(messages, split):
+    upper = along(messages[0], "face", 1)
+    lower = along(messages[1], "face", -1)
+    right = jnp.concatenate(
+        [messages[2][:split], upper[split : split + CORNERS], lower[split : split + CORNERS]], 0
+    )
+    left = jnp.concatenate(
+        [messages[3][:split], upper[split + CORNERS :], lower[split + CORNERS :]], 0
+    )
+    return [upper, lower, along(right, "tile", 1), along(left, "tile", -1)]
 
 
 def shards(latitude_rows, tile_order, neighbours, rotations, w_first, b_first, w_second, b_second):
-    faces, columns = lax.axis_size("face"), lax.axis_size("tile")
-    devices = faces * columns
+    devices = lax.axis_size("face") * lax.axis_size("tile")
     tiles = neighbours.shape[0]
     piece, chan = latitude_rows.shape[1:]
     side = int(round((piece * devices) ** 0.5))
     vmem_spec = pl.BlockSpec(memory_space=VMEM)
     smem_spec = pl.BlockSpec(memory_space=pltpu.SMEM)
+    any_spec = pl.BlockSpec(memory_space=pl.ANY)
     params = pltpu.CompilerParams(vmem_limit_bytes=LIMIT)
 
     turn = rotations[..., None] == jnp.arange(4, dtype=jnp.int32)
     strip = jnp.sum(jnp.where(turn, jnp.asarray(STRIP_TABLE)[None], 0), -1)
     flip = jnp.sum(jnp.where(turn, jnp.asarray(FLIP_TABLE)[None], 0), -1)
-    code = (flip * tiles + neighbours % tiles) * 4 + strip
-    codes = lax.all_gather(code.reshape(1, tiles * 8), AXES, axis=0, tiled=True)
-    face, column = lax.axis_index("face"), lax.axis_index("tile")
-    asking = jnp.stack(
-        [((face - f) % faces) * columns + (column - t) % columns for f, t in DIRECTIONS]
-    ).astype(jnp.int32)
-
-    ordered = latitude_rows.at[tile_order].get(mode="promise_in_bounds")
+    code = ((flip * tiles + neighbours % tiles) * 4 + strip).reshape(1, tiles * 8)
+    after, before = along(code, "face", -1), along(code, "face", 1)
+
+    ordered = pl.pallas_call(
+        gather_kernel,
+        in_specs=[smem_spec, any_spec],
+        out_specs=any_spec,
+        out_shape=jax.ShapeDtypeStruct(latitude_rows.shape, latitude_rows.dtype),
+        scratch_shapes=[pltpu.SemaphoreType.DMA],
+        compiler_params=params,
+        name="order",
+    )(tile_order, latitude_rows)
+    ordered, after, before = lax.optimization_barrier((ordered, after, before))
     gathered = lax.all_to_all(ordered, AXES, split_axis=0, concat_axis=0, tiled=True)
-    pieces = gathered.reshape(devices, tiles, piece, chan)
-    tile_spec = pl.BlockSpec((devices, 1, piece, chan), lambda t: (0, t, 0, 0))
-
-    edge_shape = jax.ShapeDtypeStruct((tiles, side, chan), BF16)
-    corner_shape = jax.ShapeDtypeStruct((16, chan), BF16)
-    lines_scratch = VMEM((8 * tiles, side, chan), BF16)
-    edge_out = pl.BlockSpec((tiles, side, chan), lambda t: (0, 0, 0))
-    corner_out = pl.BlockSpec((16, chan), lambda t: (0, 0))
-    ring, *sends = pl.pallas_call(
-        functools.partial(border_kernel, side),
-        grid=(tiles,),
-        in_specs=[smem_spec, smem_spec, tile_spec],
-        out_specs=[pl.BlockSpec((1, 8, side, chan), lambda t: (t, 0, 0, 0))]
-        + [edge_out] * 4
-        + [corner_out] * 4,
-        out_shape=[jax.ShapeDtypeStruct((tiles, 8, side, chan), BF16)]
-        + [edge_shape] * 4
-        + [corner_shape] * 4,
-        scratch_shapes=[lines_scratch],
-        compiler_params=params,
-        name="borders",
-    )(codes, asking, pieces)
-    pads_first = exchange(sends, faces, columns)
-
-    sends = pl.pallas_call(
-        ring_kernel,
-        in_specs=[smem_spec, smem_spec] + [vmem_spec] * 11,
-        out_specs=[vmem_spec] * 8,
-        out_shape=[edge_shape] * 4 + [corner_shape] * 4,
-        scratch_shapes=[lines_scratch],
-        compiler_params=params,
-        name="hidden_ring",
-    )(codes, asking, ring, edge_weights(w_first), b_first.reshape(1, chan), *pads_first)
-    pads_second = exchange(sends, faces, columns)
-
-    edge_in = pl.BlockSpec((1, side, chan), lambda t: (t, 0, 0))
-    corner_in = pl.BlockSpec((1, 8, chan), lambda t: (t, 0, 0))
-
-    def whole(array):
-        return pl.BlockSpec(array.shape, lambda t: (0,) * array.ndim)
-
-    def spread(pads):
-        corners = [jnp.broadcast_to(c[:tiles, None], (tiles, 8, chan)) for c in pads[4:]]
-        return list(pads[:4]) + corners
-
+    column = jnp.concatenate([code, after, before], 0)
+    on, back = along(column, "tile", -1), along(column, "tile", 1)
+    codes = jnp.concatenate(
+        [after, before] + [side_rows[i : i + 1] for i in range(3) for side_rows in (on, back)], 0
+    )
     constants = [
         paired_weights(w_first),
         paired_weights(w_second),
@@ -343,14 +327,58 @@
         b_first.reshape(1, chan),
         b_second.reshape(1, chan),
     ]
+    w_edges = edge_weights(w_first)
+    gathered, codes, w_edges, *constants = lax.optimization_barrier(
+        (gathered, codes, w_edges, *constants)
+    )
+    pieces = gathered.reshape(devices, tiles, piece, chan)
+    tile_spec = pl.BlockSpec((devices, 1, piece, chan), lambda t: (0, t, 0, 0))
+
+    split = tiles * side
+    message_shape = jax.ShapeDtypeStruct((split + 2 * CORNERS, chan), BF16)
+    lines_scratch = VMEM((8 * tiles, side, chan), BF16)
+    ring, *sends = pl.pallas_call(
+        functools.partial(border_kernel, side, tiles),
+        grid=(tiles,),
+        in_specs=[smem_spec, tile_spec],
+        out_specs=[pl.BlockSpec((1, 8, side, chan), lambda t: (t, 0, 0, 0))]
+        + [pl.BlockSpec(message_shape.shape, lambda t: (0, 0))] * 4,
+        out_shape=[jax.ShapeDtypeStruct((tiles, 8, side, chan), BF16)] + [message_shape] * 4,
+        scratch_shapes=[lines_scratch],
+        compiler_params=params,
+        name="borders",
+    )(codes, pieces)
+    got_first = exchange(sends, split)
+
+    sends = pl.pallas_call(
+        ring_kernel,
+        in_specs=[smem_spec] + [vmem_spec] * 7,
+        out_specs=[vmem_spec] * 4,
+        out_shape=[message_shape] * 4,
+        scratch_shapes=[lines_scratch],
+        compiler_params=params,
+        name="hidden_ring",
+    )(codes, ring, w_edges, b_first.reshape(1, chan), *got_first)
+    got_second = exchange(sends, split)
+
+    def whole(array):
+        return pl.BlockSpec(array.shape, lambda t: (0,) * array.ndim)
+
+    def group(at):
+        return pl.BlockSpec((CORNERS, chan), lambda t: (split // CORNERS + at, 0))
+
+    edge_in = pl.BlockSpec((side, chan), lambda t: (t, 0))
+    pad_specs = [edge_in] * 4 + [group(0), group(0), group(1), group(1)]
+
+    def pads(got):
+        return got + [got[2], got[3], got[2], got[3]]
+
     blocks = 4
     field = VMEM((side // 2 + 1, 2, side, chan), BF16)
     return pl.pallas_call(
         functools.partial(level_kernel, side),
         grid=(tiles,),
-        in_specs=[tile_spec]
-        + ([edge_in] * 4 + [corner_in] * 4) * 2
-        + [whole(c) for c in constants],
+        in_specs=[tile_spec] + pad_specs * 2 + [whole(c) for c in constants],
         out_specs=pl.BlockSpec((1, side, side, chan), lambda t: (t, 0, 0, 0)),
         out_shape=jax.ShapeDtypeStruct((tiles, side, side, chan), BF16),
         scratch_shapes=[
@@ -361,7 +389,7 @@
         ],
         compiler_params=params,
         name="level",
-    )(pieces, *spread(pads_first), *spread(pads_second), *constants)
+    )(pieces, *pads(got_first), *pads(got_second), *constants)
 
 
 def solution(mesh):

time: 196 us -> 158 us (0.81)
  blocking collectives: 122 us -> 0 us
  waiting for transfers between devices: 2.98 us -> 98.3 us
  starting transfers between devices: 31.7 us -> 21.1 us
  local copies, waits for them, and re-layouts: 14.6 us -> 10.6 us
  Pallas kernels: 22.6 us -> 25 us
    all_gather x1 -> x0, blocking collectives: 122 us -> none  [shards(): codes = lax.all_gather(code.reshape(1, tiles * 8), AXES, axis=0, tiled=True)]
    ppermute x16 -> x12, waiting for transfers between devices: 2.98 us -> 75.6 us  [along(): lax.ppermute(array, axis, [(i, (i + step) % size) for i in range(size)])]
    all_to_all x1, waiting for transfers between devices: 0.01 us -> 22.7 us  [shards(): lax.all_to_all(ordered, AXES, split_axis=0, concat_axis=0, tiled=True)]
    ppermute x16 -> x12, starting transfers between devices: 24.3 us -> 14.6 us  [along(): lax.ppermute(array, axis, [(i, (i + step) % size) for i in range(size)])]
    gather x1 -> x0, local copies, waits for them, and re-layouts: 5.28 us -> none  [shards(): ordered = latitude_rows.at[tile_order].get(mode='promise_in_bounds')]
    unnamed x31 -> x20, local copies, waits for them, and re-layouts: 3.09 us -> 5.74 us
    pallas_call x2 -> x3, Pallas kernels: 5.65 us -> 8.14 us  [the longest x1 3.38 us: shards(): pl.pallas_call(functools.partial(border_kernel, side, tiles), grid=(tiles...]
  transfers between devices with their start and end apart: 17 -> 13, of which waited for: 1 -> 10; matrix products, arithmetic and copies ran while one was open for 5% -> 6% of each run, Pallas kernels for 0% -> 2%
where the time goes in v2:
time: 158 us
  waiting for transfers between devices  98.3 us (62%)
  Pallas kernels  25 us (16%)
  starting transfers between devices  21.1 us (13%)
  local copies, waits for them, and re-layouts  10.6 us (7%)
  other arithmetic  2.69 us (2%)
    ppermute x12, waiting for transfers between devices, along(): lax.ppermute(array, axis, [(i, (i + step) % size) for i in range(size)])  75.6 us
    all_to_all x1, waiting for transfers between devices, shards(): lax.all_to_all(ordered, AXES, split_axis=0, concat_axis=0, tiled=True)  22.7 us
    pallas_call x1, Pallas kernels, shards(): pl.pallas_call(functools.partial(level_kernel, side), grid=(tiles,), in_s...  16.8 us
    ppermute x12, starting transfers between devices, along(): lax.ppermute(array, axis, [(i, (i + step) % size) for i in range(size)])  14.6 us
    all_to_all x1, starting transfers between devices, shards(): lax.all_to_all(ordered, AXES, split_axis=0, concat_axis=0, tiled=True)  6.46 us
    unnamed x20, local copies, waits for them, and re-layouts  5.74 us
    another operation x4, local copies, waits for them, and re-layouts, paired_weights(): return jnp.stack([first, second], 2).reshape(4 * chan_in, 6 * chan_out)  3.85 us
    pallas_call x1, Pallas kernels, shards(): pl.pallas_call(functools.partial(border_kernel, side, tiles), grid=(tiles...  3.38 us
  transfers between devices with their start and end apart: 13, of which 10 were waited for; matrix products, arithmetic and copies ran while one was open for 6% of the time, Pallas kernels for 2%

profile of v2, /device:TPU:0, one launch (start us, length us, event | category | flops | bytes accessed | tf_op | source)
XLA Modules:
  0.0 157.8 jit_solution(5209060482666218946)
XLA Ops:
  0.0 0.7 select_reduce_fusion.1
  0.7 0.7 fusion.3
  1.5 3.9 %collective-permute-start = (s32[1,32]{1,0:T(1,128)S(1)}, s32[1,32]{1,0:T(1,128)S(1)}, u32[]{:S(2)}, u32[]{:S(2)}) collective-permute-start(s32[1,32]{1,0:T(1,128)S(1)} %reshape.47), channel_id=1, source_target_pairs={{0,24},{8,0},{16,8},{24,16},{1,25},{9,1},{17,9},{25,17},{2,26},{10... | collective-permute-start | bytes 392 | tf_op jit(solution)/shard_map/ppermute | solution.py:275
  5.4 0.7 copy-done.2
  6.1 2.8 %order.1 = bf16[128,128,128]{2,1,0:T(8,128)(2,1)S(1)} custom-call(s32[128]{0:T(128)S(1)} %copy-done.2, bf16[128,128,128]{2,1,0:T(8,128)(2,1)} %x_ref.1), custom_call_target="tpu_custom_call" | custom-call | tf_op jit(solution)/shard_map/order/pallas_call | solution.py:306
  8.9 2.0 %copy-done = bf16[128,128,128]{2,1,0:T(8,128)(2,1)} copy-done((bf16[128,128,128]{2,1,0:T(8,128)(2,1)}, bf16[128,128,128]{2,1,0:T(8,128)(2,1)S(1)}, u32[]{:S(2)}) %copy-start) | copy-done | bytes 4194328
  10.9 6.5 %all-to-all-start = ((bf16[128,128,128]{2,1,0:T(8,128)(2,1)}), bf16[128,128,128]{2,1,0:T(8,128)(2,1)}, u32[]{:S(2)}, u32[]{:S(2)}) async-start(bf16[128,128,128]{2,1,0:T(8,128)(2,1)} %copy-done), calls=%async_computation | async-start | bytes 8388608 | tf_op jit(solution)/shard_map/all_to_all | solution.py:316
  17.7 0.7 rev.6
  19.1 1.0 pad_maximum_fusion.2
  20.4 1.8 %copy.30 = bf16[4,128,2,384]{3,2,1,0:T(2,128)(2,1)} copy(bf16[4,128,2,384]{1,3,0,2:T(8,128)(2,1)S(1)} %pad_maximum_fusion.1) | data formatting | bytes 1572864 | tf_op jit(solution)/shard_map/stack | solution.py:258
  22.3 1.3 copy.37
  23.6 1.8 %copy.34 = bf16[4,128,2,384]{3,2,1,0:T(2,128)(2,1)} copy(bf16[4,128,2,384]{1,3,0,2:T(8,128)(2,1)S(1)} %copy-done.5) | data formatting | bytes 1572864 | tf_op jit(solution)/shard_map/stack | solution.py:258
  25.4 1.3 copy.38
  26.7 3.4 %collective-permute-start.2 = (s32[3,32]{1,0:T(4,128)S(1)}, s32[3,32]{1,0:T(4,128)S(1)}, u32[]{:S(2)}, u32[]{:S(2)}) collective-permute-start(s32[3,32]{1,0:T(4,128)S(1)} %pad_add_fusion), channel_id=1, source_target_pairs={{0,7},{1,0},{2,1},{3,2},{4,3},{5,4},{6,5},{7,6},{8,15},{9,8},{10,9... | collective-permute-start | bytes 1160 | tf_op jit(solution)/shard_map/ppermute | solution.py:275
  30.1 59.6 %collective-permute-done.3 = s32[3,32]{1,0:T(4,128)S(1)} collective-permute-done((s32[3,32]{1,0:T(4,128)S(1)}, s32[3,32]{1,0:T(4,128)S(1)}, u32[]{:S(2)}, u32[]{:S(2)}) %collective-permute-start.3) | collective-permute-done | bytes 416 | tf_op jit(solution)/shard_map/ppermute | solution.py:275
  89.7 22.7 %all-to-all-done = bf16[128,128,128]{2,1,0:T(8,128)(2,1)} async-done(((bf16[128,128,128]{2,1,0:T(8,128)(2,1)}), bf16[128,128,128]{2,1,0:T(8,128)(2,1)}, u32[]{:S(2)}, u32[]{:S(2)}) %all-to-all-start) | async-done | bytes 4194336 | tf_op jit(solution)/shard_map/all_to_all | solution.py:316
  112.4 3.4 %borders.1 = (bf16[4,8,64,128]{3,2,1,0:T(8,128)(2,1)S(1)}, bf16[288,128]{1,0:T(8,128)(2,1)S(1)}, bf16[288,128]{1,0:T(8,128)(2,1)S(1)}, bf16[288,128]{1,0:T(8,128)(2,1)S(1)}, bf16[288,128]{1,0:T(8,128)(2,1)S(1)}) custom-call(s32[8,32]{1,0:T(8,128)S(1)} %concatenate.34.codes_ref, bf16[32,4,128,128]{3,2,1,0:T(8,128)(2,1)} %bitcast.21.x_ref), custom_call_target="tpu_custom_call" | custom-call | tf_op jit(solution)/shard_map/borders/pallas_call | solution.py:340
  115.9 2.9 %collective-permute-start.5 = (bf16[288,128]{1,0:T(8,128)(2,1)S(1)}, bf16[288,128]{1,0:T(8,128)(2,1)S(1)}, u32[]{:S(2)}, u32[]{:S(2)}) collective-permute-start(bf16[288,128]{1,0:T(8,128)(2,1)S(1)} %get-tuple-element.32), channel_id=1, source_target_pairs={{0,24},{8,0},{16,8},{24,16},{1,25},{9,1},{17,9},{25,17},{2,26},{10... | collective-permute-start | bytes 221192 | tf_op jit(solution)/shard_map/ppermute | solution.py:275
  118.8 2.6 %collective-permute-done.4.rest_0_ = bf16[288,128]{1,0:T(8,128)(2,1)S(1)} collective-permute-done((bf16[288,128]{1,0:T(8,128)(2,1)S(1)}, bf16[288,128]{1,0:T(8,128)(2,1)S(1)}, u32[]{:S(2)}, u32[]{:S(2)}) %collective-permute-start.4) | collective-permute-done | bytes 73760 | tf_op jit(solution)/shard_map/ppermute | solution.py:275
  121.4 0.5 collective-permute-done.5.rest_1_
  122.0 0.5 collective-permute-start.6
  122.5 1.6 %collective-permute-done.7.rest_3_.rest_5_.rest_7_ = bf16[288,128]{1,0:T(8,128)(2,1)S(1)} collective-permute-done((bf16[288,128]{1,0:T(8,128)(2,1)S(1)}, bf16[288,128]{1,0:T(8,128)(2,1)S(1)}, u32[]{:S(2)}, u32[]{:S(2)}) %collective-permute-start.7) | collective-permute-done | bytes 73760 | tf_op jit(solution)/shard_map/ppermute | solution.py:275
  124.1 3.5 %collective-permute-done.6.rest_2_.rest_4_.rest_6_ = bf16[288,128]{1,0:T(8,128)(2,1)S(1)} collective-permute-done((bf16[288,128]{1,0:T(8,128)(2,1)S(1)}, bf16[288,128]{1,0:T(8,128)(2,1)S(1)}, u32[]{:S(2)}, u32[]{:S(2)}) %collective-permute-start.6) | collective-permute-done | bytes 73760 | tf_op jit(solution)/shard_map/ppermute | solution.py:275
  127.7 2.0 %hidden_ring.1 = (bf16[288,128]{1,0:T(8,128)(2,1)S(1)}, bf16[288,128]{1,0:T(8,128)(2,1)S(1)}, bf16[288,128]{1,0:T(8,128)(2,1)S(1)}, bf16[288,128]{1,0:T(8,128)(2,1)S(1)}) custom-call(s32[8,32]{1,0:T(8,128)S(1)} %concatenate.34.codes_ref, bf16[4,8,64,128]{3,2,1,0:T(8,128)(2,1)S(1)} %get-tuple-element.35.ring_ref, ...), custom_call_target="tpu_custom_call" | custom-call | tf_op jit(solution)/shard_map/hidden_ring/pallas_call | solution.py:353
  129.6 1.2 collective-permute-start.8
  130.9 1.7 %collective-permute-start.9 = (bf16[288,128]{1,0:T(8,128)(2,1)S(1)}, bf16[288,128]{1,0:T(8,128)(2,1)S(1)}, u32[]{:S(2)}, u32[]{:S(2)}) collective-permute-start(bf16[288,128]{1,0:T(8,128)(2,1)S(1)} %get-tuple-element.38), channel_id=1, source_target_pairs={{0,24},{8,0},{16,8},{24,16},{1,25},{9,1},{17,9},{25,17},{2,26},{10... | collective-permute-start | bytes 221192 | tf_op jit(solution)/shard_map/ppermute | solution.py:275
  132.6 2.3 %collective-permute-done.8.rest_8_ = bf16[288,128]{1,0:T(8,128)(2,1)S(1)} collective-permute-done((bf16[288,128]{1,0:T(8,128)(2,1)S(1)}, bf16[288,128]{1,0:T(8,128)(2,1)S(1)}, u32[]{:S(2)}, u32[]{:S(2)}) %collective-permute-start.8) | collective-permute-done | bytes 73760 | tf_op jit(solution)/shard_map/ppermute | solution.py:275
  135.0 0.3 collective-permute-done.9.rest_9_
  135.4 0.5 collective-permute-start.10
  135.8 2.0 %collective-permute-done.11.rest_11_.rest_13_.rest_15_ = bf16[288,128]{1,0:T(8,128)(2,1)S(1)} collective-permute-done((bf16[288,128]{1,0:T(8,128)(2,1)S(1)}, bf16[288,128]{1,0:T(8,128)(2,1)S(1)}, u32[]{:S(2)}, u32[]{:S(2)}) %collective-permute-start.11) | collective-permute-done | bytes 73760 | tf_op jit(solution)/shard_map/ppermute | solution.py:275
  137.8 3.2 %collective-permute-done.10.rest_10_.rest_12_.rest_14_ = bf16[288,128]{1,0:T(8,128)(2,1)S(1)} collective-permute-done((bf16[288,128]{1,0:T(8,128)(2,1)S(1)}, bf16[288,128]{1,0:T(8,128)(2,1)S(1)}, u32[]{:S(2)}, u32[]{:S(2)}) %collective-permute-start.10) | collective-permute-done | bytes 73760 | tf_op jit(solution)/shard_map/ppermute | solution.py:275
  141.0 16.8 %level.1 = bf16[4,64,64,128]{3,2,1,0:T(8,128)(2,1)} custom-call(bf16[32,4,128,128]{3,2,1,0:T(8,128)(2,1)} %bitcast.21.x_ref, bf16[288,128]{1,0:T(8,128)(2,1)S(1)} %collective-permute-done.4.rest_0_, bf16[288,128]{1,0:T(8,128)(2,1)S(1)} %collective-permute-done.5.rest_1_, bf16[288,128]{1,0:T(8,128)(2,1)S(1)} %collective-permute-done.6.rest_2_.rest_4_.rest_6_, ...), custom_call_target="tpu_custom_call" | custom-call | tf_op jit(solution)/shard_map/level/pallas_call | solution.py:378
  (51 shorter events, 1.7 us)
Async XLA Ops:
  1.5 9.4 %collective-permute-start = (s32[1,32]{1,0:T(1,128)S(1)}, s32[1,32]{1,0:T(1,128)S(1)}, u32[]{:S(2)}, u32[]{:S(2)}) collective-permute-start(s32[1,32]{1,0:T(1,128)S(1)} %reshape.47), channel_id=1, source_target_pairs={{0,24},{8,0},{16,8},{24,16},{1,25},{9,1},{17,9},{25,17},{2,26},{10... | collective-permute-start | bytes 392 | tf_op jit(solution)/shard_map/ppermute | solution.py:275
  5.4 5.5 %collective-permute-start.1 = (s32[1,32]{1,0:T(1,128)S(1)}, s32[1,32]{1,0:T(1,128)S(1)}, u32[]{:S(2)}, u32[]{:S(2)}) collective-permute-start(s32[1,32]{1,0:T(1,128)S(1)} %reshape.47), channel_id=1, source_target_pairs={{0,8},{8,16},{16,24},{24,0},{1,9},{9,17},{17,25},{25,1},{2,10},{10... | collective-permute-start | bytes 392 | tf_op jit(solution)/shard_map/ppermute | solution.py:275
  5.4 0.7 copy-start.2
  8.9 2.0 %copy-start = (bf16[128,128,128]{2,1,0:T(8,128)(2,1)}, bf16[128,128,128]{2,1,0:T(8,128)(2,1)S(1)}, u32[]{:S(2)}) copy-start(bf16[128,128,128]{2,1,0:T(8,128)(2,1)S(1)} %order.1) | copy-start | bytes 12582916
  10.9 6.5 %copy-start.4 = (bf16[3,3,128,128]{3,2,1,0:T(8,128)(2,1)S(1)}, bf16[3,3,128,128]{3,2,1,0:T(8,128)(2,1)}, u32[]{:S(2)}) copy-start(bf16[3,3,128,128]{3,2,1,0:T(8,128)(2,1)} %param.14) | copy-start | bytes 884740
  10.9 101.6 %all-to-all-start = ((bf16[128,128,128]{2,1,0:T(8,128)(2,1)}), bf16[128,128,128]{2,1,0:T(8,128)(2,1)}, u32[]{:S(2)}, u32[]{:S(2)}) async-start(bf16[128,128,128]{2,1,0:T(8,128)(2,1)} %copy-done), calls=%async_computation | async-start | bytes 8388608 | tf_op jit(solution)/shard_map/all_to_all | solution.py:316
  17.4 1.0 copy-start.7
  19.0 1.0 copy-start.6
  20.2 69.5 %collective-permute-start.3 = (s32[3,32]{1,0:T(4,128)S(1)}, s32[3,32]{1,0:T(4,128)S(1)}, u32[]{:S(2)}, u32[]{:S(2)}) collective-permute-start(s32[3,32]{1,0:T(4,128)S(1)} %pad_add_fusion), channel_id=1, source_target_pairs={{0,1},{1,2},{2,3},{3,4},{4,5},{5,6},{6,7},{7,0},{8,9},{9,10},{10,1... | collective-permute-start | bytes 1160 | tf_op jit(solution)/shard_map/ppermute | solution.py:275
  22.3 1.4 copy-start.5
  26.7 63.0 %collective-permute-start.2 = (s32[3,32]{1,0:T(4,128)S(1)}, s32[3,32]{1,0:T(4,128)S(1)}, u32[]{:S(2)}, u32[]{:S(2)}) collective-permute-start(s32[3,32]{1,0:T(4,128)S(1)} %pad_add_fusion), channel_id=1, source_target_pairs={{0,7},{1,0},{2,1},{3,2},{4,3},{5,4},{6,5},{7,6},{8,15},{9,8},{10,9... | collective-permute-start | bytes 1160 | tf_op jit(solution)/shard_map/ppermute | solution.py:275
  112.4 15.2 %copy-start.1 = (f32[128]{0:T(128)S(1)}, f32[128]{0:T(128)}, u32[]{:S(2)}) copy-start(f32[128]{0:T(128)} %param.15) | copy-start | bytes 1540
  115.8 5.6 %collective-permute-start.4 = (bf16[288,128]{1,0:T(8,128)(2,1)S(1)}, bf16[288,128]{1,0:T(8,128)(2,1)S(1)}, u32[]{:S(2)}, u32[]{:S(2)}) collective-permute-start(bf16[288,128]{1,0:T(8,128)(2,1)S(1)} %get-tuple-element.31), channel_id=1, source_target_pairs={{0,8},{8,16},{16,24},{24,0},{1,9},{9,17},{17,25},{25,1},{2,10},{10... | collective-permute-start | bytes 221192 | tf_op jit(solution)/shard_map/ppermute | solution.py:275
  115.9 6.0 %collective-permute-start.5 = (bf16[288,128]{1,0:T(8,128)(2,1)S(1)}, bf16[288,128]{1,0:T(8,128)(2,1)S(1)}, u32[]{:S(2)}, u32[]{:S(2)}) collective-permute-start(bf16[288,128]{1,0:T(8,128)(2,1)S(1)} %get-tuple-element.32), channel_id=1, source_target_pairs={{0,24},{8,0},{16,8},{24,16},{1,25},{9,1},{17,9},{25,17},{2,26},{10... | collective-permute-start | bytes 221192 | tf_op jit(solution)/shard_map/ppermute | solution.py:275
  121.9 2.2 %collective-permute-start.7 = (bf16[288,128]{1,0:T(8,128)(2,1)S(1)}, bf16[288,128]{1,0:T(8,128)(2,1)S(1)}, u32[]{:S(2)}, u32[]{:S(2)}) collective-permute-start(bf16[288,128]{1,0:T(8,128)(2,1)S(1)} %pad_maximum_fusion.6), channel_id=1, source_target_pairs={{0,7},{1,0},{2,1},{3,2},{4,3},{5,4},{6,5},{7,6},{8,15},{9,8},{10,9... | collective-permute-start | bytes 221192 | tf_op jit(solution)/shard_map/ppermute | solution.py:275
  122.0 5.6 %collective-permute-start.6 = (bf16[288,128]{1,0:T(8,128)(2,1)S(1)}, bf16[288,128]{1,0:T(8,128)(2,1)S(1)}, u32[]{:S(2)}, u32[]{:S(2)}) collective-permute-start(bf16[288,128]{1,0:T(8,128)(2,1)S(1)} %pad_maximum_fusion.5), channel_id=1, source_target_pairs={{0,1},{1,2},{2,3},{3,4},{4,5},{5,6},{6,7},{7,0},{8,9},{9,10},{10,1... | collective-permute-start | bytes 221192 | tf_op jit(solution)/shard_map/ppermute | solution.py:275
  127.7 13.3 %copy-start.3 = (f32[128]{0:T(128)S(1)}, f32[128]{0:T(128)}, u32[]{:S(2)}) copy-start(f32[128]{0:T(128)} %param.17) | copy-start | bytes 1540
  129.6 5.3 %collective-permute-start.8 = (bf16[288,128]{1,0:T(8,128)(2,1)S(1)}, bf16[288,128]{1,0:T(8,128)(2,1)S(1)}, u32[]{:S(2)}, u32[]{:S(2)}) collective-permute-start(bf16[288,128]{1,0:T(8,128)(2,1)S(1)} %get-tuple-element.37), channel_id=1, source_target_pairs={{0,8},{8,16},{16,24},{24,0},{1,9},{9,17},{17,25},{25,1},{2,10},{10... | collective-permute-start | bytes 221192 | tf_op jit(solution)/shard_map/ppermute | solution.py:275
  130.9 4.4 %collective-permute-start.9 = (bf16[288,128]{1,0:T(8,128)(2,1)S(1)}, bf16[288,128]{1,0:T(8,128)(2,1)S(1)}, u32[]{:S(2)}, u32[]{:S(2)}) collective-permute-start(bf16[288,128]{1,0:T(8,128)(2,1)S(1)} %get-tuple-element.38), channel_id=1, source_target_pairs={{0,24},{8,0},{16,8},{24,16},{1,25},{9,1},{17,9},{25,17},{2,26},{10... | collective-permute-start | bytes 221192 | tf_op jit(solution)/shard_map/ppermute | solution.py:275
  135.3 2.5 %collective-permute-start.11 = (bf16[288,128]{1,0:T(8,128)(2,1)S(1)}, bf16[288,128]{1,0:T(8,128)(2,1)S(1)}, u32[]{:S(2)}, u32[]{:S(2)}) collective-permute-start(bf16[288,128]{1,0:T(8,128)(2,1)S(1)} %pad_maximum_fusion.8), channel_id=1, source_target_pairs={{0,7},{1,0},{2,1},{3,2},{4,3},{5,4},{6,5},{7,6},{8,15},{9,8},{10,9... | collective-permute-start | bytes 221192 | tf_op jit(solution)/shard_map/ppermute | solution.py:275
  135.4 5.6 %collective-permute-start.10 = (bf16[288,128]{1,0:T(8,128)(2,1)S(1)}, bf16[288,128]{1,0:T(8,128)(2,1)S(1)}, u32[]{:S(2)}, u32[]{:S(2)}) collective-permute-start(bf16[288,128]{1,0:T(8,128)(2,1)S(1)} %pad_maximum_fusion.7), channel_id=1, source_target_pairs={{0,1},{1,2},{2,3},{3,4},{4,5},{5,6},{6,7},{7,0},{8,9},{9,10},{10,1... | collective-permute-start | bytes 221192 | tf_op jit(solution)/shard_map/ppermute | solution.py:275

commit v3 on v2

v3 whole, which is shorter than its diff:
```python
import functools

import jax
import jax.numpy as jnp
import numpy as np
from jax import lax
from jax.experimental import pallas as pl
from jax.experimental.pallas import tpu as pltpu
from jax.sharding import PartitionSpec as P

STRIP_TABLE = np.array(
    [
        [1, 2, 0, 3],
        [0, 3, 1, 2],
        [3, 1, 2, 0],
        [2, 0, 3, 1],
        [1, 2, 0, 3],
        [1, 2, 0, 3],
        [0, 3, 1, 2],
        [0, 3, 1, 2],
    ],
    np.int32,
)
FLIP_TABLE = np.array(
    [
        [0, 0, 1, 1],
        [0, 0, 1, 1],
        [0, 1, 1, 0],
        [0, 1, 1, 0],
        [0, 0, 1, 1],
        [0, 0, 1, 1],
        [0, 0, 1, 1],
        [0, 0, 1, 1],
    ],
    np.int32,
)
DIRECTIONS = [(-1, 0), (1, 0), (0, -1), (0, 1), (-1, -1), (-1, 1), (1, -1), (1, 1)]
AXES = ("face", "tile")
VMEM = pltpu.VMEM
F32 = jnp.float32
BF16 = jnp.bfloat16
LIMIT = 48 * 1024 * 1024
CORNERS = 16


def shift_down(line, first):
    moved = pltpu.roll(line, 1, 0)
    rows = lax.broadcasted_iota(jnp.int32, moved.shape, 0)
    return jnp.where(rows == 0, first, moved)


def shift_up(line, last):
    size = line.shape[0]
    moved = pltpu.roll(line, size - 1, 0)
    rows = lax.broadcasted_iota(jnp.int32, moved.shape, 0)
    return jnp.where(rows == size - 1, last, moved)


def gelu(value):
    return (0.5 * value) * (1.0 + lax.erf(value * np.float32(np.sqrt(0.5))))


def pick_lines(codes_ref, lines, message_refs, tiles):
    side = lines.shape[1]
    shape = (CORNERS, lines.shape[2])
    rows = lax.broadcasted_iota(jnp.int32, shape, 0)
    for direction in range(8):
        corner = jnp.zeros(shape, F32)
        for tile in range(tiles):
            line = lines[codes_ref[direction, tile * 8 + direction]]
            if direction < 4:
                message_refs[direction][pl.ds(tile * side, side), :] = line
            else:
                at = side - 1 if direction in (4, 6) else 0
                pixel = line.astype(F32)[at : at + 1]
                corner = jnp.where(rows == tile, pixel, corner)
        if direction >= 4:
            group = tiles * side + (direction % 2) * CORNERS
            message_refs[direction // 2 - 2][pl.ds(group, CORNERS), :] = corner.astype(BF16)


def flip_line(line):
    size = line.shape[0]
    row = lax.broadcasted_iota(jnp.int32, (size, size), 0)
    col = lax.broadcasted_iota(jnp.int32, (size, size), 1)
    turn = jnp.where(row + col == size - 1, 1.0, 0.0).astype(BF16)
    return jnp.dot(turn, line, preferred_element_type=F32).astype(BF16)


def gather_kernel(order_ref, x_ref, o_ref, held, in_sems, out_sem):
    groups = in_sems.shape[0]
    size = held.shape[0] // groups

    def start(at, carry):
        pltpu.make_async_copy(
            x_ref.at[order_ref[at]], held.at[at], in_sems.at[at // size]
        ).start()
        return carry

    lax.fori_loop(0, held.shape[0], start, 0)
    for group in range(groups):
        part = pl.ds(group * size, size)
        pltpu.make_async_copy(x_ref.at[part], held.at[part], in_sems.at[group]).wait()
        pltpu.make_async_copy(held.at[part], o_ref.at[part], out_sem).start()
    pltpu.make_async_copy(held, o_ref, out_sem).wait()


def border_kernel(side, tiles, codes_ref, top_ref, low_ref, left_ref, right_ref, ring_ref, *rest):
    message_refs, lines = rest[:4], rest[4]
    tile = pl.program_id(0)
    chan = ring_ref.shape[-1]
    top = top_ref[...].reshape(-1, side, chan)
    low = low_ref[...].reshape(-1, side, chan)
    ring = [top[0], top[1], low[low.shape[0] - 2], low[low.shape[0] - 1]]
    low = left_ref[...].reshape(side, 16, chan).astype(F32)
    high = right_ref[...].reshape(side, 16, chan).astype(F32)
    ring += [v.astype(BF16) for v in (low[:, 0], low[:, 1], high[:, 14], high[:, 15])]
    for at, line in enumerate(ring):
        ring_ref[0, at] = line
    for strip, at in enumerate((0, 3, 4, 7)):
        lines[tile * 4 + strip] = ring[at]
        lines[tiles * 4 + tile * 4 + strip] = flip_line(ring[at])

    @pl.when(tile == tiles - 1)
    def _():
        pick_lines(codes_ref, lines, message_refs, tiles)


def ring_kernel(codes_ref, ring_ref, w_ref, b_ref, *rest):
    got_refs, message_refs, own_ref, lines = rest[:4], rest[4:8], rest[8], rest[9]
    tiles = ring_ref.shape[0]
    side = ring_ref.shape[2]
    pads = [[ref[pl.ds(t * side, side), :] for t in range(tiles)] for ref in got_refs]
    corners = [
        got_refs[2 + k % 2][pl.ds(tiles * side + k // 2 * CORNERS, CORNERS), :].astype(F32)
        for k in range(4)
    ]
    plans = [
        (0, 0, 1, 0, 1, 2, 3, 0, 1),
        (1, 2, 3, 3, 2, 2, 3, side - 1, side - 2),
        (2, 0, 2, 4, 5, 0, 1, 0, 1),
        (3, 1, 3, 7, 6, 0, 1, side - 1, side - 2),
    ]
    for edge, (pad, c_first, c_last, line_0, line_1, end_a, end_b, at_0, at_1) in enumerate(plans):
        stacked = []
        for tile in range(tiles):
            begin = pads[end_a][tile].astype(F32)
            finish = pads[end_b][tile].astype(F32)
            parts = []
            for line, first, last in (
                (
                    pads[pad][tile],
                    corners[c_first][tile : tile + 1],
                    corners[c_last][tile : tile + 1],
                ),
                (ring_ref[tile, line_0], begin[at_0 : at_0 + 1], finish[at_0 : at_0 + 1]),
                (ring_ref[tile, line_1], begin[at_1 : at_1 + 1], finish[at_1 : at_1 + 1]),
            ):
                wide = line.astype(F32)
                parts += [
                    shift_down(wide, first).astype(BF16),
                    line,
                    shift_up(wide, last).astype(BF16),
                ]
            stacked.append(jnp.concatenate(parts, axis=1))
        summed = jnp.dot(
            jnp.concatenate(stacked, axis=0), w_ref[edge], preferred_element_type=F32
        )
        hidden = gelu(summed + b_ref[...]).astype(BF16)
        for tile in range(tiles):
            line = hidden[tile * side : (tile + 1) * side]
            own_ref[tile, edge] = line
            lines[tile * 4 + edge] = line
            lines[tiles * 4 + tile * 4 + edge] = flip_line(line)
    pick_lines(codes_ref, lines, message_refs, tiles)


def moved_columns(pads, corners, w_side_ref, ends):
    for at in range(2):
        taps = jnp.concatenate(
            [
                shift_down(pads[at].astype(F32), corners[at]).astype(BF16),
                pads[at],
                shift_up(pads[at].astype(F32), corners[2 + at]).astype(BF16),
            ],
            axis=1,
        )
        ends[at] = jnp.dot(taps, w_side_ref[at], preferred_element_type=F32)


def convolve_tile(padded, w_ref, bias, y, ends, finish):
    side = padded.shape[2]
    chan = padded.shape[3]
    blocks = y.shape[0]
    step = side // 2 // blocks
    rows = lax.broadcasted_iota(jnp.int32, (side, chan), 0)

    def multiply(block):
        lhs = jnp.concatenate(
            [
                padded[pl.ds(step * block + j // 2, step), j % 2].reshape(step * side, chan)
                for j in range(4)
            ],
            axis=1,
        )
        y[block] = jnp.dot(lhs, w_ref[...], preferred_element_type=F32)

    multiply(0)
    for block in range(blocks):
        if block + 1 < blocks:
            multiply(block + 1)
        for i in range(step):
            for half in range(2):
                row = (block * step + i) * 2 + half
                a, b, c = (
                    y[block, pl.ds(i * side, side), pl.ds((half * 3 + dx) * chan, chan)]
                    for dx in range(3)
                )
                a = pltpu.roll(a, 1, 0)
                c = pltpu.roll(c, side - 1, 0)
                if ends is not None:
                    a = jnp.where(rows == 0, ends[0, row : row + 1], a)
                    c = jnp.where(rows == side - 1, ends[1, row : row + 1], c)
                finish(row, (a + c) + (b + bias))


def first_kernel(side, *refs):
    x_ref, w_ref, b_ref = refs[:3]
    out_ref, padded, y = refs[-3:]
    chan = x_ref.shape[-1]
    half = side // 2
    image = x_ref[...].reshape(side, side, chan)
    padded[0, 0] = jnp.zeros((side, chan), BF16)
    padded[half, 1] = jnp.zeros((side, chan), BF16)
    padded[0, 1] = image[0]
    padded[1:half] = image[1 : side - 1].reshape(half - 1, 2, side, chan)
    padded[half, 0] = image[side - 1]

    def finish(row, value):
        out_ref[0, row] = gelu(value).astype(BF16)

    convolve_tile(padded, w_ref, b_ref[...], y, None, finish)


def second_kernel(side, x_ref, h_ref, ring_ref, *rest):
    pad_refs, corner_refs = rest[:4], rest[4:8]
    w_ref, w_side_ref, b_ref, out_ref, padded, y, ends = rest[8:]
    chan = x_ref.shape[-1]
    half = side // 2
    own = lax.broadcasted_iota(jnp.int32, (CORNERS, chan), 0) == pl.program_id(0)
    corners = [
        jnp.sum(jnp.where(own, ref[...].astype(F32), 0.0), axis=0, keepdims=True)
        for ref in corner_refs
    ]
    padded[0, 0] = pad_refs[0][...]
    padded[half, 1] = pad_refs[1][...]
    padded[0, 1] = ring_ref[0, 0]
    padded[1:half] = h_ref[0, 1 : side - 1].reshape(half - 1, 2, side, chan)
    padded[half, 0] = ring_ref[0, 1]
    ends[0] = ring_ref[0, 2].astype(F32)
    ends[1] = ring_ref[0, 3].astype(F32)
    rows = lax.broadcasted_iota(jnp.int32, (16, chan), 0)
    for row in range(1, side - 1):
        m, e = (row + 1) // 2, (row + 1) % 2
        for at, first, last in ((0, 0, 0), (1, side - 16, 15)):
            old = h_ref[0, row, first : first + 16].astype(F32)
            new = jnp.where(rows == last, ends[at, row : row + 1], old)
            padded[m, e, first : first + 16] = new.astype(BF16)
    moved_columns([pad_refs[2][...], pad_refs[3][...]], corners, w_side_ref, ends)
    per_piece = x_ref.shape[2]

    def finish(row, value):
        at = row * side // per_piece
        if per_piece >= side:
            start = row * side % per_piece
            centre = x_ref[at, 0, start : start + side].astype(F32)
        else:
            count = side // per_piece
            centre = x_ref[at : at + count].reshape(side, chan).astype(F32)
        out_ref[0, row] = (centre + value).astype(BF16)

    convolve_tile(padded, w_ref, b_ref[...], y, ends, finish)


def paired_weights(weight):
    chan_in, chan_out = weight.shape[2:]
    by_tap = weight.transpose(0, 2, 1, 3).reshape(3, chan_in, 3 * chan_out)
    zero = jnp.zeros((1, chan_in, 3 * chan_out), weight.dtype)
    first = jnp.concatenate([by_tap, zero], 0)
    second = jnp.concatenate([zero, by_tap], 0)
    return jnp.stack([first, second], 2).reshape(4 * chan_in, 6 * chan_out)


def side_weights(weight):
    chan_in, chan_out = weight.shape[2:]
    return jnp.stack([weight[:, 0], weight[:, 2]], 0).reshape(2, 3 * chan_in, chan_out)


def edge_weights(weight):
    chan_in, chan_out = weight.shape[2:]
    turned = weight.transpose(1, 0, 2, 3)
    stacked = jnp.stack([weight, weight[::-1], turned, turned[::-1]], 0)
    return stacked.reshape(4, 9 * chan_in, chan_out)


def along(array, axis, step):
    size = lax.axis_size(axis)
    return lax.ppermute(array, axis, [(i, (i + step) % size) for i in range(size)])


def relay(message, upper, lower, split, at):
    group = slice(split + at * CORNERS, split + (at + 1) * CORNERS)
    return jnp.concatenate([message[:split], upper[group], lower[group]], 0)


def shards(latitude_rows, tile_order, neighbours, rotations, w_first, b_first, w_second, b_second):
    devices = lax.axis_size("face") * lax.axis_size("tile")
    tiles = neighbours.shape[0]
    piece, chan = latitude_rows.shape[1:]
    side = int(round((piece * devices) ** 0.5))
    vmem_spec = pl.BlockSpec(memory_space=VMEM)
    smem_spec = pl.BlockSpec(memory_space=pltpu.SMEM)
    hbm_spec = pl.BlockSpec(memory_space=pltpu.HBM)
    params = pltpu.CompilerParams(vmem_limit_bytes=LIMIT)

    asked = (neighbours % tiles * 4 + rotations).reshape(1, tiles * 8)
    after, before = along(asked, "face", -1), along(asked, "face", 1)

    groups = 8 if latitude_rows.shape[0] % 8 == 0 else 1
    ordered = pl.pallas_call(
        gather_kernel,
        in_specs=[smem_spec, hbm_spec],
        out_specs=hbm_spec,
        out_shape=jax.ShapeDtypeStruct(latitude_rows.shape, latitude_rows.dtype),
        scratch_shapes=[
            VMEM(latitude_rows.shape, latitude_rows.dtype),
            pltpu.SemaphoreType.DMA((groups,)),
            pltpu.SemaphoreType.DMA,
        ],
        compiler_params=params,
        name="order",
    )(tile_order, latitude_rows)
    ordered, after, before = lax.optimization_barrier((ordered, after, before))
    gathered = lax.all_to_all(ordered, AXES, split_axis=0, concat_axis=0, tiled=True)
    column = jnp.concatenate([asked, after, before], 0)
    on, back = along(column, "tile", -1), along(column, "tile", 1)
    asked = jnp.concatenate(
        [after, before] + [side_rows[i : i + 1] for i in range(3) for side_rows in (on, back)], 0
    ).reshape(8, tiles, 8)
    turn = (asked % 4)[..., None] == jnp.arange(4, dtype=jnp.int32)
    strip = jnp.sum(jnp.where(turn, jnp.asarray(STRIP_TABLE), 0), -1)
    flip = jnp.sum(jnp.where(turn, jnp.asarray(FLIP_TABLE), 0), -1)
    codes = ((flip * tiles + asked // 4) * 4 + strip).reshape(8, tiles * 8)
    constants = (
        paired_weights(w_first),
        paired_weights(w_second),
        side_weights(w_second),
        edge_weights(w_first),
        b_first.reshape(1, chan),
        b_second.reshape(1, chan),
    )
    gathered, codes, constants = lax.optimization_barrier((gathered, codes, constants))
    w_one, w_two, w_side, w_edges, b_one, b_two = constants
    pieces = gathered.reshape(devices, tiles, piece, chan)

    split = tiles * side
    message_shape = jax.ShapeDtypeStruct((split + 2 * CORNERS, chan), BF16)
    line_shape = (tiles, 8, side, chan)
    lines_scratch = VMEM((8 * tiles, side, chan), BF16)
    if piece >= 2 * side:
        count = piece // side
        view = gathered.reshape(devices, tiles, count, side, chan)
        border_specs = [
            pl.BlockSpec((1, 1, count, side, chan), lambda t: (0, t, 0, 0, 0)),
            pl.BlockSpec((1, 1, count, side, chan), lambda t: (devices - 1, t, 0, 0, 0)),
            pl.BlockSpec((devices, 1, count, 16, chan), lambda t: (0, t, 0, 0, 0)),
            pl.BlockSpec((devices, 1, count, 16, chan), lambda t: (0, t, 0, side // 16 - 1, 0)),
        ]
    else:
        count = side // piece
        view = gathered.reshape(side, count, tiles, piece, chan)
        border_specs = [
            pl.BlockSpec((2, count, 1, piece, chan), lambda t: (0, 0, t, 0, 0)),
            pl.BlockSpec((2, count, 1, piece, chan), lambda t: (side // 2 - 1, 0, t, 0, 0)),
            pl.BlockSpec((side, 1, 1, 16, chan), lambda t: (0, 0, t, 0, 0)),
            pl.BlockSpec((side, 1, 1, 16, chan), lambda t: (0, count - 1, t, piece // 16 - 1, 0)),
        ]
    ring, *sends = pl.pallas_call(
        functools.partial(border_kernel, side, tiles),
        grid=(tiles,),
        in_specs=[smem_spec] + border_specs,
        out_specs=[pl.BlockSpec((1,) + line_shape[1:], lambda t: (t, 0, 0, 0))]
        + [pl.BlockSpec(message_shape.shape, lambda t: (0, 0))] * 4,
        out_shape=[jax.ShapeDtypeStruct(line_shape, BF16)] + [message_shape] * 4,
        scratch_shapes=[lines_scratch],
        compiler_params=params,
        name="borders",
    )(codes, view, view, view, view)

    def whole(array):
        return pl.BlockSpec(array.shape, lambda t: (0,) * array.ndim)

    blocks = 4
    field = VMEM((side // 2 + 1, 2, side, chan), BF16)
    products = VMEM((blocks, side // 2 // blocks * side, 6 * chan), F32)
    field_shape = jax.ShapeDtypeStruct((tiles, side, side, chan), BF16)

    def first(begin, end, hidden):
        return pl.pallas_call(
            functools.partial(first_kernel, side),
            grid=(end - begin,),
            in_specs=[
                pl.BlockSpec((devices, 1, piece, chan), lambda t: (0, begin + t, 0, 0)),
                whole(w_one),
                whole(b_one),
            ]
            + [hbm_spec] * len(hidden),
            out_specs=pl.BlockSpec((1, side, side, chan), lambda t: (begin + t, 0, 0, 0)),
            out_shape=field_shape,
            input_output_aliases={3: 0} if hidden else {},
            scratch_shapes=[field, products],
            compiler_params=params,
            name="first",
        )(pieces, w_one, b_one, *hidden)

    upper, lower = along(sends[0], "face", 1), along(sends[1], "face", -1)
    middle = tiles // 2
    hidden = first(0, middle, ()) if middle else None
    upper, lower, hidden = lax.optimization_barrier((upper, lower, hidden))
    right = along(relay(sends[2], upper, lower, split, 0), "tile", 1)
    left = along(relay(sends[3], upper, lower, split, 1), "tile", -1)
    hidden = first(middle, tiles, (hidden,) if middle else ())
    right, left, hidden = lax.optimization_barrier((right, left, hidden))

    *sends, hidden_ring = pl.pallas_call(
        ring_kernel,
        in_specs=[smem_spec] + [vmem_spec] * 7,
        out_specs=[vmem_spec] * 5,
        out_shape=[message_shape] * 4 + [jax.ShapeDtypeStruct((tiles, 4, side, chan), BF16)],
        scratch_shapes=[lines_scratch],
        compiler_params=params,
        name="hidden_ring",
    )(codes, ring, w_edges, b_one, upper, lower, right, left)
    upper, lower = along(sends[0], "face", 1), along(sends[1], "face", -1)
    right = along(relay(sends[2], upper, lower, split, 0), "tile", 1)
    left = along(relay(sends[3], upper, lower, split, 1), "tile", -1)

    def group(at):
        return pl.BlockSpec((CORNERS, chan), lambda t: (split // CORNERS + at, 0))

    return pl.pallas_call(
        functools.partial(second_kernel, side),
        grid=(tiles,),
        in_specs=[
            pl.BlockSpec((devices, 1, piece, chan), lambda t: (0, t, 0, 0)),
            pl.BlockSpec((1, side, side, chan), lambda t: (t, 0, 0, 0)),
            pl.BlockSpec((1, 4, side, chan), lambda t: (t, 0, 0, 0)),
        ]
        + [pl.BlockSpec((side, chan), lambda t: (t, 0))] * 4
        + [group(0), group(0), group(1), group(1)]
        + [whole(w_two), whole(w_side), whole(b_two)],
        out_specs=pl.BlockSpec((1, side, side, chan), lambda t: (t, 0, 0, 0)),
        out_shape=field_shape,
        scratch_shapes=[field, products, VMEM((2, side, chan), F32)],
        compiler_params=params,
        name="second",
    )(
        pieces,
        hidden,
        hidden_ring,
        upper,
        lower,
        right,
        left,
        right,
        left,
        right,
        left,
        w_two,
        w_side,
        b_two,
    )


def solution(mesh):
    return jax.shard_map(
        shards,
        mesh=mesh,
        in_specs=(
            P(None, ("face", "tile"), None),
            P(),
            P(("face", "tile"), None),
            P(("face", "tile"), None),
            P(),
            P(),
            P(),
            P(),
        ),
        out_specs=P(("face", "tile"), None, None, None),
        check_vma=False,
    )
```

time: 158 us -> 157 us (level)
  waiting for transfers between devices: 98.3 us -> 86.3 us
  starting transfers between devices: 21.1 us -> 26.2 us
  Pallas kernels: 25 us -> 28.4 us
  local copies, waits for them, and re-layouts: 10.6 us -> 12.9 us
    ppermute x12, waiting for transfers between devices: 75.6 us -> 63.9 us  [along(): lax.ppermute(array, axis, [(i, (i + step) % size) for i in range(size)])]
    ppermute x12, starting transfers between devices: 14.6 us -> 20.7 us  [along(): lax.ppermute(array, axis, [(i, (i + step) % size) for i in range(size)])]
    pallas_call x2 -> x4, Pallas kernels: 19.6 us -> 23.4 us  [the longest x1 10.3 us: shards(): pl.pallas_call(functools.partial(second_kernel, side), grid=(tiles,), in_...]
    unnamed x20 -> x24, local copies, waits for them, and re-layouts: 5.74 us -> 8.43 us
  transfers between devices with their start and end apart: 13 -> 13, of which waited for: 10 -> 4; matrix products, arithmetic and copies ran while one was open for 6% -> 6% of each run, Pallas kernels for 2% -> 8%
where the time goes in v3:
time: 157 us; the launch traced here: 156 us
  waiting for transfers between devices  86.3 us (55%)
  Pallas kernels  28.4 us (18%)
  starting transfers between devices  26.2 us (17%)
  local copies, waits for them, and re-layouts  12.9 us (8%)
  other arithmetic  2 us (1%)
    ppermute x12, waiting for transfers between devices, along(): lax.ppermute(array, axis, [(i, (i + step) % size) for i in range(size)])  63.9 us
    all_to_all x1, waiting for transfers between devices, shards(): lax.all_to_all(ordered, AXES, split_axis=0, concat_axis=0, tiled=True)  22.4 us
    ppermute x12, starting transfers between devices, along(): lax.ppermute(array, axis, [(i, (i + step) % size) for i in range(size)])  20.7 us
    pallas_call x1, Pallas kernels, shards(): pl.pallas_call(functools.partial(second_kernel, side), grid=(tiles,), in_...  10.3 us
    pallas_call x2, Pallas kernels, first(): pl.pallas_call(functools.partial(first_kernel, side), grid=(end - begin,)...  10.1 us
    unnamed x24, local copies, waits for them, and re-layouts  8.43 us
    all_to_all x1, starting transfers between devices, shards(): lax.all_to_all(ordered, AXES, split_axis=0, concat_axis=0, tiled=True)  5.52 us
    another operation x4, local copies, waits for them, and re-layouts, paired_weights(): return jnp.stack([first, second], 2).reshape(4 * chan_in, 6 * chan_out)  3.94 us
  transfers between devices with their start and end apart: 13, of which 4 were waited for; matrix products, arithmetic and copies ran while one was open for 6% of the time, Pallas kernels for 8%

profile of v3, /device:TPU:0, one launch (start us, length us, event | category | flops | bytes accessed | tf_op | source)
XLA Modules:
  0.0 156.2 jit_solution(6951018290482159065)
XLA Ops:
  0.0 0.7 fusion.8
  0.8 2.9 %collective-permute-start.1 = (s32[1,32]{1,0:T(1,128)S(1)}, s32[1,32]{1,0:T(1,128)S(1)}, u32[]{:S(2)}, u32[]{:S(2)}) collective-permute-start(s32[1,32]{1,0:T(1,128)S(1)} %reshape.70), channel_id=1, source_target_pairs={{0,8},{8,16},{16,24},{24,0},{1,9},{9,17},{17,25},{25,1},{2,10},{10... | collective-permute-start | bytes 392 | tf_op jit(solution)/shard_map/ppermute | solution.py:308
  3.7 1.0 collective-permute-start
  4.7 0.7 copy-done.3
  5.4 3.0 %order.1 = bf16[128,128,128]{2,1,0:T(8,128)(2,1)S(1)} custom-call(s32[128]{0:T(128)S(1)} %copy-done.3, bf16[128,128,128]{2,1,0:T(8,128)(2,1)} %x_ref.1), custom_call_target="tpu_custom_call" | custom-call | tf_op jit(solution)/shard_map/order/pallas_call | solution.py:330
  8.5 2.0 %copy-done.1 = bf16[128,128,128]{2,1,0:T(8,128)(2,1)} copy-done((bf16[128,128,128]{2,1,0:T(8,128)(2,1)}, bf16[128,128,128]{2,1,0:T(8,128)(2,1)S(1)}, u32[]{:S(2)}) %copy-start.1) | copy-done | bytes 4194328
  10.5 5.5 %all-to-all-start = ((bf16[128,128,128]{2,1,0:T(8,128)(2,1)}), bf16[128,128,128]{2,1,0:T(8,128)(2,1)}, u32[]{:S(2)}, u32[]{:S(2)}) async-start(bf16[128,128,128]{2,1,0:T(8,128)(2,1)} %copy-done.1), calls=%async_computation | async-start | bytes 8388608 | tf_op jit(solution)/shard_map/all_to_all | solution.py:344
  16.1 0.2 copy.31
  16.3 0.6 copy-done.7
  17.0 0.2 copy.35
  17.6 1.0 pad_maximum_fusion.2
  18.5 0.1 pad_maximum_fusion.w_ref
  18.7 0.2 collective-permute-start.3
  18.9 1.9 %copy.34 = bf16[4,128,2,384]{3,2,1,0:T(2,128)(2,1)} copy(bf16[4,128,2,384]{1,3,0,2:T(8,128)(2,1)S(1)} %pad_maximum_fusion.1) | data formatting | bytes 1572864 | tf_op jit(solution)/shard_map/stack | solution.py:291
  20.8 1.3 copy.43
  22.2 1.8 %copy.38 = bf16[4,128,2,384]{3,2,1,0:T(2,128)(2,1)} copy(bf16[4,128,2,384]{1,3,0,2:T(8,128)(2,1)S(1)} %copy-done.6) | data formatting | bytes 1572864 | tf_op jit(solution)/shard_map/stack | solution.py:291
  24.0 1.3 copy.44
  25.3 3.4 %collective-permute-start.2 = (s32[3,32]{1,0:T(4,128)S(1)}, s32[3,32]{1,0:T(4,128)S(1)}, u32[]{:S(2)}, u32[]{:S(2)}) collective-permute-start(s32[3,32]{1,0:T(4,128)S(1)} %pad_add_fusion), channel_id=1, source_target_pairs={{0,7},{1,0},{2,1},{3,2},{4,3},{5,4},{6,5},{7,6},{8,15},{9,8},{10,9... | collective-permute-start | bytes 1160 | tf_op jit(solution)/shard_map/ppermute | solution.py:308
  28.7 59.6 %collective-permute-done.3 = s32[3,32]{1,0:T(4,128)S(1)} collective-permute-done((s32[3,32]{1,0:T(4,128)S(1)}, s32[3,32]{1,0:T(4,128)S(1)}, u32[]{:S(2)}, u32[]{:S(2)}) %collective-permute-start.3) | collective-permute-done | bytes 416 | tf_op jit(solution)/shard_map/ppermute | solution.py:308
  88.7 22.4 %all-to-all-done = bf16[128,128,128]{2,1,0:T(8,128)(2,1)} async-done(((bf16[128,128,128]{2,1,0:T(8,128)(2,1)}), bf16[128,128,128]{2,1,0:T(8,128)(2,1)}, u32[]{:S(2)}, u32[]{:S(2)}) %all-to-all-start) | async-done | bytes 4194336 | tf_op jit(solution)/shard_map/all_to_all | solution.py:344
  111.1 3.0 %borders.1 = (bf16[4,8,64,128]{3,2,1,0:T(8,128)(2,1)S(1)}, bf16[288,128]{1,0:T(8,128)(2,1)S(1)}, bf16[288,128]{1,0:T(8,128)(2,1)S(1)}, bf16[288,128]{1,0:T(8,128)(2,1)S(1)}, bf16[288,128]{1,0:T(8,128)(2,1)S(1)}) custom-call(s32[8,32]{1,0:T(8,128)S(1)} %fusion.4.codes_ref, bf16[32,4,2,64,128]{4,3,2,1,0:T(8,128)(2,1)} %bitcast.20.top_ref.low_ref.left_ref.right_ref, ...), custom_call_target="tpu_custom_call" | custom-call | tf_op jit(solution)/shard_map/borders/pallas_call | solution.py:388
  114.2 2.9 %collective-permute-start.5 = (bf16[288,128]{1,0:T(8,128)(2,1)S(1)}, bf16[288,128]{1,0:T(8,128)(2,1)S(1)}, u32[]{:S(2)}, u32[]{:S(2)}) collective-permute-start(bf16[288,128]{1,0:T(8,128)(2,1)S(1)} %get-tuple-element.39), channel_id=1, source_target_pairs={{0,24},{8,0},{16,8},{24,16},{1,25},{9,1},{17,9},{25,17},{2,26},{10... | collective-permute-start | bytes 221192 | tf_op jit(solution)/shard_map/ppermute | solution.py:308
  117.1 5.0 %first.2.refs_3_ = bf16[4,64,64,128]{3,2,1,0:T(8,128)(2,1)S(1)} custom-call(bf16[32,4,128,128]{3,2,1,0:T(8,128)(2,1)} %bitcast.19.refs_0_.x_ref, bf16[512,768]{1,0:T(8,128)(2,1)S(1)} %bitcast.31, f32[1,128]{1,0:T(1,128)S(1)} %bitcast.34), custom_call_target="tpu_custom_call" | custom-call | tf_op jit(solution)/shard_map/first/pallas_call | solution.py:409
  122.3 3.5 %collective-permute-start.7 = (bf16[288,128]{1,0:T(8,128)(2,1)S(1)}, bf16[288,128]{1,0:T(8,128)(2,1)S(1)}, u32[]{:S(2)}, u32[]{:S(2)}) collective-permute-start(bf16[288,128]{1,0:T(8,128)(2,1)S(1)} %pad_maximum_fusion.5), channel_id=1, source_target_pairs={{0,7},{1,0},{2,1},{3,2},{4,3},{5,4},{6,5},{7,6},{8,15},{9,8},{10,9... | collective-permute-start | bytes 221192 | tf_op jit(solution)/shard_map/ppermute | solution.py:308
  125.8 5.0 %first.3.h_ref = bf16[4,64,64,128]{3,2,1,0:T(8,128)(2,1)S(1)} custom-call(bf16[32,4,128,128]{3,2,1,0:T(8,128)(2,1)} %bitcast.19.refs_0_.x_ref, bf16[512,768]{1,0:T(8,128)(2,1)S(1)} %bitcast.32, f32[1,128]{1,0:T(1,128)S(1)} %bitcast.35, bf16[4,64,64,128]{3,2,1,0:T(8,128)(2,1)S(1)} %first.2.refs_3_), custom_call_target="tpu_custom_call", output_to_operand_aliasing={{}: (3, {})} | custom-call | tf_op jit(solution)/shard_map/first/pallas_call | solution.py:409
  130.9 2.0 %copy-done = bf16[4,64,64,128]{3,2,1,0:T(8,128)(2,1)} copy-done((bf16[4,64,64,128]{3,2,1,0:T(8,128)(2,1)}, bf16[4,64,64,128]{3,2,1,0:T(8,128)(2,1)S(1)}, u32[]{:S(2)}) %copy-start) | copy-done | bytes 4194328
  132.9 2.0 %hidden_ring.1 = (bf16[288,128]{1,0:T(8,128)(2,1)S(1)}, bf16[288,128]{1,0:T(8,128)(2,1)S(1)}, bf16[288,128]{1,0:T(8,128)(2,1)S(1)}, bf16[288,128]{1,0:T(8,128)(2,1)S(1)}, bf16[4,4,64,128]{3,2,1,0:T(8,128)(2,1)S(1)}) custom-call(s32[8,32]{1,0:T(8,128)S(1)} %fusion.4.codes_ref, bf16[4,8,64,128]{3,2,1,0:T(8,128)(2,1)S(1)} %get-tuple-element.47.ring_ref, ...), custom_call_target="tpu_custom_call" | custom-call | tf_op jit(solution)/shard_map/hidden_ring/pallas_call | solution.py:435
  135.0 2.9 %collective-permute-start.9 = (bf16[288,128]{1,0:T(8,128)(2,1)S(1)}, bf16[288,128]{1,0:T(8,128)(2,1)S(1)}, u32[]{:S(2)}, u32[]{:S(2)}) collective-permute-start(bf16[288,128]{1,0:T(8,128)(2,1)S(1)} %get-tuple-element.53), channel_id=1, source_target_pairs={{0,24},{8,0},{16,8},{24,16},{1,25},{9,1},{17,9},{25,17},{2,26},{10... | collective-permute-start | bytes 221192 | tf_op jit(solution)/shard_map/ppermute | solution.py:308
  137.9 2.3 %collective-permute-done.8.rest_0_ = bf16[288,128]{1,0:T(8,128)(2,1)S(1)} collective-permute-done((bf16[288,128]{1,0:T(8,128)(2,1)S(1)}, bf16[288,128]{1,0:T(8,128)(2,1)S(1)}, u32[]{:S(2)}, u32[]{:S(2)}) %collective-permute-start.8) | collective-permute-done | bytes 73760 | tf_op jit(solution)/shard_map/ppermute | solution.py:308
  140.3 3.5 %collective-permute-start.11 = (bf16[288,128]{1,0:T(8,128)(2,1)S(1)}, bf16[288,128]{1,0:T(8,128)(2,1)S(1)}, u32[]{:S(2)}, u32[]{:S(2)}) collective-permute-start(bf16[288,128]{1,0:T(8,128)(2,1)S(1)} %pad_maximum_fusion.7), channel_id=1, source_target_pairs={{0,7},{1,0},{2,1},{3,2},{4,3},{5,4},{6,5},{7,6},{8,15},{9,8},{10,9... | collective-permute-start | bytes 221192 | tf_op jit(solution)/shard_map/ppermute | solution.py:308
  143.8 2.0 %collective-permute-done.10.rest_2_.rest_4_.rest_6_ = bf16[288,128]{1,0:T(8,128)(2,1)S(1)} collective-permute-done((bf16[288,128]{1,0:T(8,128)(2,1)S(1)}, bf16[288,128]{1,0:T(8,128)(2,1)S(1)}, u32[]{:S(2)}, u32[]{:S(2)}) %collective-permute-start.10) | collective-permute-done | bytes 73760 | tf_op jit(solution)/shard_map/ppermute | solution.py:308
  145.8 10.3 %second.1 = bf16[4,64,64,128]{3,2,1,0:T(8,128)(2,1)} custom-call(bf16[32,4,128,128]{3,2,1,0:T(8,128)(2,1)} %bitcast.19.refs_0_.x_ref, bf16[4,64,64,128]{3,2,1,0:T(8,128)(2,1)} %copy-done, bf16[4,4,64,128]{3,2,1,0:T(8,128)(2,1)S(1)} %get-tuple-element.51.ring_ref, bf16[288,128]{1,0:T(8,128)(2,1)S(1)} %collective-permute-done.8.rest_0_, ...), custom_call_target="tpu_custom_call" | custom-call | tf_op jit(solution)/shard_map/second/pallas_call | solution.py:451
  (63 shorter events, 1.2 us)
Async XLA Ops:
  0.8 9.7 %collective-permute-start.1 = (s32[1,32]{1,0:T(1,128)S(1)}, s32[1,32]{1,0:T(1,128)S(1)}, u32[]{:S(2)}, u32[]{:S(2)}) collective-permute-start(s32[1,32]{1,0:T(1,128)S(1)} %reshape.70), channel_id=1, source_target_pairs={{0,8},{8,16},{16,24},{24,0},{1,9},{9,17},{17,25},{25,1},{2,10},{10... | collective-permute-start | bytes 392 | tf_op jit(solution)/shard_map/ppermute | solution.py:308
  3.7 6.7 %collective-permute-start = (s32[1,32]{1,0:T(1,128)S(1)}, s32[1,32]{1,0:T(1,128)S(1)}, u32[]{:S(2)}, u32[]{:S(2)}) collective-permute-start(s32[1,32]{1,0:T(1,128)S(1)} %reshape.70), channel_id=1, source_target_pairs={{0,24},{8,0},{16,8},{24,16},{1,25},{9,1},{17,9},{25,17},{2,26},{10... | collective-permute-start | bytes 392 | tf_op jit(solution)/shard_map/ppermute | solution.py:308
  4.7 0.7 copy-start.3
  8.4 2.0 %copy-start.1 = (bf16[128,128,128]{2,1,0:T(8,128)(2,1)}, bf16[128,128,128]{2,1,0:T(8,128)(2,1)S(1)}, u32[]{:S(2)}) copy-start(bf16[128,128,128]{2,1,0:T(8,128)(2,1)S(1)} %order.1) | copy-start | bytes 12582916
  10.5 5.5 %copy-start.5 = (bf16[3,3,128,128]{3,2,1,0:T(8,128)(2,1)S(1)}, bf16[3,3,128,128]{3,2,1,0:T(8,128)(2,1)}, u32[]{:S(2)}) copy-start(bf16[3,3,128,128]{3,2,1,0:T(8,128)(2,1)} %param.14) | copy-start | bytes 884740
  10.5 100.6 %all-to-all-start = ((bf16[128,128,128]{2,1,0:T(8,128)(2,1)}), bf16[128,128,128]{2,1,0:T(8,128)(2,1)}, u32[]{:S(2)}, u32[]{:S(2)}) async-start(bf16[128,128,128]{2,1,0:T(8,128)(2,1)} %copy-done.1), calls=%async_computation | async-start | bytes 8388608 | tf_op jit(solution)/shard_map/all_to_all | solution.py:344
  16.0 1.0 copy-start.7
  18.7 69.6 %collective-permute-start.3 = (s32[3,32]{1,0:T(4,128)S(1)}, s32[3,32]{1,0:T(4,128)S(1)}, u32[]{:S(2)}, u32[]{:S(2)}) collective-permute-start(s32[3,32]{1,0:T(4,128)S(1)} %pad_add_fusion), channel_id=1, source_target_pairs={{0,1},{1,2},{2,3},{3,4},{4,5},{5,6},{6,7},{7,0},{8,9},{9,10},{10,1... | collective-permute-start | bytes 1160 | tf_op jit(solution)/shard_map/ppermute | solution.py:308
  20.8 1.4 copy-start.6
  24.0 64.4 %copy-start.8 = (s32[8,4]{0,1:T(4,128)S(1)}, s32[8,4]{0,1:T(4,128)}, u32[]{:S(2)}) copy-start(s32[8,4]{0,1:T(4,128)} %constant.46.clone) | copy-start | bytes 388
  24.0 64.4 %copy-start.9 = (s32[8,4]{0,1:T(4,128)S(1)}, s32[8,4]{0,1:T(4,128)}, u32[]{:S(2)}) copy-start(s32[8,4]{0,1:T(4,128)} %constant.45.clone) | copy-start | bytes 388
  25.3 63.0 %collective-permute-start.2 = (s32[3,32]{1,0:T(4,128)S(1)}, s32[3,32]{1,0:T(4,128)S(1)}, u32[]{:S(2)}, u32[]{:S(2)}) collective-permute-start(s32[3,32]{1,0:T(4,128)S(1)} %pad_add_fusion), channel_id=1, source_target_pairs={{0,7},{1,0},{2,1},{3,2},{4,3},{5,4},{6,5},{7,6},{8,15},{9,8},{10,9... | collective-permute-start | bytes 1160 | tf_op jit(solution)/shard_map/ppermute | solution.py:308
  111.1 6.0 %copy-start.2 = (f32[128]{0:T(128)S(1)}, f32[128]{0:T(128)}, u32[]{:S(2)}) copy-start(f32[128]{0:T(128)} %param.15) | copy-start | bytes 1540
  114.1 8.1 %collective-permute-start.4 = (bf16[288,128]{1,0:T(8,128)(2,1)S(1)}, bf16[288,128]{1,0:T(8,128)(2,1)S(1)}, u32[]{:S(2)}, u32[]{:S(2)}) collective-permute-start(bf16[288,128]{1,0:T(8,128)(2,1)S(1)} %get-tuple-element.38), channel_id=1, source_target_pairs={{0,8},{8,16},{16,24},{24,0},{1,9},{9,17},{17,25},{25,1},{2,10},{10... | collective-permute-start | bytes 221192 | tf_op jit(solution)/shard_map/ppermute | solution.py:308
  114.2 8.0 %collective-permute-start.5 = (bf16[288,128]{1,0:T(8,128)(2,1)S(1)}, bf16[288,128]{1,0:T(8,128)(2,1)S(1)}, u32[]{:S(2)}, u32[]{:S(2)}) collective-permute-start(bf16[288,128]{1,0:T(8,128)(2,1)S(1)} %get-tuple-element.39), channel_id=1, source_target_pairs={{0,24},{8,0},{16,8},{24,16},{1,25},{9,1},{17,9},{25,17},{2,26},{10... | collective-permute-start | bytes 221192 | tf_op jit(solution)/shard_map/ppermute | solution.py:308
  122.2 10.7 %collective-permute-start.6 = (bf16[288,128]{1,0:T(8,128)(2,1)S(1)}, bf16[288,128]{1,0:T(8,128)(2,1)S(1)}, u32[]{:S(2)}, u32[]{:S(2)}) collective-permute-start(bf16[288,128]{1,0:T(8,128)(2,1)S(1)} %pad_maximum_fusion.4), channel_id=1, source_target_pairs={{0,1},{1,2},{2,3},{3,4},{4,5},{5,6},{6,7},{7,0},{8,9},{9,10},{10,1... | collective-permute-start | bytes 221192 | tf_op jit(solution)/shard_map/ppermute | solution.py:308
  122.3 10.6 %collective-permute-start.7 = (bf16[288,128]{1,0:T(8,128)(2,1)S(1)}, bf16[288,128]{1,0:T(8,128)(2,1)S(1)}, u32[]{:S(2)}, u32[]{:S(2)}) collective-permute-start(bf16[288,128]{1,0:T(8,128)(2,1)S(1)} %pad_maximum_fusion.5), channel_id=1, source_target_pairs={{0,7},{1,0},{2,1},{3,2},{4,3},{5,4},{6,5},{7,6},{8,15},{9,8},{10,9... | collective-permute-start | bytes 221192 | tf_op jit(solution)/shard_map/ppermute | solution.py:308
  130.8 2.0 %copy-start = (bf16[4,64,64,128]{3,2,1,0:T(8,128)(2,1)}, bf16[4,64,64,128]{3,2,1,0:T(8,128)(2,1)S(1)}, u32[]{:S(2)}) copy-start(bf16[4,64,64,128]{3,2,1,0:T(8,128)(2,1)S(1)} %first.3.h_ref) | copy-start | bytes 12582916
  132.9 13.0 %copy-start.4 = (f32[128]{0:T(128)S(1)}, f32[128]{0:T(128)}, u32[]{:S(2)}) copy-start(f32[128]{0:T(128)} %param.17) | copy-start | bytes 1540
  134.9 5.3 %collective-permute-start.8 = (bf16[288,128]{1,0:T(8,128)(2,1)S(1)}, bf16[288,128]{1,0:T(8,128)(2,1)S(1)}, u32[]{:S(2)}, u32[]{:S(2)}) collective-permute-start(bf16[288,128]{1,0:T(8,128)(2,1)S(1)} %get-tuple-element.52), channel_id=1, source_target_pairs={{0,8},{8,16},{16,24},{24,0},{1,9},{9,17},{17,25},{25,1},{2,10},{10... | collective-permute-start | bytes 221192 | tf_op jit(solution)/shard_map/ppermute | solution.py:308
  135.0 5.2 %collective-permute-start.9 = (bf16[288,128]{1,0:T(8,128)(2,1)S(1)}, bf16[288,128]{1,0:T(8,128)(2,1)S(1)}, u32[]{:S(2)}, u32[]{:S(2)}) collective-permute-start(bf16[288,128]{1,0:T(8,128)(2,1)S(1)} %get-tuple-element.53), channel_id=1, source_target_pairs={{0,24},{8,0},{16,8},{24,16},{1,25},{9,1},{17,9},{25,17},{2,26},{10... | collective-permute-start | bytes 221192 | tf_op jit(solution)/shard_map/ppermute | solution.py:308
  140.2 5.6 %collective-permute-start.10 = (bf16[288,128]{1,0:T(8,128)(2,1)S(1)}, bf16[288,128]{1,0:T(8,128)(2,1)S(1)}, u32[]{:S(2)}, u32[]{:S(2)}) collective-permute-start(bf16[288,128]{1,0:T(8,128)(2,1)S(1)} %pad_maximum_fusion.6), channel_id=1, source_target_pairs={{0,1},{1,2},{2,3},{3,4},{4,5},{5,6},{6,7},{7,0},{8,9},{9,10},{10,1... | collective-permute-start | bytes 221192 | tf_op jit(solution)/shard_map/ppermute | solution.py:308
  140.3 5.6 %collective-permute-start.11 = (bf16[288,128]{1,0:T(8,128)(2,1)S(1)}, bf16[288,128]{1,0:T(8,128)(2,1)S(1)}, u32[]{:S(2)}, u32[]{:S(2)}) collective-permute-start(bf16[288,128]{1,0:T(8,128)(2,1)S(1)} %pad_maximum_fusion.7), channel_id=1, source_target_pairs={{0,7},{1,0},{2,1},{3,2},{4,3},{5,4},{6,5},{7,6},{8,15},{9,8},{10,9... | collective-permute-start | bytes 221192 | tf_op jit(solution)/shard_map/ppermute | solution.py:308

commit v4 on v3

--- a/solution.py
+++ b/solution.py
@@ -39,7 +39,8 @@
 VMEM = pltpu.VMEM
 F32 = jnp.float32
 BF16 = jnp.bfloat16
-LIMIT = 48 * 1024 * 1024
+LIMIT = 24 * 1024 * 1024
+WIDE_LIMIT = 60 * 1024 * 1024
 CORNERS = 16
 
 
@@ -188,7 +189,16 @@
         ends[at] = jnp.dot(taps, w_side_ref[at], preferred_element_type=F32)
 
 
-def convolve_tile(padded, w_ref, bias, y, ends, finish):
+def read_row(x_ref, row, side):
+    piece = x_ref.shape[2]
+    at = row * side // piece
+    if piece >= side:
+        start = row * side % piece
+        return x_ref[at, 0, start : start + side]
+    return x_ref[at : at + side // piece].reshape(side, x_ref.shape[3])
+
+
+def convolve_tile(padded, prepare, w_ref, bias, y, ends, finish):
     side = padded.shape[2]
     chan = padded.shape[3]
     blocks = y.shape[0]
@@ -196,6 +206,9 @@
     rows = lax.broadcasted_iota(jnp.int32, (side, chan), 0)
 
     def multiply(block):
+        begin = 2 * step * block
+        for row in range(begin + 1 if block else -1, begin + 2 * step + 1):
+            prepare(row)
         lhs = jnp.concatenate(
             [
                 padded[pl.ds(step * block + j // 2, step), j % 2].reshape(step * side, chan)
@@ -227,59 +240,53 @@
 def first_kernel(side, *refs):
     x_ref, w_ref, b_ref = refs[:3]
     out_ref, padded, y = refs[-3:]
-    chan = x_ref.shape[-1]
-    half = side // 2
-    image = x_ref[...].reshape(side, side, chan)
-    padded[0, 0] = jnp.zeros((side, chan), BF16)
-    padded[half, 1] = jnp.zeros((side, chan), BF16)
-    padded[0, 1] = image[0]
-    padded[1:half] = image[1 : side - 1].reshape(half - 1, 2, side, chan)
-    padded[half, 0] = image[side - 1]
+
+    def prepare(row):
+        if 0 <= row < side:
+            line = read_row(x_ref, row, side)
+        else:
+            line = jnp.zeros(padded.shape[2:], BF16)
+        padded[(row + 1) // 2, (row + 1) % 2] = line
 
     def finish(row, value):
         out_ref[0, row] = gelu(value).astype(BF16)
 
-    convolve_tile(padded, w_ref, b_ref[...], y, None, finish)
+    convolve_tile(padded, prepare, w_ref, b_ref[...], y, None, finish)
 
 
 def second_kernel(side, x_ref, h_ref, ring_ref, *rest):
     pad_refs, corner_refs = rest[:4], rest[4:8]
-    w_ref, w_side_ref, b_ref, out_ref, padded, y, ends = rest[8:]
+    w_ref, w_side_ref, b_ref, out_ref, padded, y, ends, columns = rest[8:]
     chan = x_ref.shape[-1]
-    half = side // 2
     own = lax.broadcasted_iota(jnp.int32, (CORNERS, chan), 0) == pl.program_id(0)
     corners = [
         jnp.sum(jnp.where(own, ref[...].astype(F32), 0.0), axis=0, keepdims=True)
         for ref in corner_refs
     ]
-    padded[0, 0] = pad_refs[0][...]
-    padded[half, 1] = pad_refs[1][...]
-    padded[0, 1] = ring_ref[0, 0]
-    padded[1:half] = h_ref[0, 1 : side - 1].reshape(half - 1, 2, side, chan)
-    padded[half, 0] = ring_ref[0, 1]
-    ends[0] = ring_ref[0, 2].astype(F32)
-    ends[1] = ring_ref[0, 3].astype(F32)
+    columns[0] = ring_ref[0, 2].astype(F32)
+    columns[1] = ring_ref[0, 3].astype(F32)
     rows = lax.broadcasted_iota(jnp.int32, (16, chan), 0)
-    for row in range(1, side - 1):
+
+    def prepare(row):
         m, e = (row + 1) // 2, (row + 1) % 2
-        for at, first, last in ((0, 0, 0), (1, side - 16, 15)):
-            old = h_ref[0, row, first : first + 16].astype(F32)
-            new = jnp.where(rows == last, ends[at, row : row + 1], old)
-            padded[m, e, first : first + 16] = new.astype(BF16)
+        if row < 0 or row == side:
+            padded[m, e] = pad_refs[0 if row < 0 else 1][...]
+        elif row == 0 or row == side - 1:
+            padded[m, e] = ring_ref[0, 0 if row == 0 else 1]
+        else:
+            padded[m, e, 16 : side - 16] = h_ref[0, row, 16 : side - 16]
+            for at, begin, place in ((0, 0, 0), (1, side - 16, 15)):
+                old = h_ref[0, row, begin : begin + 16].astype(F32)
+                new = jnp.where(rows == place, columns[at, row : row + 1], old)
+                padded[m, e, begin : begin + 16] = new.astype(BF16)
+
     moved_columns([pad_refs[2][...], pad_refs[3][...]], corners, w_side_ref, ends)
-    per_piece = x_ref.shape[2]
 
     def finish(row, value):
-        at = row * side // per_piece
-        if per_piece >= side:
-            start = row * side % per_piece
-            centre = x_ref[at, 0, start : start + side].astype(F32)
-        else:
-            count = side // per_piece
-            centre = x_ref[at : at + count].reshape(side, chan).astype(F32)
+        centre = read_row(x_ref, row, side).astype(F32)
         out_ref[0, row] = (centre + value).astype(BF16)
 
-    convolve_tile(padded, w_ref, b_ref[...], y, ends, finish)
+    convolve_tile(padded, prepare, w_ref, b_ref[...], y, ends, finish)
 
 
 def paired_weights(weight):
@@ -337,7 +344,7 @@
             pltpu.SemaphoreType.DMA((groups,)),
             pltpu.SemaphoreType.DMA,
         ],
-        compiler_params=params,
+        compiler_params=pltpu.CompilerParams(vmem_limit_bytes=WIDE_LIMIT),
         name="order",
     )(tile_order, latitude_rows)
     ordered, after, before = lax.optimization_barrier((ordered, after, before))
@@ -423,13 +430,24 @@
             name="first",
         )(pieces, w_one, b_one, *hidden)
 
-    upper, lower = along(sends[0], "face", 1), along(sends[1], "face", -1)
-    middle = tiles // 2
-    hidden = first(0, middle, ()) if middle else None
+    ends = [(tiles * i // 4, tiles * (i + 1) // 4) for i in range(4)]
+    hidden = ()
+
+    def quarter(i, hidden):
+        begin, end = ends[i]
+        return (first(begin, end, hidden),) if end > begin else hidden
+
+    upper = along(sends[0], "face", 1)
+    hidden = quarter(0, hidden)
+    send, hidden = lax.optimization_barrier((sends[1], hidden))
+    lower = along(send, "face", -1)
+    hidden = quarter(1, hidden)
     upper, lower, hidden = lax.optimization_barrier((upper, lower, hidden))
     right = along(relay(sends[2], upper, lower, split, 0), "tile", 1)
-    left = along(relay(sends[3], upper, lower, split, 1), "tile", -1)
-    hidden = first(middle, tiles, (hidden,) if middle else ())
+    hidden = quarter(2, hidden)
+    send, hidden = lax.optimization_barrier((relay(sends[3], upper, lower, split, 1), hidden))
+    left = along(send, "tile", -1)
+    (hidden,) = quarter(3, hidden)
     right, left, hidden = lax.optimization_barrier((right, left, hidden))
 
     *sends, hidden_ring = pl.pallas_call(
@@ -461,7 +479,7 @@
         + [whole(w_two), whole(w_side), whole(b_two)],
         out_specs=pl.BlockSpec((1, side, side, chan), lambda t: (t, 0, 0, 0)),
         out_shape=field_shape,
-        scratch_shapes=[field, products, VMEM((2, side, chan), F32)],
+        scratch_shapes=[field, products] + [VMEM((2, side, chan), F32)] * 2,
         compiler_params=params,
         name="second",
     )(

time: 157 us -> 156 us (level)
  local copies, waits for them, and re-layouts: 12.9 us -> 6.75 us
  Pallas kernels: 28.4 us -> 31.6 us
  waiting for transfers between devices: 86.3 us -> 88 us
    unnamed x24 -> x16, local copies, waits for them, and re-layouts: 8.43 us -> 1.84 us
    pallas_call x2 -> x4, Pallas kernels: 10.1 us -> 12.5 us  [first(): pl.pallas_call(functools.partial(first_kernel, side), grid=(end - begin,)...]
    ppermute x12, waiting for transfers between devices: 63.9 us -> 65.7 us  [along(): lax.ppermute(array, axis, [(i, (i + step) % size) for i in range(size)])]
  transfers between devices with their start and end apart: 13 -> 13, of which waited for: 4 -> 5; matrix products, arithmetic and copies ran while one was open for 6% -> 5% of each run, Pallas kernels for 8% -> 9%
where the time goes in v4:
time: 156 us; the launch traced here: 155 us
  waiting for transfers between devices  88 us (56%)
  Pallas kernels  31.6 us (20%)
  starting transfers between devices  26.3 us (17%)
  local copies, waits for them, and re-layouts  6.75 us (4%)
  other arithmetic  2 us (1%)
    ppermute x12, waiting for transfers between devices, along(): lax.ppermute(array, axis, [(i, (i + step) % size) for i in range(size)])  65.7 us
    all_to_all x1, waiting for transfers between devices, shards(): lax.all_to_all(ordered, AXES, split_axis=0, concat_axis=0, tiled=True)  22.4 us
    ppermute x12, starting transfers between devices, along(): lax.ppermute(array, axis, [(i, (i + step) % size) for i in range(size)])  20.8 us
    pallas_call x4, Pallas kernels, first(): pl.pallas_call(functools.partial(first_kernel, side), grid=(end - begin,)...  12.5 us
    pallas_call x1, Pallas kernels, shards(): pl.pallas_call(functools.partial(second_kernel, side), grid=(tiles,), in_...  10 us
    all_to_all x1, starting transfers between devices, shards(): lax.all_to_all(ordered, AXES, split_axis=0, concat_axis=0, tiled=True)  5.52 us
    another operation x4, local copies, waits for them, and re-layouts, paired_weights(): return jnp.stack([first, second], 2).reshape(4 * chan_in, 6 * chan_out)  4.4 us
    pallas_call x1, Pallas kernels, shards(): pl.pallas_call(gather_kernel, in_specs=[smem_spec, hbm_spec], out_specs=h...  4.15 us
  transfers between devices with their start and end apart: 13, of which 5 were waited for; matrix products, arithmetic and copies ran while one was open for 5% of the time, Pallas kernels for 9%

profile of v4, /device:TPU:0, one launch (start us, length us, event | category | flops | bytes accessed | tf_op | source)
XLA Modules:
  0.0 155.1 jit_solution(3858115646684097263)
XLA Ops:
  0.0 0.7 fusion.8
  0.8 2.9 %collective-permute-start.1 = (s32[1,32]{1,0:T(1,128)S(1)}, s32[1,32]{1,0:T(1,128)S(1)}, u32[]{:S(2)}, u32[]{:S(2)}) collective-permute-start(s32[1,32]{1,0:T(1,128)S(1)} %reshape.70), channel_id=1, source_target_pairs={{0,8},{8,16},{16,24},{24,0},{1,9},{9,17},{17,25},{25,1},{2,10},{10... | collective-permute-start | bytes 392 | tf_op jit(solution)/shard_map/ppermute | solution.py:315
  3.7 1.0 collective-permute-start
  4.7 4.2 %order.1 = bf16[128,128,128]{2,1,0:T(8,128)(2,1)} custom-call(s32[128]{0:T(128)} %order_ref.1, bf16[128,128,128]{2,1,0:T(8,128)(2,1)} %x_ref.1), custom_call_target="tpu_custom_call" | custom-call | tf_op jit(solution)/shard_map/order/pallas_call | solution.py:337
  8.9 5.5 %all-to-all-start = ((bf16[128,128,128]{2,1,0:T(8,128)(2,1)}), bf16[128,128,128]{2,1,0:T(8,128)(2,1)}, u32[]{:S(2)}, u32[]{:S(2)}) async-start(bf16[128,128,128]{2,1,0:T(8,128)(2,1)} %order.1), calls=%async_computation | async-start | bytes 8388608 | tf_op jit(solution)/shard_map/all_to_all | solution.py:351
  14.5 0.2 copy.33
  14.8 0.2 copy.37
  15.4 1.0 pad_maximum_fusion.2
  16.4 0.1 pad_maximum_fusion.w_ref
  16.5 0.2 collective-permute-start.3
  16.8 1.1 copy.36
  17.9 0.1 copy.45
  18.0 3.1 %copy.40 = bf16[4,128,2,384]{3,2,1,0:T(2,128)(2,1)} copy(bf16[4,128,2,384]{1,3,0,2:T(8,128)(2,1)} %pad_maximum_fusion.2) | data formatting | bytes 1572864 | tf_op jit(solution)/shard_map/stack | solution.py:298
  21.1 1.3 copy.46
  22.4 3.4 %collective-permute-start.2 = (s32[3,32]{1,0:T(4,128)S(1)}, s32[3,32]{1,0:T(4,128)S(1)}, u32[]{:S(2)}, u32[]{:S(2)}) collective-permute-start(s32[3,32]{1,0:T(4,128)S(1)} %pad_add_fusion), channel_id=1, source_target_pairs={{0,7},{1,0},{2,1},{3,2},{4,3},{5,4},{6,5},{7,6},{8,15},{9,8},{10,9... | collective-permute-start | bytes 1160 | tf_op jit(solution)/shard_map/ppermute | solution.py:315
  25.8 61.0 %collective-permute-done.3 = s32[3,32]{1,0:T(4,128)S(1)} collective-permute-done((s32[3,32]{1,0:T(4,128)S(1)}, s32[3,32]{1,0:T(4,128)S(1)}, u32[]{:S(2)}, u32[]{:S(2)}) %collective-permute-start.3) | collective-permute-done | bytes 416 | tf_op jit(solution)/shard_map/ppermute | solution.py:315
  87.2 22.4 %all-to-all-done = bf16[128,128,128]{2,1,0:T(8,128)(2,1)} async-done(((bf16[128,128,128]{2,1,0:T(8,128)(2,1)}), bf16[128,128,128]{2,1,0:T(8,128)(2,1)}, u32[]{:S(2)}, u32[]{:S(2)}) %all-to-all-start) | async-done | bytes 4194336 | tf_op jit(solution)/shard_map/all_to_all | solution.py:351
  109.6 3.0 %borders.1 = (bf16[4,8,64,128]{3,2,1,0:T(8,128)(2,1)S(1)}, bf16[288,128]{1,0:T(8,128)(2,1)S(1)}, bf16[288,128]{1,0:T(8,128)(2,1)S(1)}, bf16[288,128]{1,0:T(8,128)(2,1)S(1)}, bf16[288,128]{1,0:T(8,128)(2,1)S(1)}) custom-call(s32[8,32]{1,0:T(8,128)S(1)} %fusion.4.codes_ref, bf16[32,4,2,64,128]{4,3,2,1,0:T(8,128)(2,1)} %bitcast.20.top_ref.low_ref.left_ref.right_ref, ...), custom_call_target="tpu_custom_call" | custom-call | tf_op jit(solution)/shard_map/borders/pallas_call | solution.py:395
  112.7 3.1 %first.4.refs_3_ = bf16[4,64,64,128]{3,2,1,0:T(8,128)(2,1)S(1)} custom-call(bf16[32,4,128,128]{3,2,1,0:T(8,128)(2,1)} %bitcast.19.refs_0_.x_ref, bf16[512,768]{1,0:T(8,128)(2,1)S(1)} %bitcast.31, f32[1,128]{1,0:T(1,128)S(1)} %bitcast.36), custom_call_target="tpu_custom_call" | custom-call | tf_op jit(solution)/shard_map/first/pallas_call | solution.py:416
  115.8 3.0 %collective-permute-start.5 = (bf16[288,128]{1,0:T(8,128)(2,1)S(1)}, bf16[288,128]{1,0:T(8,128)(2,1)S(1)}, u32[]{:S(2)}, u32[]{:S(2)}) collective-permute-start(bf16[288,128]{1,0:T(8,128)(2,1)S(1)} %get-tuple-element.46), channel_id=1, source_target_pairs={{0,24},{8,0},{16,8},{24,16},{1,25},{9,1},{17,9},{25,17},{2,26},{10... | collective-permute-start | bytes 221192 | tf_op jit(solution)/shard_map/ppermute | solution.py:315
  118.7 3.1 %first.5.refs_3_ = bf16[4,64,64,128]{3,2,1,0:T(8,128)(2,1)S(1)} custom-call(bf16[32,4,128,128]{3,2,1,0:T(8,128)(2,1)} %bitcast.19.refs_0_.x_ref, bf16[512,768]{1,0:T(8,128)(2,1)S(1)} %bitcast.32, f32[1,128]{1,0:T(1,128)S(1)} %bitcast.37, bf16[4,64,64,128]{3,2,1,0:T(8,128)(2,1)S(1)} %first.4.refs_3_), custom_call_target="tpu_custom_call", output_to_operand_aliasing={{}: (3, {})} | custom-call | tf_op jit(solution)/shard_map/first/pallas_call | solution.py:416
  121.9 3.1 %first.6.refs_3_ = bf16[4,64,64,128]{3,2,1,0:T(8,128)(2,1)S(1)} custom-call(bf16[32,4,128,128]{3,2,1,0:T(8,128)(2,1)} %bitcast.19.refs_0_.x_ref, bf16[512,768]{1,0:T(8,128)(2,1)S(1)} %bitcast.33, f32[1,128]{1,0:T(1,128)S(1)} %bitcast.38, bf16[4,64,64,128]{3,2,1,0:T(8,128)(2,1)S(1)} %first.5.refs_3_), custom_call_target="tpu_custom_call", output_to_operand_aliasing={{}: (3, {})} | custom-call | tf_op jit(solution)/shard_map/first/pallas_call | solution.py:416
  125.1 3.5 %collective-permute-start.7 = (bf16[288,128]{1,0:T(8,128)(2,1)S(1)}, bf16[288,128]{1,0:T(8,128)(2,1)S(1)}, u32[]{:S(2)}, u32[]{:S(2)}) collective-permute-start(bf16[288,128]{1,0:T(8,128)(2,1)S(1)} %pad_maximum_fusion.5), channel_id=1, source_target_pairs={{0,7},{1,0},{2,1},{3,2},{4,3},{5,4},{6,5},{7,6},{8,15},{9,8},{10,9... | collective-permute-start | bytes 221192 | tf_op jit(solution)/shard_map/ppermute | solution.py:315
  128.7 3.1 %first.7.h_ref = bf16[4,64,64,128]{3,2,1,0:T(8,128)(2,1)S(1)} custom-call(bf16[32,4,128,128]{3,2,1,0:T(8,128)(2,1)} %bitcast.19.refs_0_.x_ref, bf16[512,768]{1,0:T(8,128)(2,1)S(1)} %bitcast.34, f32[1,128]{1,0:T(1,128)S(1)} %bitcast.39, bf16[4,64,64,128]{3,2,1,0:T(8,128)(2,1)S(1)} %first.6.refs_3_), custom_call_target="tpu_custom_call", output_to_operand_aliasing={{}: (3, {})} | custom-call | tf_op jit(solution)/shard_map/first/pallas_call | solution.py:416
  131.8 2.0 %hidden_ring.1 = (bf16[288,128]{1,0:T(8,128)(2,1)S(1)}, bf16[288,128]{1,0:T(8,128)(2,1)S(1)}, bf16[288,128]{1,0:T(8,128)(2,1)S(1)}, bf16[288,128]{1,0:T(8,128)(2,1)S(1)}, bf16[4,4,64,128]{3,2,1,0:T(8,128)(2,1)S(1)}) custom-call(s32[8,32]{1,0:T(8,128)S(1)} %fusion.4.codes_ref, bf16[4,8,64,128]{3,2,1,0:T(8,128)(2,1)S(1)} %get-tuple-element.55.ring_ref, ...), custom_call_target="tpu_custom_call" | custom-call | tf_op jit(solution)/shard_map/hidden_ring/pallas_call | solution.py:453
  133.8 1.2 collective-permute-start.8
  135.0 1.8 %collective-permute-start.9 = (bf16[288,128]{1,0:T(8,128)(2,1)S(1)}, bf16[288,128]{1,0:T(8,128)(2,1)S(1)}, u32[]{:S(2)}, u32[]{:S(2)}) collective-permute-start(bf16[288,128]{1,0:T(8,128)(2,1)S(1)} %get-tuple-element.61), channel_id=1, source_target_pairs={{0,24},{8,0},{16,8},{24,16},{1,25},{9,1},{17,9},{25,17},{2,26},{10... | collective-permute-start | bytes 221192 | tf_op jit(solution)/shard_map/ppermute | solution.py:315
  136.8 2.3 %collective-permute-done.8.rest_0_ = bf16[288,128]{1,0:T(8,128)(2,1)S(1)} collective-permute-done((bf16[288,128]{1,0:T(8,128)(2,1)S(1)}, bf16[288,128]{1,0:T(8,128)(2,1)S(1)}, u32[]{:S(2)}, u32[]{:S(2)}) %collective-permute-start.8) | collective-permute-done | bytes 73760 | tf_op jit(solution)/shard_map/ppermute | solution.py:315
  139.1 0.3 collective-permute-done.9.rest_1_
  139.5 3.5 %collective-permute-start.11 = (bf16[288,128]{1,0:T(8,128)(2,1)S(1)}, bf16[288,128]{1,0:T(8,128)(2,1)S(1)}, u32[]{:S(2)}, u32[]{:S(2)}) collective-permute-start(bf16[288,128]{1,0:T(8,128)(2,1)S(1)} %pad_maximum_fusion.7), channel_id=1, source_target_pairs={{0,7},{1,0},{2,1},{3,2},{4,3},{5,4},{6,5},{7,6},{8,15},{9,8},{10,9... | collective-permute-start | bytes 221192 | tf_op jit(solution)/shard_map/ppermute | solution.py:315
  143.0 2.0 %collective-permute-done.10.rest_2_.rest_4_.rest_6_ = bf16[288,128]{1,0:T(8,128)(2,1)S(1)} collective-permute-done((bf16[288,128]{1,0:T(8,128)(2,1)S(1)}, bf16[288,128]{1,0:T(8,128)(2,1)S(1)}, u32[]{:S(2)}, u32[]{:S(2)}) %collective-permute-start.10) | collective-permute-done | bytes 73760 | tf_op jit(solution)/shard_map/ppermute | solution.py:315
  145.1 10.0 %second.1 = bf16[4,64,64,128]{3,2,1,0:T(8,128)(2,1)} custom-call(bf16[32,4,128,128]{3,2,1,0:T(8,128)(2,1)} %bitcast.19.refs_0_.x_ref, bf16[4,64,64,128]{3,2,1,0:T(8,128)(2,1)S(1)} %first.7.h_ref, bf16[4,4,64,128]{3,2,1,0:T(8,128)(2,1)S(1)} %get-tuple-element.59.ring_ref, bf16[288,128]{1,0:T(8,128)(2,1)S(1)} %collective-permute-done.8.rest_0_, ...), custom_call_target="tpu_custom_call" | custom-call | tf_op jit(solution)/shard_map/second/pallas_call | solution.py:469
  (57 shorter events, 1.1 us)
Async XLA Ops:
  0.8 8.1 %collective-permute-start.1 = (s32[1,32]{1,0:T(1,128)S(1)}, s32[1,32]{1,0:T(1,128)S(1)}, u32[]{:S(2)}, u32[]{:S(2)}) collective-permute-start(s32[1,32]{1,0:T(1,128)S(1)} %reshape.70), channel_id=1, source_target_pairs={{0,8},{8,16},{16,24},{24,0},{1,9},{9,17},{17,25},{25,1},{2,10},{10... | collective-permute-start | bytes 392 | tf_op jit(solution)/shard_map/ppermute | solution.py:315
  3.7 5.2 %collective-permute-start = (s32[1,32]{1,0:T(1,128)S(1)}, s32[1,32]{1,0:T(1,128)S(1)}, u32[]{:S(2)}, u32[]{:S(2)}) collective-permute-start(s32[1,32]{1,0:T(1,128)S(1)} %reshape.70), channel_id=1, source_target_pairs={{0,24},{8,0},{16,8},{24,16},{1,25},{9,1},{17,9},{25,17},{2,26},{10... | collective-permute-start | bytes 392 | tf_op jit(solution)/shard_map/ppermute | solution.py:315
  8.9 5.6 %copy-start.2 = (bf16[3,3,128,128]{3,2,1,0:T(8,128)(2,1)S(1)}, bf16[3,3,128,128]{3,2,1,0:T(8,128)(2,1)}, u32[]{:S(2)}) copy-start(bf16[3,3,128,128]{3,2,1,0:T(8,128)(2,1)} %param.14) | copy-start | bytes 884740
  8.9 5.9 %copy-start.3 = (bf16[3,3,128,128]{3,2,1,0:T(8,128)(2,1)S(1)}, bf16[3,3,128,128]{3,2,1,0:T(8,128)(2,1)}, u32[]{:S(2)}) copy-start(bf16[3,3,128,128]{3,2,1,0:T(8,128)(2,1)} %param.16) | copy-start | bytes 884740
  8.9 100.6 %all-to-all-start = ((bf16[128,128,128]{2,1,0:T(8,128)(2,1)}), bf16[128,128,128]{2,1,0:T(8,128)(2,1)}, u32[]{:S(2)}, u32[]{:S(2)}) async-start(bf16[128,128,128]{2,1,0:T(8,128)(2,1)} %order.1), calls=%async_computation | async-start | bytes 8388608 | tf_op jit(solution)/shard_map/all_to_all | solution.py:351
  16.4 70.6 %copy-start.4 = (s32[8,4]{0,1:T(4,128)S(1)}, s32[8,4]{0,1:T(4,128)}, u32[]{:S(2)}) copy-start(s32[8,4]{0,1:T(4,128)} %constant.46.clone) | copy-start | bytes 388
  16.4 70.6 %copy-start.5 = (s32[8,4]{0,1:T(4,128)S(1)}, s32[8,4]{0,1:T(4,128)}, u32[]{:S(2)}) copy-start(s32[8,4]{0,1:T(4,128)} %constant.45.clone) | copy-start | bytes 388
  16.5 70.3 %collective-permute-start.3 = (s32[3,32]{1,0:T(4,128)S(1)}, s32[3,32]{1,0:T(4,128)S(1)}, u32[]{:S(2)}, u32[]{:S(2)}) collective-permute-start(s32[3,32]{1,0:T(4,128)S(1)} %pad_add_fusion), channel_id=1, source_target_pairs={{0,1},{1,2},{2,3},{3,4},{4,5},{5,6},{6,7},{7,0},{8,9},{9,10},{10,1... | collective-permute-start | bytes 1160 | tf_op jit(solution)/shard_map/ppermute | solution.py:315
  22.4 64.5 %collective-permute-start.2 = (s32[3,32]{1,0:T(4,128)S(1)}, s32[3,32]{1,0:T(4,128)S(1)}, u32[]{:S(2)}, u32[]{:S(2)}) collective-permute-start(s32[3,32]{1,0:T(4,128)S(1)} %pad_add_fusion), channel_id=1, source_target_pairs={{0,7},{1,0},{2,1},{3,2},{4,3},{5,4},{6,5},{7,6},{8,15},{9,8},{10,9... | collective-permute-start | bytes 1160 | tf_op jit(solution)/shard_map/ppermute | solution.py:315
  109.6 3.1 %copy-start = (f32[128]{0:T(128)S(1)}, f32[128]{0:T(128)}, u32[]{:S(2)}) copy-start(f32[128]{0:T(128)} %param.15) | copy-start | bytes 1540
  112.6 9.3 %collective-permute-start.4 = (bf16[288,128]{1,0:T(8,128)(2,1)S(1)}, bf16[288,128]{1,0:T(8,128)(2,1)S(1)}, u32[]{:S(2)}, u32[]{:S(2)}) collective-permute-start(bf16[288,128]{1,0:T(8,128)(2,1)S(1)} %get-tuple-element.42), channel_id=1, source_target_pairs={{0,8},{8,16},{16,24},{24,0},{1,9},{9,17},{17,25},{25,1},{2,10},{10... | collective-permute-start | bytes 221192 | tf_op jit(solution)/shard_map/ppermute | solution.py:315
  115.8 6.1 %collective-permute-start.5 = (bf16[288,128]{1,0:T(8,128)(2,1)S(1)}, bf16[288,128]{1,0:T(8,128)(2,1)S(1)}, u32[]{:S(2)}, u32[]{:S(2)}) collective-permute-start(bf16[288,128]{1,0:T(8,128)(2,1)S(1)} %get-tuple-element.46), channel_id=1, source_target_pairs={{0,24},{8,0},{16,8},{24,16},{1,25},{9,1},{17,9},{25,17},{2,26},{10... | collective-permute-start | bytes 221192 | tf_op jit(solution)/shard_map/ppermute | solution.py:315
  125.0 20.0 %copy-start.1 = (f32[128]{0:T(128)S(1)}, f32[128]{0:T(128)}, u32[]{:S(2)}) copy-start(f32[128]{0:T(128)} %param.17) | copy-start | bytes 1540
  125.1 6.7 %collective-permute-start.6 = (bf16[288,128]{1,0:T(8,128)(2,1)S(1)}, bf16[288,128]{1,0:T(8,128)(2,1)S(1)}, u32[]{:S(2)}, u32[]{:S(2)}) collective-permute-start(bf16[288,128]{1,0:T(8,128)(2,1)S(1)} %pad_maximum_fusion.4), channel_id=1, source_target_pairs={{0,1},{1,2},{2,3},{3,4},{4,5},{5,6},{6,7},{7,0},{8,9},{9,10},{10,1... | collective-permute-start | bytes 221192 | tf_op jit(solution)/shard_map/ppermute | solution.py:315
  125.1 6.7 %collective-permute-start.7 = (bf16[288,128]{1,0:T(8,128)(2,1)S(1)}, bf16[288,128]{1,0:T(8,128)(2,1)S(1)}, u32[]{:S(2)}, u32[]{:S(2)}) collective-permute-start(bf16[288,128]{1,0:T(8,128)(2,1)S(1)} %pad_maximum_fusion.5), channel_id=1, source_target_pairs={{0,7},{1,0},{2,1},{3,2},{4,3},{5,4},{6,5},{7,6},{8,15},{9,8},{10,9... | collective-permute-start | bytes 221192 | tf_op jit(solution)/shard_map/ppermute | solution.py:315
  133.8 5.3 %collective-permute-start.8 = (bf16[288,128]{1,0:T(8,128)(2,1)S(1)}, bf16[288,128]{1,0:T(8,128)(2,1)S(1)}, u32[]{:S(2)}, u32[]{:S(2)}) collective-permute-start(bf16[288,128]{1,0:T(8,128)(2,1)S(1)} %get-tuple-element.60), channel_id=1, source_target_pairs={{0,8},{8,16},{16,24},{24,0},{1,9},{9,17},{17,25},{25,1},{2,10},{10... | collective-permute-start | bytes 221192 | tf_op jit(solution)/shard_map/ppermute | solution.py:315
  135.0 4.4 %collective-permute-start.9 = (bf16[288,128]{1,0:T(8,128)(2,1)S(1)}, bf16[288,128]{1,0:T(8,128)(2,1)S(1)}, u32[]{:S(2)}, u32[]{:S(2)}) collective-permute-start(bf16[288,128]{1,0:T(8,128)(2,1)S(1)} %get-tuple-element.61), channel_id=1, source_target_pairs={{0,24},{8,0},{16,8},{24,16},{1,25},{9,1},{17,9},{25,17},{2,26},{10... | collective-permute-start | bytes 221192 | tf_op jit(solution)/shard_map/ppermute | solution.py:315
  139.4 5.6 %collective-permute-start.10 = (bf16[288,128]{1,0:T(8,128)(2,1)S(1)}, bf16[288,128]{1,0:T(8,128)(2,1)S(1)}, u32[]{:S(2)}, u32[]{:S(2)}) collective-permute-start(bf16[288,128]{1,0:T(8,128)(2,1)S(1)} %pad_maximum_fusion.6), channel_id=1, source_target_pairs={{0,1},{1,2},{2,3},{3,4},{4,5},{5,6},{6,7},{7,0},{8,9},{9,10},{10,1... | collective-permute-start | bytes 221192 | tf_op jit(solution)/shard_map/ppermute | solution.py:315
  139.5 5.6 %collective-permute-start.11 = (bf16[288,128]{1,0:T(8,128)(2,1)S(1)}, bf16[288,128]{1,0:T(8,128)(2,1)S(1)}, u32[]{:S(2)}, u32[]{:S(2)}) collective-permute-start(bf16[288,128]{1,0:T(8,128)(2,1)S(1)} %pad_maximum_fusion.7), channel_id=1, source_target_pairs={{0,7},{1,0},{2,1},{3,2},{4,3},{5,4},{6,5},{7,6},{8,15},{9,8},{10,9... | collective-permute-start | bytes 221192 | tf_op jit(solution)/shard_map/ppermute | solution.py:315

commit v5 on v4

--- a/solution.py
+++ b/solution.py
@@ -39,7 +39,7 @@
 VMEM = pltpu.VMEM
 F32 = jnp.float32
 BF16 = jnp.bfloat16
-LIMIT = 24 * 1024 * 1024
+LIMIT = 32 * 1024 * 1024
 WIDE_LIMIT = 60 * 1024 * 1024
 CORNERS = 16
 
@@ -106,25 +106,40 @@
     pltpu.make_async_copy(held, o_ref, out_sem).wait()
 
 
-def border_kernel(side, tiles, codes_ref, top_ref, low_ref, left_ref, right_ref, ring_ref, *rest):
-    message_refs, lines = rest[:4], rest[4]
-    tile = pl.program_id(0)
-    chan = ring_ref.shape[-1]
-    top = top_ref[...].reshape(-1, side, chan)
-    low = low_ref[...].reshape(-1, side, chan)
-    ring = [top[0], top[1], low[low.shape[0] - 2], low[low.shape[0] - 1]]
-    low = left_ref[...].reshape(side, 16, chan).astype(F32)
-    high = right_ref[...].reshape(side, 16, chan).astype(F32)
-    ring += [v.astype(BF16) for v in (low[:, 0], low[:, 1], high[:, 14], high[:, 15])]
-    for at, line in enumerate(ring):
-        ring_ref[0, at] = line
-    for strip, at in enumerate((0, 3, 4, 7)):
-        lines[tile * 4 + strip] = ring[at]
-        lines[tiles * 4 + tile * 4 + strip] = flip_line(ring[at])
-
-    @pl.when(tile == tiles - 1)
-    def _():
-        pick_lines(codes_ref, lines, message_refs, tiles)
+def border_kernel(side, codes_ref, source, x_ref, ring_ref, *rest):
+    message_refs, lines, sems = rest[:4], rest[4], rest[5]
+    devices, tiles, piece, chan = x_ref.shape
+    copies = [
+        pltpu.make_async_copy(source.at[:, tile], x_ref.at[:, tile], sems.at[tile])
+        for tile in range(tiles)
+    ]
+    for copy in copies:
+        copy.start()
+    for tile in range(tiles):
+        copies[tile].wait()
+        ring = [read_row(x_ref, tile, row, side) for row in (0, 1, side - 2, side - 1)]
+        if piece >= side:
+            low, high = (
+                jnp.stack(
+                    [
+                        x_ref[:, tile, row * side + at : row * side + at + 16]
+                        for row in range(piece // side)
+                    ],
+                    1,
+                ).reshape(side, 16, chan)
+                for at in (0, side - 16)
+            )
+        else:
+            image = x_ref[:, tile].reshape(side, side // piece, piece, chan)
+            low, high = image[:, 0, :16], image[:, -1, piece - 16 :]
+        low, high = low.astype(F32), high.astype(F32)
+        ring += [v.astype(BF16) for v in (low[:, 0], low[:, 1], high[:, 14], high[:, 15])]
+        for at, line in enumerate(ring):
+            ring_ref[tile, at] = line
+        for strip, at in enumerate((0, 3, 4, 7)):
+            lines[tile * 4 + strip] = ring[at]
+            lines[tiles * 4 + tile * 4 + strip] = flip_line(ring[at])
+    pick_lines(codes_ref, lines, message_refs, tiles)
 
 
 def ring_kernel(codes_ref, ring_ref, w_ref, b_ref, *rest):
@@ -189,13 +204,13 @@
         ends[at] = jnp.dot(taps, w_side_ref[at], preferred_element_type=F32)
 
 
-def read_row(x_ref, row, side):
+def read_row(x_ref, tile, row, side):
     piece = x_ref.shape[2]
     at = row * side // piece
     if piece >= side:
         start = row * side % piece
-        return x_ref[at, 0, start : start + side]
-    return x_ref[at : at + side // piece].reshape(side, x_ref.shape[3])
+        return x_ref[at, tile, start : start + side]
+    return x_ref[at : at + side // piece, tile].reshape(side, x_ref.shape[3])
 
 
 def convolve_tile(padded, prepare, w_ref, bias, y, ends, finish):
@@ -237,56 +252,79 @@
                 finish(row, (a + c) + (b + bias))
 
 
-def first_kernel(side, *refs):
+def first_kernel(side, tiles, *refs):
     x_ref, w_ref, b_ref = refs[:3]
     out_ref, padded, y = refs[-3:]
-
-    def prepare(row):
-        if 0 <= row < side:
-            line = read_row(x_ref, row, side)
-        else:
-            line = jnp.zeros(padded.shape[2:], BF16)
-        padded[(row + 1) // 2, (row + 1) % 2] = line
-
-    def finish(row, value):
-        out_ref[0, row] = gelu(value).astype(BF16)
-
-    convolve_tile(padded, prepare, w_ref, b_ref[...], y, None, finish)
+    for tile in tiles:
+
+        def prepare(row):
+            if 0 <= row < side:
+                line = read_row(x_ref, tile, row, side)
+            else:
+                line = jnp.zeros(padded.shape[2:], BF16)
+            padded[(row + 1) // 2, (row + 1) % 2] = line
+
+        def finish(row, value):
+            out_ref[tile, row] = gelu(value).astype(BF16)
+
+        convolve_tile(padded, prepare, w_ref, b_ref[...], y, None, finish)
 
 
 def second_kernel(side, x_ref, h_ref, ring_ref, *rest):
-    pad_refs, corner_refs = rest[:4], rest[4:8]
-    w_ref, w_side_ref, b_ref, out_ref, padded, y, ends, columns = rest[8:]
-    chan = x_ref.shape[-1]
-    own = lax.broadcasted_iota(jnp.int32, (CORNERS, chan), 0) == pl.program_id(0)
-    corners = [
-        jnp.sum(jnp.where(own, ref[...].astype(F32), 0.0), axis=0, keepdims=True)
-        for ref in corner_refs
-    ]
-    columns[0] = ring_ref[0, 2].astype(F32)
-    columns[1] = ring_ref[0, 3].astype(F32)
+    got_refs, (w_ref, w_side_ref, b_ref), out_ref = rest[:4], rest[4:7], rest[7]
+    padded, y, ends, columns, result, sem = rest[8:]
+    tiles, chan = x_ref.shape[1], x_ref.shape[3]
+    split = tiles * side
+    blocks = y.shape[0]
+    corner_rows = lax.broadcasted_iota(jnp.int32, (CORNERS, chan), 0)
     rows = lax.broadcasted_iota(jnp.int32, (16, chan), 0)
-
-    def prepare(row):
-        m, e = (row + 1) // 2, (row + 1) % 2
-        if row < 0 or row == side:
-            padded[m, e] = pad_refs[0 if row < 0 else 1][...]
-        elif row == 0 or row == side - 1:
-            padded[m, e] = ring_ref[0, 0 if row == 0 else 1]
-        else:
-            padded[m, e, 16 : side - 16] = h_ref[0, row, 16 : side - 16]
-            for at, begin, place in ((0, 0, 0), (1, side - 16, 15)):
-                old = h_ref[0, row, begin : begin + 16].astype(F32)
-                new = jnp.where(rows == place, columns[at, row : row + 1], old)
-                padded[m, e, begin : begin + 16] = new.astype(BF16)
-
-    moved_columns([pad_refs[2][...], pad_refs[3][...]], corners, w_side_ref, ends)
-
-    def finish(row, value):
-        centre = read_row(x_ref, row, side).astype(F32)
-        out_ref[0, row] = (centre + value).astype(BF16)
-
-    convolve_tile(padded, prepare, w_ref, b_ref[...], y, ends, finish)
+    bias = b_ref[...]
+
+    def one_tile(tile, carry):
+        def corner(k):
+            group = got_refs[2 + k % 2][pl.ds(split + k // 2 * CORNERS, CORNERS), :]
+            own = jnp.where(corner_rows == tile, group.astype(F32), 0.0)
+            return jnp.sum(own, axis=0, keepdims=True)
+
+        span = pl.ds(pl.multiple_of(tile * side, side), side)
+        columns[0] = ring_ref[tile, 2].astype(F32)
+        columns[1] = ring_ref[tile, 3].astype(F32)
+
+        def prepare(row):
+            m, e = (row + 1) // 2, (row + 1) % 2
+            if row < 0 or row == side:
+                padded[m, e] = got_refs[0 if row < 0 else 1][span, :]
+            elif row == 0 or row == side - 1:
+                padded[m, e] = ring_ref[tile, 0 if row == 0 else 1]
+            else:
+                padded[m, e, 16 : side - 16] = h_ref[tile, row, 16 : side - 16]
+                for at, begin, place in ((0, 0, 0), (1, side - 16, 15)):
+                    old = h_ref[tile, row, begin : begin + 16].astype(F32)
+                    new = jnp.where(rows == place, columns[at, row : row + 1], old)
+                    padded[m, e, begin : begin + 16] = new.astype(BF16)
+
+        moved_columns(
+            [got_refs[2][span, :], got_refs[3][span, :]],
+            [corner(k) for k in range(4)],
+            w_side_ref,
+            ends,
+        )
+        size = side // blocks
+
+        def finish(row, value):
+            centre = read_row(x_ref, tile, row, side).astype(F32)
+            result[tile, row] = (centre + value).astype(BF16)
+            if (row + 1) % size == 0:
+                part = pl.ds(row + 1 - size, size)
+                pltpu.make_async_copy(
+                    result.at[tile, part], out_ref.at[tile, part], sem
+                ).start()
+
+        convolve_tile(padded, prepare, w_ref, bias, y, ends, finish)
+        return carry
+
+    lax.fori_loop(0, tiles, one_tile, 0)
+    pltpu.make_async_copy(result, out_ref, sem).wait()
 
 
 def paired_weights(weight):
@@ -374,82 +412,54 @@
     message_shape = jax.ShapeDtypeStruct((split + 2 * CORNERS, chan), BF16)
     line_shape = (tiles, 8, side, chan)
     lines_scratch = VMEM((8 * tiles, side, chan), BF16)
-    if piece >= 2 * side:
-        count = piece // side
-        view = gathered.reshape(devices, tiles, count, side, chan)
-        border_specs = [
-            pl.BlockSpec((1, 1, count, side, chan), lambda t: (0, t, 0, 0, 0)),
-            pl.BlockSpec((1, 1, count, side, chan), lambda t: (devices - 1, t, 0, 0, 0)),
-            pl.BlockSpec((devices, 1, count, 16, chan), lambda t: (0, t, 0, 0, 0)),
-            pl.BlockSpec((devices, 1, count, 16, chan), lambda t: (0, t, 0, side // 16 - 1, 0)),
+    x, ring, *sends = pl.pallas_call(
+        functools.partial(border_kernel, side),
+        in_specs=[smem_spec, hbm_spec],
+        out_specs=[vmem_spec] * 6,
+        out_shape=[
+            jax.ShapeDtypeStruct(pieces.shape, BF16),
+            jax.ShapeDtypeStruct((tiles, 8, side, chan), BF16),
         ]
-    else:
-        count = side // piece
-        view = gathered.reshape(side, count, tiles, piece, chan)
-        border_specs = [
-            pl.BlockSpec((2, count, 1, piece, chan), lambda t: (0, 0, t, 0, 0)),
-            pl.BlockSpec((2, count, 1, piece, chan), lambda t: (side // 2 - 1, 0, t, 0, 0)),
-            pl.BlockSpec((side, 1, 1, 16, chan), lambda t: (0, 0, t, 0, 0)),
-            pl.BlockSpec((side, 1, 1, 16, chan), lambda t: (0, count - 1, t, piece // 16 - 1, 0)),
-        ]
-    ring, *sends = pl.pallas_call(
-        functools.partial(border_kernel, side, tiles),
-        grid=(tiles,),
-        in_specs=[smem_spec] + border_specs,
-        out_specs=[pl.BlockSpec((1,) + line_shape[1:], lambda t: (t, 0, 0, 0))]
-        + [pl.BlockSpec(message_shape.shape, lambda t: (0, 0))] * 4,
-        out_shape=[jax.ShapeDtypeStruct(line_shape, BF16)] + [message_shape] * 4,
-        scratch_shapes=[lines_scratch],
+        + [message_shape] * 4,
+        scratch_shapes=[lines_scratch, pltpu.SemaphoreType.DMA((tiles,))],
         compiler_params=params,
         name="borders",
-    )(codes, view, view, view, view)
-
-    def whole(array):
-        return pl.BlockSpec(array.shape, lambda t: (0,) * array.ndim)
+    )(codes, pieces)
 
     blocks = 4
     field = VMEM((side // 2 + 1, 2, side, chan), BF16)
     products = VMEM((blocks, side // 2 // blocks * side, 6 * chan), F32)
     field_shape = jax.ShapeDtypeStruct((tiles, side, side, chan), BF16)
 
-    def first(begin, end, hidden):
+    def first(part, hidden):
         return pl.pallas_call(
-            functools.partial(first_kernel, side),
-            grid=(end - begin,),
-            in_specs=[
-                pl.BlockSpec((devices, 1, piece, chan), lambda t: (0, begin + t, 0, 0)),
-                whole(w_one),
-                whole(b_one),
-            ]
-            + [hbm_spec] * len(hidden),
-            out_specs=pl.BlockSpec((1, side, side, chan), lambda t: (begin + t, 0, 0, 0)),
+            functools.partial(first_kernel, side, part),
+            in_specs=[vmem_spec] * (3 + len(hidden)),
+            out_specs=vmem_spec,
             out_shape=field_shape,
             input_output_aliases={3: 0} if hidden else {},
             scratch_shapes=[field, products],
             compiler_params=params,
             name="first",
-        )(pieces, w_one, b_one, *hidden)
-
-    ends = [(tiles * i // 4, tiles * (i + 1) // 4) for i in range(4)]
+        )(x, w_one, b_one, *hidden)
+
     hidden = ()
 
     def quarter(i, hidden):
-        begin, end = ends[i]
-        return (first(begin, end, hidden),) if end > begin else hidden
-
-    upper = along(sends[0], "face", 1)
-    hidden = quarter(0, hidden)
-    send, hidden = lax.optimization_barrier((sends[1], hidden))
-    lower = along(send, "face", -1)
-    hidden = quarter(1, hidden)
-    upper, lower, hidden = lax.optimization_barrier((upper, lower, hidden))
-    right = along(relay(sends[2], upper, lower, split, 0), "tile", 1)
-    hidden = quarter(2, hidden)
-    send, hidden = lax.optimization_barrier((relay(sends[3], upper, lower, split, 1), hidden))
-    left = along(send, "tile", -1)
-    (hidden,) = quarter(3, hidden)
-    right, left, hidden = lax.optimization_barrier((right, left, hidden))
-
+        part = range(tiles * i // 4, tiles * (i + 1) // 4)
+        return (first(part, hidden),) if part else hidden
+
+    def halo(sends, at, hidden):
+        upper, lower = along(sends[0], "face", 1), along(sends[1], "face", -1)
+        hidden = quarter(at, hidden)
+        upper, lower, hidden = lax.optimization_barrier((upper, lower, hidden))
+        right = along(relay(sends[2], upper, lower, split, 0), "tile", 1)
+        left = along(relay(sends[3], upper, lower, split, 1), "tile", -1)
+        hidden = quarter(at + 1, hidden)
+        right, left, hidden = lax.optimization_barrier((right, left, hidden))
+        return (upper, lower, right, left), hidden
+
+    got_first, hidden = halo(sends, 0, hidden)
     *sends, hidden_ring = pl.pallas_call(
         ring_kernel,
         in_specs=[smem_spec] + [vmem_spec] * 7,
@@ -458,46 +468,25 @@
         scratch_shapes=[lines_scratch],
         compiler_params=params,
         name="hidden_ring",
-    )(codes, ring, w_edges, b_one, upper, lower, right, left)
-    upper, lower = along(sends[0], "face", 1), along(sends[1], "face", -1)
-    right = along(relay(sends[2], upper, lower, split, 0), "tile", 1)
-    left = along(relay(sends[3], upper, lower, split, 1), "tile", -1)
-
-    def group(at):
-        return pl.BlockSpec((CORNERS, chan), lambda t: (split // CORNERS + at, 0))
+    )(codes, ring, w_edges, b_one, *got_first)
+    got_second, hidden = halo(sends, 2, hidden)
 
     return pl.pallas_call(
         functools.partial(second_kernel, side),
-        grid=(tiles,),
-        in_specs=[
-            pl.BlockSpec((devices, 1, piece, chan), lambda t: (0, t, 0, 0)),
-            pl.BlockSpec((1, side, side, chan), lambda t: (t, 0, 0, 0)),
-            pl.BlockSpec((1, 4, side, chan), lambda t: (t, 0, 0, 0)),
-        ]
-        + [pl.BlockSpec((side, chan), lambda t: (t, 0))] * 4
-        + [group(0), group(0), group(1), group(1)]
-        + [whole(w_two), whole(w_side), whole(b_two)],
-        out_specs=pl.BlockSpec((1, side, side, chan), lambda t: (t, 0, 0, 0)),
+        in_specs=[vmem_spec] * 10,
+        out_specs=hbm_spec,
         out_shape=field_shape,
-        scratch_shapes=[field, products] + [VMEM((2, side, chan), F32)] * 2,
+        scratch_shapes=[
+            field,
+            products,
+            VMEM((2, side, chan), F32),
+            VMEM((2, side, chan), F32),
+            VMEM(field_shape.shape, BF16),
+            pltpu.SemaphoreType.DMA,
+        ],
         compiler_params=params,
         name="second",
-    )(
-        pieces,
-        hidden,
-        hidden_ring,
-        upper,
-        lower,
-        right,
-        left,
-        right,
-        left,
-        right,
-        left,
-        w_two,
-        w_side,
-        b_two,
-    )
+    )(x, *hidden, hidden_ring, *got_second, w_two, w_side, b_two)
 
 
 def solution(mesh):

time: 156 us -> 148 us (0.949)
  Pallas kernels: 31.6 us -> 25.5 us
  waiting for transfers between devices: 88 us -> 84.1 us
  local copies, waits for them, and re-layouts: 6.75 us -> 8.65 us
    pallas_call x6, Pallas kernels: 25.5 us -> 19.3 us  [the longest x1 8.63 us: shards(): pl.pallas_call(functools.partial(second_kernel, side), in_specs=[vmem_spe...]
    ppermute x12, waiting for transfers between devices: 65.7 us -> 61.7 us  [along(): lax.ppermute(array, axis, [(i, (i + step) % size) for i in range(size)])]
  transfers between devices with their start and end apart: 13 -> 13, of which waited for: 5 -> 8; matrix products, arithmetic and copies ran while one was open for 5% -> 7% of each run, Pallas kernels for 9% -> 8%
where the time goes in v5:
time: 148 us; the launch traced here: 147 us
  waiting for transfers between devices  84.1 us (57%)
  starting transfers between devices  26.4 us (18%)
  Pallas kernels  25.5 us (17%)
  local copies, waits for them, and re-layouts  8.65 us (6%)
  other arithmetic  1.99 us (1%)
    ppermute x12, waiting for transfers between devices, along(): lax.ppermute(array, axis, [(i, (i + step) % size) for i in range(size)])  61.7 us
    all_to_all x1, waiting for transfers between devices, shards(): lax.all_to_all(ordered, AXES, split_axis=0, concat_axis=0, tiled=True)  22.4 us
    ppermute x12, starting transfers between devices, along(): lax.ppermute(array, axis, [(i, (i + step) % size) for i in range(size)])  20.9 us
    pallas_call x1, Pallas kernels, shards(): pl.pallas_call(functools.partial(second_kernel, side), in_specs=[vmem_spe...  8.63 us
    pallas_call x4, Pallas kernels, first(): pl.pallas_call(functools.partial(first_kernel, side, part), in_specs=[vme...  7.65 us
    all_to_all x1, starting transfers between devices, shards(): lax.all_to_all(ordered, AXES, split_axis=0, concat_axis=0, tiled=True)  5.52 us
    another operation x4, local copies, waits for them, and re-layouts, paired_weights(): return jnp.stack([first, second], 2).reshape(4 * chan_in, 6 * chan_out)  5.17 us
    pallas_call x1, Pallas kernels, shards(): pl.pallas_call(gather_kernel, in_specs=[smem_spec, hbm_spec], out_specs=h...  4.15 us
  transfers between devices with their start and end apart: 13, of which 8 were waited for; matrix products, arithmetic and copies ran while one was open for 7% of the time, Pallas kernels for 8%

profile of v5, /device:TPU:0, one launch (start us, length us, event | category | flops | bytes accessed | tf_op | source)
XLA Modules:
  0.0 147.1 jit_solution(8552774978084994071)
XLA Ops:
  0.0 0.7 fusion.8
  0.8 2.9 %collective-permute-start.1 = (s32[1,32]{1,0:T(1,128)S(1)}, s32[1,32]{1,0:T(1,128)S(1)}, u32[]{:S(2)}, u32[]{:S(2)}) collective-permute-start(s32[1,32]{1,0:T(1,128)S(1)} %reshape.67), channel_id=1, source_target_pairs={{0,8},{8,16},{16,24},{24,0},{1,9},{9,17},{17,25},{25,1},{2,10},{10... | collective-permute-start | bytes 392 | tf_op jit(solution)/shard_map/ppermute | solution.py:353
  3.7 1.0 collective-permute-start
  4.7 4.2 %order.1 = bf16[128,128,128]{2,1,0:T(8,128)(2,1)} custom-call(s32[128]{0:T(128)} %order_ref.1, bf16[128,128,128]{2,1,0:T(8,128)(2,1)} %x_ref.1), custom_call_target="tpu_custom_call" | custom-call | tf_op jit(solution)/shard_map/order/pallas_call | solution.py:375
  8.9 5.5 %all-to-all-start = ((bf16[128,128,128]{2,1,0:T(8,128)(2,1)}), bf16[128,128,128]{2,1,0:T(8,128)(2,1)}, u32[]{:S(2)}, u32[]{:S(2)}) async-start(bf16[128,128,128]{2,1,0:T(8,128)(2,1)} %order.1), calls=%async_computation | async-start | bytes 8388608 | tf_op jit(solution)/shard_map/all_to_all | solution.py:389
  14.5 0.2 copy.33
  15.4 1.0 pad_maximum_fusion.2
  16.5 0.2 collective-permute-start.3
  16.8 1.9 %copy.36 = bf16[4,128,2,384]{3,2,1,0:T(2,128)(2,1)} copy(bf16[4,128,2,384]{1,3,0,2:T(8,128)(2,1)S(1)} %pad_maximum_fusion.1) | data formatting | bytes 1572864 | tf_op jit(solution)/shard_map/stack | solution.py:336
  18.6 1.3 copy.45
  19.9 3.1 %copy.40 = bf16[4,128,2,384]{3,2,1,0:T(2,128)(2,1)} copy(bf16[4,128,2,384]{1,3,0,2:T(8,128)(2,1)} %pad_maximum_fusion.2) | data formatting | bytes 1572864 | tf_op jit(solution)/shard_map/stack | solution.py:336
  23.0 1.3 copy.46
  24.3 3.4 %collective-permute-start.2 = (s32[3,32]{1,0:T(4,128)S(1)}, s32[3,32]{1,0:T(4,128)S(1)}, u32[]{:S(2)}, u32[]{:S(2)}) collective-permute-start(s32[3,32]{1,0:T(4,128)S(1)} %pad_add_fusion), channel_id=1, source_target_pairs={{0,7},{1,0},{2,1},{3,2},{4,3},{5,4},{6,5},{7,6},{8,15},{9,8},{10,9... | collective-permute-start | bytes 1160 | tf_op jit(solution)/shard_map/ppermute | solution.py:353
  27.7 59.1 %collective-permute-done.3 = s32[3,32]{1,0:T(4,128)S(1)} collective-permute-done((s32[3,32]{1,0:T(4,128)S(1)}, s32[3,32]{1,0:T(4,128)S(1)}, u32[]{:S(2)}, u32[]{:S(2)}) %collective-permute-start.3) | collective-permute-done | bytes 416 | tf_op jit(solution)/shard_map/ppermute | solution.py:353
  87.2 22.4 %all-to-all-done = bf16[128,128,128]{2,1,0:T(8,128)(2,1)} async-done(((bf16[128,128,128]{2,1,0:T(8,128)(2,1)}), bf16[128,128,128]{2,1,0:T(8,128)(2,1)}, u32[]{:S(2)}, u32[]{:S(2)}) %all-to-all-start) | async-done | bytes 4194336 | tf_op jit(solution)/shard_map/all_to_all | solution.py:389
  109.6 3.1 %borders.1 = (bf16[32,4,128,128]{3,2,1,0:T(8,128)(2,1)S(1)}, bf16[4,8,64,128]{3,2,1,0:T(8,128)(2,1)S(1)}, bf16[288,128]{1,0:T(8,128)(2,1)S(1)}, bf16[288,128]{1,...) custom-call(s32[8,32]{1,0:T(8,128)S(1)} %fusion.4.codes_ref, ...), custom_call_target="tpu_custom_call" | custom-call | tf_op jit(solution)/shard_map/borders/pallas_call | solution.py:415
  112.7 2.9 %collective-permute-start.5 = (bf16[288,128]{1,0:T(8,128)(2,1)S(1)}, bf16[288,128]{1,0:T(8,128)(2,1)S(1)}, u32[]{:S(2)}, u32[]{:S(2)}) collective-permute-start(bf16[288,128]{1,0:T(8,128)(2,1)S(1)} %get-tuple-element.49), channel_id=1, source_target_pairs={{0,24},{8,0},{16,8},{24,16},{1,25},{9,1},{17,9},{25,17},{2,26},{10... | collective-permute-start | bytes 221192 | tf_op jit(solution)/shard_map/ppermute | solution.py:353
  115.6 1.9 %first.4.refs_3_ = bf16[4,64,64,128]{3,2,1,0:T(8,128)(2,1)S(1)} custom-call(bf16[32,4,128,128]{3,2,1,0:T(8,128)(2,1)S(1)} %get-tuple-element.44.refs_0_.x_ref, bf16[512,768]{1,0:T(8,128)(2,1)S(1)} %bitcast.30, f32[1,128]{1,0:T(1,128)S(1)} %bitcast.35), custom_call_target="tpu_custom_call" | custom-call | tf_op jit(solution)/shard_map/first/pallas_call | solution.py:435
  117.6 0.7 collective-permute-done.4.rest_0_
  118.2 0.5 collective-permute-done.5.rest_1_
  118.8 3.5 %collective-permute-start.7 = (bf16[288,128]{1,0:T(8,128)(2,1)S(1)}, bf16[288,128]{1,0:T(8,128)(2,1)S(1)}, u32[]{:S(2)}, u32[]{:S(2)}) collective-permute-start(bf16[288,128]{1,0:T(8,128)(2,1)S(1)} %pad_maximum_fusion.5), channel_id=1, source_target_pairs={{0,7},{1,0},{2,1},{3,2},{4,3},{5,4},{6,5},{7,6},{8,15},{9,8},{10,9... | collective-permute-start | bytes 221192 | tf_op jit(solution)/shard_map/ppermute | solution.py:353
  122.3 1.9 %first.5.refs_3_ = bf16[4,64,64,128]{3,2,1,0:T(8,128)(2,1)S(1)} custom-call(bf16[32,4,128,128]{3,2,1,0:T(8,128)(2,1)S(1)} %get-tuple-element.44.refs_0_.x_ref, bf16[512,768]{1,0:T(8,128)(2,1)S(1)} %bitcast.31, f32[1,128]{1,0:T(1,128)S(1)} %bitcast.36, bf16[4,64,64,128]{3,2,1,0:T(8,128)(2,1)S(1)} %first.4.refs_3_), custom_call_target="tpu_custom_call", output_to_operand_aliasing={{}: (3, {})} | custom-call | tf_op jit(solution)/shard_map/first/pallas_call | solution.py:435
  124.4 2.0 %hidden_ring.1 = (bf16[288,128]{1,0:T(8,128)(2,1)S(1)}, bf16[288,128]{1,0:T(8,128)(2,1)S(1)}, bf16[288,128]{1,0:T(8,128)(2,1)S(1)}, bf16[288,128]{1,0:T(8,128)(2,1)S(1)}, bf16[4,4,64,128]{3,2,1,0:T(8,128)(2,1)S(1)}) custom-call(s32[8,32]{1,0:T(8,128)S(1)} %fusion.4.codes_ref, bf16[4,8,64,128]{3,2,1,0:T(8,128)(2,1)S(1)} %get-tuple-element.45.ring_ref, ...), custom_call_target="tpu_custom_call" | custom-call | tf_op jit(solution)/shard_map/hidden_ring/pallas_call | solution.py:463
  126.4 1.5 %collective-permute-start.8 = (bf16[288,128]{1,0:T(8,128)(2,1)S(1)}, bf16[288,128]{1,0:T(8,128)(2,1)S(1)}, u32[]{:S(2)}, u32[]{:S(2)}) collective-permute-start(bf16[288,128]{1,0:T(8,128)(2,1)S(1)} %get-tuple-element.59), channel_id=1, source_target_pairs={{0,8},{8,16},{16,24},{24,0},{1,9},{9,17},{17,25},{25,1},{2,10},{10... | collective-permute-start | bytes 221192 | tf_op jit(solution)/shard_map/ppermute | solution.py:353
  127.9 1.5 %collective-permute-start.9 = (bf16[288,128]{1,0:T(8,128)(2,1)S(1)}, bf16[288,128]{1,0:T(8,128)(2,1)S(1)}, u32[]{:S(2)}, u32[]{:S(2)}) collective-permute-start(bf16[288,128]{1,0:T(8,128)(2,1)S(1)} %get-tuple-element.60), channel_id=1, source_target_pairs={{0,24},{8,0},{16,8},{24,16},{1,25},{9,1},{17,9},{25,17},{2,26},{10... | collective-permute-start | bytes 221192 | tf_op jit(solution)/shard_map/ppermute | solution.py:353
  129.3 1.9 %first.6.refs_3_ = bf16[4,64,64,128]{3,2,1,0:T(8,128)(2,1)S(1)} custom-call(bf16[32,4,128,128]{3,2,1,0:T(8,128)(2,1)S(1)} %get-tuple-element.44.refs_0_.x_ref, bf16[512,768]{1,0:T(8,128)(2,1)S(1)} %bitcast.32, f32[1,128]{1,0:T(1,128)S(1)} %bitcast.38, bf16[4,64,64,128]{3,2,1,0:T(8,128)(2,1)S(1)} %first.5.refs_3_), custom_call_target="tpu_custom_call", output_to_operand_aliasing={{}: (3, {})} | custom-call | tf_op jit(solution)/shard_map/first/pallas_call | solution.py:435
  131.3 0.4 collective-permute-done.8.rest_0_
  131.7 0.5 collective-permute-done.9.rest_1_
  132.3 3.7 %collective-permute-start.11 = (bf16[288,128]{1,0:T(8,128)(2,1)S(1)}, bf16[288,128]{1,0:T(8,128)(2,1)S(1)}, u32[]{:S(2)}, u32[]{:S(2)}) collective-permute-start(bf16[288,128]{1,0:T(8,128)(2,1)S(1)} %pad_maximum_fusion.7), channel_id=1, source_target_pairs={{0,7},{1,0},{2,1},{3,2},{4,3},{5,4},{6,5},{7,6},{8,15},{9,8},{10,9... | collective-permute-start | bytes 221192 | tf_op jit(solution)/shard_map/ppermute | solution.py:353
  136.1 1.9 %first.7.h_ref = bf16[4,64,64,128]{3,2,1,0:T(8,128)(2,1)S(1)} custom-call(bf16[32,4,128,128]{3,2,1,0:T(8,128)(2,1)S(1)} %get-tuple-element.44.refs_0_.x_ref, bf16[512,768]{1,0:T(8,128)(2,1)S(1)} %bitcast.33, f32[1,128]{1,0:T(1,128)S(1)} %bitcast.39, bf16[4,64,64,128]{3,2,1,0:T(8,128)(2,1)S(1)} %first.6.refs_3_), custom_call_target="tpu_custom_call", output_to_operand_aliasing={{}: (3, {})} | custom-call | tf_op jit(solution)/shard_map/first/pallas_call | solution.py:435
  138.0 0.4 collective-permute-done.10.rest_2_
  138.3 8.6 %second.1 = bf16[4,64,64,128]{3,2,1,0:T(8,128)(2,1)} custom-call(bf16[32,4,128,128]{3,2,1,0:T(8,128)(2,1)S(1)} %get-tuple-element.44.refs_0_.x_ref, bf16[4,64,64,128]{3,2,1,0:T(8,128)(2,1)S(1)} %first.7.h_ref, bf16[4,4,64,128]{3,2,1,0:T(8,128)(2,1)S(1)} %get-tuple-element.67.ring_ref, bf16[288,128]{1,0:T(8,128)(2,1)S(1)} %collective-permute-done.8.rest_0_, ...), custom_call_target="tpu_custom_call" | custom-call | tf_op jit(solution)/shard_map/second/pallas_call | solution.py:474
  (57 shorter events, 1.6 us)
Async XLA Ops:
  0.8 8.1 %collective-permute-start.1 = (s32[1,32]{1,0:T(1,128)S(1)}, s32[1,32]{1,0:T(1,128)S(1)}, u32[]{:S(2)}, u32[]{:S(2)}) collective-permute-start(s32[1,32]{1,0:T(1,128)S(1)} %reshape.67), channel_id=1, source_target_pairs={{0,8},{8,16},{16,24},{24,0},{1,9},{9,17},{17,25},{25,1},{2,10},{10... | collective-permute-start | bytes 392 | tf_op jit(solution)/shard_map/ppermute | solution.py:353
  3.7 5.2 %collective-permute-start = (s32[1,32]{1,0:T(1,128)S(1)}, s32[1,32]{1,0:T(1,128)S(1)}, u32[]{:S(2)}, u32[]{:S(2)}) collective-permute-start(s32[1,32]{1,0:T(1,128)S(1)} %reshape.67), channel_id=1, source_target_pairs={{0,24},{8,0},{16,8},{24,16},{1,25},{9,1},{17,9},{25,17},{2,26},{10... | collective-permute-start | bytes 392 | tf_op jit(solution)/shard_map/ppermute | solution.py:353
  8.9 5.6 %copy-start.2 = (bf16[3,3,128,128]{3,2,1,0:T(8,128)(2,1)S(1)}, bf16[3,3,128,128]{3,2,1,0:T(8,128)(2,1)}, u32[]{:S(2)}) copy-start(bf16[3,3,128,128]{3,2,1,0:T(8,128)(2,1)} %param.14) | copy-start | bytes 884740
  8.9 5.9 %copy-start.3 = (bf16[3,3,128,128]{3,2,1,0:T(8,128)(2,1)S(1)}, bf16[3,3,128,128]{3,2,1,0:T(8,128)(2,1)}, u32[]{:S(2)}) copy-start(bf16[3,3,128,128]{3,2,1,0:T(8,128)(2,1)} %param.16) | copy-start | bytes 884740
  8.9 100.6 %all-to-all-start = ((bf16[128,128,128]{2,1,0:T(8,128)(2,1)}), bf16[128,128,128]{2,1,0:T(8,128)(2,1)}, u32[]{:S(2)}, u32[]{:S(2)}) async-start(bf16[128,128,128]{2,1,0:T(8,128)(2,1)} %order.1), calls=%async_computation | async-start | bytes 8388608 | tf_op jit(solution)/shard_map/all_to_all | solution.py:389
  16.4 70.6 %copy-start.4 = (s32[8,4]{0,1:T(4,128)S(1)}, s32[8,4]{0,1:T(4,128)}, u32[]{:S(2)}) copy-start(s32[8,4]{0,1:T(4,128)} %constant.46.clone) | copy-start | bytes 388
  16.5 70.4 %copy-start.5 = (s32[8,4]{0,1:T(4,128)S(1)}, s32[8,4]{0,1:T(4,128)}, u32[]{:S(2)}) copy-start(s32[8,4]{0,1:T(4,128)} %constant.45.clone) | copy-start | bytes 388
  16.5 70.3 %collective-permute-start.3 = (s32[3,32]{1,0:T(4,128)S(1)}, s32[3,32]{1,0:T(4,128)S(1)}, u32[]{:S(2)}, u32[]{:S(2)}) collective-permute-start(s32[3,32]{1,0:T(4,128)S(1)} %pad_add_fusion), channel_id=1, source_target_pairs={{0,1},{1,2},{2,3},{3,4},{4,5},{5,6},{6,7},{7,0},{8,9},{9,10},{10,1... | collective-permute-start | bytes 1160 | tf_op jit(solution)/shard_map/ppermute | solution.py:353
  19.9 95.7 %copy-start = (f32[128]{0:T(128)S(1)}, f32[128]{0:T(128)}, u32[]{:S(2)}) copy-start(f32[128]{0:T(128)} %param.15) | copy-start | bytes 1540
  24.3 62.6 %collective-permute-start.2 = (s32[3,32]{1,0:T(4,128)S(1)}, s32[3,32]{1,0:T(4,128)S(1)}, u32[]{:S(2)}, u32[]{:S(2)}) collective-permute-start(s32[3,32]{1,0:T(4,128)S(1)} %pad_add_fusion), channel_id=1, source_target_pairs={{0,7},{1,0},{2,1},{3,2},{4,3},{5,4},{6,5},{7,6},{8,15},{9,8},{10,9... | collective-permute-start | bytes 1160 | tf_op jit(solution)/shard_map/ppermute | solution.py:353
  112.6 5.6 %collective-permute-start.4 = (bf16[288,128]{1,0:T(8,128)(2,1)S(1)}, bf16[288,128]{1,0:T(8,128)(2,1)S(1)}, u32[]{:S(2)}, u32[]{:S(2)}) collective-permute-start(bf16[288,128]{1,0:T(8,128)(2,1)S(1)} %get-tuple-element.48), channel_id=1, source_target_pairs={{0,8},{8,16},{16,24},{24,0},{1,9},{9,17},{17,25},{25,1},{2,10},{10... | collective-permute-start | bytes 221192 | tf_op jit(solution)/shard_map/ppermute | solution.py:353
  112.7 6.0 %collective-permute-start.5 = (bf16[288,128]{1,0:T(8,128)(2,1)S(1)}, bf16[288,128]{1,0:T(8,128)(2,1)S(1)}, u32[]{:S(2)}, u32[]{:S(2)}) collective-permute-start(bf16[288,128]{1,0:T(8,128)(2,1)S(1)} %get-tuple-element.49), channel_id=1, source_target_pairs={{0,24},{8,0},{16,8},{24,16},{1,25},{9,1},{17,9},{25,17},{2,26},{10... | collective-permute-start | bytes 221192 | tf_op jit(solution)/shard_map/ppermute | solution.py:353
  118.7 5.6 %collective-permute-start.6 = (bf16[288,128]{1,0:T(8,128)(2,1)S(1)}, bf16[288,128]{1,0:T(8,128)(2,1)S(1)}, u32[]{:S(2)}, u32[]{:S(2)}) collective-permute-start(bf16[288,128]{1,0:T(8,128)(2,1)S(1)} %pad_maximum_fusion.4), channel_id=1, source_target_pairs={{0,1},{1,2},{2,3},{3,4},{4,5},{5,6},{6,7},{7,0},{8,9},{9,10},{10,1... | collective-permute-start | bytes 221192 | tf_op jit(solution)/shard_map/ppermute | solution.py:353
  118.8 5.6 %collective-permute-start.7 = (bf16[288,128]{1,0:T(8,128)(2,1)S(1)}, bf16[288,128]{1,0:T(8,128)(2,1)S(1)}, u32[]{:S(2)}, u32[]{:S(2)}) collective-permute-start(bf16[288,128]{1,0:T(8,128)(2,1)S(1)} %pad_maximum_fusion.5), channel_id=1, source_target_pairs={{0,7},{1,0},{2,1},{3,2},{4,3},{5,4},{6,5},{7,6},{8,15},{9,8},{10,9... | collective-permute-start | bytes 221192 | tf_op jit(solution)/shard_map/ppermute | solution.py:353
  126.4 5.3 %collective-permute-start.8 = (bf16[288,128]{1,0:T(8,128)(2,1)S(1)}, bf16[288,128]{1,0:T(8,128)(2,1)S(1)}, u32[]{:S(2)}, u32[]{:S(2)}) collective-permute-start(bf16[288,128]{1,0:T(8,128)(2,1)S(1)} %get-tuple-element.59), channel_id=1, source_target_pairs={{0,8},{8,16},{16,24},{24,0},{1,9},{9,17},{17,25},{25,1},{2,10},{10... | collective-permute-start | bytes 221192 | tf_op jit(solution)/shard_map/ppermute | solution.py:353
  127.9 4.4 %collective-permute-start.9 = (bf16[288,128]{1,0:T(8,128)(2,1)S(1)}, bf16[288,128]{1,0:T(8,128)(2,1)S(1)}, u32[]{:S(2)}, u32[]{:S(2)}) collective-permute-start(bf16[288,128]{1,0:T(8,128)(2,1)S(1)} %get-tuple-element.60), channel_id=1, source_target_pairs={{0,24},{8,0},{16,8},{24,16},{1,25},{9,1},{17,9},{25,17},{2,26},{10... | collective-permute-start | bytes 221192 | tf_op jit(solution)/shard_map/ppermute | solution.py:353
  132.2 6.1 %collective-permute-start.10 = (bf16[288,128]{1,0:T(8,128)(2,1)S(1)}, bf16[288,128]{1,0:T(8,128)(2,1)S(1)}, u32[]{:S(2)}, u32[]{:S(2)}) collective-permute-start(bf16[288,128]{1,0:T(8,128)(2,1)S(1)} %pad_maximum_fusion.6), channel_id=1, source_target_pairs={{0,1},{1,2},{2,3},{3,4},{4,5},{5,6},{6,7},{7,0},{8,9},{9,10},{10,1... | collective-permute-start | bytes 221192 | tf_op jit(solution)/shard_map/ppermute | solution.py:353
  132.3 6.0 %copy-start.1 = (f32[128]{0:T(128)S(1)}, f32[128]{0:T(128)}, u32[]{:S(2)}) copy-start(f32[128]{0:T(128)} %param.17) | copy-start | bytes 1540
  132.3 6.0 %collective-permute-start.11 = (bf16[288,128]{1,0:T(8,128)(2,1)S(1)}, bf16[288,128]{1,0:T(8,128)(2,1)S(1)}, u32[]{:S(2)}, u32[]{:S(2)}) collective-permute-start(bf16[288,128]{1,0:T(8,128)(2,1)S(1)} %pad_maximum_fusion.7), channel_id=1, source_target_pairs={{0,7},{1,0},{2,1},{3,2},{4,3},{5,4},{6,5},{7,6},{8,15},{9,8},{10,9... | collective-permute-start | bytes 221192 | tf_op jit(solution)/shard_map/ppermute | solution.py:353

commit v6 on v5

v6 whole, which is shorter than its diff:
```python
import functools

import jax
import jax.numpy as jnp
import numpy as np
from jax import lax
from jax.experimental import pallas as pl
from jax.experimental.pallas import tpu as pltpu
from jax.sharding import PartitionSpec as P

STRIP_TABLE = np.array(
    [
        [1, 2, 0, 3],
        [0, 3, 1, 2],
        [3, 1, 2, 0],
        [2, 0, 3, 1],
        [1, 2, 0, 3],
        [1, 2, 0, 3],
        [0, 3, 1, 2],
        [0, 3, 1, 2],
    ],
    np.int32,
)
FLIP_TABLE = np.array(
    [
        [0, 0, 1, 1],
        [0, 0, 1, 1],
        [0, 1, 1, 0],
        [0, 1, 1, 0],
        [0, 0, 1, 1],
        [0, 0, 1, 1],
        [0, 0, 1, 1],
        [0, 0, 1, 1],
    ],
    np.int32,
)
DIRECTIONS = [(-1, 0), (1, 0), (0, -1), (0, 1), (-1, -1), (-1, 1), (1, -1), (1, 1)]
AXES = ("face", "tile")
VMEM = pltpu.VMEM
F32 = jnp.float32
BF16 = jnp.bfloat16
LIMIT = 32 * 1024 * 1024
WIDE_LIMIT = 60 * 1024 * 1024
CORNERS = 16


def shift_down(line, first):
    moved = pltpu.roll(line, 1, 0)
    rows = lax.broadcasted_iota(jnp.int32, moved.shape, 0)
    return jnp.where(rows == 0, first, moved)


def shift_up(line, last):
    size = line.shape[0]
    moved = pltpu.roll(line, size - 1, 0)
    rows = lax.broadcasted_iota(jnp.int32, moved.shape, 0)
    return jnp.where(rows == size - 1, last, moved)


def gelu(value):
    return (0.5 * value) * (1.0 + lax.erf(value * np.float32(np.sqrt(0.5))))


def pick_lines(codes_ref, lines, picked, message_refs, tiles):
    side = lines.shape[1]
    shape = (CORNERS, lines.shape[2])
    rows = lax.broadcasted_iota(jnp.int32, shape, 0)
    for direction in range(8):
        corner = jnp.zeros(shape, F32)
        for tile in range(tiles):
            line = lines[codes_ref[direction, tile * 8 + direction]]
            if direction < 4:
                picked[direction, pl.ds(tile * side, side), :] = line
            else:
                at = side - 1 if direction in (4, 6) else 0
                pixel = line.astype(F32)[at : at + 1]
                corner = jnp.where(rows == tile, pixel, corner)
        if direction >= 4:
            group = tiles * side + (direction % 2) * CORNERS
            picked[direction // 2 - 2, pl.ds(group, CORNERS), :] = corner.astype(BF16)
            picked[direction // 2, pl.ds(group, CORNERS), :] = jnp.zeros(shape, BF16)
    for axis in range(2):
        odd = codes_ref[8, axis]
        message_refs[2 * axis][...] = picked[2 * axis + odd]
        message_refs[2 * axis + 1][...] = picked[2 * axis + 1 - odd]


def in_order(odd, first_ref, second_ref):
    first, second = first_ref[...], second_ref[...]
    return jnp.where(odd == 1, first, second), jnp.where(odd == 1, second, first)


def flip_line(line):
    size = line.shape[0]
    row = lax.broadcasted_iota(jnp.int32, (size, size), 0)
    col = lax.broadcasted_iota(jnp.int32, (size, size), 1)
    turn = jnp.where(row + col == size - 1, 1.0, 0.0).astype(BF16)
    return jnp.dot(turn, line, preferred_element_type=F32).astype(BF16)


def gather_kernel(order_ref, x_ref, o_ref, held, in_sems, out_sem):
    groups = in_sems.shape[0]
    size = held.shape[0] // groups

    def start(at, carry):
        pltpu.make_async_copy(
            x_ref.at[order_ref[at]], held.at[at], in_sems.at[at // size]
        ).start()
        return carry

    lax.fori_loop(0, held.shape[0], start, 0)
    for group in range(groups):
        part = pl.ds(group * size, size)
        pltpu.make_async_copy(x_ref.at[part], held.at[part], in_sems.at[group]).wait()
        pltpu.make_async_copy(held.at[part], o_ref.at[part], out_sem).start()
    pltpu.make_async_copy(held, o_ref, out_sem).wait()


def border_kernel(side, codes_ref, source, fields, ring_ref, *rest):
    x_ref = fields.at[0]
    message_refs, lines, picked, sems = rest[:4], rest[4], rest[5], rest[6]
    devices, tiles, piece, chan = x_ref.shape
    copies = [
        pltpu.make_async_copy(source.at[:, tile], x_ref.at[:, tile], sems.at[tile])
        for tile in range(tiles)
    ]
    for copy in copies:
        copy.start()
    for tile in range(tiles):
        copies[tile].wait()
        ring = [read_row(x_ref, tile, row, side) for row in (0, 1, side - 2, side - 1)]
        if piece >= side:
            low, high = (
                jnp.stack(
                    [
                        x_ref[:, tile, row * side + at : row * side + at + 16]
                        for row in range(piece // side)
                    ],
                    1,
                ).reshape(side, 16, chan)
                for at in (0, side - 16)
            )
        else:
            image = x_ref[:, tile].reshape(side, side // piece, piece, chan)
            low, high = image[:, 0, :16], image[:, -1, piece - 16 :]
        low, high = low.astype(F32), high.astype(F32)
        ring += [v.astype(BF16) for v in (low[:, 0], low[:, 1], high[:, 14], high[:, 15])]
        for at, line in enumerate(ring):
            ring_ref[tile, at] = line
        for strip, at in enumerate((0, 3, 4, 7)):
            lines[tile * 4 + strip] = ring[at]
            lines[tiles * 4 + tile * 4 + strip] = flip_line(ring[at])
    pick_lines(codes_ref, lines, picked, message_refs, tiles)


def ring_kernel(codes_ref, ring_ref, w_ref, b_ref, *rest):
    got_refs, message_refs, (own_ref, lines, picked, got) = rest[:4], rest[4:8], rest[8:]
    got[0], got[1] = in_order(codes_ref[8, 0], got_refs[0], got_refs[1])
    got[2], got[3] = in_order(codes_ref[8, 1], got_refs[2], got_refs[3])
    tiles = ring_ref.shape[0]
    side = ring_ref.shape[2]
    pads = [[got[k, pl.ds(t * side, side), :] for t in range(tiles)] for k in range(4)]
    corners = [
        got[2 + k % 2, pl.ds(tiles * side + k // 2 * CORNERS, CORNERS), :].astype(F32)
        for k in range(4)
    ]
    plans = [
        (0, 0, 1, 0, 1, 2, 3, 0, 1, lambda dy, dx: (dy, dx)),
        (1, 2, 3, 3, 2, 2, 3, side - 1, side - 2, lambda dy, dx: (2 - dy, dx)),
        (2, 0, 2, 4, 5, 0, 1, 0, 1, lambda dy, dx: (dx, dy)),
        (3, 1, 3, 7, 6, 0, 1, side - 1, side - 2, lambda dy, dx: (2 - dx, dy)),
    ]
    stacked = []
    for pad, c_first, c_last, line_0, line_1, end_a, end_b, at_0, at_1, tap in plans:
        for tile in range(tiles):
            begin = pads[end_a][tile].astype(F32)
            finish = pads[end_b][tile].astype(F32)
            parts = []
            for line, first, last in (
                (
                    pads[pad][tile],
                    corners[c_first][tile : tile + 1],
                    corners[c_last][tile : tile + 1],
                ),
                (ring_ref[tile, line_0], begin[at_0 : at_0 + 1], finish[at_0 : at_0 + 1]),
                (ring_ref[tile, line_1], begin[at_1 : at_1 + 1], finish[at_1 : at_1 + 1]),
            ):
                wide = line.astype(F32)
                parts.append(
                    (
                        shift_down(wide, first).astype(BF16),
                        line,
                        shift_up(wide, last).astype(BF16),
                    )
                )
            taps = [tap(dy, dx) for dy in range(3) for dx in range(3)]
            stacked.append(jnp.concatenate([parts[d][j] for d, j in taps], axis=1))
    summed = jnp.dot(
        jnp.concatenate(stacked, axis=0), w_ref[...], preferred_element_type=F32
    )
    hidden = gelu(summed + b_ref[...]).astype(BF16)
    for edge in range(4):
        for tile in range(tiles):
            at = (edge * tiles + tile) * side
            line = hidden[at : at + side]
            own_ref[tile, edge] = line
            lines[tile * 4 + edge] = line
            lines[tiles * 4 + tile * 4 + edge] = flip_line(line)
    pick_lines(codes_ref, lines, picked, message_refs, tiles)


def read_row(x_ref, tile, row, side):
    piece = x_ref.shape[2]
    at = row * side // piece
    if piece >= side:
        start = row * side % piece
        return x_ref[at, tile, start : start + side]
    return x_ref[at : at + side // piece, tile].reshape(side, x_ref.shape[3])


def write_row(ref, tile, row, side, line):
    piece = ref.shape[2]
    at = row * side // piece
    if piece >= side:
        start = row * side % piece
        ref[at, tile, start : start + side] = line
    else:
        count = side // piece
        ref[at : at + count, tile] = line.reshape(count, piece, line.shape[-1])


def row_spans(piece, side):
    cuts = [16] + list(range(piece, side, piece)) + [side - 16]
    return [(a, b) for a, b in zip(cuts, cuts[1:]) if a < b]


def read_part(ref, tile, row, side, begin, end):
    piece = ref.shape[2]
    first = row * side + begin
    start = first % piece
    return ref[first // piece, tile, start : start + end - begin]


def convolve_tile(padded, prepare, w_ref, bias, y, masked, finish):
    side = padded.shape[2]
    chan = padded.shape[3]
    blocks = y.shape[0]
    step = side // 2 // blocks
    rows = lax.broadcasted_iota(jnp.int32, (side, chan), 0)

    def multiply(block):
        begin = 2 * step * block
        for row in range(begin + 1 if block else -1, begin + 2 * step + 1):
            prepare(row)
        lhs = jnp.concatenate(
            [
                padded[pl.ds(step * block + j // 2, step), j % 2].reshape(step * side, chan)
                for j in range(4)
            ],
            axis=1,
        )
        y[block] = jnp.dot(lhs, w_ref[...], preferred_element_type=F32)

    multiply(0)
    for block in range(blocks):
        if block + 1 < blocks:
            multiply(block + 1)
        for i in range(step):
            for half in range(2):
                row = (block * step + i) * 2 + half
                a, b, c = (
                    y[block, pl.ds(i * side, side), pl.ds((half * 3 + dx) * chan, chan)]
                    for dx in range(3)
                )
                a = pltpu.roll(a, 1, 0)
                c = pltpu.roll(c, side - 1, 0)
                if masked:
                    a = jnp.where(rows == 0, 0.0, a)
                    c = jnp.where(rows == side - 1, 0.0, c)
                finish(row, (a + c) + (b + bias))


def first_kernel(side, tiles, *refs):
    w_ref, b_ref = refs[:2]
    fields, padded, y = refs[-3:]
    x_ref, h_ref = fields.at[0], fields.at[1]
    for tile in tiles:

        def prepare(row):
            if 0 <= row < side:
                line = read_row(x_ref, tile, row, side)
            else:
                line = jnp.zeros(padded.shape[2:], BF16)
            padded[(row + 1) // 2, (row + 1) % 2] = line

        def finish(row, value):
            write_row(h_ref, tile, row, side, gelu(value).astype(BF16))

        convolve_tile(padded, prepare, w_ref, b_ref[...], y, False, finish)


def second_kernel(side, tiles, *refs):
    ring_ref, w_ref, b_ref = refs[:3]
    fields, out_ref, strips, sums, padded, y, columns, result, sems = refs[-9:]
    x_ref, h_ref = fields.at[0], fields.at[1]
    chan = fields.shape[-1]
    rows = lax.broadcasted_iota(jnp.int32, (16, chan), 0)
    blocks = y.shape[0]
    size = side // blocks
    inner = pl.ds(16, side - 32)
    copies = []
    for at_tile, tile in enumerate(tiles):
        columns[0] = ring_ref[tile, 2].astype(F32)
        columns[1] = ring_ref[tile, 3].astype(F32)

        def prepare(row):
            m, e = (row + 1) // 2, (row + 1) % 2
            if row < 0 or row == side:
                padded[m, e] = jnp.zeros((side, chan), BF16)
            elif row == 0 or row == side - 1:
                padded[m, e] = ring_ref[tile, 0 if row == 0 else 1]
            else:
                for begin, end in row_spans(fields.shape[-2], side):
                    padded[m, e, begin:end] = read_part(h_ref, tile, row, side, begin, end)
                for at, begin, place in ((0, 0, 0), (1, side - 16, 15)):
                    old = read_part(h_ref, tile, row, side, begin, begin + 16).astype(F32)
                    new = jnp.where(rows == place, columns[at, row : row + 1], old)
                    padded[m, e, begin : begin + 16] = new.astype(BF16)

        def finish(row, value):
            total = read_row(x_ref, tile, row, side).astype(F32) + value
            line = total.astype(BF16)
            strips[tile, 0, row] = line[:16]
            strips[tile, 1, row] = line[side - 16 :]
            result[at_tile, row] = line[16 : side - 16]
            if row == 0 or row == side - 1:
                sums[tile, 0 if row == 0 else 1] = total
            sums[tile, 2, row : row + 1] = total[:1]
            sums[tile, 3, row : row + 1] = total[side - 1 :]
            if (row + 1) % size == 0:
                part = pl.ds(row + 1 - size, size)
                copies.append(
                    pltpu.make_async_copy(
                        result.at[at_tile, part],
                        out_ref.at[tile, part, inner],
                        sems.at[len(copies)],
                    )
                )
                copies[-1].start()

        convolve_tile(padded, prepare, w_ref, b_ref[...], y, True, finish)
    for copy in copies:
        copy.wait()


def last_kernel(side, upper, lower, before, after, w_ref, old_strips, sums, *refs):
    out_ref, ends, strips, sems = refs[-4:]
    tiles, chan = sums.shape[0], sums.shape[3]
    split = tiles * side
    got = (upper, lower, before, after)
    groups = [got[2 + k % 2][pl.ds(split + k // 2 * CORNERS, CORNERS), :] for k in range(4)]
    corners = [group.astype(F32) for group in groups]
    zero = jnp.zeros((1, chan), F32)
    added = []
    weights = (w_ref[0], w_ref[2], w_ref[:, 0], w_ref[:, 2])
    for edge in range(4):
        stacked = []
        for tile in range(tiles):
            line = got[edge][pl.ds(tile * side, side), :]
            first = corners[2 * edge][tile : tile + 1] if edge < 2 else zero
            last = corners[2 * edge + 1][tile : tile + 1] if edge < 2 else zero
            wide = line.astype(F32)
            stacked.append(
                jnp.concatenate(
                    [
                        shift_down(wide, first).astype(BF16),
                        line,
                        shift_up(wide, last).astype(BF16),
                    ],
                    axis=1,
                )
            )
        added.append(
            jnp.dot(
                jnp.concatenate(stacked, axis=0),
                weights[edge].reshape(3 * chan, chan),
                preferred_element_type=F32,
            )
        )
    rows = lax.broadcasted_iota(jnp.int32, (side, chan), 0)
    few = lax.broadcasted_iota(jnp.int32, (16, chan), 0)
    copies = []
    for tile in range(tiles):
        span = slice(tile * side, (tile + 1) * side)
        for edge in range(2):
            total = sums[tile, edge] + added[edge][span]
            at = 0 if edge == 0 else side - 1
            left = added[2][span][at : at + 1]
            right = added[3][span][at : at + 1]
            total = total + jnp.where(rows == 0, left, 0.0)
            total = total + jnp.where(rows == side - 1, right, 0.0)
            ends[tile, edge] = total.astype(BF16)
            copies.append(
                pltpu.make_async_copy(
                    ends.at[tile, edge], out_ref.at[tile, at], sems.at[len(copies)]
                )
            )
            copies[-1].start()
        for edge, begin, place in ((2, 0, 0), (3, side - 16, 15)):
            column = sums[tile, edge] + added[edge][span]
            for row in range(1, side - 1):
                old = old_strips[tile, edge - 2, row].astype(F32)
                new = jnp.where(few == place, column[row : row + 1], old)
                strips[tile, edge - 2, row] = new.astype(BF16)
            inner = pl.ds(1, side - 2)
            copies.append(
                pltpu.make_async_copy(
                    strips.at[tile, edge - 2, inner],
                    out_ref.at[tile, inner, pl.ds(begin, 16)],
                    sems.at[len(copies)],
                )
            )
            copies[-1].start()
    for copy in copies:
        copy.wait()


def paired_weights(weight):
    chan_in, chan_out = weight.shape[2:]
    by_tap = weight.transpose(0, 2, 1, 3).reshape(3, chan_in, 3 * chan_out)
    zero = jnp.zeros((1, chan_in, 3 * chan_out), weight.dtype)
    first = jnp.concatenate([by_tap, zero], 0)
    second = jnp.concatenate([zero, by_tap], 0)
    return jnp.stack([first, second], 2).reshape(4 * chan_in, 6 * chan_out)


def swap_far(array, axis):
    size = lax.axis_size(axis)
    pairs = [(i, (i + 1 if i % 2 else i - 1) % size) for i in range(size)]
    return lax.ppermute(array, axis, pairs)


def swap_near(array, axis):
    return lax.ppermute(array, axis, [(i, i ^ 1) for i in range(lax.axis_size(axis))])


def neighbours_along(array, axis):
    size = lax.axis_size(axis)
    after = lax.ppermute(array, axis, [(i, (i - 1) % size) for i in range(size)])
    before = lax.ppermute(array, axis, [(i, (i + 1) % size) for i in range(size)])
    return after, before


def shards(latitude_rows, tile_order, neighbours, rotations, w_first, b_first, w_second, b_second):
    devices = lax.axis_size("face") * lax.axis_size("tile")
    tiles = neighbours.shape[0]
    piece, chan = latitude_rows.shape[1:]
    side = int(round((piece * devices) ** 0.5))
    vmem_spec = pl.BlockSpec(memory_space=VMEM)
    smem_spec = pl.BlockSpec(memory_space=pltpu.SMEM)
    hbm_spec = pl.BlockSpec(memory_space=pltpu.HBM)
    params = pltpu.CompilerParams(vmem_limit_bytes=LIMIT)

    asked = neighbours % tiles * 4 + rotations
    after, before = neighbours_along(asked, "face")

    groups = 8 if latitude_rows.shape[0] % 8 == 0 else 1
    ordered = pl.pallas_call(
        gather_kernel,
        in_specs=[smem_spec, hbm_spec],
        out_specs=hbm_spec,
        out_shape=jax.ShapeDtypeStruct(latitude_rows.shape, latitude_rows.dtype),
        scratch_shapes=[
            VMEM(latitude_rows.shape, latitude_rows.dtype),
            pltpu.SemaphoreType.DMA((groups,)),
            pltpu.SemaphoreType.DMA,
        ],
        compiler_params=pltpu.CompilerParams(vmem_limit_bytes=WIDE_LIMIT),
        name="order",
    )(tile_order, latitude_rows)
    ordered, after, before = lax.optimization_barrier((ordered, after, before))
    gathered = lax.all_to_all(ordered, AXES, split_axis=0, concat_axis=0, tiled=True)
    column = jnp.stack([asked, after, before], 0)
    on, back = neighbours_along(column, "tile")
    asked = jnp.stack(
        [after, before] + [side_rows[i] for i in range(3) for side_rows in (on, back)], 0
    )
    turn = (asked % 4)[..., None] == jnp.arange(4, dtype=jnp.int32)
    strip = jnp.sum(jnp.where(turn, jnp.asarray(STRIP_TABLE), 0), -1)
    flip = jnp.sum(jnp.where(turn, jnp.asarray(FLIP_TABLE), 0), -1)
    codes = ((flip * tiles + asked // 4) * 4 + strip).reshape(8, tiles * 8)
    odd = jnp.stack([lax.axis_index("face") % 2, lax.axis_index("tile") % 2]).astype(jnp.int32)
    codes = jnp.concatenate([codes, jnp.pad(odd, (0, tiles * 8 - 2))[None]], 0)
    constants = (
        paired_weights(w_first),
        paired_weights(w_second),
        w_second,
        w_first.reshape(9 * chan, chan),
        b_first.reshape(1, chan),
        b_second.reshape(1, chan),
    )
    odd = (odd[0] == 1, odd[1] == 1)
    gathered, codes, odd, constants = lax.optimization_barrier((gathered, codes, odd, constants))
    w_one, w_two, w_pads, w_edges, b_one, b_two = constants
    pieces = gathered.reshape(devices, tiles, piece, chan)

    split = tiles * side
    message_shape = jax.ShapeDtypeStruct((split + 2 * CORNERS, chan), BF16)
    line_shape = (tiles, 8, side, chan)
    fields_shape = jax.ShapeDtypeStruct((2,) + pieces.shape, BF16)
    four = VMEM((4,) + message_shape.shape, BF16)
    lines_scratch = VMEM((8 * tiles, side, chan), BF16)
    fields, ring, *sends = pl.pallas_call(
        functools.partial(border_kernel, side),
        in_specs=[smem_spec, hbm_spec],
        out_specs=[vmem_spec] * 6,
        out_shape=[
            fields_shape,
            jax.ShapeDtypeStruct((tiles, 8, side, chan), BF16),
        ]
        + [message_shape] * 4,
        scratch_shapes=[lines_scratch, four, pltpu.SemaphoreType.DMA((tiles,))],
        compiler_params=params,
        name="borders",
    )(codes, pieces)

    blocks = 4
    field = VMEM((side // 2 + 1, 2, side, chan), BF16)
    products = VMEM((blocks, side // 2 // blocks * side, 6 * chan), F32)
    field_shape = jax.ShapeDtypeStruct((tiles, side, side, chan), BF16)

    def first(part, done):
        return (
            pl.pallas_call(
                functools.partial(first_kernel, side, part),
                in_specs=[vmem_spec] * 3,
                out_specs=vmem_spec,
                out_shape=fields_shape,
                input_output_aliases={2: 0},
                scratch_shapes=[field, products],
                compiler_params=params,
                name="first",
            )(w_one, b_one, *(done or (fields,))),
        )

    odd_face, odd_tile = odd

    def halo(sends, work):
        second, first = swap_far(sends[1], "face"), swap_near(sends[0], "face")
        done = work[0](())
        first, second, done = lax.optimization_barrier((first, second, done))
        groups = [
            jnp.where(odd_face, a[split:], b[split:]).reshape(2, CORNERS, chan)
            for a, b in ((first, second), (second, first))
        ]
        near, far = (
            jnp.concatenate(
                [own[:split]] + [jnp.where(odd_tile, g[1 - at], g[at]) for g in groups], 0
            )
            for at, own in enumerate(sends[2:])
        )
        third, fourth = swap_far(far, "tile"), swap_near(near, "tile")
        done = work[1](done)
        third, fourth, done = lax.optimization_barrier((third, fourth, done))
        return (first, second, fourth, third), done

    middle = (tiles + 1) // 2
    halves = [range(middle), range(middle, tiles)]
    got, fields = halo(sends, [functools.partial(first, part) for part in halves])
    *sends, hidden_ring = pl.pallas_call(
        ring_kernel,
        in_specs=[smem_spec] + [vmem_spec] * 7,
        out_specs=[vmem_spec] * 5,
        out_shape=[message_shape] * 4 + [jax.ShapeDtypeStruct((tiles, 4, side, chan), BF16)],
        scratch_shapes=[lines_scratch, four, four],
        compiler_params=params,
        name="hidden_ring",
    )(codes, ring, w_edges, b_one, *got)

    result_specs = [vmem_spec, hbm_spec, vmem_spec, vmem_spec]
    strips_shape = jax.ShapeDtypeStruct((tiles, 2, side, 16, chan), BF16)
    sums_shape = jax.ShapeDtypeStruct((tiles, 4, side, chan), F32)

    def second(part, done):
        done = done or fields
        return pl.pallas_call(
            functools.partial(second_kernel, side, part),
            in_specs=[vmem_spec] * 3 + result_specs[: len(done)],
            out_specs=result_specs,
            out_shape=[fields_shape, field_shape, strips_shape, sums_shape],
            input_output_aliases={3 + i: i for i in range(len(done))},
            scratch_shapes=[
                field,
                products,
                VMEM((2, side, chan), F32),
                VMEM((len(part), side, side - 32, chan), BF16),
                pltpu.SemaphoreType.DMA((len(part) * blocks,)),
            ],
            compiler_params=params,
            name="second",
        )(hidden_ring, w_two, b_two, *done)

    got, (_, out, strips, sums) = halo(sends, [functools.partial(second, part) for part in halves])
    pads = [
        jnp.where(flag, a, b)
        for flag, pair in ((odd_face, got[:2]), (odd_tile, got[2:]))
        for a, b in (pair, pair[::-1])
    ]
    return pl.pallas_call(
        functools.partial(last_kernel, side),
        in_specs=[vmem_spec] * 7 + [hbm_spec],
        out_specs=hbm_spec,
        out_shape=field_shape,
        input_output_aliases={7: 0},
        scratch_shapes=[
            VMEM((tiles, 2, side, chan), BF16),
            VMEM(strips_shape.shape, BF16),
            pltpu.SemaphoreType.DMA((4 * tiles,)),
        ],
        compiler_params=params,
        name="last",
    )(*pads, w_pads, strips, sums, out)


def solution(mesh):
    return jax.shard_map(
        shards,
        mesh=mesh,
        in_specs=(
            P(None, ("face", "tile"), None),
            P(),
            P(("face", "tile"), None),
            P(("face", "tile"), None),
            P(),
            P(),
            P(),
            P(),
        ),
        out_specs=P(("face", "tile"), None, None, None),
        check_vma=False,
    )
```

time: 148 us -> 142 us (0.959)
  starting transfers between devices: 26.4 us -> 19.3 us
  waiting for transfers between devices: 84.1 us -> 87.2 us
  local copies, waits for them, and re-layouts: 8.65 us -> 6.01 us
  Pallas kernels: 25.5 us -> 27 us
    ppermute x12, starting transfers between devices: 20.9 us -> 13.8 us  [the longest x4 4.68 us: swap_far(): return lax.ppermute(array, axis, pairs)]
    ppermute x12, waiting for transfers between devices: 61.7 us -> 65.4 us  [the longest x2 63.2 us: neighbours_along(): lax.ppermute(array, axis, [(i, (i + 1) % size) for i in range(size)])]
    pallas_call x1 -> x3, Pallas kernels: 8.63 us -> 10.8 us  [the longest x2 8.79 us: second(): pl.pallas_call(functools.partial(second_kernel, side, part), in_specs=[vm...]
    another operation x4, local copies, waits for them, and re-layouts: 5.17 us -> 3.17 us  [paired_weights(): return jnp.stack([first, second], 2).reshape(4 * chan_in, 6 * chan_out)]
    pallas_call x4 -> x2, Pallas kernels: 7.65 us -> 7.23 us  [first(): pl.pallas_call(functools.partial(first_kernel, side, part), in_specs=[vme...]
  transfers between devices with their start and end apart: 13 -> 13, of which waited for: 8 -> 4; matrix products, arithmetic and copies ran while one was open for 7% -> 4% of each run, Pallas kernels for 8% -> 14%
where the time goes in v6:
time: 142 us; the launch traced here: 141 us
  waiting for transfers between devices  87.2 us (61%)
  Pallas kernels  27 us (19%)
  starting transfers between devices  19.3 us (14%)
  local copies, waits for them, and re-layouts  6.01 us (4%)
    ppermute x2, waiting for transfers between devices, neighbours_along(): lax.ppermute(array, axis, [(i, (i + 1) % size) for i in range(size)])  63.2 us
    all_to_all x1, waiting for transfers between devices, shards(): lax.all_to_all(ordered, AXES, split_axis=0, concat_axis=0, tiled=True)  21.8 us
    pallas_call x2, Pallas kernels, second(): pl.pallas_call(functools.partial(second_kernel, side, part), in_specs=[vm...  8.79 us
    pallas_call x2, Pallas kernels, first(): pl.pallas_call(functools.partial(first_kernel, side, part), in_specs=[vme...  7.23 us
    all_to_all x1, starting transfers between devices, shards(): lax.all_to_all(ordered, AXES, split_axis=0, concat_axis=0, tiled=True)  5.51 us
    ppermute x4, starting transfers between devices, swap_far(): return lax.ppermute(array, axis, pairs)  4.68 us
    ppermute x2, starting transfers between devices, neighbours_along(): lax.ppermute(array, axis, [(i, (i - 1) % size) for i in range(size)])  4.54 us
    pallas_call x1, Pallas kernels, shards(): pl.pallas_call(gather_kernel, in_specs=[smem_spec, hbm_spec], out_specs=h...  4.15 us
  transfers between devices with their start and end apart: 13, of which 4 were waited for; matrix products, arithmetic and copies ran while one was open for 4% of the time, Pallas kernels for 14%

profile of v6, /device:TPU:0, one launch (start us, length us, event | category | flops | bytes accessed | tf_op | source)
XLA Modules:
  0.0 141.3 jit_solution(7023829660016769648)
XLA Ops:
  0.0 0.7 fusion.8
  0.7 2.9 %collective-permute-start.1 = (s32[4,8]{1,0:T(4,128)S(1)}, s32[4,8]{1,0:T(4,128)S(1)}, u32[]{:S(2)}, u32[]{:S(2)}) collective-permute-start(s32[4,8]{1,0:T(4,128)S(1)} %fusion.8), channel_id=1, source_target_pairs={{0,8},{8,16},{16,24},{24,0},{1,9},{9,17},{17,25},{25,1},{2,10},{10... | collective-permute-start | bytes 392 | tf_op jit(solution)/shard_map/ppermute | solution.py:450
  3.6 1.0 collective-permute-start
  4.7 4.2 %order.1 = bf16[128,128,128]{2,1,0:T(8,128)(2,1)} custom-call(s32[128]{0:T(128)} %order_ref.1, bf16[128,128,128]{2,1,0:T(8,128)(2,1)} %x_ref.1), custom_call_target="tpu_custom_call" | custom-call | tf_op jit(solution)/shard_map/order/pallas_call | solution.py:468
  8.9 5.5 %all-to-all-start = ((bf16[128,128,128]{2,1,0:T(8,128)(2,1)}), bf16[128,128,128]{2,1,0:T(8,128)(2,1)}, u32[]{:S(2)}, u32[]{:S(2)}) async-start(bf16[128,128,128]{2,1,0:T(8,128)(2,1)} %order.1), calls=%async_computation | async-start | bytes 8388608 | tf_op jit(solution)/shard_map/all_to_all | solution.py:482
  14.4 0.2 copy.36
  14.6 0.2 copy.40
  14.9 0.1 pad_bitcast_fusion.1
  15.1 1.1 copy.43
  16.3 0.1 pad_bitcast_fusion.3
  16.5 0.2 collective-permute-start.3
  16.7 0.1 copy.47
  16.9 1.9 %copy.39 = bf16[4,128,2,384]{3,2,1,0:T(2,128)(2,1)} copy(bf16[4,128,2,384]{1,3,0,2:T(8,128)(2,1)S(1)} %pad_maximum_fusion) | data formatting | bytes 1572864 | tf_op jit(solution)/shard_map/stack | solution.py:434
  18.7 1.3 copy.46
  20.1 3.5 %collective-permute-start.2 = (s32[3,4,8]{2,0,1:T(4,128)S(1)}, s32[3,4,8]{2,0,1:T(4,128)S(1)}, u32[]{:S(2)}, u32[]{:S(2)}) collective-permute-start(s32[3,4,8]{2,0,1:T(4,128)S(1)} %pad_add_fusion), channel_id=1, source_target_pairs={{0,7},{1,0},{2,1},{3,2},{4,3},{5,4},{6,5},{7,6},{8,15},{9,8},{10,9... | collective-permute-start | bytes 1160 | tf_op jit(solution)/shard_map/ppermute | solution.py:449
  23.7 63.2 %collective-permute-done.3 = s32[3,4,8]{2,0,1:T(4,128)S(1)} collective-permute-done((s32[3,4,8]{2,0,1:T(4,128)S(1)}, s32[3,4,8]{2,0,1:T(4,128)S(1)}, u32[]{:S(2)}, u32[]{:S(2)}) %collective-permute-start.3) | collective-permute-done | bytes 416 | tf_op jit(solution)/shard_map/ppermute | solution.py:450
  87.2 0.1 stack.73
  87.6 0.1 reduce_sum.22
  87.8 21.8 %all-to-all-done = bf16[128,128,128]{2,1,0:T(8,128)(2,1)} async-done(((bf16[128,128,128]{2,1,0:T(8,128)(2,1)}), bf16[128,128,128]{2,1,0:T(8,128)(2,1)}, u32[]{:S(2)}, u32[]{:S(2)}) %all-to-all-start) | async-done | bytes 4194336 | tf_op jit(solution)/shard_map/all_to_all | solution.py:482
  109.5 3.2 %borders.1 = (bf16[2,32,4,128,128]{4,3,2,1,0:T(8,128)(2,1)S(1)}, bf16[4,8,64,128]{3,2,1,0:T(8,128)(2,1)S(1)}, bf16[288,128]{1,0:T(8,128)(2,1)S(1)}, bf16[288,128...) custom-call(s32[9,32]{1,0:T(8,128)S(1)} %pad_add_fusion.1.codes_ref, ...), custom_call_target="tpu_custom_call" | custom-call | tf_op jit(solution)/shard_map/borders/pallas_call | solution.py:513
  112.8 2.0 %collective-permute-start.5 = (bf16[288,128]{1,0:T(8,128)(2,1)S(1)}, bf16[288,128]{1,0:T(8,128)(2,1)S(1)}, u32[]{:S(2)}, u32[]{:S(2)}) collective-permute-start(bf16[288,128]{1,0:T(8,128)(2,1)S(1)} %get-tuple-element.63), channel_id=1, source_target_pairs={{0,24},{8,16},{16,8},{24,0},{1,25},{9,17},{17,9},{25,1},{2,26},{10... | collective-permute-start | bytes 221192 | tf_op jit(solution)/shard_map/ppermute | solution.py:440
  114.8 3.6 %first.2.refs_2_ = bf16[2,32,4,128,128]{4,3,2,1,0:T(8,128)(2,1)S(1)} custom-call(bf16[512,768]{1,0:T(8,128)(2,1)S(1)} %bitcast.37, f32[1,128]{1,0:T(1,128)S(1)} %bitcast.42, bf16[2,32,4,128,128]{4,3,2,1,0:T(8,128)(2,1)S(1)} %get-tuple-element.65.refs_2_), custom_call_target="tpu_custom_call", output_to_operand_aliasing={{}: (2, {})} | custom-call | tf_op jit(solution)/shard_map/first/pallas_call | solution.py:534
  118.4 0.4 collective-permute-done.5.rest_1_
  119.0 3.6 %first.3.refs_3_ = bf16[2,32,4,128,128]{4,3,2,1,0:T(8,128)(2,1)S(1)} custom-call(bf16[512,768]{1,0:T(8,128)(2,1)S(1)} %bitcast.38, f32[1,128]{1,0:T(1,128)S(1)} %bitcast.43, bf16[2,32,4,128,128]{4,3,2,1,0:T(8,128)(2,1)S(1)} %first.2.refs_2_), custom_call_target="tpu_custom_call", output_to_operand_aliasing={{}: (2, {})} | custom-call | tf_op jit(solution)/shard_map/first/pallas_call | solution.py:534
  122.7 1.8 %collective-permute-done.6.rest_3_ = bf16[288,128]{1,0:T(8,128)(2,1)S(1)} collective-permute-done((bf16[288,128]{1,0:T(8,128)(2,1)S(1)}, bf16[288,128]{1,0:T(8,128)(2,1)S(1)}, u32[]{:S(2)}, u32[]{:S(2)}) %collective-permute-start.6) | collective-permute-done | bytes 73760 | tf_op jit(solution)/shard_map/ppermute | solution.py:440
  124.5 1.7 %hidden_ring.1 = (bf16[288,128]{1,0:T(8,128)(2,1)S(1)}, bf16[288,128]{1,0:T(8,128)(2,1)S(1)}, bf16[288,128]{1,0:T(8,128)(2,1)S(1)}, bf16[288,128]{1,0:T(8,128)(2,1)S(1)}, bf16[4,4,64,128]{3,2,1,0:T(8,128)(2,1)S(1)}) custom-call(s32[9,32]{1,0:T(8,128)S(1)} %pad_add_fusion.1.codes_ref, bf16[4,8,64,128]{3,2,1,0:T(8,128)(2,1)S(1)} %get-tuple-element.59.ring_ref, ...), custom_call_target="tpu_custom_call" | custom-call | tf_op jit(solution)/shard_map/hidden_ring/pallas_call | solution.py:570
  126.2 1.3 collective-permute-start.8
  127.5 1.4 %collective-permute-start.9 = (bf16[288,128]{1,0:T(8,128)(2,1)S(1)}, bf16[288,128]{1,0:T(8,128)(2,1)S(1)}, u32[]{:S(2)}, u32[]{:S(2)}) collective-permute-start(bf16[288,128]{1,0:T(8,128)(2,1)S(1)} %get-tuple-element.75), channel_id=1, source_target_pairs={{0,24},{8,16},{16,8},{24,0},{1,25},{9,17},{17,9},{25,1},{2,26},{10... | collective-permute-start | bytes 221192 | tf_op jit(solution)/shard_map/ppermute | solution.py:440
  129.0 4.3 %second.2 = (bf16[2,32,4,128,128]{4,3,2,1,0:T(8,128)(2,1)S(1)}, bf16[4,64,64,128]{3,2,1,0:T(8,128)(2,1)}, bf16[4,2,64,16,128]{4,3,2,1,0:T(8,128)(2,1)S(1)}, f32[4,4,64,128]{3,2,1,0:T(8,128)S(1)}) custom-call(bf16[4,4,64,128]{3,2,1,0:T(8,128)(2,1)S(1)} %get-tuple-element.76.refs_0_, bf16[512,768]{1,0:T(8,128)(2,1)S(1)} %bitcast.39, ...), custom_call_target="tpu_custom_call", output_to_operand_aliasing={{0}: (3, {})} | custom-call | tf_op jit(solution)/shard_map/second/pallas_call | solution.py:586
  133.3 1.2 collective-permute-start.10
  134.6 4.5 %second.3 = (bf16[2,32,4,128,128]{4,3,2,1,0:T(8,128)(2,1)S(1)}, bf16[4,64,64,128]{3,2,1,0:T(8,128)(2,1)}, bf16[4,2,64,16,128]{4,3,2,1,0:T(8,128)(2,1)S(1)}, f32[4,4,64,128]{3,2,1,0:T(8,128)S(1)}) custom-call(bf16[4,4,64,128]{3,2,1,0:T(8,128)(2,1)S(1)} %get-tuple-element.76.refs_0_, ...), custom_call_target="tpu_custom_call", output_to_operand_aliasing={{0}: (3, {}), {1}: (4, {}), {2}: (5, {}), {3}: (6, {})} | custom-call | tf_op jit(solution)/shard_map/second/pallas_call | solution.py:586
  139.2 2.0 %last.1 = bf16[4,64,64,128]{3,2,1,0:T(8,128)(2,1)} custom-call(bf16[288,128]{1,0:T(8,128)(2,1)S(1)} %get-tuple-element.118.upper, bf16[288,128]{1,0:T(8,128)(2,1)S(1)} %get-tuple-element.117.lower, bf16[288,128]{1,0:T(8,128)(2,1)S(1)} %get-tuple-element.114.before, bf16[288,128]{1,0:T(8,128)(2,1)S(1)} %get-tuple-element.113.after, ...), custom_call_target="tpu_custom_call", output_to_operand_aliasing={{}: (7, {})} | custom-call | tf_op jit(solution)/shard_map/last/pallas_call | solution.py:609
  (64 shorter events, 1.5 us)
Async XLA Ops:
  0.7 8.1 %collective-permute-start.1 = (s32[4,8]{1,0:T(4,128)S(1)}, s32[4,8]{1,0:T(4,128)S(1)}, u32[]{:S(2)}, u32[]{:S(2)}) collective-permute-start(s32[4,8]{1,0:T(4,128)S(1)} %fusion.8), channel_id=1, source_target_pairs={{0,8},{8,16},{16,24},{24,0},{1,9},{9,17},{17,25},{25,1},{2,10},{10... | collective-permute-start | bytes 392 | tf_op jit(solution)/shard_map/ppermute | solution.py:450
  3.6 5.2 %collective-permute-start = (s32[4,8]{1,0:T(4,128)S(1)}, s32[4,8]{1,0:T(4,128)S(1)}, u32[]{:S(2)}, u32[]{:S(2)}) collective-permute-start(s32[4,8]{1,0:T(4,128)S(1)} %fusion.8), channel_id=1, source_target_pairs={{0,24},{8,0},{16,8},{24,16},{1,25},{9,1},{17,9},{25,17},{2,26},{10... | collective-permute-start | bytes 392 | tf_op jit(solution)/shard_map/ppermute | solution.py:449
  8.8 5.6 %copy-start.1 = (bf16[3,3,128,128]{3,2,1,0:T(8,128)(2,1)S(1)}, bf16[3,3,128,128]{3,2,1,0:T(8,128)(2,1)}, u32[]{:S(2)}) copy-start(bf16[3,3,128,128]{3,2,1,0:T(8,128)(2,1)} %param.14) | copy-start | bytes 884740
  8.8 5.8 %copy-start = (bf16[3,3,128,128]{3,2,1,0:T(8,128)(2,1)S(1)}, bf16[3,3,128,128]{3,2,1,0:T(8,128)(2,1)}, u32[]{:S(2)}) copy-start(bf16[3,3,128,128]{3,2,1,0:T(8,128)(2,1)} %w_ref) | copy-start | bytes 884740
  8.9 100.7 %all-to-all-start = ((bf16[128,128,128]{2,1,0:T(8,128)(2,1)}), bf16[128,128,128]{2,1,0:T(8,128)(2,1)}, u32[]{:S(2)}, u32[]{:S(2)}) async-start(bf16[128,128,128]{2,1,0:T(8,128)(2,1)} %order.1), calls=%async_computation | async-start | bytes 8388608 | tf_op jit(solution)/shard_map/all_to_all | solution.py:482
  15.1 72.4 %copy-start.4 = (s32[8,4]{0,1:T(4,128)S(1)}, s32[8,4]{0,1:T(4,128)}, u32[]{:S(2)}) copy-start(s32[8,4]{0,1:T(4,128)} %constant.69.clone) | copy-start | bytes 388
  15.1 72.4 %copy-start.5 = (s32[8,4]{0,1:T(4,128)S(1)}, s32[8,4]{0,1:T(4,128)}, u32[]{:S(2)}) copy-start(s32[8,4]{0,1:T(4,128)} %constant.68.clone) | copy-start | bytes 388
  16.5 70.4 %collective-permute-start.3 = (s32[3,4,8]{2,0,1:T(4,128)S(1)}, s32[3,4,8]{2,0,1:T(4,128)S(1)}, u32[]{:S(2)}, u32[]{:S(2)}) collective-permute-start(s32[3,4,8]{2,0,1:T(4,128)S(1)} %pad_add_fusion), channel_id=1, source_target_pairs={{0,1},{1,2},{2,3},{3,4},{4,5},{5,6},{6,7},{7,0},{8,9},{9,10},{10,1... | collective-permute-start | bytes 1160 | tf_op jit(solution)/shard_map/ppermute | solution.py:450
  16.8 97.9 %copy-start.2 = (f32[128]{0:T(128)S(1)}, f32[128]{0:T(128)}, u32[]{:S(2)}) copy-start(f32[128]{0:T(128)} %param.15) | copy-start | bytes 1540
  20.1 67.0 %collective-permute-start.2 = (s32[3,4,8]{2,0,1:T(4,128)S(1)}, s32[3,4,8]{2,0,1:T(4,128)S(1)}, u32[]{:S(2)}, u32[]{:S(2)}) collective-permute-start(s32[3,4,8]{2,0,1:T(4,128)S(1)} %pad_add_fusion), channel_id=1, source_target_pairs={{0,7},{1,0},{2,1},{3,2},{4,3},{5,4},{6,5},{7,6},{8,15},{9,8},{10,9... | collective-permute-start | bytes 1160 | tf_op jit(solution)/shard_map/ppermute | solution.py:449
  112.7 5.7 %collective-permute-start.4 = (bf16[288,128]{1,0:T(8,128)(2,1)S(1)}, bf16[288,128]{1,0:T(8,128)(2,1)S(1)}, u32[]{:S(2)}, u32[]{:S(2)}) collective-permute-start(bf16[288,128]{1,0:T(8,128)(2,1)S(1)} %get-tuple-element.62), channel_id=1, source_target_pairs={{0,8},{8,0},{16,24},{24,16},{1,9},{9,1},{17,25},{25,17},{2,10},{10... | collective-permute-start | bytes 221192 | tf_op jit(solution)/shard_map/ppermute | solution.py:444
  112.8 6.0 %collective-permute-start.5 = (bf16[288,128]{1,0:T(8,128)(2,1)S(1)}, bf16[288,128]{1,0:T(8,128)(2,1)S(1)}, u32[]{:S(2)}, u32[]{:S(2)}) collective-permute-start(bf16[288,128]{1,0:T(8,128)(2,1)S(1)} %get-tuple-element.63), channel_id=1, source_target_pairs={{0,24},{8,16},{16,8},{24,0},{1,25},{9,17},{17,9},{25,1},{2,26},{10... | collective-permute-start | bytes 221192 | tf_op jit(solution)/shard_map/ppermute | solution.py:440
  118.9 5.6 %collective-permute-start.6 = (bf16[288,128]{1,0:T(8,128)(2,1)S(1)}, bf16[288,128]{1,0:T(8,128)(2,1)S(1)}, u32[]{:S(2)}, u32[]{:S(2)}) collective-permute-start(bf16[288,128]{1,0:T(8,128)(2,1)S(1)} %pad_maximum_fusion.2), channel_id=1, source_target_pairs={{0,7},{1,2},{2,1},{3,4},{4,3},{5,6},{6,5},{7,0},{8,15},{9,10},{10,... | collective-permute-start | bytes 221192 | tf_op jit(solution)/shard_map/ppermute | solution.py:440
  119.0 10.0 %copy-start.3 = (f32[128]{0:T(128)S(1)}, f32[128]{0:T(128)}, u32[]{:S(2)}) copy-start(f32[128]{0:T(128)} %param.17) | copy-start | bytes 1540
  119.0 5.5 %collective-permute-start.7 = (bf16[288,128]{1,0:T(8,128)(2,1)S(1)}, bf16[288,128]{1,0:T(8,128)(2,1)S(1)}, u32[]{:S(2)}, u32[]{:S(2)}) collective-permute-start(bf16[288,128]{1,0:T(8,128)(2,1)S(1)} %pad_maximum_fusion.3), channel_id=1, source_target_pairs={{0,1},{1,0},{2,3},{3,2},{4,5},{5,4},{6,7},{7,6},{8,9},{9,8},{10,11... | collective-permute-start | bytes 221192 | tf_op jit(solution)/shard_map/ppermute | solution.py:444
  126.2 7.0 %collective-permute-start.8 = (bf16[288,128]{1,0:T(8,128)(2,1)S(1)}, bf16[288,128]{1,0:T(8,128)(2,1)S(1)}, u32[]{:S(2)}, u32[]{:S(2)}) collective-permute-start(bf16[288,128]{1,0:T(8,128)(2,1)S(1)} %get-tuple-element.74), channel_id=1, source_target_pairs={{0,8},{8,0},{16,24},{24,16},{1,9},{9,1},{17,25},{25,17},{2,10},{10... | collective-permute-start | bytes 221192 | tf_op jit(solution)/shard_map/ppermute | solution.py:444
  127.5 5.7 %collective-permute-start.9 = (bf16[288,128]{1,0:T(8,128)(2,1)S(1)}, bf16[288,128]{1,0:T(8,128)(2,1)S(1)}, u32[]{:S(2)}, u32[]{:S(2)}) collective-permute-start(bf16[288,128]{1,0:T(8,128)(2,1)S(1)} %get-tuple-element.75), channel_id=1, source_target_pairs={{0,24},{8,16},{16,8},{24,0},{1,25},{9,17},{17,9},{25,1},{2,26},{10... | collective-permute-start | bytes 221192 | tf_op jit(solution)/shard_map/ppermute | solution.py:440
  133.3 5.8 %collective-permute-start.10 = (bf16[288,128]{1,0:T(8,128)(2,1)S(1)}, bf16[288,128]{1,0:T(8,128)(2,1)S(1)}, u32[]{:S(2)}, u32[]{:S(2)}) collective-permute-start(bf16[288,128]{1,0:T(8,128)(2,1)S(1)} %pad_maximum_fusion.4), channel_id=1, source_target_pairs={{0,7},{1,2},{2,1},{3,4},{4,3},{5,6},{6,5},{7,0},{8,15},{9,10},{10,... | collective-permute-start | bytes 221192 | tf_op jit(solution)/shard_map/ppermute | solution.py:440
  134.5 4.6 %collective-permute-start.11 = (bf16[288,128]{1,0:T(8,128)(2,1)S(1)}, bf16[288,128]{1,0:T(8,128)(2,1)S(1)}, u32[]{:S(2)}, u32[]{:S(2)}) collective-permute-start(bf16[288,128]{1,0:T(8,128)(2,1)S(1)} %pad_maximum_fusion.5), channel_id=1, source_target_pairs={{0,1},{1,0},{2,3},{3,2},{4,5},{5,4},{6,7},{7,6},{8,9},{9,8},{10,11... | collective-permute-start | bytes 221192 | tf_op jit(solution)/shard_map/ppermute | solution.py:444

commit v7 on v6

--- a/solution.py
+++ b/solution.py
@@ -461,9 +461,6 @@
     hbm_spec = pl.BlockSpec(memory_space=pltpu.HBM)
     params = pltpu.CompilerParams(vmem_limit_bytes=LIMIT)
 
-    asked = neighbours % tiles * 4 + rotations
-    after, before = neighbours_along(asked, "face")
-
     groups = 8 if latitude_rows.shape[0] % 8 == 0 else 1
     ordered = pl.pallas_call(
         gather_kernel,
@@ -478,8 +475,10 @@
         compiler_params=pltpu.CompilerParams(vmem_limit_bytes=WIDE_LIMIT),
         name="order",
     )(tile_order, latitude_rows)
-    ordered, after, before = lax.optimization_barrier((ordered, after, before))
     gathered = lax.all_to_all(ordered, AXES, split_axis=0, concat_axis=0, tiled=True)
+
+    asked = neighbours % tiles * 4 + rotations
+    after, before = neighbours_along(asked, "face")
     column = jnp.stack([asked, after, before], 0)
     on, back = neighbours_along(column, "tile")
     asked = jnp.stack(

time: 142 us -> 139 us (0.979)
  waiting for transfers between devices: 87.2 us -> 83.4 us
  starting transfers between devices: 19.3 us -> 23 us
  local copies, waits for them, and re-layouts: 6.01 us -> 4.15 us
    ppermute x2, waiting for transfers between devices: 63.2 us -> 59.4 us  [neighbours_along(): lax.ppermute(array, axis, [(i, (i + 1) % size) for i in range(size)])]
    ppermute x2, starting transfers between devices: 4.54 us -> 7.62 us  [neighbours_along(): lax.ppermute(array, axis, [(i, (i - 1) % size) for i in range(size)])]
    all_to_all x1, starting transfers between devices: 5.51 us -> 7.43 us  [shards(): lax.all_to_all(ordered, AXES, split_axis=0, concat_axis=0, tiled=True)]
  transfers between devices with their start and end apart: 13 -> 13, of which waited for: 4 -> 5; matrix products, arithmetic and copies ran while one was open for 4% -> 3% of each run, Pallas kernels for 14% -> 12%
where the time goes in v7:
time: 139 us
  waiting for transfers between devices  83.4 us (60%)
  Pallas kernels  27 us (19%)
  starting transfers between devices  23 us (17%)
  local copies, waits for them, and re-layouts  4.15 us (3%)
    ppermute x2, waiting for transfers between devices, neighbours_along(): lax.ppermute(array, axis, [(i, (i + 1) % size) for i in range(size)])  59.4 us
    all_to_all x1, waiting for transfers between devices, shards(): lax.all_to_all(ordered, AXES, split_axis=0, concat_axis=0, tiled=True)  21.8 us
    pallas_call x2, Pallas kernels, second(): pl.pallas_call(functools.partial(second_kernel, side, part), in_specs=[vm...  8.79 us
    ppermute x2, starting transfers between devices, neighbours_along(): lax.ppermute(array, axis, [(i, (i - 1) % size) for i in range(size)])  7.62 us
    all_to_all x1, starting transfers between devices, shards(): lax.all_to_all(ordered, AXES, split_axis=0, concat_axis=0, tiled=True)  7.43 us
    pallas_call x2, Pallas kernels, first(): pl.pallas_call(functools.partial(first_kernel, side, part), in_specs=[vme...  7.24 us
    ppermute x4, starting transfers between devices, swap_far(): return lax.ppermute(array, axis, pairs)  4.69 us
    pallas_call x1, Pallas kernels, shards(): pl.pallas_call(gather_kernel, in_specs=[smem_spec, hbm_spec], out_specs=h...  4.15 us
  transfers between devices with their start and end apart: 13, of which 5 were waited for; matrix products, arithmetic and copies ran while one was open for 3% of the time, Pallas kernels for 12%

profile of v7, /device:TPU:0, one launch (start us, length us, event | category | flops | bytes accessed | tf_op | source)
XLA Modules:
  0.0 138.6 jit_solution(2246201832729363654)
XLA Ops:
  0.0 4.2 %order.1 = bf16[128,128,128]{2,1,0:T(8,128)(2,1)} custom-call(s32[128]{0:T(128)} %order_ref.1, bf16[128,128,128]{2,1,0:T(8,128)(2,1)} %x_ref.1), custom_call_target="tpu_custom_call" | custom-call | tf_op jit(solution)/shard_map/order/pallas_call | solution.py:465
  4.2 7.4 %all-to-all-start = ((bf16[128,128,128]{2,1,0:T(8,128)(2,1)}), bf16[128,128,128]{2,1,0:T(8,128)(2,1)}, u32[]{:S(2)}, u32[]{:S(2)}) async-start(bf16[128,128,128]{2,1,0:T(8,128)(2,1)} %order.1), calls=%async_computation | async-start | bytes 8388608 | tf_op jit(solution)/shard_map/all_to_all | solution.py:478
  11.7 1.7 %collective-permute-start.1 = (s32[4,8]{1,0:T(4,128)S(1)}, s32[4,8]{1,0:T(4,128)S(1)}, u32[]{:S(2)}, u32[]{:S(2)}) collective-permute-start(s32[4,8]{1,0:T(4,128)S(1)} %fusion.8), channel_id=1, source_target_pairs={{0,8},{8,16},{16,24},{24,0},{1,9},{9,17},{17,25},{25,1},{2,10},{10... | collective-permute-start | bytes 392 | tf_op jit(solution)/shard_map/ppermute | solution.py:450
  13.4 1.2 collective-permute-start
  14.7 0.2 copy.36
  14.9 0.2 copy.40
  15.2 0.1 pad_bitcast_fusion.1
  15.3 0.1 pad_bitcast_fusion.3
  15.6 1.1 copy.43
  16.7 21.7 %collective-permute-done.1 = s32[4,8]{1,0:T(4,128)S(1)} collective-permute-done((s32[4,8]{1,0:T(4,128)S(1)}, s32[4,8]{1,0:T(4,128)S(1)}, u32[]{:S(2)}, u32[]{:S(2)}) %collective-permute-start.1) | collective-permute-done | bytes 160 | tf_op jit(solution)/shard_map/ppermute | solution.py:450
  38.5 0.1 copy.47
  38.6 1.1 copy.39
  39.7 0.1 copy.46
  39.9 6.4 %collective-permute-start.2 = (s32[3,4,8]{2,0,1:T(4,128)S(1)}, s32[3,4,8]{2,0,1:T(4,128)S(1)}, u32[]{:S(2)}, u32[]{:S(2)}) collective-permute-start(s32[3,4,8]{2,0,1:T(4,128)S(1)} %pad_add_fusion), channel_id=1, source_target_pairs={{0,7},{1,0},{2,1},{3,2},{4,3},{5,4},{6,5},{7,6},{8,15},{9,8},{10,9... | collective-permute-start | bytes 1160 | tf_op jit(solution)/shard_map/ppermute | solution.py:449
  46.2 0.1 stack.68
  46.4 37.7 %collective-permute-done.3 = s32[3,4,8]{2,0,1:T(4,128)S(1)} collective-permute-done((s32[3,4,8]{2,0,1:T(4,128)S(1)}, s32[3,4,8]{2,0,1:T(4,128)S(1)}, u32[]{:S(2)}, u32[]{:S(2)}) %collective-permute-start.3) | collective-permute-done | bytes 416 | tf_op jit(solution)/shard_map/ppermute | solution.py:450
  84.4 0.1 stack.73
  84.9 0.1 reduce_sum.22
  85.0 21.8 %all-to-all-done = bf16[128,128,128]{2,1,0:T(8,128)(2,1)} async-done(((bf16[128,128,128]{2,1,0:T(8,128)(2,1)}), bf16[128,128,128]{2,1,0:T(8,128)(2,1)}, u32[]{:S(2)}, u32[]{:S(2)}) %all-to-all-start) | async-done | bytes 4194336 | tf_op jit(solution)/shard_map/all_to_all | solution.py:478
  106.8 3.2 %borders.1 = (bf16[2,32,4,128,128]{4,3,2,1,0:T(8,128)(2,1)S(1)}, bf16[4,8,64,128]{3,2,1,0:T(8,128)(2,1)S(1)}, bf16[288,128]{1,0:T(8,128)(2,1)S(1)}, bf16[288,128...) custom-call(s32[9,32]{1,0:T(8,128)S(1)} %pad_add_fusion.1.codes_ref, ...), custom_call_target="tpu_custom_call" | custom-call | tf_op jit(solution)/shard_map/borders/pallas_call | solution.py:512
  110.0 2.0 %collective-permute-start.5 = (bf16[288,128]{1,0:T(8,128)(2,1)S(1)}, bf16[288,128]{1,0:T(8,128)(2,1)S(1)}, u32[]{:S(2)}, u32[]{:S(2)}) collective-permute-start(bf16[288,128]{1,0:T(8,128)(2,1)S(1)} %get-tuple-element.57), channel_id=1, source_target_pairs={{0,24},{8,16},{16,8},{24,0},{1,25},{9,17},{17,9},{25,1},{2,26},{10... | collective-permute-start | bytes 221192 | tf_op jit(solution)/shard_map/ppermute | solution.py:440
  112.1 3.6 %first.2.refs_2_ = bf16[2,32,4,128,128]{4,3,2,1,0:T(8,128)(2,1)S(1)} custom-call(bf16[512,768]{1,0:T(8,128)(2,1)S(1)} %bitcast.37, f32[1,128]{1,0:T(1,128)S(1)} %bitcast.42, bf16[2,32,4,128,128]{4,3,2,1,0:T(8,128)(2,1)S(1)} %get-tuple-element.59.refs_2_), custom_call_target="tpu_custom_call", output_to_operand_aliasing={{}: (2, {})} | custom-call | tf_op jit(solution)/shard_map/first/pallas_call | solution.py:533
  115.7 0.4 collective-permute-done.5.rest_1_
  116.3 3.6 %first.3.refs_3_ = bf16[2,32,4,128,128]{4,3,2,1,0:T(8,128)(2,1)S(1)} custom-call(bf16[512,768]{1,0:T(8,128)(2,1)S(1)} %bitcast.38, f32[1,128]{1,0:T(1,128)S(1)} %bitcast.43, bf16[2,32,4,128,128]{4,3,2,1,0:T(8,128)(2,1)S(1)} %first.2.refs_2_), custom_call_target="tpu_custom_call", output_to_operand_aliasing={{}: (2, {})} | custom-call | tf_op jit(solution)/shard_map/first/pallas_call | solution.py:533
  119.9 1.8 %collective-permute-done.6.rest_3_ = bf16[288,128]{1,0:T(8,128)(2,1)S(1)} collective-permute-done((bf16[288,128]{1,0:T(8,128)(2,1)S(1)}, bf16[288,128]{1,0:T(8,128)(2,1)S(1)}, u32[]{:S(2)}, u32[]{:S(2)}) %collective-permute-start.6) | collective-permute-done | bytes 73760 | tf_op jit(solution)/shard_map/ppermute | solution.py:440
  121.8 1.7 %hidden_ring.1 = (bf16[288,128]{1,0:T(8,128)(2,1)S(1)}, bf16[288,128]{1,0:T(8,128)(2,1)S(1)}, bf16[288,128]{1,0:T(8,128)(2,1)S(1)}, bf16[288,128]{1,0:T(8,128)(2,1)S(1)}, bf16[4,4,64,128]{3,2,1,0:T(8,128)(2,1)S(1)}) custom-call(s32[9,32]{1,0:T(8,128)S(1)} %pad_add_fusion.1.codes_ref, bf16[4,8,64,128]{3,2,1,0:T(8,128)(2,1)S(1)} %get-tuple-element.53.ring_ref, ...), custom_call_target="tpu_custom_call" | custom-call | tf_op jit(solution)/shard_map/hidden_ring/pallas_call | solution.py:569
  123.5 1.3 collective-permute-start.8
  124.8 1.4 %collective-permute-start.9 = (bf16[288,128]{1,0:T(8,128)(2,1)S(1)}, bf16[288,128]{1,0:T(8,128)(2,1)S(1)}, u32[]{:S(2)}, u32[]{:S(2)}) collective-permute-start(bf16[288,128]{1,0:T(8,128)(2,1)S(1)} %get-tuple-element.69), channel_id=1, source_target_pairs={{0,24},{8,16},{16,8},{24,0},{1,25},{9,17},{17,9},{25,1},{2,26},{10... | collective-permute-start | bytes 221192 | tf_op jit(solution)/shard_map/ppermute | solution.py:440
  126.3 4.3 %second.2 = (bf16[2,32,4,128,128]{4,3,2,1,0:T(8,128)(2,1)S(1)}, bf16[4,64,64,128]{3,2,1,0:T(8,128)(2,1)}, bf16[4,2,64,16,128]{4,3,2,1,0:T(8,128)(2,1)S(1)}, f32[4,4,64,128]{3,2,1,0:T(8,128)S(1)}) custom-call(bf16[4,4,64,128]{3,2,1,0:T(8,128)(2,1)S(1)} %get-tuple-element.70.refs_0_, bf16[512,768]{1,0:T(8,128)(2,1)S(1)} %bitcast.39, ...), custom_call_target="tpu_custom_call", output_to_operand_aliasing={{0}: (3, {})} | custom-call | tf_op jit(solution)/shard_map/second/pallas_call | solution.py:585
  130.6 1.2 collective-permute-start.10
  131.9 4.5 %second.3 = (bf16[2,32,4,128,128]{4,3,2,1,0:T(8,128)(2,1)S(1)}, bf16[4,64,64,128]{3,2,1,0:T(8,128)(2,1)}, bf16[4,2,64,16,128]{4,3,2,1,0:T(8,128)(2,1)S(1)}, f32[4,4,64,128]{3,2,1,0:T(8,128)S(1)}) custom-call(bf16[4,4,64,128]{3,2,1,0:T(8,128)(2,1)S(1)} %get-tuple-element.70.refs_0_, ...), custom_call_target="tpu_custom_call", output_to_operand_aliasing={{0}: (3, {}), {1}: (4, {}), {2}: (5, {}), {3}: (6, {})} | custom-call | tf_op jit(solution)/shard_map/second/pallas_call | solution.py:585
  136.4 2.0 %last.1 = bf16[4,64,64,128]{3,2,1,0:T(8,128)(2,1)} custom-call(bf16[288,128]{1,0:T(8,128)(2,1)S(1)} %get-tuple-element.112.upper, bf16[288,128]{1,0:T(8,128)(2,1)S(1)} %get-tuple-element.111.lower, bf16[288,128]{1,0:T(8,128)(2,1)S(1)} %get-tuple-element.108.before, bf16[288,128]{1,0:T(8,128)(2,1)S(1)} %get-tuple-element.107.after, ...), custom_call_target="tpu_custom_call", output_to_operand_aliasing={{}: (7, {})} | custom-call | tf_op jit(solution)/shard_map/last/pallas_call | solution.py:608
  (68 shorter events, 1.5 us)
Async XLA Ops:
  4.2 7.5 %copy-start.4 = (s32[4,8]{1,0:T(4,128)S(1)}, s32[4,8]{1,0:T(4,128)}, u32[]{:S(2)}) copy-start(s32[4,8]{1,0:T(4,128)} %param.13) | copy-start | bytes 388
  4.2 7.5 %copy-start.5 = (s32[4,8]{1,0:T(4,128)S(1)}, s32[4,8]{1,0:T(4,128)}, u32[]{:S(2)}) copy-start(s32[4,8]{1,0:T(4,128)} %param.12) | copy-start | bytes 388
  4.2 10.5 %copy-start.1 = (bf16[3,3,128,128]{3,2,1,0:T(8,128)(2,1)S(1)}, bf16[3,3,128,128]{3,2,1,0:T(8,128)(2,1)}, u32[]{:S(2)}) copy-start(bf16[3,3,128,128]{3,2,1,0:T(8,128)(2,1)} %param.14) | copy-start | bytes 884740
  4.2 10.7 %copy-start = (bf16[3,3,128,128]{3,2,1,0:T(8,128)(2,1)S(1)}, bf16[3,3,128,128]{3,2,1,0:T(8,128)(2,1)}, u32[]{:S(2)}) copy-start(bf16[3,3,128,128]{3,2,1,0:T(8,128)(2,1)} %w_ref) | copy-start | bytes 884740
  4.2 102.6 %all-to-all-start = ((bf16[128,128,128]{2,1,0:T(8,128)(2,1)}), bf16[128,128,128]{2,1,0:T(8,128)(2,1)}, u32[]{:S(2)}, u32[]{:S(2)}) async-start(bf16[128,128,128]{2,1,0:T(8,128)(2,1)} %order.1), calls=%async_computation | async-start | bytes 8388608 | tf_op jit(solution)/shard_map/all_to_all | solution.py:478
  11.7 26.7 %collective-permute-start.1 = (s32[4,8]{1,0:T(4,128)S(1)}, s32[4,8]{1,0:T(4,128)S(1)}, u32[]{:S(2)}, u32[]{:S(2)}) collective-permute-start(s32[4,8]{1,0:T(4,128)S(1)} %fusion.8), channel_id=1, source_target_pairs={{0,8},{8,16},{16,24},{24,0},{1,9},{9,17},{17,25},{25,1},{2,10},{10... | collective-permute-start | bytes 392 | tf_op jit(solution)/shard_map/ppermute | solution.py:450
  13.4 25.0 %collective-permute-start = (s32[4,8]{1,0:T(4,128)S(1)}, s32[4,8]{1,0:T(4,128)S(1)}, u32[]{:S(2)}, u32[]{:S(2)}) collective-permute-start(s32[4,8]{1,0:T(4,128)S(1)} %fusion.8), channel_id=1, source_target_pairs={{0,24},{8,0},{16,8},{24,16},{1,25},{9,1},{17,9},{25,17},{2,26},{10... | collective-permute-start | bytes 392 | tf_op jit(solution)/shard_map/ppermute | solution.py:449
  15.5 69.2 %copy-start.6 = (s32[8,4]{0,1:T(4,128)S(1)}, s32[8,4]{0,1:T(4,128)}, u32[]{:S(2)}) copy-start(s32[8,4]{0,1:T(4,128)} %constant.69.clone) | copy-start | bytes 388
  15.5 69.2 %copy-start.7 = (s32[8,4]{0,1:T(4,128)S(1)}, s32[8,4]{0,1:T(4,128)}, u32[]{:S(2)}) copy-start(s32[8,4]{0,1:T(4,128)} %constant.68.clone) | copy-start | bytes 388
  38.4 45.7 %collective-permute-start.3 = (s32[3,4,8]{2,0,1:T(4,128)S(1)}, s32[3,4,8]{2,0,1:T(4,128)S(1)}, u32[]{:S(2)}, u32[]{:S(2)}) collective-permute-start(s32[3,4,8]{2,0,1:T(4,128)S(1)} %pad_add_fusion), channel_id=1, source_target_pairs={{0,1},{1,2},{2,3},{3,4},{4,5},{5,6},{6,7},{7,0},{8,9},{9,10},{10,1... | collective-permute-start | bytes 1160 | tf_op jit(solution)/shard_map/ppermute | solution.py:450
  38.6 73.4 %copy-start.2 = (f32[128]{0:T(128)S(1)}, f32[128]{0:T(128)}, u32[]{:S(2)}) copy-start(f32[128]{0:T(128)} %param.15) | copy-start | bytes 1540
  39.9 44.5 %collective-permute-start.2 = (s32[3,4,8]{2,0,1:T(4,128)S(1)}, s32[3,4,8]{2,0,1:T(4,128)S(1)}, u32[]{:S(2)}, u32[]{:S(2)}) collective-permute-start(s32[3,4,8]{2,0,1:T(4,128)S(1)} %pad_add_fusion), channel_id=1, source_target_pairs={{0,7},{1,0},{2,1},{3,2},{4,3},{5,4},{6,5},{7,6},{8,15},{9,8},{10,9... | collective-permute-start | bytes 1160 | tf_op jit(solution)/shard_map/ppermute | solution.py:449
  110.0 5.7 %collective-permute-start.4 = (bf16[288,128]{1,0:T(8,128)(2,1)S(1)}, bf16[288,128]{1,0:T(8,128)(2,1)S(1)}, u32[]{:S(2)}, u32[]{:S(2)}) collective-permute-start(bf16[288,128]{1,0:T(8,128)(2,1)S(1)} %get-tuple-element.56), channel_id=1, source_target_pairs={{0,8},{8,0},{16,24},{24,16},{1,9},{9,1},{17,25},{25,17},{2,10},{10... | collective-permute-start | bytes 221192 | tf_op jit(solution)/shard_map/ppermute | solution.py:444
  110.0 6.0 %collective-permute-start.5 = (bf16[288,128]{1,0:T(8,128)(2,1)S(1)}, bf16[288,128]{1,0:T(8,128)(2,1)S(1)}, u32[]{:S(2)}, u32[]{:S(2)}) collective-permute-start(bf16[288,128]{1,0:T(8,128)(2,1)S(1)} %get-tuple-element.57), channel_id=1, source_target_pairs={{0,24},{8,16},{16,8},{24,0},{1,25},{9,17},{17,9},{25,1},{2,26},{10... | collective-permute-start | bytes 221192 | tf_op jit(solution)/shard_map/ppermute | solution.py:440
  116.1 5.6 %collective-permute-start.6 = (bf16[288,128]{1,0:T(8,128)(2,1)S(1)}, bf16[288,128]{1,0:T(8,128)(2,1)S(1)}, u32[]{:S(2)}, u32[]{:S(2)}) collective-permute-start(bf16[288,128]{1,0:T(8,128)(2,1)S(1)} %pad_maximum_fusion.2), channel_id=1, source_target_pairs={{0,7},{1,2},{2,1},{3,4},{4,3},{5,6},{6,5},{7,0},{8,15},{9,10},{10,... | collective-permute-start | bytes 221192 | tf_op jit(solution)/shard_map/ppermute | solution.py:440
  116.2 10.0 %copy-start.3 = (f32[128]{0:T(128)S(1)}, f32[128]{0:T(128)}, u32[]{:S(2)}) copy-start(f32[128]{0:T(128)} %param.17) | copy-start | bytes 1540
  116.2 5.5 %collective-permute-start.7 = (bf16[288,128]{1,0:T(8,128)(2,1)S(1)}, bf16[288,128]{1,0:T(8,128)(2,1)S(1)}, u32[]{:S(2)}, u32[]{:S(2)}) collective-permute-start(bf16[288,128]{1,0:T(8,128)(2,1)S(1)} %pad_maximum_fusion.3), channel_id=1, source_target_pairs={{0,1},{1,0},{2,3},{3,2},{4,5},{5,4},{6,7},{7,6},{8,9},{9,8},{10,11... | collective-permute-start | bytes 221192 | tf_op jit(solution)/shard_map/ppermute | solution.py:444
  123.5 7.0 %collective-permute-start.8 = (bf16[288,128]{1,0:T(8,128)(2,1)S(1)}, bf16[288,128]{1,0:T(8,128)(2,1)S(1)}, u32[]{:S(2)}, u32[]{:S(2)}) collective-permute-start(bf16[288,128]{1,0:T(8,128)(2,1)S(1)} %get-tuple-element.68), channel_id=1, source_target_pairs={{0,8},{8,0},{16,24},{24,16},{1,9},{9,1},{17,25},{25,17},{2,10},{10... | collective-permute-start | bytes 221192 | tf_op jit(solution)/shard_map/ppermute | solution.py:444
  124.8 5.8 %collective-permute-start.9 = (bf16[288,128]{1,0:T(8,128)(2,1)S(1)}, bf16[288,128]{1,0:T(8,128)(2,1)S(1)}, u32[]{:S(2)}, u32[]{:S(2)}) collective-permute-start(bf16[288,128]{1,0:T(8,128)(2,1)S(1)} %get-tuple-element.69), channel_id=1, source_target_pairs={{0,24},{8,16},{16,8},{24,0},{1,25},{9,17},{17,9},{25,1},{2,26},{10... | collective-permute-start | bytes 221192 | tf_op jit(solution)/shard_map/ppermute | solution.py:440
  130.6 5.8 %collective-permute-start.10 = (bf16[288,128]{1,0:T(8,128)(2,1)S(1)}, bf16[288,128]{1,0:T(8,128)(2,1)S(1)}, u32[]{:S(2)}, u32[]{:S(2)}) collective-permute-start(bf16[288,128]{1,0:T(8,128)(2,1)S(1)} %pad_maximum_fusion.4), channel_id=1, source_target_pairs={{0,7},{1,2},{2,1},{3,4},{4,3},{5,6},{6,5},{7,0},{8,15},{9,10},{10,... | collective-permute-start | bytes 221192 | tf_op jit(solution)/shard_map/ppermute | solution.py:440
  131.8 4.6 %collective-permute-start.11 = (bf16[288,128]{1,0:T(8,128)(2,1)S(1)}, bf16[288,128]{1,0:T(8,128)(2,1)S(1)}, u32[]{:S(2)}, u32[]{:S(2)}) collective-permute-start(bf16[288,128]{1,0:T(8,128)(2,1)S(1)} %pad_maximum_fusion.5), channel_id=1, source_target_pairs={{0,1},{1,0},{2,3},{3,2},{4,5},{5,4},{6,7},{7,6},{8,9},{9,8},{10,11... | collective-permute-start | bytes 221192 | tf_op jit(solution)/shard_map/ppermute | solution.py:444

commit v8 on v7

--- a/solution.py
+++ b/solution.py
@@ -86,8 +86,9 @@
 
 
 def in_order(odd, first_ref, second_ref):
-    first, second = first_ref[...], second_ref[...]
-    return jnp.where(odd == 1, first, second), jnp.where(odd == 1, second, first)
+    first, second = first_ref[...].astype(F32), second_ref[...].astype(F32)
+    before, after = jnp.where(odd == 1, first, second), jnp.where(odd == 1, second, first)
+    return before.astype(BF16), after.astype(BF16)
 
 
 def flip_line(line):
@@ -116,14 +117,15 @@
     pltpu.make_async_copy(held, o_ref, out_sem).wait()
 
 
-def border_kernel(side, codes_ref, source, fields, ring_ref, *rest):
+def border_kernel(side, codes, source, fields, ring_ref, *rest):
     x_ref = fields.at[0]
-    message_refs, lines, picked, sems = rest[:4], rest[4], rest[5], rest[6]
+    message_refs, (lines, picked, codes_ref, sems) = rest[:4], rest[4:]
     devices, tiles, piece, chan = x_ref.shape
     copies = [
         pltpu.make_async_copy(source.at[:, tile], x_ref.at[:, tile], sems.at[tile])
         for tile in range(tiles)
     ]
+    copies.append(pltpu.make_async_copy(codes, codes_ref, sems.at[tiles]))
     for copy in copies:
         copy.start()
     for tile in range(tiles):
@@ -150,13 +152,21 @@
         for strip, at in enumerate((0, 3, 4, 7)):
             lines[tile * 4 + strip] = ring[at]
             lines[tiles * 4 + tile * 4 + strip] = flip_line(ring[at])
+    copies[tiles].wait()
     pick_lines(codes_ref, lines, picked, message_refs, tiles)
 
 
-def ring_kernel(codes_ref, ring_ref, w_ref, b_ref, *rest):
-    got_refs, message_refs, (own_ref, lines, picked, got) = rest[:4], rest[4:8], rest[8:]
-    got[0], got[1] = in_order(codes_ref[8, 0], got_refs[0], got_refs[1])
-    got[2], got[3] = in_order(codes_ref[8, 1], got_refs[2], got_refs[3])
+def ring_kernel(codes, odd_ref, ring_ref, w_ref, b_ref, *rest):
+    got_refs, message_refs, (own_ref, lines, picked, got, codes_ref, sem) = (
+        rest[:4],
+        rest[4:8],
+        rest[8:],
+    )
+    copy = pltpu.make_async_copy(codes, codes_ref, sem)
+    copy.start()
+    for axis in range(2):
+        first, second = got_refs[2 * axis], got_refs[2 * axis + 1]
+        got[2 * axis], got[2 * axis + 1] = in_order(odd_ref[axis : axis + 1], first, second)
     tiles = ring_ref.shape[0]
     side = ring_ref.shape[2]
     pads = [[got[k, pl.ds(t * side, side), :] for t in range(tiles)] for k in range(4)]
@@ -206,6 +216,7 @@
             own_ref[tile, edge] = line
             lines[tile * 4 + edge] = line
             lines[tiles * 4 + tile * 4 + edge] = flip_line(line)
+    copy.wait()
     pick_lines(codes_ref, lines, picked, message_refs, tiles)
 
 
@@ -299,9 +310,10 @@
         convolve_tile(padded, prepare, w_ref, b_ref[...], y, False, finish)
 
 
-def second_kernel(side, tiles, *refs):
+def second_kernel(side, tiles, first_tile, *refs):
     ring_ref, w_ref, b_ref = refs[:3]
-    fields, out_ref, strips, sums, padded, y, columns, result, sems = refs[-9:]
+    late = refs[3] if first_tile else None
+    fields, out_ref, strips, sums, kept, padded, y, columns, result, sems = refs[-10:]
     x_ref, h_ref = fields.at[0], fields.at[1]
     chan = fields.shape[-1]
     rows = lax.broadcasted_iota(jnp.int32, (16, chan), 0)
@@ -309,6 +321,14 @@
     size = side // blocks
     inner = pl.ds(16, side - 32)
     copies = []
+    if first_tile:
+        part = pl.ds(side - size, size)
+        copies.append(
+            pltpu.make_async_copy(
+                late, out_ref.at[first_tile - 1, part, inner], sems.at[len(tiles) * blocks]
+            )
+        )
+        copies[-1].start()
     for at_tile, tile in enumerate(tiles):
         columns[0] = ring_ref[tile, 2].astype(F32)
         columns[1] = ring_ref[tile, 3].astype(F32)
@@ -332,18 +352,24 @@
             line = total.astype(BF16)
             strips[tile, 0, row] = line[:16]
             strips[tile, 1, row] = line[side - 16 :]
-            result[at_tile, row] = line[16 : side - 16]
+            held = tile == tiles[-1] and row >= side - size
+            if held and first_tile and row == side - size:
+                copies.pop(0).wait()
+            if held:
+                kept[row - (side - size)] = line[16 : side - 16]
+            else:
+                result[at_tile, row] = line[16 : side - 16]
             if row == 0 or row == side - 1:
                 sums[tile, 0 if row == 0 else 1] = total
             sums[tile, 2, row : row + 1] = total[:1]
             sums[tile, 3, row : row + 1] = total[side - 1 :]
-            if (row + 1) % size == 0:
+            if (row + 1) % size == 0 and not held:
                 part = pl.ds(row + 1 - size, size)
                 copies.append(
                     pltpu.make_async_copy(
                         result.at[at_tile, part],
                         out_ref.at[tile, part, inner],
-                        sems.at[len(copies)],
+                        sems.at[at_tile * blocks + row // size],
                     )
                 )
                 copies[-1].start()
@@ -353,10 +379,20 @@
         copy.wait()
 
 
-def last_kernel(side, upper, lower, before, after, w_ref, old_strips, sums, *refs):
+def last_kernel(side, upper, lower, before, after, w_ref, old_strips, sums, late, *refs):
     out_ref, ends, strips, sems = refs[-4:]
     tiles, chan = sums.shape[0], sums.shape[3]
     split = tiles * side
+    count = late.shape[0] - 1
+    part = pl.ds(side - 1 - count, count)
+    copies = [
+        pltpu.make_async_copy(
+            late.at[pl.ds(0, count)],
+            out_ref.at[tiles - 1, part, pl.ds(16, side - 32)],
+            sems.at[4 * tiles],
+        )
+    ]
+    copies[-1].start()
     got = (upper, lower, before, after)
     groups = [got[2 + k % 2][pl.ds(split + k // 2 * CORNERS, CORNERS), :] for k in range(4)]
     corners = [group.astype(F32) for group in groups]
@@ -389,7 +425,6 @@
         )
     rows = lax.broadcasted_iota(jnp.int32, (side, chan), 0)
     few = lax.broadcasted_iota(jnp.int32, (16, chan), 0)
-    copies = []
     for tile in range(tiles):
         span = slice(tile * side, (tile + 1) * side)
         for edge in range(2):
@@ -402,7 +437,7 @@
             ends[tile, edge] = total.astype(BF16)
             copies.append(
                 pltpu.make_async_copy(
-                    ends.at[tile, edge], out_ref.at[tile, at], sems.at[len(copies)]
+                    ends.at[tile, edge], out_ref.at[tile, at], sems.at[len(copies) - 1]
                 )
             )
             copies[-1].start()
@@ -417,7 +452,7 @@
                 pltpu.make_async_copy(
                     strips.at[tile, edge - 2, inner],
                     out_ref.at[tile, inner, pl.ds(begin, 16)],
-                    sems.at[len(copies)],
+                    sems.at[len(copies) - 1],
                 )
             )
             copies[-1].start()
@@ -498,8 +533,11 @@
         b_first.reshape(1, chan),
         b_second.reshape(1, chan),
     )
+    odd_rows = jnp.broadcast_to(jnp.pad(odd, (0, 6))[:, None], (8, chan))
     odd = (odd[0] == 1, odd[1] == 1)
-    gathered, codes, odd, constants = lax.optimization_barrier((gathered, codes, odd, constants))
+    gathered, codes, odd, odd_rows, constants = lax.optimization_barrier(
+        (gathered, codes, odd, odd_rows, constants)
+    )
     w_one, w_two, w_pads, w_edges, b_one, b_two = constants
     pieces = gathered.reshape(devices, tiles, piece, chan)
 
@@ -507,18 +545,19 @@
     message_shape = jax.ShapeDtypeStruct((split + 2 * CORNERS, chan), BF16)
     line_shape = (tiles, 8, side, chan)
     fields_shape = jax.ShapeDtypeStruct((2,) + pieces.shape, BF16)
+    codes_scratch = pltpu.SMEM(codes.shape, jnp.int32)
     four = VMEM((4,) + message_shape.shape, BF16)
     lines_scratch = VMEM((8 * tiles, side, chan), BF16)
     fields, ring, *sends = pl.pallas_call(
         functools.partial(border_kernel, side),
-        in_specs=[smem_spec, hbm_spec],
+        in_specs=[hbm_spec, hbm_spec],
         out_specs=[vmem_spec] * 6,
         out_shape=[
             fields_shape,
             jax.ShapeDtypeStruct((tiles, 8, side, chan), BF16),
         ]
         + [message_shape] * 4,
-        scratch_shapes=[lines_scratch, four, pltpu.SemaphoreType.DMA((tiles,))],
+        scratch_shapes=[lines_scratch, four, codes_scratch, pltpu.SemaphoreType.DMA((tiles + 1,))],
         compiler_params=params,
         name="borders",
     )(codes, pieces)
@@ -568,38 +607,42 @@
     got, fields = halo(sends, [functools.partial(first, part) for part in halves])
     *sends, hidden_ring = pl.pallas_call(
         ring_kernel,
-        in_specs=[smem_spec] + [vmem_spec] * 7,
+        in_specs=[hbm_spec] + [vmem_spec] * 8,
         out_specs=[vmem_spec] * 5,
         out_shape=[message_shape] * 4 + [jax.ShapeDtypeStruct((tiles, 4, side, chan), BF16)],
-        scratch_shapes=[lines_scratch, four, four],
+        scratch_shapes=[lines_scratch, four, four, codes_scratch, pltpu.SemaphoreType.DMA],
         compiler_params=params,
         name="hidden_ring",
-    )(codes, ring, w_edges, b_one, *got)
+    )(codes, odd_rows, ring, w_edges, b_one, *got)
 
     result_specs = [vmem_spec, hbm_spec, vmem_spec, vmem_spec]
     strips_shape = jax.ShapeDtypeStruct((tiles, 2, side, 16, chan), BF16)
     sums_shape = jax.ShapeDtypeStruct((tiles, 4, side, chan), F32)
+    kept_shape = jax.ShapeDtypeStruct((side // blocks, side - 32, chan), BF16)
 
     def second(part, done):
-        done = done or fields
+        *done, late = done or (*fields, None)
+        late = [] if late is None else [late]
         return pl.pallas_call(
-            functools.partial(second_kernel, side, part),
-            in_specs=[vmem_spec] * 3 + result_specs[: len(done)],
-            out_specs=result_specs,
-            out_shape=[fields_shape, field_shape, strips_shape, sums_shape],
-            input_output_aliases={3 + i: i for i in range(len(done))},
+            functools.partial(second_kernel, side, part, part[0]),
+            in_specs=[vmem_spec] * (3 + len(late)) + result_specs[: len(done)],
+            out_specs=result_specs + [vmem_spec],
+            out_shape=[fields_shape, field_shape, strips_shape, sums_shape, kept_shape],
+            input_output_aliases={3 + len(late) + i: i for i in range(len(done))},
             scratch_shapes=[
                 field,
                 products,
                 VMEM((2, side, chan), F32),
                 VMEM((len(part), side, side - 32, chan), BF16),
-                pltpu.SemaphoreType.DMA((len(part) * blocks,)),
+                pltpu.SemaphoreType.DMA((len(part) * blocks + 1,)),
             ],
             compiler_params=params,
             name="second",
-        )(hidden_ring, w_two, b_two, *done)
-
-    got, (_, out, strips, sums) = halo(sends, [functools.partial(second, part) for part in halves])
+        )(hidden_ring, w_two, b_two, *late, *done)
+
+    got, (_, out, strips, sums, late) = halo(
+        sends, [functools.partial(second, part) for part in halves]
+    )
     pads = [
         jnp.where(flag, a, b)
         for flag, pair in ((odd_face, got[:2]), (odd_tile, got[2:]))
@@ -607,18 +650,18 @@
     ]
     return pl.pallas_call(
         functools.partial(last_kernel, side),
-        in_specs=[vmem_spec] * 7 + [hbm_spec],
+        in_specs=[vmem_spec] * 8 + [hbm_spec],
         out_specs=hbm_spec,
         out_shape=field_shape,
-        input_output_aliases={7: 0},
+        input_output_aliases={8: 0},
         scratch_shapes=[
             VMEM((tiles, 2, side, chan), BF16),
             VMEM(strips_shape.shape, BF16),
-            pltpu.SemaphoreType.DMA((4 * tiles,)),
+            pltpu.SemaphoreType.DMA((4 * tiles + 1,)),
         ],
         compiler_params=params,
         name="last",
-    )(*pads, w_pads, strips, sums, out)
+    )(*pads, w_pads, strips, sums, late, out)
 
 
 def solution(mesh):

time: 139 us -> 137 us (0.986)
  Pallas kernels: 27 us -> 25.2 us
    pallas_call x4, Pallas kernels: 13.7 us -> 11.9 us  [the longest x2 8.24 us: second(): pl.pallas_call(functools.partial(second_kernel, side, part, part[0]), in_...]
  transfers between devices with their start and end apart: 13 -> 13, of which waited for: 5 -> 6; matrix products, arithmetic and copies ran while one was open for 3% -> 3% of each run, Pallas kernels for 12% -> 11%
where the time goes in v8:
time: 137 us
  waiting for transfers between devices  83.5 us (61%)
  Pallas kernels  25.2 us (18%)
  starting transfers between devices  23 us (17%)
  local copies, waits for them, and re-layouts  4.22 us (3%)
    ppermute x2, waiting for transfers between devices, neighbours_along(): lax.ppermute(array, axis, [(i, (i + 1) % size) for i in range(size)])  59.4 us
    all_to_all x1, waiting for transfers between devices, shards(): lax.all_to_all(ordered, AXES, split_axis=0, concat_axis=0, tiled=True)  21.8 us
    pallas_call x2, Pallas kernels, second(): pl.pallas_call(functools.partial(second_kernel, side, part, part[0]), in_...  8.24 us
    ppermute x2, starting transfers between devices, neighbours_along(): lax.ppermute(array, axis, [(i, (i - 1) % size) for i in range(size)])  7.62 us
    all_to_all x1, starting transfers between devices, shards(): lax.all_to_all(ordered, AXES, split_axis=0, concat_axis=0, tiled=True)  7.43 us
    pallas_call x2, Pallas kernels, first(): pl.pallas_call(functools.partial(first_kernel, side, part), in_specs=[vme...  7.24 us
    ppermute x4, starting transfers between devices, swap_far(): return lax.ppermute(array, axis, pairs)  4.71 us
    pallas_call x1, Pallas kernels, shards(): pl.pallas_call(gather_kernel, in_specs=[smem_spec, hbm_spec], out_specs=h...  4.15 us
  transfers between devices with their start and end apart: 13, of which 6 were waited for; matrix products, arithmetic and copies ran while one was open for 3% of the time, Pallas kernels for 11%

profile of v8, /device:TPU:0, one launch (start us, length us, event | category | flops | bytes accessed | tf_op | source)
XLA Modules:
  0.0 137.0 jit_solution(4724899106231175718)
XLA Ops:
  0.0 4.2 %order.1 = bf16[128,128,128]{2,1,0:T(8,128)(2,1)} custom-call(s32[128]{0:T(128)} %order_ref.1, bf16[128,128,128]{2,1,0:T(8,128)(2,1)} %x_ref.1), custom_call_target="tpu_custom_call" | custom-call | tf_op jit(solution)/shard_map/order/pallas_call | solution.py:500
  4.2 7.4 %all-to-all-start = ((bf16[128,128,128]{2,1,0:T(8,128)(2,1)}), bf16[128,128,128]{2,1,0:T(8,128)(2,1)}, u32[]{:S(2)}, u32[]{:S(2)}) async-start(bf16[128,128,128]{2,1,0:T(8,128)(2,1)} %order.1), calls=%async_computation | async-start | bytes 8388608 | tf_op jit(solution)/shard_map/all_to_all | solution.py:513
  11.7 1.7 %collective-permute-start.1 = (s32[4,8]{1,0:T(4,128)S(1)}, s32[4,8]{1,0:T(4,128)S(1)}, u32[]{:S(2)}, u32[]{:S(2)}) collective-permute-start(s32[4,8]{1,0:T(4,128)S(1)} %fusion.8), channel_id=1, source_target_pairs={{0,8},{8,16},{16,24},{24,0},{1,9},{9,17},{17,25},{25,1},{2,10},{10... | collective-permute-start | bytes 392 | tf_op jit(solution)/shard_map/ppermute | solution.py:485
  13.4 1.2 collective-permute-start
  14.7 0.2 copy.36
  14.9 0.2 copy.40
  15.2 0.1 pad_bitcast_fusion.1
  15.3 0.1 pad_bitcast_fusion.3
  15.6 1.1 copy.43
  16.7 21.7 %collective-permute-done.1 = s32[4,8]{1,0:T(4,128)S(1)} collective-permute-done((s32[4,8]{1,0:T(4,128)S(1)}, s32[4,8]{1,0:T(4,128)S(1)}, u32[]{:S(2)}, u32[]{:S(2)}) %collective-permute-start.1) | collective-permute-done | bytes 160 | tf_op jit(solution)/shard_map/ppermute | solution.py:485
  38.5 0.1 copy.47
  38.6 1.1 copy.39
  39.7 0.1 copy.46
  39.9 6.4 %collective-permute-start.2 = (s32[3,4,8]{2,0,1:T(4,128)S(1)}, s32[3,4,8]{2,0,1:T(4,128)S(1)}, u32[]{:S(2)}, u32[]{:S(2)}) collective-permute-start(s32[3,4,8]{2,0,1:T(4,128)S(1)} %pad_add_fusion), channel_id=1, source_target_pairs={{0,7},{1,0},{2,1},{3,2},{4,3},{5,4},{6,5},{7,6},{8,15},{9,8},{10,9... | collective-permute-start | bytes 1160 | tf_op jit(solution)/shard_map/ppermute | solution.py:484
  46.4 37.7 %collective-permute-done.3 = s32[3,4,8]{2,0,1:T(4,128)S(1)} collective-permute-done((s32[3,4,8]{2,0,1:T(4,128)S(1)}, s32[3,4,8]{2,0,1:T(4,128)S(1)}, u32[]{:S(2)}, u32[]{:S(2)}) %collective-permute-start.3) | collective-permute-done | bytes 416 | tf_op jit(solution)/shard_map/ppermute | solution.py:485
  84.4 0.1 stack.73
  84.9 0.1 reduce_sum.22
  85.0 21.8 %all-to-all-done = bf16[128,128,128]{2,1,0:T(8,128)(2,1)} async-done(((bf16[128,128,128]{2,1,0:T(8,128)(2,1)}), bf16[128,128,128]{2,1,0:T(8,128)(2,1)}, u32[]{:S(2)}, u32[]{:S(2)}) %all-to-all-start) | async-done | bytes 4194336 | tf_op jit(solution)/shard_map/all_to_all | solution.py:513
  106.9 2.5 %borders.1 = (bf16[2,32,4,128,128]{4,3,2,1,0:T(8,128)(2,1)S(1)}, bf16[4,8,64,128]{3,2,1,0:T(8,128)(2,1)S(1)}, bf16[288,128]{1,0:T(8,128)(2,1)S(1)}, bf16[288,128...) custom-call(s32[9,32]{1,0:T(8,128)S(1)} %pad_add_fusion.1.codes, ...), custom_call_target="tpu_custom_call" | custom-call | tf_op jit(solution)/shard_map/borders/pallas_call | solution.py:551
  109.5 2.0 %collective-permute-start.5 = (bf16[288,128]{1,0:T(8,128)(2,1)S(1)}, bf16[288,128]{1,0:T(8,128)(2,1)S(1)}, u32[]{:S(2)}, u32[]{:S(2)}) collective-permute-start(bf16[288,128]{1,0:T(8,128)(2,1)S(1)} %get-tuple-element.63), channel_id=1, source_target_pairs={{0,24},{8,16},{16,8},{24,0},{1,25},{9,17},{17,9},{25,1},{2,26},{10... | collective-permute-start | bytes 221192 | tf_op jit(solution)/shard_map/ppermute | solution.py:475
  111.5 3.6 %first.2.refs_2_ = bf16[2,32,4,128,128]{4,3,2,1,0:T(8,128)(2,1)S(1)} custom-call(bf16[512,768]{1,0:T(8,128)(2,1)S(1)} %bitcast.37, f32[1,128]{1,0:T(1,128)S(1)} %bitcast.42, bf16[2,32,4,128,128]{4,3,2,1,0:T(8,128)(2,1)S(1)} %get-tuple-element.65.refs_2_), custom_call_target="tpu_custom_call", output_to_operand_aliasing={{}: (2, {})} | custom-call | tf_op jit(solution)/shard_map/first/pallas_call | solution.py:572
  115.1 0.4 collective-permute-done.5.rest_1_
  115.7 3.6 %first.3.refs_3_ = bf16[2,32,4,128,128]{4,3,2,1,0:T(8,128)(2,1)S(1)} custom-call(bf16[512,768]{1,0:T(8,128)(2,1)S(1)} %bitcast.38, f32[1,128]{1,0:T(1,128)S(1)} %bitcast.43, bf16[2,32,4,128,128]{4,3,2,1,0:T(8,128)(2,1)S(1)} %first.2.refs_2_), custom_call_target="tpu_custom_call", output_to_operand_aliasing={{}: (2, {})} | custom-call | tf_op jit(solution)/shard_map/first/pallas_call | solution.py:572
  119.4 1.8 %collective-permute-done.6.rest_3_ = bf16[288,128]{1,0:T(8,128)(2,1)S(1)} collective-permute-done((bf16[288,128]{1,0:T(8,128)(2,1)S(1)}, bf16[288,128]{1,0:T(8,128)(2,1)S(1)}, u32[]{:S(2)}, u32[]{:S(2)}) %collective-permute-start.6) | collective-permute-done | bytes 73760 | tf_op jit(solution)/shard_map/ppermute | solution.py:475
  121.2 1.1 hidden_ring.1
  122.3 1.3 collective-permute-start.8
  123.6 1.4 %collective-permute-start.9 = (bf16[288,128]{1,0:T(8,128)(2,1)S(1)}, bf16[288,128]{1,0:T(8,128)(2,1)S(1)}, u32[]{:S(2)}, u32[]{:S(2)}) collective-permute-start(bf16[288,128]{1,0:T(8,128)(2,1)S(1)} %get-tuple-element.75), channel_id=1, source_target_pairs={{0,24},{8,16},{16,8},{24,0},{1,25},{9,17},{17,9},{25,1},{2,26},{10... | collective-permute-start | bytes 221192 | tf_op jit(solution)/shard_map/ppermute | solution.py:475
  125.1 4.0 %second.2 = (bf16[2,32,4,128,128]{4,3,2,1,0:T(8,128)(2,1)S(1)}, bf16[4,64,64,128]{3,2,1,0:T(8,128)(2,1)}, bf16[4,2,64,16,128]{4,3,2,1,0:T(8,128)(2,1)S(1)}, f32[...) custom-call(bf16[4,4,64,128]{3,2,1,0:T(8,128)(2,1)S(1)} %get-tuple-element.76.refs_0_, ...), custom_call_target="tpu_custom_call", output_to_operand_aliasing={{0}: (3, {})} | custom-call | tf_op jit(solution)/shard_map/second/pallas_call | solution.py:626
  129.1 1.2 collective-permute-start.10
  130.4 4.2 %second.3 = (bf16[2,32,4,128,128]{4,3,2,1,0:T(8,128)(2,1)S(1)}, bf16[4,64,64,128]{3,2,1,0:T(8,128)(2,1)}, bf16[4,2,64,16,128]{4,3,2,1,0:T(8,128)(2,1)S(1)}, f32[...) custom-call(bf16[4,4,64,128]{3,2,1,0:T(8,128)(2,1)S(1)} %get-tuple-e, ...), custom_call_target="tpu_custom_call", output_to_operand_aliasing={{0}: (4, {}), {1}: (5, {}), {2}: (6, {}), {3}: (7, {})} | custom-call | tf_op jit(solution)/shard_map/second/pallas_call | solution.py:626
  134.6 0.1 collective-permute-done.10
  134.8 2.0 %last.1 = bf16[4,64,64,128]{3,2,1,0:T(8,128)(2,1)} custom-call(bf16[288,128]{1,0:T(8,128)(2,1)S(1)} %get-tuple-element.122.upper, bf16[288,128]{1,0:T(8,128)(2,1)S(1)} %get-tuple-element.121.lower, bf16[288,128]{1,0:T(8,128)(2,1)S(1)} %get-tuple-element.118.before, bf16[288,128]{1,0:T(8,128)(2,1)S(1)} %get-tuple-element.117.after, ...), custom_call_target="tpu_custom_call", output_to_operand_aliasing={{}: (8, {})} | custom-call | tf_op jit(solution)/shard_map/last/pallas_call | solution.py:651
  (70 shorter events, 1.6 us)
Async XLA Ops:
  4.2 7.5 %copy-start.4 = (s32[4,8]{1,0:T(4,128)S(1)}, s32[4,8]{1,0:T(4,128)}, u32[]{:S(2)}) copy-start(s32[4,8]{1,0:T(4,128)} %param.13) | copy-start | bytes 388
  4.2 7.5 %copy-start.5 = (s32[4,8]{1,0:T(4,128)S(1)}, s32[4,8]{1,0:T(4,128)}, u32[]{:S(2)}) copy-start(s32[4,8]{1,0:T(4,128)} %param.12) | copy-start | bytes 388
  4.2 10.5 %copy-start.1 = (bf16[3,3,128,128]{3,2,1,0:T(8,128)(2,1)S(1)}, bf16[3,3,128,128]{3,2,1,0:T(8,128)(2,1)}, u32[]{:S(2)}) copy-start(bf16[3,3,128,128]{3,2,1,0:T(8,128)(2,1)} %param.14) | copy-start | bytes 884740
  4.2 10.7 %copy-start = (bf16[3,3,128,128]{3,2,1,0:T(8,128)(2,1)S(1)}, bf16[3,3,128,128]{3,2,1,0:T(8,128)(2,1)}, u32[]{:S(2)}) copy-start(bf16[3,3,128,128]{3,2,1,0:T(8,128)(2,1)} %w_ref) | copy-start | bytes 884740
  4.2 102.6 %all-to-all-start = ((bf16[128,128,128]{2,1,0:T(8,128)(2,1)}), bf16[128,128,128]{2,1,0:T(8,128)(2,1)}, u32[]{:S(2)}, u32[]{:S(2)}) async-start(bf16[128,128,128]{2,1,0:T(8,128)(2,1)} %order.1), calls=%async_computation | async-start | bytes 8388608 | tf_op jit(solution)/shard_map/all_to_all | solution.py:513
  11.7 26.7 %collective-permute-start.1 = (s32[4,8]{1,0:T(4,128)S(1)}, s32[4,8]{1,0:T(4,128)S(1)}, u32[]{:S(2)}, u32[]{:S(2)}) collective-permute-start(s32[4,8]{1,0:T(4,128)S(1)} %fusion.8), channel_id=1, source_target_pairs={{0,8},{8,16},{16,24},{24,0},{1,9},{9,17},{17,25},{25,1},{2,10},{10... | collective-permute-start | bytes 392 | tf_op jit(solution)/shard_map/ppermute | solution.py:485
  13.4 25.0 %collective-permute-start = (s32[4,8]{1,0:T(4,128)S(1)}, s32[4,8]{1,0:T(4,128)S(1)}, u32[]{:S(2)}, u32[]{:S(2)}) collective-permute-start(s32[4,8]{1,0:T(4,128)S(1)} %fusion.8), channel_id=1, source_target_pairs={{0,24},{8,0},{16,8},{24,16},{1,25},{9,1},{17,9},{25,17},{2,26},{10... | collective-permute-start | bytes 392 | tf_op jit(solution)/shard_map/ppermute | solution.py:484
  15.5 69.2 %copy-start.6 = (s32[8,4]{0,1:T(4,128)S(1)}, s32[8,4]{0,1:T(4,128)}, u32[]{:S(2)}) copy-start(s32[8,4]{0,1:T(4,128)} %constant.69.clone) | copy-start | bytes 388
  15.5 69.2 %copy-start.7 = (s32[8,4]{0,1:T(4,128)S(1)}, s32[8,4]{0,1:T(4,128)}, u32[]{:S(2)}) copy-start(s32[8,4]{0,1:T(4,128)} %constant.68.clone) | copy-start | bytes 388
  38.4 45.7 %collective-permute-start.3 = (s32[3,4,8]{2,0,1:T(4,128)S(1)}, s32[3,4,8]{2,0,1:T(4,128)S(1)}, u32[]{:S(2)}, u32[]{:S(2)}) collective-permute-start(s32[3,4,8]{2,0,1:T(4,128)S(1)} %pad_add_fusion), channel_id=1, source_target_pairs={{0,1},{1,2},{2,3},{3,4},{4,5},{5,6},{6,7},{7,0},{8,9},{9,10},{10,1... | collective-permute-start | bytes 1160 | tf_op jit(solution)/shard_map/ppermute | solution.py:485
  38.6 72.9 %copy-start.2 = (f32[128]{0:T(128)S(1)}, f32[128]{0:T(128)}, u32[]{:S(2)}) copy-start(f32[128]{0:T(128)} %param.15) | copy-start | bytes 1540
  39.9 44.5 %collective-permute-start.2 = (s32[3,4,8]{2,0,1:T(4,128)S(1)}, s32[3,4,8]{2,0,1:T(4,128)S(1)}, u32[]{:S(2)}, u32[]{:S(2)}) collective-permute-start(s32[3,4,8]{2,0,1:T(4,128)S(1)} %pad_add_fusion), channel_id=1, source_target_pairs={{0,7},{1,0},{2,1},{3,2},{4,3},{5,4},{6,5},{7,6},{8,15},{9,8},{10,9... | collective-permute-start | bytes 1160 | tf_op jit(solution)/shard_map/ppermute | solution.py:484
  109.4 5.7 %collective-permute-start.4 = (bf16[288,128]{1,0:T(8,128)(2,1)S(1)}, bf16[288,128]{1,0:T(8,128)(2,1)S(1)}, u32[]{:S(2)}, u32[]{:S(2)}) collective-permute-start(bf16[288,128]{1,0:T(8,128)(2,1)S(1)} %get-tuple-element.62), channel_id=1, source_target_pairs={{0,8},{8,0},{16,24},{24,16},{1,9},{9,1},{17,25},{25,17},{2,10},{10... | collective-permute-start | bytes 221192 | tf_op jit(solution)/shard_map/ppermute | solution.py:479
  109.5 6.0 %collective-permute-start.5 = (bf16[288,128]{1,0:T(8,128)(2,1)S(1)}, bf16[288,128]{1,0:T(8,128)(2,1)S(1)}, u32[]{:S(2)}, u32[]{:S(2)}) collective-permute-start(bf16[288,128]{1,0:T(8,128)(2,1)S(1)} %get-tuple-element.63), channel_id=1, source_target_pairs={{0,24},{8,16},{16,8},{24,0},{1,25},{9,17},{17,9},{25,1},{2,26},{10... | collective-permute-start | bytes 221192 | tf_op jit(solution)/shard_map/ppermute | solution.py:475
  115.6 5.6 %collective-permute-start.6 = (bf16[288,128]{1,0:T(8,128)(2,1)S(1)}, bf16[288,128]{1,0:T(8,128)(2,1)S(1)}, u32[]{:S(2)}, u32[]{:S(2)}) collective-permute-start(bf16[288,128]{1,0:T(8,128)(2,1)S(1)} %pad_maximum_fusion.2), channel_id=1, source_target_pairs={{0,7},{1,2},{2,1},{3,4},{4,3},{5,6},{6,5},{7,0},{8,15},{9,10},{10,... | collective-permute-start | bytes 221192 | tf_op jit(solution)/shard_map/ppermute | solution.py:475
  115.6 9.4 %copy-start.3 = (f32[128]{0:T(128)S(1)}, f32[128]{0:T(128)}, u32[]{:S(2)}) copy-start(f32[128]{0:T(128)} %param.17) | copy-start | bytes 1540
  115.7 5.5 %collective-permute-start.7 = (bf16[288,128]{1,0:T(8,128)(2,1)S(1)}, bf16[288,128]{1,0:T(8,128)(2,1)S(1)}, u32[]{:S(2)}, u32[]{:S(2)}) collective-permute-start(bf16[288,128]{1,0:T(8,128)(2,1)S(1)} %pad_maximum_fusion.3), channel_id=1, source_target_pairs={{0,1},{1,0},{2,3},{3,2},{4,5},{5,4},{6,7},{7,6},{8,9},{9,8},{10,11... | collective-permute-start | bytes 221192 | tf_op jit(solution)/shard_map/ppermute | solution.py:479
  122.3 6.8 %collective-permute-start.8 = (bf16[288,128]{1,0:T(8,128)(2,1)S(1)}, bf16[288,128]{1,0:T(8,128)(2,1)S(1)}, u32[]{:S(2)}, u32[]{:S(2)}) collective-permute-start(bf16[288,128]{1,0:T(8,128)(2,1)S(1)} %get-tuple-element.74), channel_id=1, source_target_pairs={{0,8},{8,0},{16,24},{24,16},{1,9},{9,1},{17,25},{25,17},{2,10},{10... | collective-permute-start | bytes 221192 | tf_op jit(solution)/shard_map/ppermute | solution.py:479
  123.6 5.5 %collective-permute-start.9 = (bf16[288,128]{1,0:T(8,128)(2,1)S(1)}, bf16[288,128]{1,0:T(8,128)(2,1)S(1)}, u32[]{:S(2)}, u32[]{:S(2)}) collective-permute-start(bf16[288,128]{1,0:T(8,128)(2,1)S(1)} %get-tuple-element.75), channel_id=1, source_target_pairs={{0,24},{8,16},{16,8},{24,0},{1,25},{9,17},{17,9},{25,1},{2,26},{10... | collective-permute-start | bytes 221192 | tf_op jit(solution)/shard_map/ppermute | solution.py:475
  129.1 5.6 %collective-permute-start.10 = (bf16[288,128]{1,0:T(8,128)(2,1)S(1)}, bf16[288,128]{1,0:T(8,128)(2,1)S(1)}, u32[]{:S(2)}, u32[]{:S(2)}) collective-permute-start(bf16[288,128]{1,0:T(8,128)(2,1)S(1)} %pad_maximum_fusion.4), channel_id=1, source_target_pairs={{0,7},{1,2},{2,1},{3,4},{4,3},{5,6},{6,5},{7,0},{8,15},{9,10},{10,... | collective-permute-start | bytes 221192 | tf_op jit(solution)/shard_map/ppermute | solution.py:475
  130.4 4.4 %collective-permute-start.11 = (bf16[288,128]{1,0:T(8,128)(2,1)S(1)}, bf16[288,128]{1,0:T(8,128)(2,1)S(1)}, u32[]{:S(2)}, u32[]{:S(2)}) collective-permute-start(bf16[288,128]{1,0:T(8,128)(2,1)S(1)} %pad_maximum_fusion.5), channel_id=1, source_target_pairs={{0,1},{1,0},{2,3},{3,2},{4,5},{5,4},{6,7},{7,6},{8,9},{9,8},{10,11... | collective-permute-start | bytes 221192 | tf_op jit(solution)/shard_map/ppermute | solution.py:479

commit v9 on v8

--- a/solution.py
+++ b/solution.py
@@ -319,10 +319,11 @@
     rows = lax.broadcasted_iota(jnp.int32, (16, chan), 0)
     blocks = y.shape[0]
     size = side // blocks
+    hold = kept.shape[0]
     inner = pl.ds(16, side - 32)
     copies = []
     if first_tile:
-        part = pl.ds(side - size, size)
+        part = pl.ds(side - hold, hold)
         copies.append(
             pltpu.make_async_copy(
                 late, out_ref.at[first_tile - 1, part, inner], sems.at[len(tiles) * blocks]
@@ -352,11 +353,9 @@
             line = total.astype(BF16)
             strips[tile, 0, row] = line[:16]
             strips[tile, 1, row] = line[side - 16 :]
-            held = tile == tiles[-1] and row >= side - size
-            if held and first_tile and row == side - size:
-                copies.pop(0).wait()
+            held = tile == tiles[-1] and row >= side - hold
             if held:
-                kept[row - (side - size)] = line[16 : side - 16]
+                kept[row - (side - hold)] = line[16 : side - 16]
             else:
                 result[at_tile, row] = line[16 : side - 16]
             if row == 0 or row == side - 1:
@@ -397,9 +396,9 @@
     groups = [got[2 + k % 2][pl.ds(split + k // 2 * CORNERS, CORNERS), :] for k in range(4)]
     corners = [group.astype(F32) for group in groups]
     zero = jnp.zeros((1, chan), F32)
-    added = []
+    added = {}
     weights = (w_ref[0], w_ref[2], w_ref[:, 0], w_ref[:, 2])
-    for edge in range(4):
+    for edge in (2, 3, 0, 1):
         stacked = []
         for tile in range(tiles):
             line = got[edge][pl.ds(tile * side, side), :]
@@ -416,43 +415,42 @@
                     axis=1,
                 )
             )
-        added.append(
-            jnp.dot(
-                jnp.concatenate(stacked, axis=0),
-                weights[edge].reshape(3 * chan, chan),
-                preferred_element_type=F32,
-            )
+        added[edge] = jnp.dot(
+            jnp.concatenate(stacked, axis=0),
+            weights[edge].reshape(3 * chan, chan),
+            preferred_element_type=F32,
         )
     rows = lax.broadcasted_iota(jnp.int32, (side, chan), 0)
     few = lax.broadcasted_iota(jnp.int32, (16, chan), 0)
+    spans = [slice(tile * side, (tile + 1) * side) for tile in range(tiles)]
+    inner = pl.ds(1, side - 2)
     for tile in range(tiles):
-        span = slice(tile * side, (tile + 1) * side)
+        for edge, begin, place in ((2, 0, 0), (3, side - 16, 15)):
+            column = sums[tile, edge] + added[edge][spans[tile]]
+            for row in range(1, side - 1):
+                old = old_strips[tile, edge - 2, row].astype(F32)
+                new = jnp.where(few == place, column[row : row + 1], old)
+                strips[tile, edge - 2, row] = new.astype(BF16)
+            copies.append(
+                pltpu.make_async_copy(
+                    strips.at[tile, edge - 2, inner],
+                    out_ref.at[tile, inner, pl.ds(begin, 16)],
+                    sems.at[len(copies) - 1],
+                )
+            )
+            copies[-1].start()
+    for tile in range(tiles):
         for edge in range(2):
-            total = sums[tile, edge] + added[edge][span]
+            total = sums[tile, edge] + added[edge][spans[tile]]
             at = 0 if edge == 0 else side - 1
-            left = added[2][span][at : at + 1]
-            right = added[3][span][at : at + 1]
+            left = added[2][spans[tile]][at : at + 1]
+            right = added[3][spans[tile]][at : at + 1]
             total = total + jnp.where(rows == 0, left, 0.0)
             total = total + jnp.where(rows == side - 1, right, 0.0)
             ends[tile, edge] = total.astype(BF16)
             copies.append(
                 pltpu.make_async_copy(
                     ends.at[tile, edge], out_ref.at[tile, at], sems.at[len(copies) - 1]
-                )
-            )
-            copies[-1].start()
-        for edge, begin, place in ((2, 0, 0), (3, side - 16, 15)):
-            column = sums[tile, edge] + added[edge][span]
-            for row in range(1, side - 1):
-                old = old_strips[tile, edge - 2, row].astype(F32)
-                new = jnp.where(few == place, column[row : row + 1], old)
-                strips[tile, edge - 2, row] = new.astype(BF16)
-            inner = pl.ds(1, side - 2)
-            copies.append(
-                pltpu.make_async_copy(
-                    strips.at[tile, edge - 2, inner],
-                    out_ref.at[tile, inner, pl.ds(begin, 16)],
-                    sems.at[len(copies) - 1],
                 )
             )
             copies[-1].start()
@@ -618,7 +616,7 @@
     result_specs = [vmem_spec, hbm_spec, vmem_spec, vmem_spec]
     strips_shape = jax.ShapeDtypeStruct((tiles, 2, side, 16, chan), BF16)
     sums_shape = jax.ShapeDtypeStruct((tiles, 4, side, chan), F32)
-    kept_shape = jax.ShapeDtypeStruct((side // blocks, side - 32, chan), BF16)
+    kept_shape = jax.ShapeDtypeStruct((2 * (side // blocks), side - 32, chan), BF16)
 
     def second(part, done):
         *done, late = done or (*fields, None)

time: 137 us -> 137 us (level)
  transfers between devices with their start and end apart: 13 -> 13, of which waited for: 6 -> 7; matrix products, arithmetic and copies ran while one was open for 3% -> 3% of each run, Pallas kernels for 11% -> 11%
where the time goes in v9:
time: 137 us
  waiting for transfers between devices  84 us (61%)
  Pallas kernels  24.4 us (18%)
  starting transfers between devices  23 us (17%)
  local copies, waits for them, and re-layouts  4.22 us (3%)
    ppermute x2, waiting for transfers between devices, neighbours_along(): lax.ppermute(array, axis, [(i, (i + 1) % size) for i in range(size)])  59.4 us
    all_to_all x1, waiting for transfers between devices, shards(): lax.all_to_all(ordered, AXES, split_axis=0, concat_axis=0, tiled=True)  21.8 us
    ppermute x2, starting transfers between devices, neighbours_along(): lax.ppermute(array, axis, [(i, (i - 1) % size) for i in range(size)])  7.62 us
    pallas_call x2, Pallas kernels, second(): pl.pallas_call(functools.partial(second_kernel, side, part, part[0]), in_...  7.51 us
    all_to_all x1, starting transfers between devices, shards(): lax.all_to_all(ordered, AXES, split_axis=0, concat_axis=0, tiled=True)  7.43 us
    pallas_call x2, Pallas kernels, first(): pl.pallas_call(functools.partial(first_kernel, side, part), in_specs=[vme...  7.24 us
    ppermute x4, starting transfers between devices, swap_far(): return lax.ppermute(array, axis, pairs)  4.71 us
    pallas_call x1, Pallas kernels, shards(): pl.pallas_call(gather_kernel, in_specs=[smem_spec, hbm_spec], out_specs=h...  4.15 us
  transfers between devices with their start and end apart: 13, of which 7 were waited for; matrix products, arithmetic and copies ran while one was open for 3% of the time, Pallas kernels for 11%

profile of v9, /device:TPU:0, one launch (start us, length us, event | category | flops | bytes accessed | tf_op | source)
XLA Modules:
  0.0 136.6 jit_solution(12010875784079386443)
XLA Ops:
  0.0 4.2 %order.1 = bf16[128,128,128]{2,1,0:T(8,128)(2,1)} custom-call(s32[128]{0:T(128)} %order_ref.1, bf16[128,128,128]{2,1,0:T(8,128)(2,1)} %x_ref.1), custom_call_target="tpu_custom_call" | custom-call | tf_op jit(solution)/shard_map/order/pallas_call | solution.py:498
  4.2 7.4 %all-to-all-start = ((bf16[128,128,128]{2,1,0:T(8,128)(2,1)}), bf16[128,128,128]{2,1,0:T(8,128)(2,1)}, u32[]{:S(2)}, u32[]{:S(2)}) async-start(bf16[128,128,128]{2,1,0:T(8,128)(2,1)} %order.1), calls=%async_computation | async-start | bytes 8388608 | tf_op jit(solution)/shard_map/all_to_all | solution.py:511
  11.7 1.7 %collective-permute-start.1 = (s32[4,8]{1,0:T(4,128)S(1)}, s32[4,8]{1,0:T(4,128)S(1)}, u32[]{:S(2)}, u32[]{:S(2)}) collective-permute-start(s32[4,8]{1,0:T(4,128)S(1)} %fusion.8), channel_id=1, source_target_pairs={{0,8},{8,16},{16,24},{24,0},{1,9},{9,17},{17,25},{25,1},{2,10},{10... | collective-permute-start | bytes 392 | tf_op jit(solution)/shard_map/ppermute | solution.py:483
  13.4 1.2 collective-permute-start
  14.7 0.2 copy.36
  14.9 0.2 copy.40
  15.2 0.1 pad_bitcast_fusion.1
  15.3 0.1 pad_bitcast_fusion.3
  15.6 1.1 copy.43
  16.7 21.7 %collective-permute-done.1 = s32[4,8]{1,0:T(4,128)S(1)} collective-permute-done((s32[4,8]{1,0:T(4,128)S(1)}, s32[4,8]{1,0:T(4,128)S(1)}, u32[]{:S(2)}, u32[]{:S(2)}) %collective-permute-start.1) | collective-permute-done | bytes 160 | tf_op jit(solution)/shard_map/ppermute | solution.py:483
  38.5 0.1 copy.47
  38.6 1.1 copy.39
  39.7 0.1 copy.46
  39.9 6.4 %collective-permute-start.2 = (s32[3,4,8]{2,0,1:T(4,128)S(1)}, s32[3,4,8]{2,0,1:T(4,128)S(1)}, u32[]{:S(2)}, u32[]{:S(2)}) collective-permute-start(s32[3,4,8]{2,0,1:T(4,128)S(1)} %pad_add_fusion), channel_id=1, source_target_pairs={{0,7},{1,0},{2,1},{3,2},{4,3},{5,4},{6,5},{7,6},{8,15},{9,8},{10,9... | collective-permute-start | bytes 1160 | tf_op jit(solution)/shard_map/ppermute | solution.py:482
  46.4 37.7 %collective-permute-done.3 = s32[3,4,8]{2,0,1:T(4,128)S(1)} collective-permute-done((s32[3,4,8]{2,0,1:T(4,128)S(1)}, s32[3,4,8]{2,0,1:T(4,128)S(1)}, u32[]{:S(2)}, u32[]{:S(2)}) %collective-permute-start.3) | collective-permute-done | bytes 416 | tf_op jit(solution)/shard_map/ppermute | solution.py:483
  84.4 0.1 stack.73
  85.0 21.8 %all-to-all-done = bf16[128,128,128]{2,1,0:T(8,128)(2,1)} async-done(((bf16[128,128,128]{2,1,0:T(8,128)(2,1)}), bf16[128,128,128]{2,1,0:T(8,128)(2,1)}, u32[]{:S(2)}, u32[]{:S(2)}) %all-to-all-start) | async-done | bytes 4194336 | tf_op jit(solution)/shard_map/all_to_all | solution.py:511
  106.9 2.5 %borders.1 = (bf16[2,32,4,128,128]{4,3,2,1,0:T(8,128)(2,1)S(1)}, bf16[4,8,64,128]{3,2,1,0:T(8,128)(2,1)S(1)}, bf16[288,128]{1,0:T(8,128)(2,1)S(1)}, bf16[288,128...) custom-call(s32[9,32]{1,0:T(8,128)S(1)} %pad_add_fusion.1.codes, ...), custom_call_target="tpu_custom_call" | custom-call | tf_op jit(solution)/shard_map/borders/pallas_call | solution.py:549
  109.5 2.0 %collective-permute-start.5 = (bf16[288,128]{1,0:T(8,128)(2,1)S(1)}, bf16[288,128]{1,0:T(8,128)(2,1)S(1)}, u32[]{:S(2)}, u32[]{:S(2)}) collective-permute-start(bf16[288,128]{1,0:T(8,128)(2,1)S(1)} %get-tuple-element.63), channel_id=1, source_target_pairs={{0,24},{8,16},{16,8},{24,0},{1,25},{9,17},{17,9},{25,1},{2,26},{10... | collective-permute-start | bytes 221192 | tf_op jit(solution)/shard_map/ppermute | solution.py:473
  111.5 3.6 %first.2.refs_2_ = bf16[2,32,4,128,128]{4,3,2,1,0:T(8,128)(2,1)S(1)} custom-call(bf16[512,768]{1,0:T(8,128)(2,1)S(1)} %bitcast.37, f32[1,128]{1,0:T(1,128)S(1)} %bitcast.42, bf16[2,32,4,128,128]{4,3,2,1,0:T(8,128)(2,1)S(1)} %get-tuple-element.65.refs_2_), custom_call_target="tpu_custom_call", output_to_operand_aliasing={{}: (2, {})} | custom-call | tf_op jit(solution)/shard_map/first/pallas_call | solution.py:570
  115.1 0.4 collective-permute-done.5.rest_1_
  115.7 3.6 %first.3.refs_3_ = bf16[2,32,4,128,128]{4,3,2,1,0:T(8,128)(2,1)S(1)} custom-call(bf16[512,768]{1,0:T(8,128)(2,1)S(1)} %bitcast.38, f32[1,128]{1,0:T(1,128)S(1)} %bitcast.43, bf16[2,32,4,128,128]{4,3,2,1,0:T(8,128)(2,1)S(1)} %first.2.refs_2_), custom_call_target="tpu_custom_call", output_to_operand_aliasing={{}: (2, {})} | custom-call | tf_op jit(solution)/shard_map/first/pallas_call | solution.py:570
  119.4 1.8 %collective-permute-done.6.rest_3_ = bf16[288,128]{1,0:T(8,128)(2,1)S(1)} collective-permute-done((bf16[288,128]{1,0:T(8,128)(2,1)S(1)}, bf16[288,128]{1,0:T(8,128)(2,1)S(1)}, u32[]{:S(2)}, u32[]{:S(2)}) %collective-permute-start.6) | collective-permute-done | bytes 73760 | tf_op jit(solution)/shard_map/ppermute | solution.py:473
  121.2 1.1 hidden_ring.1
  122.3 1.3 collective-permute-start.8
  123.6 1.4 %collective-permute-start.9 = (bf16[288,128]{1,0:T(8,128)(2,1)S(1)}, bf16[288,128]{1,0:T(8,128)(2,1)S(1)}, u32[]{:S(2)}, u32[]{:S(2)}) collective-permute-start(bf16[288,128]{1,0:T(8,128)(2,1)S(1)} %get-tuple-element.75), channel_id=1, source_target_pairs={{0,24},{8,16},{16,8},{24,0},{1,25},{9,17},{17,9},{25,1},{2,26},{10... | collective-permute-start | bytes 221192 | tf_op jit(solution)/shard_map/ppermute | solution.py:473
  125.1 3.6 %second.2 = (bf16[2,32,4,128,128]{4,3,2,1,0:T(8,128)(2,1)S(1)}, bf16[4,64,64,128]{3,2,1,0:T(8,128)(2,1)}, bf16[4,2,64,16,128]{4,3,2,1,0:T(8,128)(2,1)S(1)}, f32[...) custom-call(bf16[4,4,64,128]{3,2,1,0:T(8,128)(2,1)S(1)} %get-tuple-element.76.refs_0_, ...), custom_call_target="tpu_custom_call", output_to_operand_aliasing={{0}: (3, {})} | custom-call | tf_op jit(solution)/shard_map/second/pallas_call | solution.py:624
  128.7 0.1 collective-permute-done.9
  128.9 1.2 collective-permute-start.10
  130.1 3.9 %second.3 = (bf16[2,32,4,128,128]{4,3,2,1,0:T(8,128)(2,1)S(1)}, bf16[4,64,64,128]{3,2,1,0:T(8,128)(2,1)}, bf16[4,2,64,16,128]{4,3,2,1,0:T(8,128)(2,1)S(1)}, f32[...) custom-call(bf16[4,4,64,128]{3,2,1,0:T(8,128)(2,1)S(1)} %get-tuple-e, ...), custom_call_target="tpu_custom_call", output_to_operand_aliasing={{0}: (4, {}), {1}: (5, {}), {2}: (6, {}), {3}: (7, {})} | custom-call | tf_op jit(solution)/shard_map/second/pallas_call | solution.py:624
  134.0 0.5 collective-permute-done.10
  134.5 1.9 %last.1 = bf16[4,64,64,128]{3,2,1,0:T(8,128)(2,1)} custom-call(bf16[288,128]{1,0:T(8,128)(2,1)S(1)} %get-tuple-element.122.upper, bf16[288,128]{1,0:T(8,128)(2,1)S(1)} %get-tuple-element.121.lower, bf16[288,128]{1,0:T(8,128)(2,1)S(1)} %get-tuple-element.118.before, bf16[288,128]{1,0:T(8,128)(2,1)S(1)} %get-tuple-element.117.after, ...), custom_call_target="tpu_custom_call", output_to_operand_aliasing={{}: (8, {})} | custom-call | tf_op jit(solution)/shard_map/last/pallas_call | solution.py:649
  (70 shorter events, 1.7 us)
Async XLA Ops:
  4.2 7.5 %copy-start.4 = (s32[4,8]{1,0:T(4,128)S(1)}, s32[4,8]{1,0:T(4,128)}, u32[]{:S(2)}) copy-start(s32[4,8]{1,0:T(4,128)} %param.13) | copy-start | bytes 388
  4.2 7.5 %copy-start.5 = (s32[4,8]{1,0:T(4,128)S(1)}, s32[4,8]{1,0:T(4,128)}, u32[]{:S(2)}) copy-start(s32[4,8]{1,0:T(4,128)} %param.12) | copy-start | bytes 388
  4.2 10.5 %copy-start.1 = (bf16[3,3,128,128]{3,2,1,0:T(8,128)(2,1)S(1)}, bf16[3,3,128,128]{3,2,1,0:T(8,128)(2,1)}, u32[]{:S(2)}) copy-start(bf16[3,3,128,128]{3,2,1,0:T(8,128)(2,1)} %param.14) | copy-start | bytes 884740
  4.2 10.7 %copy-start = (bf16[3,3,128,128]{3,2,1,0:T(8,128)(2,1)S(1)}, bf16[3,3,128,128]{3,2,1,0:T(8,128)(2,1)}, u32[]{:S(2)}) copy-start(bf16[3,3,128,128]{3,2,1,0:T(8,128)(2,1)} %w_ref) | copy-start | bytes 884740
  4.2 102.6 %all-to-all-start = ((bf16[128,128,128]{2,1,0:T(8,128)(2,1)}), bf16[128,128,128]{2,1,0:T(8,128)(2,1)}, u32[]{:S(2)}, u32[]{:S(2)}) async-start(bf16[128,128,128]{2,1,0:T(8,128)(2,1)} %order.1), calls=%async_computation | async-start | bytes 8388608 | tf_op jit(solution)/shard_map/all_to_all | solution.py:511
  11.7 26.7 %collective-permute-start.1 = (s32[4,8]{1,0:T(4,128)S(1)}, s32[4,8]{1,0:T(4,128)S(1)}, u32[]{:S(2)}, u32[]{:S(2)}) collective-permute-start(s32[4,8]{1,0:T(4,128)S(1)} %fusion.8), channel_id=1, source_target_pairs={{0,8},{8,16},{16,24},{24,0},{1,9},{9,17},{17,25},{25,1},{2,10},{10... | collective-permute-start | bytes 392 | tf_op jit(solution)/shard_map/ppermute | solution.py:483
  13.4 25.0 %collective-permute-start = (s32[4,8]{1,0:T(4,128)S(1)}, s32[4,8]{1,0:T(4,128)S(1)}, u32[]{:S(2)}, u32[]{:S(2)}) collective-permute-start(s32[4,8]{1,0:T(4,128)S(1)} %fusion.8), channel_id=1, source_target_pairs={{0,24},{8,0},{16,8},{24,16},{1,25},{9,1},{17,9},{25,17},{2,26},{10... | collective-permute-start | bytes 392 | tf_op jit(solution)/shard_map/ppermute | solution.py:482
  15.5 69.2 %copy-start.6 = (s32[8,4]{0,1:T(4,128)S(1)}, s32[8,4]{0,1:T(4,128)}, u32[]{:S(2)}) copy-start(s32[8,4]{0,1:T(4,128)} %constant.69.clone) | copy-start | bytes 388
  15.5 69.2 %copy-start.7 = (s32[8,4]{0,1:T(4,128)S(1)}, s32[8,4]{0,1:T(4,128)}, u32[]{:S(2)}) copy-start(s32[8,4]{0,1:T(4,128)} %constant.68.clone) | copy-start | bytes 388
  38.4 45.7 %collective-permute-start.3 = (s32[3,4,8]{2,0,1:T(4,128)S(1)}, s32[3,4,8]{2,0,1:T(4,128)S(1)}, u32[]{:S(2)}, u32[]{:S(2)}) collective-permute-start(s32[3,4,8]{2,0,1:T(4,128)S(1)} %pad_add_fusion), channel_id=1, source_target_pairs={{0,1},{1,2},{2,3},{3,4},{4,5},{5,6},{6,7},{7,0},{8,9},{9,10},{10,1... | collective-permute-start | bytes 1160 | tf_op jit(solution)/shard_map/ppermute | solution.py:483
  38.6 72.9 %copy-start.2 = (f32[128]{0:T(128)S(1)}, f32[128]{0:T(128)}, u32[]{:S(2)}) copy-start(f32[128]{0:T(128)} %param.15) | copy-start | bytes 1540
  39.9 44.5 %collective-permute-start.2 = (s32[3,4,8]{2,0,1:T(4,128)S(1)}, s32[3,4,8]{2,0,1:T(4,128)S(1)}, u32[]{:S(2)}, u32[]{:S(2)}) collective-permute-start(s32[3,4,8]{2,0,1:T(4,128)S(1)} %pad_add_fusion), channel_id=1, source_target_pairs={{0,7},{1,0},{2,1},{3,2},{4,3},{5,4},{6,5},{7,6},{8,15},{9,8},{10,9... | collective-permute-start | bytes 1160 | tf_op jit(solution)/shard_map/ppermute | solution.py:482
  109.4 5.7 %collective-permute-start.4 = (bf16[288,128]{1,0:T(8,128)(2,1)S(1)}, bf16[288,128]{1,0:T(8,128)(2,1)S(1)}, u32[]{:S(2)}, u32[]{:S(2)}) collective-permute-start(bf16[288,128]{1,0:T(8,128)(2,1)S(1)} %get-tuple-element.62), channel_id=1, source_target_pairs={{0,8},{8,0},{16,24},{24,16},{1,9},{9,1},{17,25},{25,17},{2,10},{10... | collective-permute-start | bytes 221192 | tf_op jit(solution)/shard_map/ppermute | solution.py:477
  109.5 6.0 %collective-permute-start.5 = (bf16[288,128]{1,0:T(8,128)(2,1)S(1)}, bf16[288,128]{1,0:T(8,128)(2,1)S(1)}, u32[]{:S(2)}, u32[]{:S(2)}) collective-permute-start(bf16[288,128]{1,0:T(8,128)(2,1)S(1)} %get-tuple-element.63), channel_id=1, source_target_pairs={{0,24},{8,16},{16,8},{24,0},{1,25},{9,17},{17,9},{25,1},{2,26},{10... | collective-permute-start | bytes 221192 | tf_op jit(solution)/shard_map/ppermute | solution.py:473
  115.6 5.6 %collective-permute-start.6 = (bf16[288,128]{1,0:T(8,128)(2,1)S(1)}, bf16[288,128]{1,0:T(8,128)(2,1)S(1)}, u32[]{:S(2)}, u32[]{:S(2)}) collective-permute-start(bf16[288,128]{1,0:T(8,128)(2,1)S(1)} %pad_maximum_fusion.2), channel_id=1, source_target_pairs={{0,7},{1,2},{2,1},{3,4},{4,3},{5,6},{6,5},{7,0},{8,15},{9,10},{10,... | collective-permute-start | bytes 221192 | tf_op jit(solution)/shard_map/ppermute | solution.py:473
  115.6 9.4 %copy-start.3 = (f32[128]{0:T(128)S(1)}, f32[128]{0:T(128)}, u32[]{:S(2)}) copy-start(f32[128]{0:T(128)} %param.17) | copy-start | bytes 1540
  115.7 5.5 %collective-permute-start.7 = (bf16[288,128]{1,0:T(8,128)(2,1)S(1)}, bf16[288,128]{1,0:T(8,128)(2,1)S(1)}, u32[]{:S(2)}, u32[]{:S(2)}) collective-permute-start(bf16[288,128]{1,0:T(8,128)(2,1)S(1)} %pad_maximum_fusion.3), channel_id=1, source_target_pairs={{0,1},{1,0},{2,3},{3,2},{4,5},{5,4},{6,7},{7,6},{8,9},{9,8},{10,11... | collective-permute-start | bytes 221192 | tf_op jit(solution)/shard_map/ppermute | solution.py:477
  122.3 6.4 %collective-permute-start.8 = (bf16[288,128]{1,0:T(8,128)(2,1)S(1)}, bf16[288,128]{1,0:T(8,128)(2,1)S(1)}, u32[]{:S(2)}, u32[]{:S(2)}) collective-permute-start(bf16[288,128]{1,0:T(8,128)(2,1)S(1)} %get-tuple-element.74), channel_id=1, source_target_pairs={{0,8},{8,0},{16,24},{24,16},{1,9},{9,1},{17,25},{25,17},{2,10},{10... | collective-permute-start | bytes 221192 | tf_op jit(solution)/shard_map/ppermute | solution.py:477
  123.6 5.3 %collective-permute-start.9 = (bf16[288,128]{1,0:T(8,128)(2,1)S(1)}, bf16[288,128]{1,0:T(8,128)(2,1)S(1)}, u32[]{:S(2)}, u32[]{:S(2)}) collective-permute-start(bf16[288,128]{1,0:T(8,128)(2,1)S(1)} %get-tuple-element.75), channel_id=1, source_target_pairs={{0,24},{8,16},{16,8},{24,0},{1,25},{9,17},{17,9},{25,1},{2,26},{10... | collective-permute-start | bytes 221192 | tf_op jit(solution)/shard_map/ppermute | solution.py:473
  128.9 5.6 %collective-permute-start.10 = (bf16[288,128]{1,0:T(8,128)(2,1)S(1)}, bf16[288,128]{1,0:T(8,128)(2,1)S(1)}, u32[]{:S(2)}, u32[]{:S(2)}) collective-permute-start(bf16[288,128]{1,0:T(8,128)(2,1)S(1)} %pad_maximum_fusion.4), channel_id=1, source_target_pairs={{0,7},{1,2},{2,1},{3,4},{4,3},{5,6},{6,5},{7,0},{8,15},{9,10},{10,... | collective-permute-start | bytes 221192 | tf_op jit(solution)/shard_map/ppermute | solution.py:473
  130.1 4.4 %collective-permute-start.11 = (bf16[288,128]{1,0:T(8,128)(2,1)S(1)}, bf16[288,128]{1,0:T(8,128)(2,1)S(1)}, u32[]{:S(2)}, u32[]{:S(2)}) collective-permute-start(bf16[288,128]{1,0:T(8,128)(2,1)S(1)} %pad_maximum_fusion.5), channel_id=1, source_target_pairs={{0,1},{1,0},{2,3},{3,2},{4,5},{5,4},{6,7},{7,6},{8,9},{9,8},{10,11... | collective-permute-start | bytes 221192 | tf_op jit(solution)/shard_map/ppermute | solution.py:477

commit v10 on v9

--- a/solution.py
+++ b/solution.py
@@ -595,7 +595,7 @@
             )
             for at, own in enumerate(sends[2:])
         )
-        third, fourth = swap_far(far, "tile"), swap_near(near, "tile")
+        fourth, third = swap_near(near, "tile"), swap_far(far, "tile")
         done = work[1](done)
         third, fourth, done = lax.optimization_barrier((third, fourth, done))
         return (first, second, fourth, third), done

time: 137 us -> 137 us (level)
  no operation moved by 1% of the time
where the time goes in v10:
time: 137 us
  waiting for transfers between devices  84 us (61%)
  Pallas kernels  24.4 us (18%)
  starting transfers between devices  23 us (17%)
  local copies, waits for them, and re-layouts  4.22 us (3%)
    ppermute x2, waiting for transfers between devices, neighbours_along(): lax.ppermute(array, axis, [(i, (i + 1) % size) for i in range(size)])  59.4 us
    all_to_all x1, waiting for transfers between devices, shards(): lax.all_to_all(ordered, AXES, split_axis=0, concat_axis=0, tiled=True)  21.8 us
    ppermute x2, starting transfers between devices, neighbours_along(): lax.ppermute(array, axis, [(i, (i - 1) % size) for i in range(size)])  7.62 us
    pallas_call x2, Pallas kernels, second(): pl.pallas_call(functools.partial(second_kernel, side, part, part[0]), in_...  7.51 us
    all_to_all x1, starting transfers between devices, shards(): lax.all_to_all(ordered, AXES, split_axis=0, concat_axis=0, tiled=True)  7.43 us
    pallas_call x2, Pallas kernels, first(): pl.pallas_call(functools.partial(first_kernel, side, part), in_specs=[vme...  7.24 us
    ppermute x4, starting transfers between devices, swap_far(): return lax.ppermute(array, axis, pairs)  4.71 us
    pallas_call x1, Pallas kernels, shards(): pl.pallas_call(gather_kernel, in_specs=[smem_spec, hbm_spec], out_specs=h...  4.15 us
  transfers between devices with their start and end apart: 13, of which 7 were waited for; matrix products, arithmetic and copies ran while one was open for 3% of the time, Pallas kernels for 11%

profile of v10, /device:TPU:0, one launch (start us, length us, event | category | flops | bytes accessed | tf_op | source)
XLA Modules:
  0.0 136.6 jit_solution(12010875784079386443)
XLA Ops:
  0.0 4.2 %order.1 = bf16[128,128,128]{2,1,0:T(8,128)(2,1)} custom-call(s32[128]{0:T(128)} %order_ref.1, bf16[128,128,128]{2,1,0:T(8,128)(2,1)} %x_ref.1), custom_call_target="tpu_custom_call" | custom-call | tf_op jit(solution)/shard_map/order/pallas_call | solution.py:498
  4.2 7.4 %all-to-all-start = ((bf16[128,128,128]{2,1,0:T(8,128)(2,1)}), bf16[128,128,128]{2,1,0:T(8,128)(2,1)}, u32[]{:S(2)}, u32[]{:S(2)}) async-start(bf16[128,128,128]{2,1,0:T(8,128)(2,1)} %order.1), calls=%async_computation | async-start | bytes 8388608 | tf_op jit(solution)/shard_map/all_to_all | solution.py:511
  11.7 1.7 %collective-permute-start.1 = (s32[4,8]{1,0:T(4,128)S(1)}, s32[4,8]{1,0:T(4,128)S(1)}, u32[]{:S(2)}, u32[]{:S(2)}) collective-permute-start(s32[4,8]{1,0:T(4,128)S(1)} %fusion.8), channel_id=1, source_target_pairs={{0,8},{8,16},{16,24},{24,0},{1,9},{9,17},{17,25},{25,1},{2,10},{10... | collective-permute-start | bytes 392 | tf_op jit(solution)/shard_map/ppermute | solution.py:483
  13.4 1.2 collective-permute-start
  14.7 0.2 copy.36
  14.9 0.2 copy.40
  15.2 0.1 pad_bitcast_fusion.1
  15.3 0.1 pad_bitcast_fusion.3
  15.6 1.1 copy.43
  16.7 21.7 %collective-permute-done.1 = s32[4,8]{1,0:T(4,128)S(1)} collective-permute-done((s32[4,8]{1,0:T(4,128)S(1)}, s32[4,8]{1,0:T(4,128)S(1)}, u32[]{:S(2)}, u32[]{:S(2)}) %collective-permute-start.1) | collective-permute-done | bytes 160 | tf_op jit(solution)/shard_map/ppermute | solution.py:483
  38.5 0.1 copy.47
  38.6 1.1 copy.39
  39.7 0.1 copy.46
  39.9 6.4 %collective-permute-start.2 = (s32[3,4,8]{2,0,1:T(4,128)S(1)}, s32[3,4,8]{2,0,1:T(4,128)S(1)}, u32[]{:S(2)}, u32[]{:S(2)}) collective-permute-start(s32[3,4,8]{2,0,1:T(4,128)S(1)} %pad_add_fusion), channel_id=1, source_target_pairs={{0,7},{1,0},{2,1},{3,2},{4,3},{5,4},{6,5},{7,6},{8,15},{9,8},{10,9... | collective-permute-start | bytes 1160 | tf_op jit(solution)/shard_map/ppermute | solution.py:482
  46.4 37.7 %collective-permute-done.3 = s32[3,4,8]{2,0,1:T(4,128)S(1)} collective-permute-done((s32[3,4,8]{2,0,1:T(4,128)S(1)}, s32[3,4,8]{2,0,1:T(4,128)S(1)}, u32[]{:S(2)}, u32[]{:S(2)}) %collective-permute-start.3) | collective-permute-done | bytes 416 | tf_op jit(solution)/shard_map/ppermute | solution.py:483
  84.4 0.1 stack.73
  85.0 21.8 %all-to-all-done = bf16[128,128,128]{2,1,0:T(8,128)(2,1)} async-done(((bf16[128,128,128]{2,1,0:T(8,128)(2,1)}), bf16[128,128,128]{2,1,0:T(8,128)(2,1)}, u32[]{:S(2)}, u32[]{:S(2)}) %all-to-all-start) | async-done | bytes 4194336 | tf_op jit(solution)/shard_map/all_to_all | solution.py:511
  106.9 2.5 %borders.1 = (bf16[2,32,4,128,128]{4,3,2,1,0:T(8,128)(2,1)S(1)}, bf16[4,8,64,128]{3,2,1,0:T(8,128)(2,1)S(1)}, bf16[288,128]{1,0:T(8,128)(2,1)S(1)}, bf16[288,128...) custom-call(s32[9,32]{1,0:T(8,128)S(1)} %pad_add_fusion.1.codes, ...), custom_call_target="tpu_custom_call" | custom-call | tf_op jit(solution)/shard_map/borders/pallas_call | solution.py:549
  109.5 2.0 %collective-permute-start.5 = (bf16[288,128]{1,0:T(8,128)(2,1)S(1)}, bf16[288,128]{1,0:T(8,128)(2,1)S(1)}, u32[]{:S(2)}, u32[]{:S(2)}) collective-permute-start(bf16[288,128]{1,0:T(8,128)(2,1)S(1)} %get-tuple-element.63), channel_id=1, source_target_pairs={{0,24},{8,16},{16,8},{24,0},{1,25},{9,17},{17,9},{25,1},{2,26},{10... | collective-permute-start | bytes 221192 | tf_op jit(solution)/shard_map/ppermute | solution.py:473
  111.5 3.6 %first.2.refs_2_ = bf16[2,32,4,128,128]{4,3,2,1,0:T(8,128)(2,1)S(1)} custom-call(bf16[512,768]{1,0:T(8,128)(2,1)S(1)} %bitcast.37, f32[1,128]{1,0:T(1,128)S(1)} %bitcast.42, bf16[2,32,4,128,128]{4,3,2,1,0:T(8,128)(2,1)S(1)} %get-tuple-element.65.refs_2_), custom_call_target="tpu_custom_call", output_to_operand_aliasing={{}: (2, {})} | custom-call | tf_op jit(solution)/shard_map/first/pallas_call | solution.py:570
  115.1 0.4 collective-permute-done.5.rest_1_
  115.7 3.6 %first.3.refs_3_ = bf16[2,32,4,128,128]{4,3,2,1,0:T(8,128)(2,1)S(1)} custom-call(bf16[512,768]{1,0:T(8,128)(2,1)S(1)} %bitcast.38, f32[1,128]{1,0:T(1,128)S(1)} %bitcast.43, bf16[2,32,4,128,128]{4,3,2,1,0:T(8,128)(2,1)S(1)} %first.2.refs_2_), custom_call_target="tpu_custom_call", output_to_operand_aliasing={{}: (2, {})} | custom-call | tf_op jit(solution)/shard_map/first/pallas_call | solution.py:570
  119.4 1.8 %collective-permute-done.6.rest_3_ = bf16[288,128]{1,0:T(8,128)(2,1)S(1)} collective-permute-done((bf16[288,128]{1,0:T(8,128)(2,1)S(1)}, bf16[288,128]{1,0:T(8,128)(2,1)S(1)}, u32[]{:S(2)}, u32[]{:S(2)}) %collective-permute-start.6) | collective-permute-done | bytes 73760 | tf_op jit(solution)/shard_map/ppermute | solution.py:473
  121.2 1.1 hidden_ring.1
  122.3 1.3 collective-permute-start.8
  123.6 1.4 %collective-permute-start.9 = (bf16[288,128]{1,0:T(8,128)(2,1)S(1)}, bf16[288,128]{1,0:T(8,128)(2,1)S(1)}, u32[]{:S(2)}, u32[]{:S(2)}) collective-permute-start(bf16[288,128]{1,0:T(8,128)(2,1)S(1)} %get-tuple-element.75), channel_id=1, source_target_pairs={{0,24},{8,16},{16,8},{24,0},{1,25},{9,17},{17,9},{25,1},{2,26},{10... | collective-permute-start | bytes 221192 | tf_op jit(solution)/shard_map/ppermute | solution.py:473
  125.1 3.6 %second.2 = (bf16[2,32,4,128,128]{4,3,2,1,0:T(8,128)(2,1)S(1)}, bf16[4,64,64,128]{3,2,1,0:T(8,128)(2,1)}, bf16[4,2,64,16,128]{4,3,2,1,0:T(8,128)(2,1)S(1)}, f32[...) custom-call(bf16[4,4,64,128]{3,2,1,0:T(8,128)(2,1)S(1)} %get-tuple-element.76.refs_0_, ...), custom_call_target="tpu_custom_call", output_to_operand_aliasing={{0}: (3, {})} | custom-call | tf_op jit(solution)/shard_map/second/pallas_call | solution.py:624
  128.7 0.1 collective-permute-done.9
  128.9 1.2 collective-permute-start.10
  130.1 3.9 %second.3 = (bf16[2,32,4,128,128]{4,3,2,1,0:T(8,128)(2,1)S(1)}, bf16[4,64,64,128]{3,2,1,0:T(8,128)(2,1)}, bf16[4,2,64,16,128]{4,3,2,1,0:T(8,128)(2,1)S(1)}, f32[...) custom-call(bf16[4,4,64,128]{3,2,1,0:T(8,128)(2,1)S(1)} %get-tuple-e, ...), custom_call_target="tpu_custom_call", output_to_operand_aliasing={{0}: (4, {}), {1}: (5, {}), {2}: (6, {}), {3}: (7, {})} | custom-call | tf_op jit(solution)/shard_map/second/pallas_call | solution.py:624
  134.0 0.5 collective-permute-done.10
  134.5 1.9 %last.1 = bf16[4,64,64,128]{3,2,1,0:T(8,128)(2,1)} custom-call(bf16[288,128]{1,0:T(8,128)(2,1)S(1)} %get-tuple-element.122.upper, bf16[288,128]{1,0:T(8,128)(2,1)S(1)} %get-tuple-element.121.lower, bf16[288,128]{1,0:T(8,128)(2,1)S(1)} %get-tuple-element.118.before, bf16[288,128]{1,0:T(8,128)(2,1)S(1)} %get-tuple-element.117.after, ...), custom_call_target="tpu_custom_call", output_to_operand_aliasing={{}: (8, {})} | custom-call | tf_op jit(solution)/shard_map/last/pallas_call | solution.py:649
  (70 shorter events, 1.7 us)
Async XLA Ops:
  4.2 7.5 %copy-start.4 = (s32[4,8]{1,0:T(4,128)S(1)}, s32[4,8]{1,0:T(4,128)}, u32[]{:S(2)}) copy-start(s32[4,8]{1,0:T(4,128)} %param.13) | copy-start | bytes 388
  4.2 7.5 %copy-start.5 = (s32[4,8]{1,0:T(4,128)S(1)}, s32[4,8]{1,0:T(4,128)}, u32[]{:S(2)}) copy-start(s32[4,8]{1,0:T(4,128)} %param.12) | copy-start | bytes 388
  4.2 10.5 %copy-start.1 = (bf16[3,3,128,128]{3,2,1,0:T(8,128)(2,1)S(1)}, bf16[3,3,128,128]{3,2,1,0:T(8,128)(2,1)}, u32[]{:S(2)}) copy-start(bf16[3,3,128,128]{3,2,1,0:T(8,128)(2,1)} %param.14) | copy-start | bytes 884740
  4.2 10.7 %copy-start = (bf16[3,3,128,128]{3,2,1,0:T(8,128)(2,1)S(1)}, bf16[3,3,128,128]{3,2,1,0:T(8,128)(2,1)}, u32[]{:S(2)}) copy-start(bf16[3,3,128,128]{3,2,1,0:T(8,128)(2,1)} %w_ref) | copy-start | bytes 884740
  4.2 102.6 %all-to-all-start = ((bf16[128,128,128]{2,1,0:T(8,128)(2,1)}), bf16[128,128,128]{2,1,0:T(8,128)(2,1)}, u32[]{:S(2)}, u32[]{:S(2)}) async-start(bf16[128,128,128]{2,1,0:T(8,128)(2,1)} %order.1), calls=%async_computation | async-start | bytes 8388608 | tf_op jit(solution)/shard_map/all_to_all | solution.py:511
  11.7 26.7 %collective-permute-start.1 = (s32[4,8]{1,0:T(4,128)S(1)}, s32[4,8]{1,0:T(4,128)S(1)}, u32[]{:S(2)}, u32[]{:S(2)}) collective-permute-start(s32[4,8]{1,0:T(4,128)S(1)} %fusion.8), channel_id=1, source_target_pairs={{0,8},{8,16},{16,24},{24,0},{1,9},{9,17},{17,25},{25,1},{2,10},{10... | collective-permute-start | bytes 392 | tf_op jit(solution)/shard_map/ppermute | solution.py:483
  13.4 25.0 %collective-permute-start = (s32[4,8]{1,0:T(4,128)S(1)}, s32[4,8]{1,0:T(4,128)S(1)}, u32[]{:S(2)}, u32[]{:S(2)}) collective-permute-start(s32[4,8]{1,0:T(4,128)S(1)} %fusion.8), channel_id=1, source_target_pairs={{0,24},{8,0},{16,8},{24,16},{1,25},{9,1},{17,9},{25,17},{2,26},{10... | collective-permute-start | bytes 392 | tf_op jit(solution)/shard_map/ppermute | solution.py:482
  15.5 69.2 %copy-start.6 = (s32[8,4]{0,1:T(4,128)S(1)}, s32[8,4]{0,1:T(4,128)}, u32[]{:S(2)}) copy-start(s32[8,4]{0,1:T(4,128)} %constant.69.clone) | copy-start | bytes 388
  15.5 69.2 %copy-start.7 = (s32[8,4]{0,1:T(4,128)S(1)}, s32[8,4]{0,1:T(4,128)}, u32[]{:S(2)}) copy-start(s32[8,4]{0,1:T(4,128)} %constant.68.clone) | copy-start | bytes 388
  38.4 45.7 %collective-permute-start.3 = (s32[3,4,8]{2,0,1:T(4,128)S(1)}, s32[3,4,8]{2,0,1:T(4,128)S(1)}, u32[]{:S(2)}, u32[]{:S(2)}) collective-permute-start(s32[3,4,8]{2,0,1:T(4,128)S(1)} %pad_add_fusion), channel_id=1, source_target_pairs={{0,1},{1,2},{2,3},{3,4},{4,5},{5,6},{6,7},{7,0},{8,9},{9,10},{10,1... | collective-permute-start | bytes 1160 | tf_op jit(solution)/shard_map/ppermute | solution.py:483
  38.6 72.9 %copy-start.2 = (f32[128]{0:T(128)S(1)}, f32[128]{0:T(128)}, u32[]{:S(2)}) copy-start(f32[128]{0:T(128)} %param.15) | copy-start | bytes 1540
  39.9 44.5 %collective-permute-start.2 = (s32[3,4,8]{2,0,1:T(4,128)S(1)}, s32[3,4,8]{2,0,1:T(4,128)S(1)}, u32[]{:S(2)}, u32[]{:S(2)}) collective-permute-start(s32[3,4,8]{2,0,1:T(4,128)S(1)} %pad_add_fusion), channel_id=1, source_target_pairs={{0,7},{1,0},{2,1},{3,2},{4,3},{5,4},{6,5},{7,6},{8,15},{9,8},{10,9... | collective-permute-start | bytes 1160 | tf_op jit(solution)/shard_map/ppermute | solution.py:482
  109.4 5.7 %collective-permute-start.4 = (bf16[288,128]{1,0:T(8,128)(2,1)S(1)}, bf16[288,128]{1,0:T(8,128)(2,1)S(1)}, u32[]{:S(2)}, u32[]{:S(2)}) collective-permute-start(bf16[288,128]{1,0:T(8,128)(2,1)S(1)} %get-tuple-element.62), channel_id=1, source_target_pairs={{0,8},{8,0},{16,24},{24,16},{1,9},{9,1},{17,25},{25,17},{2,10},{10... | collective-permute-start | bytes 221192 | tf_op jit(solution)/shard_map/ppermute | solution.py:477
  109.5 6.0 %collective-permute-start.5 = (bf16[288,128]{1,0:T(8,128)(2,1)S(1)}, bf16[288,128]{1,0:T(8,128)(2,1)S(1)}, u32[]{:S(2)}, u32[]{:S(2)}) collective-permute-start(bf16[288,128]{1,0:T(8,128)(2,1)S(1)} %get-tuple-element.63), channel_id=1, source_target_pairs={{0,24},{8,16},{16,8},{24,0},{1,25},{9,17},{17,9},{25,1},{2,26},{10... | collective-permute-start | bytes 221192 | tf_op jit(solution)/shard_map/ppermute | solution.py:473
  115.6 5.6 %collective-permute-start.6 = (bf16[288,128]{1,0:T(8,128)(2,1)S(1)}, bf16[288,128]{1,0:T(8,128)(2,1)S(1)}, u32[]{:S(2)}, u32[]{:S(2)}) collective-permute-start(bf16[288,128]{1,0:T(8,128)(2,1)S(1)} %pad_maximum_fusion.2), channel_id=1, source_target_pairs={{0,7},{1,2},{2,1},{3,4},{4,3},{5,6},{6,5},{7,0},{8,15},{9,10},{10,... | collective-permute-start | bytes 221192 | tf_op jit(solution)/shard_map/ppermute | solution.py:473
  115.6 9.4 %copy-start.3 = (f32[128]{0:T(128)S(1)}, f32[128]{0:T(128)}, u32[]{:S(2)}) copy-start(f32[128]{0:T(128)} %param.17) | copy-start | bytes 1540
  115.7 5.5 %collective-permute-start.7 = (bf16[288,128]{1,0:T(8,128)(2,1)S(1)}, bf16[288,128]{1,0:T(8,128)(2,1)S(1)}, u32[]{:S(2)}, u32[]{:S(2)}) collective-permute-start(bf16[288,128]{1,0:T(8,128)(2,1)S(1)} %pad_maximum_fusion.3), channel_id=1, source_target_pairs={{0,1},{1,0},{2,3},{3,2},{4,5},{5,4},{6,7},{7,6},{8,9},{9,8},{10,11... | collective-permute-start | bytes 221192 | tf_op jit(solution)/shard_map/ppermute | solution.py:477
  122.3 6.4 %collective-permute-start.8 = (bf16[288,128]{1,0:T(8,128)(2,1)S(1)}, bf16[288,128]{1,0:T(8,128)(2,1)S(1)}, u32[]{:S(2)}, u32[]{:S(2)}) collective-permute-start(bf16[288,128]{1,0:T(8,128)(2,1)S(1)} %get-tuple-element.74), channel_id=1, source_target_pairs={{0,8},{8,0},{16,24},{24,16},{1,9},{9,1},{17,25},{25,17},{2,10},{10... | collective-permute-start | bytes 221192 | tf_op jit(solution)/shard_map/ppermute | solution.py:477
  123.6 5.3 %collective-permute-start.9 = (bf16[288,128]{1,0:T(8,128)(2,1)S(1)}, bf16[288,128]{1,0:T(8,128)(2,1)S(1)}, u32[]{:S(2)}, u32[]{:S(2)}) collective-permute-start(bf16[288,128]{1,0:T(8,128)(2,1)S(1)} %get-tuple-element.75), channel_id=1, source_target_pairs={{0,24},{8,16},{16,8},{24,0},{1,25},{9,17},{17,9},{25,1},{2,26},{10... | collective-permute-start | bytes 221192 | tf_op jit(solution)/shard_map/ppermute | solution.py:473
  128.9 5.6 %collective-permute-start.10 = (bf16[288,128]{1,0:T(8,128)(2,1)S(1)}, bf16[288,128]{1,0:T(8,128)(2,1)S(1)}, u32[]{:S(2)}, u32[]{:S(2)}) collective-permute-start(bf16[288,128]{1,0:T(8,128)(2,1)S(1)} %pad_maximum_fusion.4), channel_id=1, source_target_pairs={{0,7},{1,2},{2,1},{3,4},{4,3},{5,6},{6,5},{7,0},{8,15},{9,10},{10,... | collective-permute-start | bytes 221192 | tf_op jit(solution)/shard_map/ppermute | solution.py:473
  130.1 4.4 %collective-permute-start.11 = (bf16[288,128]{1,0:T(8,128)(2,1)S(1)}, bf16[288,128]{1,0:T(8,128)(2,1)S(1)}, u32[]{:S(2)}, u32[]{:S(2)}) collective-permute-start(bf16[288,128]{1,0:T(8,128)(2,1)S(1)} %pad_maximum_fusion.5), channel_id=1, source_target_pairs={{0,1},{1,0},{2,3},{3,2},{4,5},{5,4},{6,7},{7,6},{8,9},{9,8},{10,11... | collective-permute-start | bytes 221192 | tf_op jit(solution)/shard_map/ppermute | solution.py:477
